TPU v7x, 32 devices: a whole 2x2x4 slice. The times are simulated.
32 devices in a mesh: ctx: 8 (over y, x, core), wa: 4 (over z).
Axes of the slice: x: 2, y: 2, z: 4, core: 2. Of those that a mesh axis runs over, the one named last changes fastest.
Arguments:
- tokens: bfloat16 [4, 1024, 1152], P('wa', 'ctx'), may hold values from -6 to 6
- out_grad: bfloat16 [4, 1024, 1152], P('wa', 'ctx'), may hold values from -6 to 6
- doc_starts: int32 [4, 4], P('wa'), may hold values from 0 to 1023, as said below
- routes: int32 [4, 1024, 1], P('wa', 'ctx'), may hold values from 0 to 3; in each aligned block of 128 rows (0 to 127, 128 to 255, ..., all dimensions but the last counted through in order) at most 64 rows name the same one
- keep_mask: int32 [4, 1024], P('wa', 'ctx'), may hold values 0 or 1
- norm_mix: bfloat16 [1152], P('wa'), may hold values from 0.5 to 1.5
- w_in: bfloat16 [1152, 4608], P(None, 'wa'), may hold values from -0.1875 to 0.1875
- conv_w: bfloat16 [4, 2304], P(None, 'wa'), may hold values from -3 to 3
- conv_b: bfloat16 [2304], P('wa'), may hold values from -3 to 3
- w_x: bfloat16 [2304, 104], P('wa'), may hold values from -0.125 to 0.125
- w_dt: bfloat16 [72, 2304], P(None, 'wa'), may hold values from -0.75 to 0.75
- dt_bias: bfloat16 [2304], P('wa'), may hold values from -4 to 0
- a_log: bfloat16 [16, 2304], P(None, 'wa'), may hold values from -9 to 0
- d_skip: bfloat16 [2304], P('wa'), may hold values from 0.5 to 1.5
- w_out: bfloat16 [2304, 1152], P('wa'), may hold values from -0.125 to 0.125
- norm_moe: bfloat16 [1152], P('wa'), may hold values from 0.5 to 1.5
- w_router: bfloat16 [1152, 4], P('wa'), may hold values from -0.1875 to 0.1875
- w_up: bfloat16 [4, 1152, 3072], P('wa', None, 'ctx'), may hold values from -0.1875 to 0.1875
- w_down: bfloat16 [4, 3072, 1152], P('wa', 'ctx'), may hold values from -0.3125 to 0.3125
Outputs:
- layer_out: float32 [4, 1024, 1152], P('wa', 'ctx')
- input_grad: float32 [4, 1024, 1152], P('wa', 'ctx')
- grad_norm_mix: float32 [1152], P('wa')
- grad_w_in: float32 [1152, 4608], P(None, 'wa')
- grad_conv_w: float32 [4, 2304], P(None, 'wa')
- grad_conv_b: float32 [2304], P('wa')
- grad_w_x: float32 [2304, 104], P('wa')
- grad_w_dt: float32 [72, 2304], P(None, 'wa')
- grad_dt_bias: float32 [2304], P('wa')
- grad_a_log: float32 [16, 2304], P(None, 'wa')
- grad_d_skip: float32 [2304], P('wa')
- grad_w_out: float32 [2304, 1152], P('wa')
- grad_norm_moe: float32 [1152], P('wa')
- grad_w_router: float32 [1152, 4], P('wa')
- grad_w_up: float32 [4, 1152, 3072], P('wa', None, 'ctx')
- grad_w_down: float32 [4, 3072, 1152], P('wa', 'ctx')
- rms_stats: float32 [4, 3], P('wa')
Inputs may be any that keep to these rules, and one draw needn't show every extreme that they name: `doc_starts`: each row holds 4 strictly ascending document starts, the first 0. `routes`: in each aligned block of 128 positions of a stream (the tokens of one device), no expert is named by more than 64 tokens.
All inputs are finite; a program needn't handle non-finite values. No bound on the sum of `keep_mask` on one device may be relied on, other than what follows from the above.
Results may differ from a plain program's by a relative error of at most 0.018.
Values may be sent and summed in bfloat16 or wider, within the bound.
A program may use at most 256 MiB of HBM per device.

v0:
```python
import math

import jax
import jax.numpy as jnp
from jax import lax
from jax.sharding import PartitionSpec as P

EPS = 1e-05


def passed_along(array, axis, by):
    length = lax.axis_size(axis)
    pairs = [(i, i + by) for i in range(length) if 0 <= i + by < length]
    return lax.ppermute(array, axis, pairs)


def entering(part, axis, combine, identity, reverse):
    count = lax.axis_size(axis)
    place = lax.axis_index(axis)
    ahead = count - 1 - place if reverse else place
    gathered = jax.tree.map(lambda a: lax.all_gather(a, axis), part)
    state = jax.tree.map(lambda a, e: jnp.zeros_like(a) + jnp.asarray(e, a.dtype), part, identity)

    def one(lap, state):
        source = count - 1 - lap if reverse else lap
        return combine(
            state, jax.tree.map(lambda a: lax.dynamic_index_in_dim(a, source, 0, False), gathered)
        )

    return lax.fori_loop(0, ahead, one, state)


def normed(values, gain):
    scale = lax.rsqrt(jnp.mean(values * values, axis=-1, keepdims=True) + EPS)
    return values * scale * gain


def affine(former, latter):
    return (former[0] * latter[0], latter[0] * former[1] + latter[1])


def body(
    tokens,
    out_grad,
    doc_starts,
    routes,
    keep_mask,
    norm_mix,
    w_in,
    conv_w,
    conv_b,
    w_x,
    w_dt,
    dt_bias,
    a_log,
    d_skip,
    w_out,
    norm_moe,
    w_router,
    w_up,
    w_down,
):
    gathered = (
        lax.all_gather(norm_mix, "wa", axis=0, tiled=True),
        lax.all_gather(w_in, "wa", axis=1, tiled=True),
        lax.all_gather(conv_w, "wa", axis=1, tiled=True),
        lax.all_gather(conv_b, "wa", axis=0, tiled=True),
        lax.all_gather(w_x, "wa", axis=0, tiled=True),
        lax.all_gather(w_dt, "wa", axis=1, tiled=True),
        lax.all_gather(dt_bias, "wa", axis=0, tiled=True),
        lax.all_gather(a_log, "wa", axis=1, tiled=True),
        lax.all_gather(d_skip, "wa", axis=0, tiled=True),
        lax.all_gather(w_out, "wa", axis=0, tiled=True),
        lax.all_gather(norm_moe, "wa", axis=0, tiled=True),
        lax.all_gather(w_router, "wa", axis=0, tiled=True),
    )
    gain_mix = gathered[0].astype(jnp.float32)
    proj_in = gathered[1]
    conv_taps = gathered[2].astype(jnp.float32)
    conv_bias = gathered[3].astype(jnp.float32)
    proj_x = gathered[4]
    proj_dt = gathered[5]
    step_bias = gathered[6].astype(jnp.float32)
    decay_log = gathered[7].astype(jnp.float32)
    skip_gain = gathered[8].astype(jnp.float32)
    proj_out = gathered[9]
    gain_moe = gathered[10].astype(jnp.float32)
    router = gathered[11]
    expert_up, expert_down = (
        lax.all_gather(w_up, "ctx", axis=2, tiled=True),
        lax.all_gather(w_down, "ctx", axis=1, tiled=True),
    )
    stream = tokens[0].astype(jnp.float32)
    length = stream.shape[0]
    inner = proj_in.shape[1] // 2
    states = decay_log.shape[0]
    ranked = proj_dt.shape[0]
    taps = conv_taps.shape[0]
    place = lax.axis_index("ctx") * length + lax.iota(jnp.int32, length)
    starts = doc_starts[0]
    resets = jnp.any(place[:, None] == starts[None, :], axis=1)
    keeps = 1.0 - resets.astype(jnp.float32)
    lag_keep = [jnp.ones((length,), jnp.float32)]
    for offset in range(1, taps):
        cut = jnp.any(
            (starts[None, :] > place[:, None] - offset) & (starts[None, :] <= place[:, None]),
            axis=1,
        )
        lag_keep.append(1.0 - cut.astype(jnp.float32))
    normed_mix = normed(stream, gain_mix).astype(jnp.bfloat16)
    joined = jnp.dot(normed_mix, proj_in, preferred_element_type=jnp.float32).astype(jnp.bfloat16)
    x_inner = joined[:, :inner]
    gate_z = joined[:, inner:].astype(jnp.float32)
    edge = passed_along(x_inner[length - (taps - 1) :], "ctx", 1)
    extended = jnp.concatenate([edge, x_inner], axis=0).astype(jnp.float32)
    pre_conv = conv_bias + jnp.zeros((length, inner), jnp.float32)
    for offset in range(taps):
        window = extended[taps - 1 - offset : taps - 1 - offset + length]
        pre_conv = pre_conv + conv_taps[offset] * window * lag_keep[offset][:, None]
    mixed_in = jax.nn.silu(pre_conv).astype(jnp.bfloat16)
    mixed_f = mixed_in.astype(jnp.float32)
    projected = jnp.dot(mixed_in, proj_x, preferred_element_type=jnp.float32).astype(jnp.bfloat16)
    dt_low = projected[:, :ranked]
    b_sel = projected[:, ranked : ranked + states].astype(jnp.float32)
    c_sel = projected[:, ranked + states :].astype(jnp.float32)
    step_pre = jnp.dot(dt_low, proj_dt, preferred_element_type=jnp.float32) + step_bias
    step_size = jax.nn.softplus(step_pre)
    a_mat = -jnp.exp(decay_log)
    block = math.gcd(64, length)
    count = length // block

    def blocked(array):
        return array.reshape((count, block) + array.shape[1:])

    ones_state = jnp.ones((states, inner), jnp.float32)
    zero_state = jnp.zeros((states, inner), jnp.float32)

    def decay_of(step_t, keep_t):
        return jnp.exp(step_t[None, :] * a_mat) * keep_t

    def summary_step(carried, pieces):
        step_t, input_t, b_t, keep_t = pieces
        decay_t = decay_of(step_t, keep_t)
        return (
            (
                carried[0] * decay_t,
                decay_t * carried[1] + b_t[:, None] * (step_t * input_t)[None, :],
            ),
            None,
        )

    flat_in = (step_size, mixed_f, b_sel, keeps)
    (through, local_state), _ = lax.scan(summary_step, (ones_state, zero_state), flat_in)
    _, incoming = entering((through, local_state), "ctx", affine, (ones_state, zero_state), False)

    def output_token(state, pieces):
        step_t, input_t, b_t, keep_t, c_t = pieces
        state = decay_of(step_t, keep_t) * state + b_t[:, None] * (step_t * input_t)[None, :]
        return (state, jnp.sum(c_t[:, None] * state, axis=0))

    def output_block(state, pieces):
        final, outputs = lax.scan(output_token, state, pieces)
        return (final, (outputs, state))

    scan_in = (blocked(step_size), blocked(mixed_f), blocked(b_sel), blocked(keeps), blocked(c_sel))
    _, (scanned, block_starts) = lax.scan(output_block, incoming, scan_in)
    y_full = scanned.reshape(length, inner) + skip_gain * mixed_f
    silu_z, silu_back = jax.vjp(jax.nn.silu, gate_z)
    gated = (y_full * silu_z).astype(jnp.bfloat16)
    mix = jnp.dot(gated, proj_out, preferred_element_type=jnp.float32)
    after_mix = stream + mix
    normed_moe = normed(after_mix, gain_moe).astype(jnp.bfloat16)
    logits = jnp.dot(normed_moe, router, preferred_element_type=jnp.float32)
    experts = logits.shape[1]
    route = routes[0, :, 0]
    onehot = route[:, None] == lax.iota(jnp.int32, experts)[None, :]
    onehot_f = onehot.astype(jnp.float32)
    sigmoid_pick = jax.nn.sigmoid(jnp.sum(logits * onehot_f, axis=1))
    kept = keep_mask[0].astype(jnp.float32)
    gates = kept * sigmoid_pick
    onehot_i = onehot.astype(jnp.int32)
    before = jnp.cumsum(onehot_i, axis=0) - onehot_i
    within = jnp.sum(before * onehot_i, axis=1)
    capacity = length // 2
    slot = route * capacity + within
    slot_count = experts * capacity
    match = slot[None, :] == lax.iota(jnp.int32, slot_count)[:, None]
    filled_b = jnp.any(match, axis=1).astype(jnp.bfloat16)[:, None]
    source = jnp.sum(match.astype(jnp.int32) * lax.iota(jnp.int32, length)[None, :], axis=1)
    group = lax.axis_size("wa")
    layout = (group, experts // group, capacity, normed_moe.shape[1])
    sent = (normed_moe[source] * filled_b).reshape(layout)
    arrived = lax.all_to_all(sent, "wa", split_axis=0, concat_axis=0, tiled=True)
    hidden_pre = jnp.einsum(
        "skcd,kdf->skcf", arrived, expert_up, preferred_element_type=jnp.float32
    )
    activated, gelu_back = jax.vjp(jax.nn.gelu, hidden_pre)
    activated = activated.astype(jnp.bfloat16)
    produced = jnp.einsum(
        "skcf,kfd->skcd", activated, expert_down, preferred_element_type=jnp.float32
    ).astype(jnp.bfloat16)
    returned = lax.all_to_all(produced, "wa", split_axis=0, concat_axis=0, tiled=True).reshape(
        slot_count, -1
    )
    expert_rows = returned[slot].astype(jnp.float32)
    moe = gates[:, None] * expert_rows
    result = after_mix + moe
    sums = jnp.stack([jnp.sum(result * result), jnp.sum(mix * mix), jnp.sum(moe * moe)])
    upstream = out_grad[0].astype(jnp.float32)
    d_rows = (gates[:, None] * upstream).astype(jnp.bfloat16)
    d_slots = (d_rows[source] * filled_b).reshape(layout)
    d_back = lax.all_to_all(d_slots, "wa", split_axis=0, concat_axis=0, tiled=True)
    d_gate = jnp.sum(expert_rows * upstream, axis=1)
    d_pick = d_gate * kept * sigmoid_pick * (1.0 - sigmoid_pick)
    d_logits = (onehot_f * d_pick[:, None]).astype(jnp.bfloat16)
    grad_router = jnp.einsum("td,te->de", normed_moe, d_logits, preferred_element_type=jnp.float32)
    d_act = jnp.einsum("skcd,kfd->skcf", d_back, expert_down, preferred_element_type=jnp.float32)
    d_pre = gelu_back(d_act)[0].astype(jnp.bfloat16)
    grad_down = jnp.einsum("skcf,skcd->kfd", activated, d_back, preferred_element_type=jnp.float32)
    grad_up = jnp.einsum("skcd,skcf->kdf", arrived, d_pre, preferred_element_type=jnp.float32)
    d_sent = jnp.einsum(
        "skcf,kdf->skcd", d_pre, expert_up, preferred_element_type=jnp.float32
    ).astype(jnp.bfloat16)
    d_came = lax.all_to_all(d_sent, "wa", split_axis=0, concat_axis=0, tiled=True).reshape(
        slot_count, -1
    )
    share_up, share_down = (
        lax.psum_scatter(
            grad_up.astype(jnp.bfloat16), "ctx", scatter_dimension=2, tiled=True
        ).astype(jnp.float32),
        lax.psum_scatter(
            grad_down.astype(jnp.bfloat16), "ctx", scatter_dimension=1, tiled=True
        ).astype(jnp.float32),
    )
    d_normed = d_came[slot].astype(jnp.float32) + jnp.einsum(
        "te,de->td", d_logits, router, preferred_element_type=jnp.float32
    )
    _, moe_norm_back = jax.vjp(normed, after_mix, gain_moe)
    d_after_norm, grad_gain_moe = moe_norm_back(d_normed)
    d_after = upstream + d_after_norm
    d_mix = d_after.astype(jnp.bfloat16)
    grad_proj_out = jnp.einsum("td,te->de", gated, d_mix, preferred_element_type=jnp.float32)
    d_gated = jnp.einsum("te,de->td", d_mix, proj_out, preferred_element_type=jnp.float32)
    d_y = d_gated * silu_z
    d_z = silu_back(d_gated * y_full)[0]
    grad_skip = jnp.sum(d_y * mixed_f, axis=0)

    def summary_back(carried, pieces):
        step_t, keep_t, c_t, dy_t = pieces
        d_state = c_t[:, None] * dy_t[None, :] + carried
        return (decay_of(step_t, keep_t) * d_state, None)

    local_grad, _ = lax.scan(summary_back, zero_state, (step_size, keeps, c_sel, d_y), reverse=True)
    _, outgoing = entering((through, local_grad), "ctx", affine, (ones_state, zero_state), True)

    def prior_token(state, pieces):
        step_t, input_t, b_t, keep_t = pieces
        return (
            decay_of(step_t, keep_t) * state + b_t[:, None] * (step_t * input_t)[None, :],
            state,
        )

    def grad_token(carried, pieces):
        flowing, grad_a = carried
        step_t, input_t, b_t, keep_t, c_t, dy_t, prior = pieces
        decay_t = decay_of(step_t, keep_t)
        drive_in = step_t * input_t
        hidden = decay_t * prior + b_t[:, None] * drive_in[None, :]
        d_state = c_t[:, None] * dy_t[None, :] + flowing
        grad_c = jnp.sum(hidden * dy_t[None, :], axis=1)
        grad_b = jnp.sum(d_state * drive_in[None, :], axis=1)
        d_drive = jnp.sum(d_state * b_t[:, None], axis=0)
        d_log = d_state * prior * decay_t
        d_step = jnp.sum(d_log * a_mat, axis=0) + d_drive * input_t
        grad_a = grad_a + d_log * step_t[None, :]
        return ((decay_t * d_state, grad_a), (grad_b, grad_c, d_step, d_drive * step_t))

    def grad_block(carried, pieces):
        step_blk, input_blk, b_blk, keep_blk, c_blk, dy_blk, start_blk = pieces
        _, priors = lax.scan(prior_token, start_blk, (step_blk, input_blk, b_blk, keep_blk))
        carried, outputs = lax.scan(
            grad_token,
            carried,
            (step_blk, input_blk, b_blk, keep_blk, c_blk, dy_blk, priors),
            reverse=True,
        )
        return (carried, outputs)

    (_, grad_a_total), (grad_b, grad_c, d_step, d_input) = lax.scan(
        grad_block, (outgoing, zero_state), scan_in + (blocked(d_y), block_starts), reverse=True
    )
    grad_b = grad_b.reshape(length, states)
    grad_c = grad_c.reshape(length, states)
    d_step = d_step.reshape(length, inner)
    d_input = d_input.reshape(length, inner)
    d_step_pre = d_step * jax.nn.sigmoid(step_pre)
    grad_step_bias = jnp.sum(d_step_pre, axis=0)
    d_proj_dt = d_step_pre.astype(jnp.bfloat16)
    grad_proj_dt = jnp.einsum("tr,td->rd", dt_low, d_proj_dt, preferred_element_type=jnp.float32)
    d_dt_low = jnp.einsum("td,rd->tr", d_proj_dt, proj_dt, preferred_element_type=jnp.float32)
    d_projected = jnp.concatenate([d_dt_low, grad_b, grad_c], axis=1).astype(jnp.bfloat16)
    grad_proj_x = jnp.einsum("td,tx->dx", mixed_in, d_projected, preferred_element_type=jnp.float32)
    d_mixed = (
        jnp.einsum("tx,dx->td", d_projected, proj_x, preferred_element_type=jnp.float32)
        + d_input
        + d_y * skip_gain
    )
    grad_decay_log = grad_a_total * a_mat
    _, conv_back = jax.vjp(jax.nn.silu, pre_conv)
    d_pre_conv = conv_back(d_mixed)[0]
    grad_conv_bias = jnp.sum(d_pre_conv, axis=0)
    tap_grads = []
    d_extended = jnp.zeros((length + taps - 1, inner), jnp.float32)
    for offset in range(taps):
        window = extended[taps - 1 - offset : taps - 1 - offset + length]
        weighted = d_pre_conv * lag_keep[offset][:, None]
        tap_grads.append(jnp.sum(weighted * window, axis=0))
        d_extended = d_extended + jnp.pad(
            weighted * conv_taps[offset], ((taps - 1 - offset, offset), (0, 0))
        )
    grad_conv_taps = jnp.stack(tap_grads, axis=0)
    came_edge = passed_along(d_extended[: taps - 1], "ctx", -1)
    d_inner = d_extended[taps - 1 :] + jnp.pad(came_edge, ((length - (taps - 1), 0), (0, 0)))
    d_joined = jnp.concatenate([d_inner, d_z], axis=1).astype(jnp.bfloat16)
    grad_proj_in = jnp.einsum("td,tf->df", normed_mix, d_joined, preferred_element_type=jnp.float32)
    d_normed_mix = jnp.einsum("tf,df->td", d_joined, proj_in, preferred_element_type=jnp.float32)
    _, mix_norm_back = jax.vjp(normed, stream, gain_mix)
    d_stream, grad_gain_mix = mix_norm_back(d_normed_mix)
    input_grad = d_after + d_stream
    denom = length * lax.axis_size("ctx") * stream.shape[1]
    position = lax.axis_index("wa")
    stat_rows = (lax.iota(jnp.int32, group) == position).astype(jnp.float32)[:, None] * sums[
        None, :
    ]
    totals = lax.psum(
        (
            grad_gain_mix,
            grad_proj_in,
            grad_conv_taps,
            grad_conv_bias,
            grad_proj_x,
            grad_proj_dt,
            grad_step_bias,
            grad_decay_log,
            grad_skip,
            grad_proj_out,
            grad_gain_moe,
            grad_router,
            stat_rows,
        ),
        ("ctx", "wa"),
    )
    split_dims = (0, 1, 1, 0, 0, 1, 0, 1, 0, 0, 0, 0)
    shares = [
        lax.dynamic_slice_in_dim(
            summed,
            position * (summed.shape[axis_dim] // group),
            summed.shape[axis_dim] // group,
            axis_dim,
        )
        for summed, axis_dim in zip(totals[:12], split_dims)
    ]
    stat_sums = lax.dynamic_slice_in_dim(totals[12], position, 1, 0)
    rms_stats = jnp.sqrt(stat_sums / denom)
    return (
        result[None],
        input_grad[None],
        shares[0],
        shares[1],
        shares[2],
        shares[3],
        shares[4],
        shares[5],
        shares[6],
        shares[7],
        shares[8],
        shares[9],
        shares[10],
        shares[11],
        share_up,
        share_down,
        rms_stats,
    )


def solution(mesh):
    placed = (
        P("wa", "ctx", None),
        P("wa", "ctx", None),
        P("wa", None),
        P("wa", "ctx", None),
        P("wa", "ctx"),
        P("wa"),
        P(None, "wa"),
        P(None, "wa"),
        P("wa"),
        P("wa", None),
        P(None, "wa"),
        P("wa"),
        P(None, "wa"),
        P("wa"),
        P("wa", None),
        P("wa"),
        P("wa", None),
        P("wa", None, "ctx"),
        P("wa", "ctx", None),
    )
    return jax.shard_map(
        body,
        mesh=mesh,
        in_specs=placed,
        out_specs=(
            P("wa", "ctx", None),
            P("wa", "ctx", None),
            P("wa"),
            P(None, "wa"),
            P(None, "wa"),
            P("wa"),
            P("wa", None),
            P(None, "wa"),
            P("wa"),
            P(None, "wa"),
            P("wa"),
            P("wa", None),
            P("wa"),
            P("wa", None),
            P("wa", None, "ctx"),
            P("wa", "ctx", None),
            P("wa", None),
        ),
        check_vma=False,
    )
```

profile of v0, /device:TPU:11, one launch (start us, length us, event | category | flops | bytes accessed | tf_op | source)
XLA Modules:
  0.0 3494.1 jit_solution(14665816258455780318)
XLA Ops:
  38.7 20.1 all-gather.6
  58.9 18.9 all-gather.5
  77.9 25.9 all-gather.4
  105.9 104.5 %all-gather.16.cloned.1.call-done = bf16[1152,4608]{1,0:T(8,128)(2,1)} async-done(((bf16[1152,1152]{1,0:T(8,128)(2,1)}), bf16[1152,4608]{1,0:T(8,128)(2,1)}) %all-gather.16.cloned.1.call-update) | async-done | bytes 10616848 | tf_op jit(solution)/shard_map/all_gather | solution.py:65
  230.1 294.9 %while.199 = (s32[]{:T(128)}, f32[16,2304]{1,0:T(8,128)S(1)}, f32[16,2304]{1,0:T(8,128)S(1)}, f32[128,2304]{1,0:T(8,128)S(1)}, f32[16,2304]{1,0:T(8,128)S(1)}, /...) while((s32[]{:T(128)}, f32[16,2304]{1,0:T(8,128)S(1)}, ...), condition=%wide.region_6.7_spmd.clone, body=%wide.region_5.6_spmd.clone.sunk | while | flops 297219 | bytes 792911 | solution.py:153
  532.1 17.8 all-gather.26.cloned.1.call-done
  549.9 26.6 all-gather.24.cloned.1.call-done
  580.8 398.5 %while.194 = (s32[]{:T(128)}, f32[16,2304]{1,0:T(8,128)S(1)}, f32[2,64,2304]{2,1,0:T(8,128)}, f32[2,16,2304]{2,1,0:T(8,128)}, f32[2,64,2304]{2,1,0:T(8,128)S(1)}...) while((s32[]{:T(128)}, f32[16,2304]{1,0:T(8,128)S(1)}, ...), condition=%wide.region_13.14_spmd, body=%wide.region_9.13_spmd.sunk | while | flops 258052 | bytes 4465026 | solution.py:166
  584.5 194.7 %while.201 = (s32[]{:T(128)}, f32[16,2304]{1,0:T(8,128)S(1)}, f32[64,2304]{1,0:T(8,128)S(1)}, f32[64,2304]{1,0:T(8,128)S(1)}, f32[16,2304]{1,0:T(8,128)S(1)}, /*...) while((s32[]{:T(128)}, f32[16,2304]{1,0:T(8,128)S(1)}, ...), condition=%wide.region_12.12_spmd, body=%wide.region_10.11_spmd.sunk | while | flops 258050 | bytes 544273 | solution.py:162
  783.9 194.5 %while.201 = (s32[]{:T(128)}, f32[16,2304]{1,0:T(8,128)S(1)}, f32[64,2304]{1,0:T(8,128)S(1)}, f32[64,2304]{1,0:T(8,128)S(1)}, f32[16,2304]{1,0:T(8,128)S(1)}, /*...) while((s32[]{:T(128)}, f32[16,2304]{1,0:T(8,128)S(1)}, ...), condition=%wide.region_12.12_spmd, body=%wide.region_10.11_spmd.sunk | while | flops 258050 | bytes 544273 | solution.py:162
  1027.5 17.7 all-gather.7
  1051.3 17.2 all_to_all.20
  1112.3 379.9 %while.200 = (s32[]{:T(128)}, f32[16,2304]{1,0:T(8,128)S(1)}, f32[128,2304]{1,0:T(8,128)S(1)}, f32[16,2304]{1,0:T(8,128)S(1)}, f32[128]{0:T(128)S(1)}, /*index=5...) while((s32[]{:T(128)}, f32[16,2304]{1,0:T(8,128)S(1)}, ...), condition=%wide.region_23.24_spmd.clone, body=%wide.region_22.23_spmd.clone.sunk | while | flops 221188 | bytes 498011 | solution.py:253
  1496.3 27.8 all-gather.28.cloned.1.call-done
  1532.0 1005.7 %while.198 = (s32[]{:T(128)}, f32[16,2304]{1,0:T(8,128)S(1)}, f32[16,2304]{1,0:T(8,128)S(1)}, bf16[2,64,16]{2,1,0:T(8,128)(2,1)}, bf16[2,64,16]{2,1,0:T(8,128)(2...) while((s32[]{:T(128)}, f32[16,2304]{1,0:T(8,128)S(1)}, ...), condition=%wide.region_35.36_spmd, body=%wide.region_26.35_spmd.sunk | while | flops 928488 | bytes 11678855 | solution.py:289
  1537.5 132.9 %while.202 = (s32[]{:T(128)}, f32[16,2304]{1,0:T(8,128)S(1)}, f32[64,16,2304]{2,1,0:T(8,128)}, f32[64,2304]{1,0:T(8,128)S(1)}, f32[16,2304]{1,0:T(8,128)S(1)}, /...) while((s32[]{:T(128)}, f32[16,2304]{1,0:T(8,128)S(1)}, ...), condition=%wide.region_28.28_spmd, body=%wide.region_27.27_spmd.sunk | while | flops 186626 | bytes 792897 | solution.py:280
  1671.3 361.8 %while.203 = (s32[]{:T(128)}, f32[16,2304]{1,0:T(8,128)S(1)}, f32[16,2304]{1,0:T(8,128)S(1)}, bf16[64,16]{1,0:T(8,128)(2,1)S(1)}, bf16[64,16]{1,0:T(8,128)(2,1)S...) while((s32[]{:T(128)}, f32[16,2304]{1,0:T(8,128)S(1)}, ...), condition=%wide.region_34.34_spmd, body=%wide.region_29.33_spmd.sunk | while | flops 741859 | bytes 1079073 | solution.py:281
  2040.3 132.9 %while.202 = (s32[]{:T(128)}, f32[16,2304]{1,0:T(8,128)S(1)}, f32[64,16,2304]{2,1,0:T(8,128)}, f32[64,2304]{1,0:T(8,128)S(1)}, f32[16,2304]{1,0:T(8,128)S(1)}, /...) while((s32[]{:T(128)}, f32[16,2304]{1,0:T(8,128)S(1)}, ...), condition=%wide.region_28.28_spmd, body=%wide.region_27.27_spmd.sunk | while | flops 186626 | bytes 792897 | solution.py:280
  2174.1 361.8 %while.203 = (s32[]{:T(128)}, f32[16,2304]{1,0:T(8,128)S(1)}, f32[16,2304]{1,0:T(8,128)S(1)}, bf16[64,16]{1,0:T(8,128)(2,1)S(1)}, bf16[64,16]{1,0:T(8,128)(2,1)S...) while((s32[]{:T(128)}, f32[16,2304]{1,0:T(8,128)S(1)}, ...), condition=%wide.region_34.34_spmd, body=%wide.region_29.33_spmd.sunk | while | flops 741859 | bytes 1079073 | solution.py:281
  2563.2 30.2 copy.120
  2631.5 182.7 %all-reduce.16.cloned.1.call-done = (f32[1152]{0:T(1024)}, f32[4,2304]{1,0:T(4,128)}, f32[2304]{0:T(1024)}, f32[2304]{0:T(1024)}, f32[2304]{0:T(1024)}, /*index=...) async-done(((f32[1152]{0:T(1024)}, f32[4,2304]{1,0:T(4,128)}, f32[2304]{0:T(1024)}, f32[2304]{0:T(1024)}, f32[2304]{0:T(1024)}, /*index=5*/f32[1152]{0:T(1024)}, ...) | async-done | bytes 92224 | tf_op jit(solution)/shard_map/psum | solution.py:335
  2824.8 61.3 %reduce-scatter.7.cloned.1.call-done = bf16[384,1152]{1,0:T(8,128)(2,1)} async-done(((bf16[3072,1152]{1,0:T(8,128)(2,1)}), bf16[384,1152]{1,0:T(8,128)(2,1)}) %reduce-scatter.7.cloned.1.call-update) | async-done | bytes 884752
  2891.5 63.5 %reduce-scatter.5.cloned.1.call-done = bf16[1,384,1152]{2,1,0:T(8,128)(2,1)} async-done(((bf16[1,3072,1152]{2,1,0:T(8,128)(2,1)}), bf16[1,384,1152]{2,1,0:T(8,128)(2,1)}) %reduce-scatter.5.cloned.1.call-update) | async-done | bytes 884752 | tf_op jit(solution)/shard_map/reduce_scatter | solution.py:231
  2957.5 515.9 %all-reduce.18.cloned.1.call-done = (f32[1152,4608]{1,0:T(8,128)}, f32[2304,104]{0,1:T(8,128)}, f32[72,2304]{1,0:T(8,128)}, f32[16,2304]{1,0:T(8,128)}, f32[2304,1152]{1,0:T(8,128)}) async-done(((f32[1152,4608]{1,0:T(8,128)}, f32[2304,104]{0,1:T(8,128)}, f32[72,2304]{1,0:T(8,128)}, f32[16,2304]{1,0:T(8,128)}, f32[2304,1152]{1,0:T(8,128)}), (f32[1152,4608]{1,0:T(8,128)}, f32[2304,104]{0,1:T(8,128)}, ...) | async-done | bytes 33619984 | tf_op jit(solution)/shard_map/psum | solution.py:335
  (4034 shorter events, 2334.6 us)
Async XLA Ops:
  7.3 51.5 %copy-start.88 = (s32[1,4]{1,0:T(1,128)S(1)}, s32[1,4]{1,0:T(1,128)}, u32[]{:S(2)}) copy-start(s32[1,4]{1,0:T(1,128)} %param.39) | copy-start | bytes 52
  7.3 51.6 %copy-start.45 = (bf16[72,576]{1,0:T(8,128)(2,1)S(1)}, bf16[72,576]{1,0:T(8,128)(2,1)}, u32[]{:S(2)}) copy-start(bf16[72,576]{1,0:T(8,128)(2,1)} %param.47) | copy-start | bytes 248836
  7.3 70.5 %copy-start.3 = (bf16[1,128,1152]{2,1,0:T(8,128)(2,1)S(1)}, bf16[1,128,1152]{2,1,0:T(8,128)(2,1)}, u32[]{:S(2)}) copy-start(bf16[1,128,1152]{2,1,0:T(8,128)(2,1)} %param.37) | copy-start | bytes 884740
  7.3 203.2 %all-gather.16.cloned.1.call-start = ((), (), s32[]{:S(2)}) async-start(), calls=%async_computation.6 | async-start | bytes 13271040 | tf_op jit(solution)/shard_map/all_gather | solution.py:65
  8.0 69.9 %copy-start.40 = (bf16[576,104]{0,1:T(8,128)(2,1)S(1)}, bf16[576,104]{0,1:T(8,128)(2,1)}, u32[]{:S(2)}) copy-start(bf16[576,104]{0,1:T(8,128)(2,1)} %param.46) | copy-start | bytes 359428
  8.1 541.8 %all-gather.26.cloned.1.call-start = ((), (), s32[]{:S(2)}) async-start(), calls=%async_computation.12 | async-start | bytes 1327104 | tf_op jit(solution)/shard_map/all_gather | solution.py:21
  24.0 192.3 %copy-start.36 = (f32[1152]{0:T(1024)}, f32[1152]{0:T(1024)S(1)}, u32[]{:S(2)}) copy-start(f32[1152]{0:T(1024)S(1)} %convert_element_type.209) | copy-start | bytes 13828
  77.9 138.4 %copy-start.78 = (f32[128]{0:T(128)}, f32[128]{0:T(128)S(1)}, u32[]{:S(2)}) copy-start(f32[128]{0:T(128)S(1)} %fusion.83) | copy-start | bytes 1540
  217.0 6.6 collective-permute-start
  525.7 50.8 %all-gather.24.cloned.1.call-start = ((), (), s32[]{:S(2)}) async-start(), calls=%async_computation.11 | async-start | bytes 1327104 | tf_op jit(solution)/shard_map/all_gather | solution.py:21
  526.4 455.6 %all-gather.18.cloned.1.call-start = ((), (), s32[]{:S(2)}) async-start(), calls=%async_computation.7 | async-start | bytes 6635520 | tf_op jit(solution)/shard_map/all_gather | solution.py:73
  527.0 466.3 %all-gather.20.cloned.1.call-start = ((), (), s32[]{:S(2)}) async-start(), calls=%async_computation.8 | async-start | bytes 7962624 | tf_op jit(solution)/shard_map/all_gather | solution.py:90
  527.6 486.2 %all-gather.22.cloned.1.call-start = ((), (), s32[]{:S(2)}) async-start(), calls=%async_computation.9 | async-start | bytes 7962624 | tf_op jit(solution)/shard_map/all_gather | solution.py:91
  528.7 47.8 %copy-start.89 = (s32[128]{0:T(128)}, s32[128]{0:T(128)S(1)}, u32[]{:S(2)}) copy-start(s32[128]{0:T(128)S(1)} %select_reduce_fusion.1) | copy-start | bytes 1540
  988.8 18.0 all-to-all-start
  1021.0 25.1 all-to-all-start.1
  1081.8 17.1 all-to-all-start.3
  1087.1 437.1 %all-gather.28.cloned.1.call-start = ((), (), s32[]{:S(2)}) async-start(), calls=%async_computation.13 | async-start | bytes 1327104 | tf_op jit(solution)/shard_map/all_gather | solution.py:21
  1112.3 380.6 %copy-start.64 = (bf16[128]{0:T(256)(128)(2,1)S(1)}, bf16[128]{0:T(256)(128)(2,1)}, u32[]{:S(2)}) copy-start(bf16[128]{0:T(256)(128)(2,1)} %fusion.119) | copy-start | bytes 772
  1492.8 1321.3 %all-reduce.16.cloned.1.call-start = ((), (), s32[]{:S(2)}) async-start(), calls=%async_computation.15 | async-start | bytes 221184 | tf_op jit(solution)/shard_map/psum | solution.py:335
  2546.1 6.3 collective-permute-start.1
  2556.6 329.5 %reduce-scatter.7.cloned.1.call-start = ((), (), s32[]{:S(2)}) async-start(), calls=%async_computation.14 | async-start | bytes 7962624
  2602.5 352.5 %reduce-scatter.5.cloned.1.call-start = ((), (), s32[]{:S(2)}) async-start(), calls=%async_computation.10 | async-start | bytes 7962624 | tf_op jit(solution)/shard_map/reduce_scatter | solution.py:231
  2611.2 862.2 %all-reduce.18.cloned.1.call-start = ((), (), s32[]{:S(2)}) async-start(), calls=%async_computation.16 | async-start | bytes 67239936 | tf_op jit(solution)/shard_map/psum | solution.py:335
  (102 other events, 436.4 us)
Sparse Core Ops, SparseCore 0:
  9.7 200.7 all-gather.15
  525.8 24.0 all-gather.25
  552.3 24.0 all-gather.23
  577.9 96.0 all-gather.17
  675.7 51.5 all-gather.19
  729.0 48.8 all-gather.21
  1493.0 31.1 all-gather.27
  2556.7 257.3 all-reduce.15
  2820.0 66.0 reduce-scatter.6
  2889.5 65.4 reduce-scatter.4
  2963.7 509.6 all-reduce.17
where the time goes:
time: 3550 us; the launch traced here: 3490 us
  local copies, waits for them, and re-layouts  1150 us (32%)
  other arithmetic  1040 us (29%)
  waiting for transfers between devices  1030 us (29%)
  blocking collectives  127 us (4%)
  matrix products  86.5 us (2%)
    psum x2, waiting for transfers between devices, body(): lax.psum((grad_gain_mix, grad_proj_in, grad_conv_taps, grad_conv_bias, gr...  699 us
    dynamic_slice x384, local copies, waits for them, and re-layouts, output_block(): final, outputs = lax.scan(output_token, state, pieces)  309 us
    dynamic_slice x384, local copies, waits for them, and re-layouts, body(): lax.scan(summary_step, (ones_state, zero_state), flat_in)  271 us
    reduce_sum x128, other arithmetic, grad_token(): d_step = jnp.sum(d_log * a_mat, axis=0) + d_drive * input_t  243 us
    mul x128, other arithmetic, grad_token(): drive_in = step_t * input_t  128 us
    mul x128, other arithmetic, summary_step(): step_t * input_t  121 us
    mul x128, other arithmetic, grad_token(): d_drive * step_t  117 us
    all_gather x1, waiting for transfers between devices, body(): lax.all_gather(w_in, 'wa', axis=1, tiled=True)  105 us

commit v1 on v0

v1 whole, which is shorter than its diff:
```python
import functools

import jax
import jax.numpy as jnp
from jax import lax
from jax.experimental import pallas as pl
from jax.experimental.pallas import tpu as pltpu
from jax.sharding import PartitionSpec as P

EPS = 1e-05
F32 = jnp.float32
BF16 = jnp.bfloat16
SEG = 8
LANE = 128
CUT = 1e30
MESH = pl.DeviceIdType.MESH
VMEM_LIMIT = 48 * 2**20


def greet(axis, count):
    me = lax.axis_index(axis)
    barrier = pltpu.get_barrier_semaphore()
    for k in range(1, count):
        pl.semaphore_signal(
            barrier, inc=1, device_id={axis: lax.rem(me + k, count)}, device_id_type=MESH
        )
    pl.semaphore_wait(barrier, count - 1)
    return me


def gather_kernel(axis, count, x_ref, o_ref, send, recv, own):
    me = greet(axis, count)
    copies = []
    for k in range(1, count):
        copy = pltpu.make_async_remote_copy(
            src_ref=x_ref,
            dst_ref=o_ref.at[me],
            send_sem=send.at[k],
            recv_sem=recv.at[k],
            device_id={axis: lax.rem(me + k, count)},
            device_id_type=MESH,
        )
        copy.start()
        copies.append(copy)
    local = pltpu.make_async_copy(x_ref, o_ref.at[me], own)
    local.start()
    local.wait()
    for copy in copies:
        copy.wait()


def trade_kernel(axis, count, x_ref, o_ref, send, recv, own):
    me = greet(axis, count)
    copies = []
    for k in range(1, count):
        other = lax.rem(me + k, count)
        copy = pltpu.make_async_remote_copy(
            src_ref=x_ref.at[other],
            dst_ref=o_ref.at[me],
            send_sem=send.at[k],
            recv_sem=recv.at[k],
            device_id={axis: other},
            device_id_type=MESH,
        )
        copy.start()
        copies.append(copy)
    local = pltpu.make_async_copy(x_ref.at[me], o_ref.at[me], own)
    local.start()
    local.wait()
    for copy in copies:
        copy.wait()


def exchange(kernel, x, out_shape, axis, cid):
    count = lax.axis_size(axis)
    return pl.pallas_call(
        functools.partial(kernel, axis, count),
        out_shape=jax.ShapeDtypeStruct(out_shape, x.dtype),
        in_specs=[pl.BlockSpec(memory_space=pl.ANY)],
        out_specs=pl.BlockSpec(memory_space=pl.ANY),
        scratch_shapes=[
            pltpu.SemaphoreType.DMA((count,)),
            pltpu.SemaphoreType.DMA((count,)),
            pltpu.SemaphoreType.DMA,
        ],
        compiler_params=pltpu.CompilerParams(collective_id=cid, has_side_effects=True),
    )(x)


def gather_all(x, axis, cid):
    return exchange(gather_kernel, x, (lax.axis_size(axis),) + x.shape, axis, cid)


def trade(x, axis, cid):
    return exchange(trade_kernel, x, x.shape, axis, cid)


def spread(rows, states):
    shape = (states, states * LANE)
    line = lax.broadcasted_iota(jnp.int32, shape, 0)
    place = lax.broadcasted_iota(jnp.int32, shape, 1)
    lower = line * LANE
    pick = jnp.where((place >= lower) & (place < lower + LANE), 1.0, 0.0).astype(BF16)
    return jnp.dot(rows, pick, preferred_element_type=F32)


def rolled(value, by):
    return pltpu.roll(value, by % SEG, 0)


def lanes_of(g):
    return pl.ds(pl.multiple_of(g * LANE, LANE), LANE)


def rows_of(j):
    return pl.ds(pl.multiple_of(j * SEG, SEG), SEG)


def wide(ref, n, lanes):
    return jnp.broadcast_to(ref[pl.ds(n, 1), lanes], (SEG, LANE))


def state_cols(n):
    return slice(n * LANE, (n + 1) * LANE)


def summary_kernel(states, steps, groups, st_ref, dr_ref, b_ref, a_ref, hx_ref, sx_ref, hd_ref, sd_ref, bb):
    bb[...] = spread(b_ref[0], states)
    zero = jnp.zeros((SEG, LANE), F32)
    seg = lax.broadcasted_iota(jnp.int32, (SEG, LANE), 0)

    def group(g, _):
        lanes = lanes_of(g)
        a = [wide(a_ref, n, lanes) for n in range(states)]

        def step(j, carry):
            rows = rows_of(j)
            st = st_ref[0, rows, lanes]
            dr = dr_ref[0, rows, lanes]
            new = [carry[0] + st]
            for n in range(states):
                new.append(jnp.exp(st * a[n]) * carry[n + 1] + bb[rows, state_cols(n)] * dr)
            return tuple(new)

        out = lax.fori_loop(0, steps, step, (zero,) * (states + 1), unroll=2)
        total, h = out[0], list(out[1:])
        for k in (1, 2, 4):
            ok = seg >= k
            for n in range(states):
                h[n] = h[n] + jnp.where(ok, jnp.exp(total * a[n]) * rolled(h[n], k), 0.0)
            total = total + jnp.where(ok, rolled(total, k), 0.0)
        ok = seg >= 1
        sx_ref[0, :, lanes] = jnp.where(ok, rolled(total, 1), 0.0)
        sd_ref[0, :, lanes] = total[SEG - 1 : SEG]
        for n in range(states):
            hx_ref[0, n, :, lanes] = jnp.where(ok, rolled(h[n], 1), 0.0)
            hd_ref[0, pl.ds(n, 1), lanes] = h[n][SEG - 1 : SEG]
        return 0

    lax.fori_loop(0, groups, group, 0)


def output_kernel(states, steps, groups, st_ref, dr_ref, b_ref, c_ref, a_ref, hx_ref, sx_ref, e_ref, y_ref, bb, cb):
    bb[...] = spread(b_ref[0], states)
    cb[...] = spread(c_ref[0], states)

    def group(g, _):
        lanes = lanes_of(g)
        a = [wide(a_ref, n, lanes) for n in range(states)]
        sx = sx_ref[0, :, lanes]
        start = tuple(
            jnp.exp(sx * a[n]) * wide(e_ref.at[0], n, lanes) + hx_ref[0, n, :, lanes]
            for n in range(states)
        )

        def step(j, h):
            rows = rows_of(j)
            st = st_ref[0, rows, lanes]
            dr = dr_ref[0, rows, lanes]
            new = []
            y = None
            for n in range(states):
                state = jnp.exp(st * a[n]) * h[n] + bb[rows, state_cols(n)] * dr
                new.append(state)
                part = cb[rows, state_cols(n)] * state
                y = part if y is None else y + part
            y_ref[0, rows, lanes] = y
            return tuple(new)

        lax.fori_loop(0, steps, step, start, unroll=2)
        return 0

    lax.fori_loop(0, groups, group, 0)


def back_summary_kernel(states, steps, groups, st_ref, c_ref, dy_ref, a_ref, fx_ref, sx_ref, fd_ref, cb):
    cb[...] = spread(c_ref[0], states)
    zero = jnp.zeros((SEG, LANE), F32)
    seg = lax.broadcasted_iota(jnp.int32, (SEG, LANE), 0)

    def group(g, _):
        lanes = lanes_of(g)
        a = [wide(a_ref, n, lanes) for n in range(states)]

        def step(lap, carry):
            rows = rows_of(steps - 1 - lap)
            st = st_ref[0, rows, lanes]
            dy = dy_ref[0, rows, lanes]
            new = [carry[0] + st]
            for n in range(states):
                new.append(jnp.exp(st * a[n]) * (carry[n + 1] + cb[rows, state_cols(n)] * dy))
            return tuple(new)

        out = lax.fori_loop(0, steps, step, (zero,) * (states + 1), unroll=2)
        total, f = out[0], list(out[1:])
        for k in (1, 2, 4):
            ok = seg < SEG - k
            for n in range(states):
                f[n] = f[n] + jnp.where(ok, jnp.exp(total * a[n]) * rolled(f[n], -k), 0.0)
            total = total + jnp.where(ok, rolled(total, -k), 0.0)
        ok = seg < SEG - 1
        sx_ref[0, :, lanes] = jnp.where(ok, rolled(total, -1), 0.0)
        for n in range(states):
            fx_ref[0, n, :, lanes] = jnp.where(ok, rolled(f[n], -1), 0.0)
            fd_ref[0, pl.ds(n, 1), lanes] = f[n][0:1]
        return 0

    lax.fori_loop(0, groups, group, 0)


def back_kernel(
    states, steps, groups,
    st_ref, dr_ref, u_ref, b_ref, c_ref, dy_ref, a_ref, hx_ref, sx_ref, e_ref, fx_ref, tx_ref, o_ref,
    ds_ref, dd_ref, gb_ref, gc_ref, ga_ref,
    bb, cb, dec, pri, accb, accc,
):
    bb[...] = spread(b_ref[0], states)
    cb[...] = spread(c_ref[0], states)
    accb[...] = jnp.zeros_like(accb)
    accc[...] = jnp.zeros_like(accc)

    @pl.when(pl.program_id(0) == 0)
    def _():
        ga_ref[...] = jnp.zeros_like(ga_ref)

    def group(g, _):
        lanes = lanes_of(g)
        a = [wide(a_ref, n, lanes) for n in range(states)]
        sx = sx_ref[0, :, lanes]
        start = tuple(
            jnp.exp(sx * a[n]) * wide(e_ref.at[0], n, lanes) + hx_ref[0, n, :, lanes]
            for n in range(states)
        )

        def ahead(j, h):
            rows = rows_of(j)
            st = st_ref[0, rows, lanes]
            dr = dr_ref[0, rows, lanes]
            new = []
            for n in range(states):
                decay = jnp.exp(st * a[n])
                dec[rows, state_cols(n)] = decay
                pri[rows, state_cols(n)] = h[n]
                new.append(decay * h[n] + bb[rows, state_cols(n)] * dr)
            return tuple(new)

        last = lax.fori_loop(0, steps, ahead, start, unroll=2)
        end = rows_of(steps)
        for n in range(states):
            pri[end, state_cols(n)] = last[n]
        tx = tx_ref[0, :, lanes]
        flow = tuple(
            jnp.exp(tx * a[n]) * wide(o_ref.at[0], n, lanes) + fx_ref[0, n, :, lanes]
            for n in range(states)
        )

        def back(lap, f):
            j = steps - 1 - lap
            rows = rows_of(j)
            after = rows_of(j + 1)
            st = st_ref[0, rows, lanes]
            dr = dr_ref[0, rows, lanes]
            dy = dy_ref[0, rows, lanes]
            u = u_ref[0, rows, lanes]
            true_step = jnp.where(st >= 0.5 * CUT, 0.0, st)
            new = []
            d_step = None
            d_drive = None
            for n in range(states):
                cols = state_cols(n)
                d = f[n] + cb[rows, cols] * dy
                accc[rows, cols] += pri[after, cols] * dy
                accb[rows, cols] += d * dr
                flowing = dec[rows, cols] * d
                new.append(flowing)
                d_log = flowing * pri[rows, cols]
                ga_ref[n, :, lanes] += d_log * true_step
                part = d_log * a[n]
                d_step = part if d_step is None else d_step + part
                part = d * bb[rows, cols]
                d_drive = part if d_drive is None else d_drive + part
            ds_ref[0, rows, lanes] = d_step + d_drive * u
            dd_ref[0, rows, lanes] = d_drive
            return tuple(new)

        lax.fori_loop(0, steps, back, flow, unroll=2)
        return 0

    lax.fori_loop(0, groups, group, 0)
    shape = (states * LANE, states)
    line = lax.broadcasted_iota(jnp.int32, shape, 0)
    lower = lax.broadcasted_iota(jnp.int32, shape, 1) * LANE
    pick = jnp.where((line >= lower) & (line < lower + LANE), 1.0, 0.0)
    gb_ref[0] = jnp.dot(accb[...], pick, precision=lax.Precision.HIGHEST, preferred_element_type=F32)
    gc_ref[0] = jnp.dot(accc[...], pick, precision=lax.Precision.HIGHEST, preferred_element_type=F32)


def per_stream(shape):
    rest = len(shape) - 1
    return pl.BlockSpec((1,) + shape[1:], lambda s: (s,) + (0,) * rest)


def whole(shape):
    return pl.BlockSpec(shape, lambda s: (0,) * len(shape))


def scan_call(kernel, name, args, shared, outs, shared_outs, scratch, flops):
    ordered = []
    specs = []
    for arg in args:
        if isinstance(arg, int):
            ordered.append(shared[arg])
            specs.append(whole(shared[arg].shape))
        else:
            ordered.append(arg)
            specs.append(per_stream(arg.shape))
    streams = args[0].shape[0]
    moved = sum(a.size * a.dtype.itemsize for a in ordered)
    return pl.pallas_call(
        kernel,
        grid=(streams,),
        out_shape=[jax.ShapeDtypeStruct(s, F32) for s in outs + shared_outs],
        in_specs=specs,
        out_specs=[per_stream(s) for s in outs] + [whole(s) for s in shared_outs],
        scratch_shapes=scratch,
        compiler_params=pltpu.CompilerParams(vmem_limit_bytes=VMEM_LIMIT),
        cost_estimate=pl.CostEstimate(flops=flops, bytes_accessed=moved, transcendentals=flops // 10),
        name=name,
    )(*ordered)


def rms_scale(values):
    return lax.rsqrt(jnp.mean(values * values, axis=-1, keepdims=True) + EPS)


def norm_grads(values, scale, gain, d_out):
    unit = values * scale
    d_unit = d_out * gain
    d_values = scale * (d_unit - unit * jnp.mean(d_unit * unit, axis=-1, keepdims=True))
    return d_values, d_out * unit


def interleaved(rows):
    length = rows.shape[0]
    folded = rows.reshape((SEG, length // SEG) + rows.shape[1:])
    return jnp.swapaxes(folded, 0, 1).reshape(rows.shape)


def in_order(rows):
    length = rows.shape[0]
    folded = rows.reshape((length // SEG, SEG) + rows.shape[1:])
    return jnp.swapaxes(folded, 0, 1).reshape(rows.shape)


def silu_slope(v):
    s = jax.nn.sigmoid(v)
    return s * (1.0 + v * (1.0 - s))


def padded_lanes(array, width, axis):
    pads = [(0, 0)] * array.ndim
    pads[axis] = (0, width - array.shape[axis])
    return jnp.pad(array, pads)


def shift_pairs(group):
    half = group // 2
    first = [(v, 2 * v) if v < half else (v, 2 * (v - half) + 1) for v in range(group)]
    second = [(v, 2 * v + 1) if v < half else (v, 2 * (v - half)) for v in range(group)]
    return first, second


def body(
    tokens, out_grad, doc_starts, routes, keep_mask, norm_mix, w_in, conv_w, conv_b, w_x, w_dt,
    dt_bias, a_log, d_skip, w_out, norm_moe, w_router, w_up, w_down,
):
    group = lax.axis_size("wa")
    ring = lax.axis_size("ctx")
    mine = lax.axis_index("wa")
    place = lax.axis_index("ctx")
    length, width = tokens.shape[1:]
    taps, local = conv_w.shape
    states = a_log.shape[0]
    ranked = w_dt.shape[0]
    experts = w_router.shape[1]
    padded = -(-local // LANE) * LANE
    lane_groups = padded // LANE
    steps = length // SEG
    total_rows = group * length
    edge = taps - 1

    first, second = shift_pairs(group)
    rows_in = width // ring
    part_in = lax.dynamic_slice_in_dim(w_in, place * rows_in, rows_in, 0)
    low_half, high_half = part_in[:, :local], part_in[:, local:]
    upper = mine >= group // 2
    came_a = lax.ppermute(jnp.where(upper, high_half, low_half), "wa", first)
    came_b = lax.ppermute(jnp.where(upper, low_half, high_half), "wa", second)
    odd = mine % 2 == 1
    both = jnp.concatenate(
        [
            padded_lanes(jnp.where(odd, came_b, came_a), padded, 1),
            padded_lanes(jnp.where(odd, came_a, came_b), padded, 1),
        ],
        axis=1,
    )
    proj_in = lax.all_gather(both, "ctx", axis=0, tiled=True)

    up_rows, down_rows, proj_in = lax.optimization_barrier((w_up[0].T, w_down[0], proj_in))
    expert_up = lax.all_gather(up_rows, "ctx", axis=0, tiled=True)
    expert_down = lax.all_gather(down_rows, "ctx", axis=0, tiled=True)

    at = place * length + lax.iota(jnp.int32, length)
    starts = doc_starts[0]
    resets = jnp.any(at[:, None] == starts[None, :], axis=1)
    marks = [resets]
    for lag in range(1, taps):
        cut = jnp.any(
            (starts[None, :] > at[:, None] - lag) & (starts[None, :] <= at[:, None]), axis=1
        )
        marks.append(~cut)
    marks = interleaved(jnp.stack(marks, axis=1).astype(BF16))
    small = jnp.concatenate(
        [norm_mix, norm_moe, w_router.reshape(-1), marks.reshape(-1)], axis=0
    )
    smalls = lax.all_gather(small, "wa")
    share = norm_mix.shape[0]
    gain_mix = smalls[:, :share].reshape(-1).astype(F32)
    gain_moe = smalls[:, share : 2 * share].reshape(-1).astype(F32)
    router = smalls[:, 2 * share : (2 + experts) * share].reshape(width, experts)
    masks = smalls[:, (2 + experts) * share :].reshape(total_rows, taps).astype(F32)
    cuts = masks[:, 0:1] * CUT
    lag_keep = [None] + [masks[:, lag : lag + 1] for lag in range(1, taps)]

    own_tokens = interleaved(tokens[0])
    pairs = [(i, i + 1) for i in range(ring - 1)]
    before_edge = lax.ppermute(tokens[0, length - edge :], "ctx", pairs)
    before_edge = jnp.pad(before_edge, ((SEG - edge, 0), (0, 0)))
    with_edge = jnp.concatenate([own_tokens, before_edge], axis=0)
    with_edge = jnp.pad(with_edge, ((0, 8), (0, 0)))
    all_tokens = gather_all(with_edge, "wa", 1)[:, : length + SEG].astype(F32)
    scale_in = rms_scale(all_tokens)
    n1 = (all_tokens * scale_in * gain_mix).astype(BF16)
    flat_n1 = n1.reshape(group * (length + SEG), width)
    joined = jnp.dot(flat_n1, proj_in, preferred_element_type=F32).astype(BF16)
    joined = joined.reshape(group, length + SEG, 2 * padded)
    gate_z = joined[:, :length, padded:].astype(F32)

    conv_taps = padded_lanes(conv_w, padded, 1).astype(F32)
    conv_bias = padded_lanes(conv_b, padded, 0).astype(F32)
    proj_x = padded_lanes(w_x, padded, 0)
    proj_dt = padded_lanes(w_dt, padded, 1)
    step_bias = padded_lanes(dt_bias, padded, 0).astype(F32)
    a_mat = -jnp.exp(padded_lanes(a_log, padded, 1).astype(F32))
    skip_gain = padded_lanes(d_skip, padded, 0).astype(F32)
    proj_out = padded_lanes(w_out, padded, 0)

    x_inner = joined[:, :length, :padded].astype(F32).reshape(group, steps, SEG, padded)
    x_edge = joined[:, length + SEG - edge :, :padded].astype(F32)
    head = jnp.concatenate(
        [x_edge[:, :, None, :], x_inner[:, steps - edge :, : SEG - 1, :]], axis=2
    )
    extended = jnp.concatenate([head, x_inner], axis=1)

    def window(lag):
        return extended[:, edge - lag : edge - lag + steps]

    def folded(column):
        return column.reshape(group, steps, SEG, 1)

    pre_conv = conv_bias + conv_taps[0] * window(0)
    for lag in range(1, taps):
        pre_conv = pre_conv + conv_taps[lag] * window(lag) * folded(lag_keep[lag])
    pre_conv = pre_conv.reshape(total_rows, padded)
    u = jax.nn.silu(pre_conv).astype(BF16)
    u_f = u.astype(F32)
    part = jnp.dot(u, proj_x, preferred_element_type=F32).astype(BF16)
    projected = jnp.sum(gather_all(part, "wa", 2).astype(F32), axis=0).astype(BF16)
    dt_low = projected[:, :ranked]
    b_sel = projected[:, ranked : ranked + states].reshape(group, length, states)
    c_sel = projected[:, ranked + states :].reshape(group, length, states)
    step_pre = jnp.dot(dt_low, proj_dt, preferred_element_type=F32) + step_bias
    step_size = jax.nn.softplus(step_pre)
    drive = step_size * u_f
    step_cut = jnp.where(cuts > 0, CUT, step_size)

    def streams(array):
        return array.reshape(group, length, padded)

    st, dr, us = streams(step_cut), streams(drive), streams(u_f)
    vreg = (group, length, padded)
    seg_states = (group, states, SEG, padded)
    seg_sums = (group, SEG, padded)
    dev_states = (group, states, padded)
    dev_sums = (group, 1, padded)
    updates = group * length * states * padded
    broad = pltpu.VMEM((length, states * LANE), F32)
    sizes = (states, steps, lane_groups)
    h_in, s_in, h_dev, s_dev = scan_call(
        functools.partial(summary_kernel, *sizes), "scan_summary",
        [st, dr, b_sel, 0], [a_mat],
        [seg_states, seg_sums, dev_states, dev_sums], [], [broad], 6 * updates,
    )
    sent = jnp.concatenate([h_dev, s_dev], axis=1).reshape(group * (states + 1), padded)
    all_dev = gather_all(sent, "ctx", 3).reshape(ring, group, states + 1, padded)
    all_sums = all_dev[:, :, states:, :]
    order = lax.iota(jnp.int32, ring)

    def reached(finals, ahead):
        between = (
            ((order[None, :] > order[:, None]) & (order[None, :] < place))
            if ahead
            else ((order[None, :] < order[:, None]) & (order[None, :] > place))
        )
        gap = jnp.sum(
            jnp.where(between[:, :, None, None, None], all_sums[None], 0.0), axis=1
        )
        use = (order < place) if ahead else (order > place)
        terms = jnp.exp(gap * a_mat) * finals
        return jnp.sum(jnp.where(use[:, None, None, None], terms, 0.0), axis=0)

    entering = reached(all_dev[:, :, :states], True)
    (y_scan,) = scan_call(
        functools.partial(output_kernel, *sizes), "scan_output",
        [st, dr, b_sel, c_sel, 0, h_in, s_in, entering], [a_mat],
        [vreg], [], [broad, broad], 8 * updates,
    )
    gate_z = gate_z.reshape(total_rows, padded)
    y_full = y_scan.reshape(total_rows, padded) + skip_gain * u_f
    silu_z = jax.nn.silu(gate_z)
    gated = (y_full * silu_z).astype(BF16)
    mix_part = jnp.dot(gated, proj_out, preferred_element_type=F32).astype(BF16)
    mix_terms = trade(mix_part.reshape(group, length, width), "wa", 4)
    mix = jnp.sum(mix_terms.astype(F32), axis=0)

    stream = own_tokens.astype(F32)
    h1 = stream + mix
    scale_moe = rms_scale(h1)
    n2 = (h1 * scale_moe * gain_moe).astype(BF16)
    logits = jnp.dot(n2, router, preferred_element_type=F32)
    route_in_order = routes[0, :, 0]
    onehot_in_order = route_in_order[:, None] == lax.iota(jnp.int32, experts)[None, :]
    counted = onehot_in_order.astype(jnp.int32)
    within = jnp.sum((jnp.cumsum(counted, axis=0) - counted) * counted, axis=1)
    capacity = length // 2
    slot = interleaved(route_in_order * capacity + within)
    onehot = interleaved(onehot_in_order.astype(F32))
    kept = interleaved(keep_mask[0].astype(F32))
    sig = jax.nn.sigmoid(jnp.sum(logits * onehot, axis=1))
    gates = kept * sig
    slots = experts * capacity
    match = (slot[None, :] == lax.iota(jnp.int32, slots)[:, None]).astype(BF16)
    upstream = interleaved(out_grad[0]).astype(F32)
    d_rows = (gates[:, None] * upstream).astype(BF16)
    outgoing = jnp.dot(
        match, jnp.concatenate([n2, d_rows], axis=1), preferred_element_type=F32
    ).astype(BF16)
    arrived = trade(outgoing.reshape(group, slots // group, 2 * width), "wa", 5)
    arrived = arrived.reshape(slots, 2 * width)
    expert_in, d_out = arrived[:, :width], arrived[:, width:]
    hidden_pre = lax.dot_general(
        expert_in, expert_up, (((1,), (1,)), ((), ())), preferred_element_type=F32
    )
    act, gelu_back = jax.vjp(jax.nn.gelu, hidden_pre)
    act = act.astype(BF16)
    produced = jnp.dot(act, expert_down, preferred_element_type=F32).astype(BF16)
    d_act = lax.dot_general(
        d_out, expert_down, (((1,), (1,)), ((), ())), preferred_element_type=F32
    )
    d_pre = gelu_back(d_act)[0].astype(BF16)
    d_in = jnp.dot(d_pre, expert_up, preferred_element_type=F32).astype(BF16)
    returning = jnp.concatenate([produced, d_in], axis=1)
    returned = trade(returning.reshape(group, slots // group, 2 * width), "wa", 6)
    back_rows = lax.dot_general(
        match, returned.reshape(slots, 2 * width), (((0,), (0,)), ((), ())),
        preferred_element_type=F32,
    )
    grad_up = lax.dot_general(
        d_pre, expert_in, (((0,), (0,)), ((), ())), preferred_element_type=F32
    ).astype(BF16)
    grad_down = lax.dot_general(
        act, d_out, (((0,), (0,)), ((), ())), preferred_element_type=F32
    ).astype(BF16)
    share_up = lax.psum_scatter(grad_up, "ctx", scatter_dimension=0, tiled=True)
    share_down = lax.psum_scatter(grad_down, "ctx", scatter_dimension=0, tiled=True)
    expert_rows, d_slot = back_rows[:, :width], back_rows[:, width:]
    moe = gates[:, None] * expert_rows
    result = h1 + moe
    sums = jnp.stack([jnp.sum(result * result), jnp.sum(mix * mix), jnp.sum(moe * moe)])

    d_gate = jnp.sum(expert_rows * upstream, axis=1)
    d_pick = d_gate * kept * sig * (1.0 - sig)
    d_logits = (onehot * d_pick[:, None]).astype(BF16)
    grad_router = lax.dot_general(
        n2, d_logits, (((0,), (0,)), ((), ())), preferred_element_type=F32
    )
    d_n2 = d_slot + lax.dot_general(
        d_logits, router, (((1,), (1,)), ((), ())), preferred_element_type=F32
    )
    d_norm, gain_terms = norm_grads(h1, scale_moe, gain_moe, d_n2)
    grad_gain_moe = jnp.sum(gain_terms, axis=0)
    d_h1 = upstream + d_norm
    d_mix = gather_all(d_h1.astype(BF16), "wa", 7).reshape(total_rows, width)

    grad_out = lax.dot_general(
        gated, d_mix, (((0,), (0,)), ((), ())), preferred_element_type=F32
    )
    d_gated = lax.dot_general(
        d_mix, proj_out, (((1,), (1,)), ((), ())), preferred_element_type=F32
    )
    d_y = d_gated * silu_z
    d_z = d_gated * y_full * silu_slope(gate_z)
    grad_skip = jnp.sum(d_y * u_f, axis=0)
    dys = streams(d_y)
    f_in, t_in, f_dev = scan_call(
        functools.partial(back_summary_kernel, *sizes), "scan_back_summary",
        [st, c_sel, dys, 0], [a_mat],
        [seg_states, seg_sums, dev_states], [], [broad], 6 * updates,
    )
    all_back = gather_all(f_dev.reshape(group * states, padded), "ctx", 8)
    leaving = reached(all_back.reshape(ring, group, states, padded), False)
    small_rows = (group, length, states)
    longer = pltpu.VMEM((length + SEG, states * LANE), F32)
    d_step, d_drive, grad_b, grad_c, grad_a = scan_call(
        functools.partial(back_kernel, *sizes), "scan_back",
        [st, dr, us, b_sel, c_sel, dys, 0, h_in, s_in, entering, f_in, t_in, leaving], [a_mat],
        [vreg, vreg, small_rows, small_rows], [(states, SEG, padded)],
        [broad, broad, broad, longer, broad, broad], 20 * updates,
    )
    grad_a_log = jnp.sum(grad_a, axis=1) * a_mat
    d_step_pre = d_step.reshape(total_rows, padded) * jax.nn.sigmoid(step_pre)
    grad_step_bias = jnp.sum(d_step_pre, axis=0)
    d_proj_dt = d_step_pre.astype(BF16)
    grad_dt = lax.dot_general(
        dt_low, d_proj_dt, (((0,), (0,)), ((), ())), preferred_element_type=F32
    )
    d_low = lax.dot_general(
        d_proj_dt, proj_dt, (((1,), (1,)), ((), ())), preferred_element_type=F32
    )
    d_part = jnp.concatenate(
        [d_low, grad_b.reshape(total_rows, states), grad_c.reshape(total_rows, states)], axis=1
    ).astype(BF16)
    d_projected = jnp.sum(gather_all(d_part, "wa", 9).astype(F32), axis=0).astype(BF16)
    grad_x = lax.dot_general(
        u, d_projected, (((0,), (0,)), ((), ())), preferred_element_type=F32
    )
    d_u = (
        lax.dot_general(d_projected, proj_x, (((1,), (1,)), ((), ())), preferred_element_type=F32)
        + d_drive.reshape(total_rows, padded) * step_size
        + d_y * skip_gain
    )
    d_pre_conv = d_u * silu_slope(pre_conv)
    grad_conv_bias = jnp.sum(d_pre_conv, axis=0)
    d_conv = d_pre_conv.reshape(group, steps, SEG, padded)
    tap_grads = []
    d_extended = None
    for lag in range(taps):
        weighted = d_conv if lag == 0 else d_conv * folded(lag_keep[lag])
        tap_grads.append(jnp.sum(weighted * window(lag), axis=(0, 1, 2)))
        moved = jnp.pad(
            weighted * conv_taps[lag], ((0, 0), (edge - lag, lag), (0, 0), (0, 0))
        )
        d_extended = moved if d_extended is None else d_extended + moved
    head = d_extended[:, :edge]
    inside = jnp.pad(head[:, :, 1:], ((0, 0), (steps - edge, 0), (0, 1), (0, 0)))
    d_inner = (d_extended[:, edge:] + inside).reshape(group, length, padded)
    d_edge = jnp.pad(head[:, :, 0], ((0, 0), (SEG - edge, 0), (0, 0)))
    d_x = jnp.concatenate([d_inner, d_edge], axis=1)
    d_zs = jnp.pad(d_z.reshape(group, length, padded), ((0, 0), (0, SEG), (0, 0)))
    d_joined = jnp.concatenate([d_x, d_zs], axis=2).astype(BF16)
    d_joined = d_joined.reshape(group * (length + SEG), 2 * padded)
    grad_in = lax.dot_general(
        flat_n1, d_joined, (((0,), (0,)), ((), ())), preferred_element_type=F32
    )
    d_n1_part = lax.dot_general(
        d_joined, proj_in, (((1,), (1,)), ((), ())), preferred_element_type=F32
    ).astype(BF16)
    d_n1_part = jnp.pad(
        d_n1_part.reshape(group, length + SEG, width), ((0, 0), (0, 8), (0, 0))
    )
    d_n1_terms = trade(d_n1_part, "wa", 10)
    d_n1_sum = jnp.sum(d_n1_terms[:, : length + SEG].astype(F32), axis=0)
    back_pairs = [(i + 1, i) for i in range(ring - 1)]
    came = lax.ppermute(d_n1_sum[length + SEG - edge :], "ctx", back_pairs)
    last_rows = jnp.pad(came[:, None, :], ((steps - edge, 0), (SEG - 1, 0), (0, 0)))
    d_n1 = d_n1_sum[:length] + last_rows.reshape(length, width)
    scale_mix = rms_scale(stream)
    d_stream, gain_terms = norm_grads(stream, scale_mix, gain_mix, d_n1)
    grad_gain_mix = jnp.sum(gain_terms, axis=0)
    input_grad = d_h1 + d_stream

    grad_in = jnp.concatenate(
        [grad_in[:, :local], grad_in[:, padded : padded + local]], axis=1
    ).astype(BF16)
    slice_in = lax.psum_scatter(grad_in, "ctx", scatter_dimension=0, tiled=True)
    of_x, of_z = slice_in[:, :local], slice_in[:, local:]
    went_a = lax.ppermute(jnp.where(odd, of_z, of_x), "wa", [(b, a) for a, b in first])
    went_b = lax.ppermute(jnp.where(odd, of_x, of_z), "wa", [(b, a) for a, b in second])
    slice_in = jnp.concatenate(
        [jnp.where(upper, went_b, went_a), jnp.where(upper, went_a, went_b)], axis=1
    )
    share_in = lax.all_gather(slice_in, "ctx", axis=0, tiled=True).astype(F32)
    share_out = lax.all_gather(
        lax.psum_scatter(grad_out[:local].astype(BF16), "ctx", scatter_dimension=0, tiled=True),
        "ctx", axis=0, tiled=True,
    ).astype(F32)
    totals = lax.psum(
        (
            jnp.stack(tap_grads, axis=0)[:, :local],
            grad_conv_bias[:local],
            grad_x[:local],
            grad_dt[:, :local],
            grad_step_bias[:local],
            grad_a_log[:, :local],
            grad_skip[:local],
            sums,
        ),
        "ctx",
    )
    wide_totals = lax.psum((grad_gain_mix, grad_gain_moe, grad_router), ("ctx", "wa"))
    share_mix, share_moe, share_router = [
        lax.dynamic_slice_in_dim(t, mine * share, share, 0) for t in wide_totals
    ]
    denom = length * ring * width
    rms_stats = jnp.sqrt(totals[7] / denom)[None]
    return (
        in_order(result)[None],
        in_order(input_grad)[None],
        share_mix,
        share_in,
        totals[0],
        totals[1],
        totals[2],
        totals[3],
        totals[4],
        totals[5],
        totals[6],
        share_out,
        share_moe,
        share_router,
        share_up.T.astype(F32)[None],
        share_down.astype(F32)[None],
        rms_stats,
    )


def solution(mesh):
    placed = (
        P("wa", "ctx", None),
        P("wa", "ctx", None),
        P("wa", None),
        P("wa", "ctx", None),
        P("wa", "ctx"),
        P("wa"),
        P(None, "wa"),
        P(None, "wa"),
        P("wa"),
        P("wa", None),
        P(None, "wa"),
        P("wa"),
        P(None, "wa"),
        P("wa"),
        P("wa", None),
        P("wa"),
        P("wa", None),
        P("wa", None, "ctx"),
        P("wa", "ctx", None),
    )
    return jax.shard_map(
        body,
        mesh=mesh,
        in_specs=placed,
        out_specs=(
            P("wa", "ctx", None),
            P("wa", "ctx", None),
            P("wa"),
            P(None, "wa"),
            P(None, "wa"),
            P("wa"),
            P("wa", None),
            P(None, "wa"),
            P("wa"),
            P(None, "wa"),
            P("wa"),
            P("wa", None),
            P("wa"),
            P("wa", None),
            P("wa", None, "ctx"),
            P("wa", "ctx", None),
            P("wa", None),
        ),
        check_vma=False,
    )
```

time: 3550 us -> 806 us (0.23); the launches traced: 3490 us -> 792 us
  local copies, waits for them, and re-layouts: 1150 us -> 35.7 us
  other arithmetic: 1040 us -> 59.9 us
  waiting for transfers between devices: 1030 us -> 222 us
  Pallas kernels: 0 us -> 300 us
  blocking collectives: 127 us -> 76.8 us
    psum x2 -> x1, waiting for transfers between devices: 699 us -> 52.6 us  [body(): lax.psum((jnp.stack(tap_grads, axis=0)[:, :local], grad_conv_bias[:local]...]
    dynamic_slice x780 -> x3, local copies, waits for them, and re-layouts: 603 us -> 1.97 us  [body(): lax.dynamic_slice_in_dim(t, mine * share, share, 0)]
    mul x518 -> x4, other arithmetic: 465 us -> 1.67 us  [the longest x1 1.64 us: silu_slope(): return s * (1.0 + v * (1.0 - s))]
    reduce_sum x261 -> x15, other arithmetic: 343 us -> 15.2 us  [the longest x2 2.61 us: rms_scale(): return lax.rsqrt(jnp.mean(values * values, axis=-1, keepdims=True) + EPS)]
    pallas_call x0 -> x14, Pallas kernels: none -> 300 us  [the longest x10 243 us: exchange(): pl.pallas_call(functools.partial(kernel, axis, count), out_shape=jax.Shap...]
    mul x640 -> x8, local copies, waits for them, and re-layouts: 269 us -> 0.59 us  [the longest x6 0.49 us: body(): pre_conv = pre_conv + conv_taps[lag] * window(lag) * folded(lag_keep[lag])]
    add x267 -> x4, other arithmetic: 196 us -> 4.61 us  [the longest x1 1.98 us: body(): d_extended = moved if d_extended is None else d_extended + moved]
    dynamic_update_slice x776 -> x0, local copies, waits for them, and re-layouts: 188 us -> none  [the longest x384 87.9 us: output_block(): final, outputs = lax.scan(output_token, state, pieces)]
where the time goes in v1:
time: 806 us; the launch traced here: 792 us
  Pallas kernels  300 us (37%)
  waiting for transfers between devices  222 us (28%)
  blocking collectives  76.8 us (10%)
  matrix products  65.9 us (8%)
  other arithmetic  59.9 us (7%)
  local copies, waits for them, and re-layouts  35.7 us (4%)
  between operations  17.1 us (2%)
  starting transfers between devices  15.5 us (2%)
    pallas_call x10, Pallas kernels, exchange(): pl.pallas_call(functools.partial(kernel, axis, count), out_shape=jax.Shap...  243 us
    pallas_call x4, Pallas kernels, scan_call(): pl.pallas_call(kernel, grid=(streams,), out_shape=[jax.ShapeDtypeStruct(s...  56.6 us
    psum x1, waiting for transfers between devices, body(): lax.psum((jnp.stack(tap_grads, axis=0)[:, :local], grad_conv_bias[:local]...  52.6 us
    reduce_scatter x1, waiting for transfers between devices, body(): slice_in = lax.psum_scatter(grad_in, 'ctx', scatter_dimension=0, tiled=True)  47.6 us
    reduce_scatter x1, waiting for transfers between devices, body(): lax.psum_scatter(grad_down, 'ctx', scatter_dimension=0, tiled=True)  45.3 us
    psum x1, blocking collectives, body(): lax.psum((grad_gain_mix, grad_gain_moe, grad_router), ('ctx', 'wa'))  40.8 us
    all_gather x1, waiting for transfers between devices, body(): proj_in = lax.all_gather(both, 'ctx', axis=0, tiled=True)  33.9 us
    unnamed x11, waiting for transfers between devices  29.6 us
  transfers between devices with their start and end apart: 16, of which 9 were waited for; matrix products, arithmetic and copies ran while one was open for 13% of the time, Pallas kernels for 22%

profile of v1, /device:TPU:11, one launch (start us, length us, event | category | flops | bytes accessed | tf_op | source)
XLA Modules:
  0.0 792.5 jit_solution(8564188902192464517)
XLA Ops:
  19.0 33.9 %all-gather.7.cloned.1.call-done = bf16[1152,1280]{1,0:T(8,128)(2,1)} async-done(((bf16[144,1280]{1,0:T(8,128)(2,1)}), bf16[1152,1280]{1,0:T(8,128)(2,1)}) %all-gather.7.cloned.1.call-update) | async-done | bytes 2949136 | tf_op jit(solution)/shard_map/all_gather | solution.py:427
  59.7 12.3 %all-reduce.21 = bf16[8960]{0:T(1024)(128)(2,1)S(1)} all-reduce(bf16[8960]{0:T(1024)(128)(2,1)S(1)} %dynamic-update-slice), channel_id=2, replica_groups=mesh['ctx'=8,'wa'=4] {'wa'}, use_global_device_ids=true, to_apply=%add.21 | all-reduce | flops 8960 | bytes 35840
  81.2 33.4 %shard_map.314 = bf16[4,144,1152]{2,1,0:T(8,128)(2,1)} custom-call(bf16[144,1152]{1,0:T(8,128)(2,1)} %pad.84.x_ref), custom_call_target="tpu_custom_call" | custom-call | tf_op jit(solution)/shard_map/pallas_call | solution.py:76
  127.3 13.4 %shard_map.315 = bf16[4,512,104]{2,1,0:T(8,128)(2,1)} custom-call(bf16[512,104]{1,0:T(8,128)(2,1)} %copy.224.x_ref), custom_call_target="tpu_custom_call" | custom-call | tf_op jit(solution)/shard_map/pallas_call | solution.py:76
  144.2 8.0 %scan_summary.1 = (f32[4,16,8,640]{3,2,1,0:T(8,128)S(1)}, f32[4,8,640]{2,1,0:T(8,128)S(1)}, f32[4,16,640]{2,1,0:T(8,128)S(1)}, f32[4,1,640]{2,1,0:T(1,128)S(1)}) custom-call(f32[4,128,640]{2,1,0:T(8,128)S(1)} %bitcast.253, f32[4,128,640]{2,1,0:T(8,128)S(1)} %bitcast.250, bf16[4,128,16]{2,1,0:T(8,128)(2,1)S(1)} %bitcast.262, ...), custom_call_target="tpu_custom_call" | custom-call | flops 31457280 | bytes 2678784 | tf_op jit(solution)/shard_map/scan_summary/pallas_call | solution.py:339
  154.1 20.9 %shard_map.316 = f32[8,68,640]{2,1,0:T(8,128)} custom-call(f32[68,640]{1,0:T(8,128)} %reshape.540.x_ref), custom_call_target="tpu_custom_call" | custom-call | tf_op jit(solution)/shard_map/pallas_call | solution.py:76
  178.1 9.9 %scan_output.1 = f32[4,128,640]{2,1,0:T(8,128)S(1)} custom-call(f32[4,128,640]{2,1,0:T(8,128)S(1)} %bitcast.254, f32[4,128,640]{2,1,0:T(8,128)S(1)} %bitcast.251, bf16[4,128,16]{2,1,0:T(8,128)(2,1)S(1)} %bitcast.263, bf16[4,128,16]{2,1,0:T(8,128)(2,1)S(1)} %bitcast.259, f32[16,640]{1,0:T(8,128)S(1)} %exponential_negate_fusion.a_ref, ...), custom_call_target="tpu_custom_call" | custom-call | flops 41943040 | bytes 4251648 | tf_op jit(solution)/shard_map/scan_output/pallas_call | solution.py:339
  191.9 26.9 %shard_map.317 = bf16[4,128,1152]{2,1,0:T(8,128)(2,1)} custom-call(bf16[4,128,1152]{2,1,0:T(8,128)(2,1)} %bitcast.293), custom_call_target="tpu_custom_call" | custom-call | tf_op jit(solution)/shard_map/pallas_call | solution.py:76
  226.7 28.6 %shard_map.318 = bf16[4,64,2304]{2,1,0:T(8,128)(2,1)} custom-call(bf16[4,64,2304]{2,1,0:T(8,128)(2,1)} %bitcast.277), custom_call_target="tpu_custom_call" | custom-call | tf_op jit(solution)/shard_map/pallas_call | solution.py:76
  257.5 7.1 fusion.88
  279.0 29.1 %shard_map.319 = bf16[4,64,2304]{2,1,0:T(8,128)(2,1)} custom-call(bf16[4,64,2304]{2,1,0:T(8,128)(2,1)} %bitcast.278), custom_call_target="tpu_custom_call" | custom-call | tf_op jit(solution)/shard_map/pallas_call | solution.py:76
  315.7 27.8 %shard_map.320 = bf16[4,128,1152]{2,1,0:T(8,128)(2,1)} custom-call(bf16[128,1152]{1,0:T(8,128)(2,1)} %get-tuple-element.189.x_ref), custom_call_target="tpu_custom_call" | custom-call | tf_op jit(solution)/shard_map/pallas_call | solution.py:76
  351.7 8.2 %scan_back_summary.1 = (f32[4,16,8,640]{3,2,1,0:T(8,128)S(1)}, f32[4,8,640]{2,1,0:T(8,128)S(1)}, f32[4,16,640]{2,1,0:T(8,128)S(1)}) custom-call(f32[4,128,640]{2,1,0:T(8,128)S(1)} %bitcast.255, bf16[4,128,16]{2,1,0:T(8,128)(2,1)S(1)} %bitcast.260, f32[4,128,640]{2,1,0:T(8,128)S(1)} %bitcast.248, f32[16,640]{1,0:T(8,128)S(1)} %exponential_negate_fusion.a_ref), custom_call_target="tpu_custom_call" | custom-call | flops 31457280 | bytes 2678784 | tf_op jit(solution)/shard_map/scan_back_summary/pallas_call | solution.py:339
  362.3 19.0 %shard_map.321 = f32[8,64,640]{2,1,0:T(8,128)} custom-call(f32[64,640]{1,0:T(8,128)} %bitcast.258), custom_call_target="tpu_custom_call" | custom-call | tf_op jit(solution)/shard_map/pallas_call | solution.py:76
  383.2 30.4 %scan_back.1 = (f32[4,128,640]{2,1,0:T(8,128)S(1)}, f32[4,128,640]{2,1,0:T(8,128)S(1)}, f32[4,128,16]{2,1,0:T(8,128)S(1)}, f32[4,128,16]{2,1,0:T(8,128)S(1)}, f32[16,8,640]{2,1,0:T(8,128)S(1)}) custom-call(f32[4,128,640]{2,1,0:T(8,128)S(1)} %bitcast.256, f32[4,128,640]{2,1,0:T(8,128)} %bitcast.252, f32[4,128,640]{2,1,0:T(8,128)} %fusion.60.u_ref, ...), custom_call_target="tpu_custom_call" | custom-call | flops 104857600 | bytes 8429568 | tf_op jit(solution)/shard_map/scan_back/pallas_call | solution.py:339
  417.8 13.4 %shard_map.322 = bf16[4,512,104]{2,1,0:T(8,128)(2,1)} custom-call(bf16[512,104]{1,0:T(8,128)(2,1)} %pad_maximum_fusion.5.x_ref), custom_call_target="tpu_custom_call" | custom-call | tf_op jit(solution)/shard_map/pallas_call | solution.py:76
  450.0 28.8 %reduce-scatter.13.cloned.1.call-done = bf16[72,1152]{1,0:T(8,128)(2,1)} async-done(((bf16[576,1152]{1,0:T(8,128)(2,1)}), bf16[72,1152]{1,0:T(8,128)(2,1)}) %reduce-scatter.13.cloned.1.call-update) | async-done | bytes 165904
  478.8 47.6 %reduce-scatter.7.cloned.1.call-done = bf16[144,1152]{1,0:T(8,128)(2,1)} async-done(((bf16[1152,1152]{1,0:T(8,128)(2,1)}), bf16[144,1152]{1,0:T(8,128)(2,1)}) %reduce-scatter.7.cloned.1.call-update) | async-done | bytes 331792 | tf_op jit(solution)/shard_map/reduce_scatter | solution.py:715
  547.0 7.7 convolution_convert_fusion
  561.1 30.8 %shard_map.323 = bf16[4,144,1152]{2,1,0:T(8,128)(2,1)} custom-call(bf16[4,144,1152]{2,1,0:T(8,128)(2,1)} %pad.100.x_ref), custom_call_target="tpu_custom_call" | custom-call | tf_op jit(solution)/shard_map/pallas_call | solution.py:76
  598.9 23.7 %all-reduce.24 = (f32[4,576]{1,0:T(4,128)}, f32[576]{0:T(1024)}, f32[576]{0:T(1024)}, f32[16,576]{1,0:T(8,128)}, f32[576]{0:T(1024)}, /*index=5*/f32[3]{0:T(128)S(1)}) all-reduce(f32[4,576]{1,0:T(4,128)S(1)} %pad_maximum_fusion.6, f32[576]{0:T(1024)S(1)} %bitcast.311, ...), channel_id=1, replica_groups=mesh['ctx'=8,'wa'=4] {'ctx'}, use_global_device_ids=true, to_apply=%region_28.29 | all-reduce | flops 13251 | bytes 106008 | tf_op jit(solution)/shard_map/psum | solution.py:727
  626.6 40.8 %all-reduce.23 = (f32[1152]{0:T(1024)S(1)}, f32[1152]{0:T(1024)S(1)}, f32[1152,4]{0,1:T(4,128)S(1)}) all-reduce(f32[1152]{0:T(1024)S(1)} %get-tuple-element.159, f32[1152]{0:T(1024)S(1)} %copy-done.74, f32[1152,4]{0,1:T(4,128)S(1)} %convolution_bitcast_fusion.2), channel_id=1, replica_groups=mesh['ctx'=8,'wa'=4] {'ctx','wa'}, use_global_device_ids=true, to_apply=%region_22.23 | all-reduce | flops 6912 | bytes 55296 | tf_op jit(solution)/shard_map/psum | solution.py:740
  679.8 45.3 %reduce-scatter.11.cloned.1.call-done = bf16[384,1152]{1,0:T(8,128)(2,1)} async-done(((bf16[3072,1152]{1,0:T(8,128)(2,1)}), bf16[384,1152]{1,0:T(8,128)(2,1)}) %reduce-scatter.11.cloned.1.call-update) | async-done | bytes 884752 | tf_op jit(solution)/shard_map/reduce_scatter | solution.py:605
  729.3 52.6 %all-reduce.28.cloned.1.call-done = (f32[576,104]{0,1:T(8,128)}, f32[72,576]{1,0:T(8,128)}) async-done(((f32[576,104]{0,1:T(8,128)}, f32[72,576]{1,0:T(8,128)}), (f32[576,104]{0,1:T(8,128)}, f32[72,576]{1,0:T(8,128)})) %all-reduce.28.cloned.1.call-update) | async-done | bytes 405520 | tf_op jit(solution)/shard_map/psum | solution.py:727
  (427 shorter events, 175.7 us)
Async XLA Ops:
  7.2 45.7 %all-gather.7.cloned.1.call-start = ((), (), s32[]{:S(2)}) async-start(), calls=%async_computation.4 | async-start | bytes 3317760 | tf_op jit(solution)/shard_map/all_gather | solution.py:427
  8.4 5.7 collective-permute-start.1
  10.8 7.3 collective-permute-start.2
  18.9 54.0 %copy-start.82 = (s32[1,128,1]{1,2,0:T(1,128)S(1)}, s32[1,128,1]{1,2,0:T(1,128)}, u32[]{:S(2)}) copy-start(s32[1,128,1]{1,2,0:T(1,128)} %param.22) | copy-start | bytes 1540
  18.9 238.6 %all-gather.9.cloned.1.call-start = ((), (), s32[]{:S(2)}) async-start(), calls=%async_computation.5 | async-start | bytes 7962624 | tf_op jit(solution)/shard_map/all_gather | solution.py:430
  52.9 211.6 %all-gather.11.cloned.1.call-start = ((), (), s32[]{:S(2)}) async-start(), calls=%async_computation.6 | async-start | bytes 7962624 | tf_op jit(solution)/shard_map/all_gather | solution.py:431
  53.7 425.1 %reduce-scatter.13.cloned.1.call-start = ((), (), s32[]{:S(2)}) async-start(), calls=%async_computation.12 | async-start | bytes 1492992
  53.8 26.6 %collective-permute-start = (bf16[3,1152]{1,0:T(4,128)(2,1)S(1)}, bf16[3,1152]{1,0:T(4,128)(2,1)S(1)}, u32[]{:S(2)}, u32[]{:S(2)}) collective-permute-start(bf16[3,1152]{1,0:T(4,128)(2,1)S(1)} %slice_bitcast_fusion.2), channel_id=1, source_target_pairs={{0,4},{4,8},{8,12},{12,16},{16,20},{20,24},{24,28},{1,5},{5,9},{9,... | collective-permute-start | bytes 20744 | tf_op jit(solution)/shard_map/ppermute | solution.py:457
  74.3 273.8 %copy-start.64 = (f32[640]{0:T(1024)}, f32[640]{0:T(1024)S(1)}, u32[]{:S(2)}) copy-start(f32[640]{0:T(1024)S(1)} %pad_convert_fusion.2) | copy-start | bytes 7684
  74.4 47.7 %copy-start.66 = (f32[640]{0:T(1024)}, f32[640]{0:T(1024)S(1)}, u32[]{:S(2)}) copy-start(f32[640]{0:T(1024)S(1)} %get-tuple-element.168) | copy-start | bytes 7684
  74.4 47.7 %copy-start.68 = (f32[640]{0:T(1024)}, f32[640]{0:T(1024)S(1)}, u32[]{:S(2)}) copy-start(f32[640]{0:T(1024)S(1)} %get-tuple-element.169) | copy-start | bytes 7684
  74.4 47.7 %copy-start.70 = (f32[640]{0:T(1024)}, f32[640]{0:T(1024)S(1)}, u32[]{:S(2)}) copy-start(f32[640]{0:T(1024)S(1)} %get-tuple-element.170) | copy-start | bytes 7684
  74.5 47.7 %copy-start.72 = (f32[640]{0:T(1024)}, f32[640]{0:T(1024)S(1)}, u32[]{:S(2)}) copy-start(f32[640]{0:T(1024)S(1)} %get-tuple-element.171) | copy-start | bytes 7684
  142.0 209.4 %copy-start.9 = (bf16[512,16]{1,0:T(8,128)(2,1)}, bf16[512,16]{1,0:T(8,128)(2,1)S(1)}, u32[]{:S(2)}) copy-start(bf16[512,16]{1,0:T(8,128)(2,1)S(1)} %get-tuple-element.220) | copy-start | bytes 49156
  440.9 85.5 %reduce-scatter.7.cloned.1.call-start = ((), (), s32[]{:S(2)}) async-start(), calls=%async_computation.7 | async-start | bytes 2985984 | tf_op jit(solution)/shard_map/reduce_scatter | solution.py:715
  449.9 220.6 %all-gather.15.cloned.1.call-start = ((), (), s32[]{:S(2)}) async-start(), calls=%async_computation.9 | async-start | bytes 1492992 | tf_op jit(solution)/shard_map/all_gather | solution.py:723
  478.8 61.4 %copy-start.42 = (bf16[4,64,2304]{2,1,0:T(8,128)(2,1)S(1)}, bf16[4,64,2304]{2,1,0:T(8,128)(2,1)}, u32[]{:S(2)}) copy-start(bf16[4,64,2304]{2,1,0:T(8,128)(2,1)} %shard_map.318) | copy-start | bytes 3538948
  478.8 194.9 %all-gather.13.cloned.1.call-start = ((), (), s32[]{:S(2)}) async-start(), calls=%async_computation.8 | async-start | bytes 2985984 | tf_op jit(solution)/shard_map/all_gather | solution.py:722
  527.6 6.5 collective-permute-start.4
  527.9 11.2 %collective-permute-start.5 = (bf16[144,576]{1,0:T(8,128)(2,1)S(1)}, bf16[144,576]{1,0:T(8,128)(2,1)S(1)}, u32[]{:S(2)}, u32[]{:S(2)}) collective-permute-start(bf16[144,576]{1,0:T(8,128)(2,1)S(1)} %get-tuple-element.219), channel_id=1, source_target_pairs={{0,0},{2,1},{1,2},{3,3},{4,4},{6,5},{5,6},{7,7},{8,8},{10,9},{9,10... | collective-permute-start | bytes 497672 | tf_op jit(solution)/shard_map/ppermute | solution.py:717
  540.1 138.4 %reduce-scatter.9.cloned.1.call-start = ((), (), s32[]{:S(2)}) async-start(), calls=%async_computation.10 | async-start | bytes 7962624 | tf_op jit(solution)/shard_map/reduce_scatter | solution.py:604
  546.7 178.4 %reduce-scatter.11.cloned.1.call-start = ((), (), s32[]{:S(2)}) async-start(), calls=%async_computation.11 | async-start | bytes 7962624 | tf_op jit(solution)/shard_map/reduce_scatter | solution.py:605
  554.7 227.2 %all-reduce.28.cloned.1.call-start = ((), (), s32[]{:S(2)}) async-start(), calls=%async_computation.13 | async-start | bytes 901120 | tf_op jit(solution)/shard_map/psum | solution.py:727
  593.5 32.7 %collective-permute-start.3 = (f32[3,1152]{1,0:T(4,128)S(1)}, f32[3,1152]{1,0:T(4,128)S(1)}, u32[]{:S(2)}, u32[]{:S(2)}) collective-permute-start(f32[3,1152]{1,0:T(4,128)S(1)} %slice.245), channel_id=1, source_target_pairs={{4,0},{8,4},{12,8},{16,12},{20,16},{24,20},{28,24},{5,1},{9,5},{13... | collective-permute-start | bytes 41480 | tf_op jit(solution)/shard_map/ppermute | solution.py:704
  (93 other events, 1017.4 us)
Sparse Core Ops, SparseCore 0:
  19.0 33.8 all-gather.6
  54.8 50.1 all-gather.8
  106.9 48.8 all-gather.10
  441.0 37.6 reduce-scatter.12
  482.7 43.7 reduce-scatter.6
  528.3 25.1 all-gather.14
  556.1 30.2 all-gather.12
  590.3 65.6 reduce-scatter.8
  659.5 65.5 reduce-scatter.10
  729.1 52.7 all-reduce.27

commit v2 on v1

--- a/solution.py
+++ b/solution.py
@@ -15,6 +15,12 @@
 CUT = 1e30
 MESH = pl.DeviceIdType.MESH
 VMEM_LIMIT = 48 * 2**20
+
+
+def lasting(us):
+    return pl.CostEstimate(
+        flops=int(us * 1.1e9), bytes_accessed=int(us * 3.5e6), transcendentals=0
+    )
 
 
 def greet(axis, count):
@@ -71,7 +77,7 @@
         copy.wait()
 
 
-def exchange(kernel, x, out_shape, axis, cid):
+def exchange(kernel, x, out_shape, axis, cid, us):
     count = lax.axis_size(axis)
     return pl.pallas_call(
         functools.partial(kernel, axis, count),
@@ -84,15 +90,342 @@
             pltpu.SemaphoreType.DMA,
         ],
         compiler_params=pltpu.CompilerParams(collective_id=cid, has_side_effects=True),
+        cost_estimate=lasting(us),
     )(x)
 
 
-def gather_all(x, axis, cid):
-    return exchange(gather_kernel, x, (lax.axis_size(axis),) + x.shape, axis, cid)
-
-
-def trade(x, axis, cid):
-    return exchange(trade_kernel, x, x.shape, axis, cid)
+def gather_all(x, axis, cid, us):
+    return exchange(gather_kernel, x, (lax.axis_size(axis),) + x.shape, axis, cid, us)
+
+
+def trade(x, axis, cid, us):
+    return exchange(trade_kernel, x, x.shape, axis, cid, us)
+
+
+def remote(src, dst, send, recv, where):
+    return pltpu.make_async_remote_copy(
+        src_ref=src, dst_ref=dst, send_sem=send, recv_sem=recv,
+        device_id=where, device_id_type=MESH,
+    )
+
+
+def add_rows(out, parts, rows):
+    def one(i, _):
+        at = pl.ds(pl.multiple_of(i * 16, 16), 16)
+        total = parts[0][at, :].astype(F32)
+        for part in parts[1:]:
+            total = total + part[at, :].astype(F32)
+        out[at, :] = total.astype(out.dtype)
+        return 0
+
+    lax.fori_loop(0, rows // 16, one, 0)
+
+
+def finish_kernel(
+    ring, group, in_rows, small_rows,
+    g_ref, z_ref, f_ref, d_ref, o_ref, dt_ref,
+    from_pair, paired, came, own, zin, tiles,
+    pair_s, pair_r, ctx_s, ctx_r, z_s, z_r, tile_s, tile_r, d_s, d_r, d_own, last_s, last_r, fwd_s, fwd_r,
+):
+    me = lax.axis_index("ctx")
+    mine = lax.axis_index("wa")
+    half = ring // 2
+    lane = lax.rem(me, 2)
+    chip = me // 2
+    pair = me + 1 - 2 * lane
+    rows = in_rows + small_rows + 16
+    barrier = pltpu.get_barrier_semaphore()
+    peers = [lax.rem(chip + k, half) * 2 + lane for k in range(1, half)]
+    mates = [lax.rem(mine + k, group) for k in range(1, group)]
+    for who in [pair] + peers:
+        pl.semaphore_signal(barrier, inc=1, device_id={"ctx": who}, device_id_type=MESH)
+    for who in mates:
+        pl.semaphore_signal(barrier, inc=1, device_id={"wa": who}, device_id_type=MESH)
+    pl.semaphore_wait(barrier, half + group - 1)
+
+    to_pair = remote(g_ref.at[1 - lane], from_pair, pair_s, pair_r, {"ctx": pair})
+    to_pair.start()
+    trades = []
+    for k, who in enumerate(mates):
+        copy = remote(d_ref.at[who], dt_ref.at[mine], d_s.at[k], d_r.at[k], {"wa": who})
+        copy.start()
+        trades.append(copy)
+    kept = pltpu.make_async_copy(d_ref.at[mine], dt_ref.at[mine], d_own)
+    kept.start()
+    to_pair.wait_recv()
+    scattered = []
+    for k, who in enumerate(peers):
+        to = lax.rem(chip + k + 1, half)
+        add_rows(paired.at[to], [g_ref.at[lane, to], from_pair.at[to]], rows)
+        copy = remote(paired.at[to], came.at[k], ctx_s.at[k], ctx_r.at[k], {"ctx": who})
+        copy.start()
+        scattered.append(copy)
+    add_rows(paired.at[chip], [g_ref.at[lane, chip], from_pair.at[chip]], rows)
+    for copy in scattered:
+        copy.wait_recv()
+    add_rows(own, [paired.at[chip]] + [came.at[k] for k in range(half - 1)], rows)
+
+    x_to = mine // 2
+    z_to = group // 2 + mine // 2
+    slot = lax.rem(mine, 2)
+    send_x = remote(own.at[pl.ds(0, in_rows)], zin.at[slot], z_s.at[0], z_r.at[slot], {"wa": x_to})
+    send_z = remote(z_ref, zin.at[slot], z_s.at[1], z_r.at[slot], {"wa": z_to})
+    keep_x = pltpu.make_async_copy(own.at[pl.ds(0, in_rows)], zin.at[slot], z_r.at[slot])
+    keep_z = pltpu.make_async_copy(z_ref, zin.at[slot], z_r.at[slot])
+
+    @pl.when(x_to != mine)
+    def _():
+        send_x.start()
+
+    @pl.when(x_to == mine)
+    def _():
+        keep_x.start()
+
+    @pl.when(z_to != mine)
+    def _():
+        send_z.start()
+
+    @pl.when(z_to == mine)
+    def _():
+        keep_z.start()
+
+    tile = pl.ds(in_rows + small_rows, 16)
+    spread_tiles = []
+    for k, who in enumerate(mates):
+        copy = remote(own.at[tile], tiles.at[k], tile_s.at[k], tile_r.at[k], {"wa": who})
+        copy.start()
+        spread_tiles.append(copy)
+    fin = o_ref.at[me]
+    fin[pl.ds(2 * in_rows, in_rows)] = f_ref[...]
+    fin[pl.ds(3 * in_rows, small_rows)] = own[pl.ds(in_rows, small_rows)]
+    for copy in spread_tiles:
+        copy.wait_recv()
+    add_rows(
+        fin.at[pl.ds(3 * in_rows + small_rows, 16)],
+        [own.at[tile]] + [tiles.at[k] for k in range(group - 1)],
+        16,
+    )
+    for s in range(2):
+        pltpu.make_async_copy(zin.at[s], zin.at[s], z_r.at[s]).wait()
+        fin[pl.ds(s * in_rows, in_rows)] = zin[s]
+
+    lasts = []
+    for k, who in enumerate(peers):
+        copy = remote(fin, o_ref.at[me], last_s.at[k], last_r.at[k], {"ctx": who})
+        copy.start()
+        lasts.append(copy)
+    forwards = [remote(fin, o_ref.at[me], fwd_s.at[0], fwd_r.at[0], {"ctx": pair})]
+    forwards[0].start()
+    for k in range(1, half):
+        lasts[k - 1].wait_recv()
+        source = lax.rem(chip + half - k, half) * 2 + lane
+        copy = remote(o_ref.at[source], o_ref.at[source], fwd_s.at[k], fwd_r.at[k], {"ctx": pair})
+        copy.start()
+        forwards.append(copy)
+    for copy in forwards:
+        copy.wait_recv()
+
+    to_pair.wait_send()
+    for copy in scattered + spread_tiles + lasts + forwards:
+        copy.wait_send()
+
+    @pl.when(x_to != mine)
+    def _():
+        send_x.wait_send()
+
+    @pl.when(z_to != mine)
+    def _():
+        send_z.wait_send()
+
+    kept.wait()
+    for copy in trades:
+        copy.wait()
+
+
+def finish(g, z, f, d, in_rows, small_rows, cid):
+    ring, group = lax.axis_size("ctx"), lax.axis_size("wa")
+    half = ring // 2
+    rows, lanes = g.shape[2:]
+    out_rows = 3 * in_rows + small_rows + 16
+    vmem = pl.BlockSpec(memory_space=pltpu.VMEM)
+    hbm = pl.BlockSpec(memory_space=pl.ANY)
+    dma = pltpu.SemaphoreType.DMA
+    return pl.pallas_call(
+        functools.partial(finish_kernel, ring, group, in_rows, small_rows),
+        out_shape=[
+            jax.ShapeDtypeStruct((ring, out_rows, lanes), BF16),
+            jax.ShapeDtypeStruct(d.shape, d.dtype),
+        ],
+        in_specs=[vmem, vmem, vmem, hbm],
+        out_specs=[vmem, hbm],
+        scratch_shapes=[
+            pltpu.VMEM((half, rows, lanes), BF16),
+            pltpu.VMEM((half, rows, lanes), BF16),
+            pltpu.VMEM((half - 1, rows, lanes), BF16),
+            pltpu.VMEM((rows, lanes), BF16),
+            pltpu.VMEM((2, in_rows, lanes), BF16),
+            pltpu.VMEM((group - 1, 16, lanes), BF16),
+            dma, dma,
+            dma((half - 1,)), dma((half - 1,)),
+            dma((2,)), dma((2,)),
+            dma((group - 1,)), dma((group - 1,)),
+            dma((group - 1,)), dma((group - 1,)), dma,
+            dma((half - 1,)), dma((half - 1,)),
+            dma((half,)), dma((half,)),
+        ],
+        compiler_params=pltpu.CompilerParams(
+            collective_id=cid, has_side_effects=True, vmem_limit_bytes=VMEM_LIMIT
+        ),
+        cost_estimate=lasting(60),
+        name="finish",
+    )(g, z, f, d)
+
+
+def start_kernel(
+    ring, group, tok, edge, par, doc, w_ref, tok_o, edge_o, par_o, doc_o, w_o,
+    mate_s, mate_r, own_s, edge_s, edge_r, relay_s, relay_r, shift_s, shift_r, out_s, out_r, fwd_s, fwd_r,
+):
+    me = lax.axis_index("ctx")
+    mine = lax.axis_index("wa")
+    half = ring // 2
+    lane = lax.rem(me, 2)
+    chip = me // 2
+    pair = me + 1 - 2 * lane
+    peers = [lax.rem(chip + k, half) * 2 + lane for k in range(1, half)]
+    mates = [lax.rem(mine + k, group) for k in range(1, group)]
+    barrier = pltpu.get_barrier_semaphore()
+    for who in [pair] + peers:
+        pl.semaphore_signal(barrier, inc=1, device_id={"ctx": who}, device_id_type=MESH)
+    for who in mates:
+        pl.semaphore_signal(barrier, inc=1, device_id={"wa": who}, device_id_type=MESH)
+    has_next = me < ring - 1
+    has_last = me > 0
+
+    @pl.when(has_next)
+    def _():
+        pl.semaphore_signal(barrier, inc=1, device_id={"ctx": me + 1}, device_id_type=MESH)
+
+    @pl.when(has_last)
+    def _():
+        pl.semaphore_signal(barrier, inc=1, device_id={"ctx": me - 1}, device_id_type=MESH)
+
+    around = jnp.where(has_next, 1, 0) + jnp.where(has_last, 1, 0)
+    pl.semaphore_wait(barrier, half + group - 1 + around)
+
+    to_next = remote(edge, edge_o.at[mine], edge_s, edge_r, {"ctx": me + 1})
+
+    @pl.when(has_next)
+    def _():
+        to_next.start()
+
+    kind = mine // (group // 2)
+    base = 2 * lax.rem(mine, group // 2)
+    for h in range(2):
+        where = base + h
+        send = remote(
+            w_ref.at[h], w_o.at[kind, me], shift_s.at[h], shift_r.at[kind], {"wa": where}
+        )
+        keep = pltpu.make_async_copy(w_ref.at[h], w_o.at[kind, me], shift_r.at[kind])
+
+        @pl.when(where != mine)
+        def _():
+            send.start()
+
+        @pl.when(where == mine)
+        def _():
+            keep.start()
+
+    trades = []
+    for i, (src, dst) in enumerate(((par, par_o), (doc, doc_o), (tok, tok_o))):
+        for k, who in enumerate(mates):
+            copy = remote(src, dst.at[mine], mate_s.at[i, k], mate_r.at[i, k], {"wa": who})
+            copy.start()
+            trades.append(copy)
+        keep = pltpu.make_async_copy(src, dst.at[mine], own_s.at[i])
+        keep.start()
+
+    @pl.when(has_last)
+    def _():
+        to_next.wait_recv()
+        for k, who in enumerate(mates):
+            remote(
+                edge_o.at[mine], edge_o.at[mine], relay_s.at[k], relay_r.at[k], {"wa": who}
+            ).start()
+
+    sends = []
+    for t in range(2):
+        block = w_o.at[t, me]
+        pltpu.make_async_copy(block, block, shift_r.at[t]).wait()
+        for k, who in enumerate(peers):
+            copy = remote(block, block, out_s.at[t, k], out_r.at[t, k], {"ctx": who})
+            copy.start()
+            sends.append(copy)
+        copy = remote(block, block, fwd_s.at[t, 0], fwd_r.at[t, 0], {"ctx": pair})
+        copy.start()
+        sends.append(copy)
+    forwards = []
+    for t in range(2):
+        for k in range(1, half):
+            source = lax.rem(chip + half - k, half) * 2 + lane
+            block = w_o.at[t, source]
+            pltpu.make_async_copy(block, block, out_r.at[t, k - 1]).wait()
+            copy = remote(block, block, fwd_s.at[t, k], fwd_r.at[t, k], {"ctx": pair})
+            copy.start()
+            forwards.append(copy)
+    for t in range(2):
+        for k in range(half):
+            pltpu.make_async_copy(w_o.at[t, me], w_o.at[t, me], fwd_r.at[t, k]).wait()
+    for copy in sends + forwards:
+        copy.wait_send()
+    for h in range(2):
+
+        @pl.when(base + h != mine)
+        def _():
+            remote(
+                w_ref.at[h], w_o.at[kind, me], shift_s.at[h], shift_r.at[kind], {"wa": mine}
+            ).wait_send()
+
+    for copy in trades:
+        copy.wait()
+    for i, (src, dst) in enumerate(((par, par_o), (doc, doc_o), (tok, tok_o))):
+        pltpu.make_async_copy(src, dst.at[mine], own_s.at[i]).wait()
+
+    @pl.when(has_next)
+    def _():
+        to_next.wait_send()
+
+    @pl.when(has_last)
+    def _():
+        for k, who in enumerate(mates):
+            remote(
+                edge_o.at[mine], edge_o.at[mine], relay_s.at[k], relay_r.at[k], {"wa": who}
+            ).wait()
+
+
+def start(tok, edge, par, doc, halves, cid):
+    ring, group = lax.axis_size("ctx"), lax.axis_size("wa")
+    half = ring // 2
+    hbm = pl.BlockSpec(memory_space=pl.ANY)
+    dma = pltpu.SemaphoreType.DMA
+    outs = [(group,) + a.shape for a in (tok, edge, par, doc)] + [(2, ring) + halves.shape[1:]]
+    types = [a.dtype for a in (tok, edge, par, doc, halves)]
+    return pl.pallas_call(
+        functools.partial(start_kernel, ring, group),
+        out_shape=[jax.ShapeDtypeStruct(s, t) for s, t in zip(outs, types)],
+        in_specs=[hbm] * 5,
+        out_specs=[hbm] * 5,
+        scratch_shapes=[
+            dma((3, group - 1)), dma((3, group - 1)), dma((3,)),
+            dma, dma,
+            dma((group - 1,)), dma((group - 1,)),
+            dma((2,)), dma((2,)),
+            dma((2, half - 1)), dma((2, half - 1)),
+            dma((2, half)), dma((2, half)),
+        ],
+        compiler_params=pltpu.CompilerParams(collective_id=cid, has_side_effects=True),
+        cost_estimate=lasting(35),
+        name="start",
+    )(tok, edge, par, doc, halves)
 
 
 def spread(rows, states):
@@ -324,7 +657,7 @@
     return pl.BlockSpec(shape, lambda s: (0,) * len(shape))
 
 
-def scan_call(kernel, name, args, shared, outs, shared_outs, scratch, flops):
+def scan_call(kernel, name, args, shared, outs, shared_outs, scratch, us):
     ordered = []
     specs = []
     for arg in args:
@@ -335,7 +668,6 @@
             ordered.append(arg)
             specs.append(per_stream(arg.shape))
     streams = args[0].shape[0]
-    moved = sum(a.size * a.dtype.itemsize for a in ordered)
     return pl.pallas_call(
         kernel,
         grid=(streams,),
@@ -344,7 +676,7 @@
         out_specs=[per_stream(s) for s in outs] + [whole(s) for s in shared_outs],
         scratch_shapes=scratch,
         compiler_params=pltpu.CompilerParams(vmem_limit_bytes=VMEM_LIMIT),
-        cost_estimate=pl.CostEstimate(flops=flops, bytes_accessed=moved, transcendentals=flops // 10),
+        cost_estimate=lasting(us),
         name=name,
     )(*ordered)
 
@@ -381,13 +713,6 @@
     pads = [(0, 0)] * array.ndim
     pads[axis] = (0, width - array.shape[axis])
     return jnp.pad(array, pads)
-
-
-def shift_pairs(group):
-    half = group // 2
-    first = [(v, 2 * v) if v < half else (v, 2 * (v - half) + 1) for v in range(group)]
-    second = [(v, 2 * v + 1) if v < half else (v, 2 * (v - half)) for v in range(group)]
-    return first, second
 
 
 def body(
@@ -409,62 +734,50 @@
     total_rows = group * length
     edge = taps - 1
 
-    first, second = shift_pairs(group)
-    rows_in = width // ring
-    part_in = lax.dynamic_slice_in_dim(w_in, place * rows_in, rows_in, 0)
-    low_half, high_half = part_in[:, :local], part_in[:, local:]
-    upper = mine >= group // 2
-    came_a = lax.ppermute(jnp.where(upper, high_half, low_half), "wa", first)
-    came_b = lax.ppermute(jnp.where(upper, low_half, high_half), "wa", second)
-    odd = mine % 2 == 1
-    both = jnp.concatenate(
-        [
-            padded_lanes(jnp.where(odd, came_b, came_a), padded, 1),
-            padded_lanes(jnp.where(odd, came_a, came_b), padded, 1),
-        ],
-        axis=1,
-    )
-    proj_in = lax.all_gather(both, "ctx", axis=0, tiled=True)
-
-    up_rows, down_rows, proj_in = lax.optimization_barrier((w_up[0].T, w_down[0], proj_in))
-    expert_up = lax.all_gather(up_rows, "ctx", axis=0, tiled=True)
-    expert_down = lax.all_gather(down_rows, "ctx", axis=0, tiled=True)
-
-    at = place * length + lax.iota(jnp.int32, length)
-    starts = doc_starts[0]
-    resets = jnp.any(at[:, None] == starts[None, :], axis=1)
-    marks = [resets]
+    def up16(n):
+        return -(-n // 16) * 16
+
+    expert_up = lax.all_gather(w_up[0].T, "ctx", axis=0, tiled=True)
+    expert_down = lax.all_gather(w_down[0], "ctx", axis=0, tiled=True)
+
+    in_each = -(-width // ring)
+    in_rows = up16(in_each)
+    part_in = lax.dynamic_slice_in_dim(w_in, place * in_each, in_each, 0)
+    halves = jnp.stack([part_in[:, :local], part_in[:, local:]], axis=0)
+    halves = jnp.pad(halves, ((0, 0), (0, in_rows - in_each), (0, padded - local)))
+    share = norm_mix.shape[0]
+    small = jnp.concatenate([norm_mix, norm_moe, w_router.T.reshape(-1)], axis=0)
+    small_count = up16(-(-small.shape[0] // LANE))
+    small = jnp.pad(small, (0, small_count * LANE - small.shape[0])).reshape(small_count, LANE)
+    first_rows = doc_starts.shape[1]
+    doc_tile = jnp.pad(doc_starts, ((0, 7), (0, LANE - first_rows)))
+    own_tokens = interleaved(tokens[0])
+    all_rows, all_edges, smalls, docs, w_blocks = start(
+        own_tokens, tokens[0, length - 16 :], small, doc_tile, halves, 1
+    )
+    proj_in_x, proj_in_z = [w_blocks[t, :, :in_each].reshape(width, padded) for t in range(2)]
+    smalls = smalls.reshape(group, -1)[:, : (2 + experts) * share]
+    smalls = smalls.reshape(group, 2 + experts, share).swapaxes(0, 1).reshape(2 + experts, width)
+    gain_mix, gain_moe = smalls[0].astype(F32), smalls[1].astype(F32)
+    router = smalls[2:]
+
+    at = interleaved(place * length + lax.iota(jnp.int32, length))[None, :, None]
+    begins = docs[:, :1, :first_rows]
+    cuts = jnp.any(at == begins, axis=2).reshape(total_rows, 1)
+    lag_keep = [None]
     for lag in range(1, taps):
-        cut = jnp.any(
-            (starts[None, :] > at[:, None] - lag) & (starts[None, :] <= at[:, None]), axis=1
-        )
-        marks.append(~cut)
-    marks = interleaved(jnp.stack(marks, axis=1).astype(BF16))
-    small = jnp.concatenate(
-        [norm_mix, norm_moe, w_router.reshape(-1), marks.reshape(-1)], axis=0
-    )
-    smalls = lax.all_gather(small, "wa")
-    share = norm_mix.shape[0]
-    gain_mix = smalls[:, :share].reshape(-1).astype(F32)
-    gain_moe = smalls[:, share : 2 * share].reshape(-1).astype(F32)
-    router = smalls[:, 2 * share : (2 + experts) * share].reshape(width, experts)
-    masks = smalls[:, (2 + experts) * share :].reshape(total_rows, taps).astype(F32)
-    cuts = masks[:, 0:1] * CUT
-    lag_keep = [None] + [masks[:, lag : lag + 1] for lag in range(1, taps)]
-
-    own_tokens = interleaved(tokens[0])
-    pairs = [(i, i + 1) for i in range(ring - 1)]
-    before_edge = lax.ppermute(tokens[0, length - edge :], "ctx", pairs)
-    before_edge = jnp.pad(before_edge, ((SEG - edge, 0), (0, 0)))
-    with_edge = jnp.concatenate([own_tokens, before_edge], axis=0)
-    with_edge = jnp.pad(with_edge, ((0, 8), (0, 0)))
-    all_tokens = gather_all(with_edge, "wa", 1)[:, : length + SEG].astype(F32)
+        cut = jnp.any((begins > at - lag) & (begins <= at), axis=2)
+        lag_keep.append(1.0 - cut.astype(F32).reshape(total_rows, 1))
+
+    edge_rows = jnp.where(place > 0, all_edges[:, 16 - SEG :], jnp.zeros((), BF16))
+    all_tokens = jnp.concatenate([all_rows, edge_rows], axis=1).astype(F32)
     scale_in = rms_scale(all_tokens)
     n1 = (all_tokens * scale_in * gain_mix).astype(BF16)
     flat_n1 = n1.reshape(group * (length + SEG), width)
-    joined = jnp.dot(flat_n1, proj_in, preferred_element_type=F32).astype(BF16)
-    joined = joined.reshape(group, length + SEG, 2 * padded)
-    gate_z = joined[:, :length, padded:].astype(F32)
+    n1_rows = n1[:, :length].reshape(total_rows, width)
+    joined_x = jnp.dot(flat_n1, proj_in_x, preferred_element_type=F32).astype(BF16)
+    joined_x = joined_x.reshape(group, length + SEG, padded)
+    gate_z = jnp.dot(n1_rows, proj_in_z, preferred_element_type=F32).astype(BF16).astype(F32)
 
     conv_taps = padded_lanes(conv_w, padded, 1).astype(F32)
     conv_bias = padded_lanes(conv_b, padded, 0).astype(F32)
@@ -475,8 +788,8 @@
     skip_gain = padded_lanes(d_skip, padded, 0).astype(F32)
     proj_out = padded_lanes(w_out, padded, 0)
 
-    x_inner = joined[:, :length, :padded].astype(F32).reshape(group, steps, SEG, padded)
-    x_edge = joined[:, length + SEG - edge :, :padded].astype(F32)
+    x_inner = joined_x[:, :length].astype(F32).reshape(group, steps, SEG, padded)
+    x_edge = joined_x[:, length + SEG - edge :].astype(F32)
     head = jnp.concatenate(
         [x_edge[:, :, None, :], x_inner[:, steps - edge :, : SEG - 1, :]], axis=2
     )
@@ -495,14 +808,14 @@
     u = jax.nn.silu(pre_conv).astype(BF16)
     u_f = u.astype(F32)
     part = jnp.dot(u, proj_x, preferred_element_type=F32).astype(BF16)
-    projected = jnp.sum(gather_all(part, "wa", 2).astype(F32), axis=0).astype(BF16)
+    projected = jnp.sum(gather_all(part, "wa", 2, 15).astype(F32), axis=0).astype(BF16)
     dt_low = projected[:, :ranked]
     b_sel = projected[:, ranked : ranked + states].reshape(group, length, states)
     c_sel = projected[:, ranked + states :].reshape(group, length, states)
     step_pre = jnp.dot(dt_low, proj_dt, preferred_element_type=F32) + step_bias
     step_size = jax.nn.softplus(step_pre)
     drive = step_size * u_f
-    step_cut = jnp.where(cuts > 0, CUT, step_size)
+    step_cut = jnp.where(cuts, CUT, step_size)
 
     def streams(array):
         return array.reshape(group, length, padded)
@@ -513,16 +826,15 @@
     seg_sums = (group, SEG, padded)
     dev_states = (group, states, padded)
     dev_sums = (group, 1, padded)
-    updates = group * length * states * padded
     broad = pltpu.VMEM((length, states * LANE), F32)
     sizes = (states, steps, lane_groups)
     h_in, s_in, h_dev, s_dev = scan_call(
         functools.partial(summary_kernel, *sizes), "scan_summary",
         [st, dr, b_sel, 0], [a_mat],
-        [seg_states, seg_sums, dev_states, dev_sums], [], [broad], 6 * updates,
+        [seg_states, seg_sums, dev_states, dev_sums], [], [broad], 8,
     )
     sent = jnp.concatenate([h_dev, s_dev], axis=1).reshape(group * (states + 1), padded)
-    all_dev = gather_all(sent, "ctx", 3).reshape(ring, group, states + 1, padded)
+    all_dev = gather_all(sent, "ctx", 3, 18).reshape(ring, group, states + 1, padded)
     all_sums = all_dev[:, :, states:, :]
     order = lax.iota(jnp.int32, ring)
 
@@ -543,21 +855,22 @@
     (y_scan,) = scan_call(
         functools.partial(output_kernel, *sizes), "scan_output",
         [st, dr, b_sel, c_sel, 0, h_in, s_in, entering], [a_mat],
-        [vreg], [], [broad, broad], 8 * updates,
-    )
-    gate_z = gate_z.reshape(total_rows, padded)
+        [vreg], [], [broad, broad], 10,
+    )
     y_full = y_scan.reshape(total_rows, padded) + skip_gain * u_f
     silu_z = jax.nn.silu(gate_z)
     gated = (y_full * silu_z).astype(BF16)
     mix_part = jnp.dot(gated, proj_out, preferred_element_type=F32).astype(BF16)
-    mix_terms = trade(mix_part.reshape(group, length, width), "wa", 4)
+    mix_terms = trade(mix_part.reshape(group, length, width), "wa", 4, 25)
     mix = jnp.sum(mix_terms.astype(F32), axis=0)
 
     stream = own_tokens.astype(F32)
     h1 = stream + mix
     scale_moe = rms_scale(h1)
     n2 = (h1 * scale_moe * gain_moe).astype(BF16)
-    logits = jnp.dot(n2, router, preferred_element_type=F32)
+    logits = lax.dot_general(
+        n2, router, (((1,), (1,)), ((), ())), preferred_element_type=F32
+    )
     route_in_order = routes[0, :, 0]
     onehot_in_order = route_in_order[:, None] == lax.iota(jnp.int32, experts)[None, :]
     counted = onehot_in_order.astype(jnp.int32)
@@ -575,7 +888,7 @@
     outgoing = jnp.dot(
         match, jnp.concatenate([n2, d_rows], axis=1), preferred_element_type=F32
     ).astype(BF16)
-    arrived = trade(outgoing.reshape(group, slots // group, 2 * width), "wa", 5)
+    arrived = trade(outgoing.reshape(group, slots // group, 2 * width), "wa", 5, 29)
     arrived = arrived.reshape(slots, 2 * width)
     expert_in, d_out = arrived[:, :width], arrived[:, width:]
     hidden_pre = lax.dot_general(
@@ -590,19 +903,21 @@
     d_pre = gelu_back(d_act)[0].astype(BF16)
     d_in = jnp.dot(d_pre, expert_up, preferred_element_type=F32).astype(BF16)
     returning = jnp.concatenate([produced, d_in], axis=1)
-    returned = trade(returning.reshape(group, slots // group, 2 * width), "wa", 6)
-    back_rows = lax.dot_general(
-        match, returned.reshape(slots, 2 * width), (((0,), (0,)), ((), ())),
-        preferred_element_type=F32,
-    )
     grad_up = lax.dot_general(
         d_pre, expert_in, (((0,), (0,)), ((), ())), preferred_element_type=F32
     ).astype(BF16)
     grad_down = lax.dot_general(
         act, d_out, (((0,), (0,)), ((), ())), preferred_element_type=F32
     ).astype(BF16)
-    share_up = lax.psum_scatter(grad_up, "ctx", scatter_dimension=0, tiled=True)
-    share_down = lax.psum_scatter(grad_down, "ctx", scatter_dimension=0, tiled=True)
+    returning, grad_up, grad_down = lax.optimization_barrier((returning, grad_up, grad_down))
+    share_up, share_down = lax.psum_scatter(
+        (grad_up, grad_down), "ctx", scatter_dimension=0, tiled=True
+    )
+    returned = trade(returning.reshape(group, slots // group, 2 * width), "wa", 6, 29)
+    back_rows = lax.dot_general(
+        match, returned.reshape(slots, 2 * width), (((0,), (0,)), ((), ())),
+        preferred_element_type=F32,
+    )
     expert_rows, d_slot = back_rows[:, :width], back_rows[:, width:]
     moe = gates[:, None] * expert_rows
     result = h1 + moe
@@ -614,30 +929,37 @@
     grad_router = lax.dot_general(
         n2, d_logits, (((0,), (0,)), ((), ())), preferred_element_type=F32
     )
-    d_n2 = d_slot + lax.dot_general(
-        d_logits, router, (((1,), (1,)), ((), ())), preferred_element_type=F32
-    )
+    d_n2 = d_slot + jnp.dot(d_logits, router, preferred_element_type=F32)
     d_norm, gain_terms = norm_grads(h1, scale_moe, gain_moe, d_n2)
     grad_gain_moe = jnp.sum(gain_terms, axis=0)
     d_h1 = upstream + d_norm
-    d_mix = gather_all(d_h1.astype(BF16), "wa", 7).reshape(total_rows, width)
-
-    grad_out = lax.dot_general(
-        gated, d_mix, (((0,), (0,)), ((), ())), preferred_element_type=F32
-    )
+    d_mix = gather_all(d_h1.astype(BF16), "wa", 7, 28).reshape(total_rows, width)
+
     d_gated = lax.dot_general(
         d_mix, proj_out, (((1,), (1,)), ((), ())), preferred_element_type=F32
     )
     d_y = d_gated * silu_z
     d_z = d_gated * y_full * silu_slope(gate_z)
     grad_skip = jnp.sum(d_y * u_f, axis=0)
+    d_zs = d_z.astype(BF16)
+    grad_in_z = lax.dot_general(
+        n1_rows, d_zs, (((0,), (0,)), ((), ())), preferred_element_type=F32
+    )
+    grad_out = lax.dot_general(
+        d_mix, gated, (((0,), (0,)), ((), ())), preferred_element_type=F32
+    )
+    grad_zo = jnp.concatenate([grad_in_z[:, :local], grad_out[:, :local]], axis=1).astype(BF16)
     dys = streams(d_y)
     f_in, t_in, f_dev = scan_call(
         functools.partial(back_summary_kernel, *sizes), "scan_back_summary",
         [st, c_sel, dys, 0], [a_mat],
-        [seg_states, seg_sums, dev_states], [], [broad], 6 * updates,
-    )
-    all_back = gather_all(f_dev.reshape(group * states, padded), "ctx", 8)
+        [seg_states, seg_sums, dev_states], [], [broad], 8,
+    )
+    all_back = gather_all(f_dev.reshape(group * states, padded), "ctx", 8, 18)
+    all_back, share_up, share_down, grad_zo = lax.optimization_barrier(
+        (all_back, share_up, share_down, grad_zo)
+    )
+    chunk_zo = lax.psum_scatter(grad_zo, "ctx", scatter_dimension=0, tiled=True)
     leaving = reached(all_back.reshape(ring, group, states, padded), False)
     small_rows = (group, length, states)
     longer = pltpu.VMEM((length + SEG, states * LANE), F32)
@@ -645,7 +967,7 @@
         functools.partial(back_kernel, *sizes), "scan_back",
         [st, dr, us, b_sel, c_sel, dys, 0, h_in, s_in, entering, f_in, t_in, leaving], [a_mat],
         [vreg, vreg, small_rows, small_rows], [(states, SEG, padded)],
-        [broad, broad, broad, longer, broad, broad], 20 * updates,
+        [broad, broad, broad, longer, broad, broad], 30,
     )
     grad_a_log = jnp.sum(grad_a, axis=1) * a_mat
     d_step_pre = d_step.reshape(total_rows, padded) * jax.nn.sigmoid(step_pre)
@@ -660,7 +982,7 @@
     d_part = jnp.concatenate(
         [d_low, grad_b.reshape(total_rows, states), grad_c.reshape(total_rows, states)], axis=1
     ).astype(BF16)
-    d_projected = jnp.sum(gather_all(d_part, "wa", 9).astype(F32), axis=0).astype(BF16)
+    d_projected = jnp.sum(gather_all(d_part, "wa", 9, 14).astype(F32), axis=0).astype(BF16)
     grad_x = lax.dot_general(
         u, d_projected, (((0,), (0,)), ((), ())), preferred_element_type=F32
     )
@@ -686,78 +1008,104 @@
     d_inner = (d_extended[:, edge:] + inside).reshape(group, length, padded)
     d_edge = jnp.pad(head[:, :, 0], ((0, 0), (SEG - edge, 0), (0, 0)))
     d_x = jnp.concatenate([d_inner, d_edge], axis=1)
-    d_zs = jnp.pad(d_z.reshape(group, length, padded), ((0, 0), (0, SEG), (0, 0)))
-    d_joined = jnp.concatenate([d_x, d_zs], axis=2).astype(BF16)
-    d_joined = d_joined.reshape(group * (length + SEG), 2 * padded)
-    grad_in = lax.dot_general(
-        flat_n1, d_joined, (((0,), (0,)), ((), ())), preferred_element_type=F32
-    )
+    d_x = d_x.astype(BF16).reshape(group * (length + SEG), padded)
+    grad_in_x = lax.dot_general(
+        flat_n1, d_x, (((0,), (0,)), ((), ())), preferred_element_type=F32
+    )[:, :local]
+    d_n1_z = lax.dot_general(
+        d_zs, proj_in_z, (((1,), (1,)), ((), ())), preferred_element_type=F32
+    ).reshape(group, length, width)
     d_n1_part = lax.dot_general(
-        d_joined, proj_in, (((1,), (1,)), ((), ())), preferred_element_type=F32
-    ).astype(BF16)
-    d_n1_part = jnp.pad(
-        d_n1_part.reshape(group, length + SEG, width), ((0, 0), (0, 8), (0, 0))
-    )
-    d_n1_terms = trade(d_n1_part, "wa", 10)
+        d_x, proj_in_x, (((1,), (1,)), ((), ())), preferred_element_type=F32
+    )
+    d_n1_part = d_n1_part.reshape(group, length + SEG, width)
+    d_n1_part = d_n1_part + jnp.pad(d_n1_z, ((0, 0), (0, SEG), (0, 0)))
+    unit = all_tokens * scale_in
+    grad_gain_mix = jnp.sum(d_n1_part * unit, axis=(0, 1))
+    d_n1_part = jnp.pad(d_n1_part.astype(BF16), ((0, 0), (0, 8), (0, 0)))
+
+    def dealt(rows, count):
+        each = -(-rows.shape[0] // ring)
+        rows = jnp.pad(rows, ((0, each * ring - rows.shape[0]), (0, 0)))
+        return jnp.pad(rows.reshape(ring, each, -1), ((0, 0), (0, count - each), (0, 0)))
+
+    small = jnp.concatenate(
+        [
+            jnp.stack(tap_grads, axis=0),
+            grad_conv_bias[None],
+            grad_step_bias[None],
+            grad_skip[None],
+            grad_a_log,
+            grad_dt,
+            grad_x.T,
+        ],
+        axis=0,
+    )[:, :local].astype(BF16)
+    small_each = -(-small.shape[0] // ring)
+    small_rows = up16(small_each)
+    fulls = jnp.stack([grad_gain_mix, grad_gain_moe] + [grad_router[:, e] for e in range(experts)])
+    fulls = fulls.reshape(2 + experts, group, share).swapaxes(0, 1).reshape(group, -1)
+    full_each = -(-fulls.shape[1] // ring)
+    fulls = jnp.pad(fulls, ((0, 0), (0, full_each * ring - fulls.shape[1])))
+    fulls = fulls.reshape(group, ring, full_each).swapaxes(0, 1)
+    coarse = sums.astype(BF16).astype(F32)
+    stat_row = jnp.concatenate([coarse, (sums - coarse)])
+    is_mine = (lax.iota(jnp.int32, group) == mine).astype(F32)
+    stat_rows = jnp.broadcast_to(
+        is_mine[None, :, None] * stat_row[None, None, :], (ring, group, stat_row.shape[0])
+    )
+    fulls = jnp.pad(fulls, ((0, 0), (0, 0), (0, local - full_each)))
+    stat_rows = jnp.pad(stat_rows, ((0, 0), (0, 0), (0, local - stat_row.shape[0])))
+    tile = jnp.concatenate([fulls, stat_rows], axis=1)
+    tile = jnp.pad(tile, ((0, 0), (0, 16 - tile.shape[1]), (0, 0))).astype(BF16)
+    packed = jnp.concatenate(
+        [dealt(grad_in_x.astype(BF16), in_rows), dealt(small, small_rows), tile], axis=1
+    )
+    packed = packed.reshape((ring // 2, 2) + packed.shape[1:]).swapaxes(0, 1)
+    chunk_zo = jnp.pad(chunk_zo, ((0, in_rows - in_each), (0, 0)))
+    chunk_z, chunk_o = chunk_zo[:, :local], chunk_zo[:, local:]
+    done, d_n1_terms = finish(packed, chunk_z, chunk_o, d_n1_part, in_rows, small_rows, 11)
+    share_in = jnp.concatenate(
+        [done[:, :in_each], done[:, in_rows : in_rows + in_each]], axis=2
+    ).reshape(width, 2 * local).astype(F32)
+    base = 2 * in_rows
+    share_out = done[:, base : base + in_each].reshape(width, local).T.astype(F32)
+    base = base + in_rows
+    smalls_sum = done[:, base : base + small_each].reshape(ring * small_each, local).astype(F32)
+    base = base + small_rows
+    full_sum = lax.dynamic_index_in_dim(done, base + mine, 1, False)[:, :full_each]
+    full_sum = full_sum.reshape(-1)[: (2 + experts) * share].reshape(2 + experts, share).astype(F32)
+    stat_sum = lax.dynamic_index_in_dim(done, base + group + mine, 1, False)[0, :6].astype(F32)
+
     d_n1_sum = jnp.sum(d_n1_terms[:, : length + SEG].astype(F32), axis=0)
     back_pairs = [(i + 1, i) for i in range(ring - 1)]
     came = lax.ppermute(d_n1_sum[length + SEG - edge :], "ctx", back_pairs)
     last_rows = jnp.pad(came[:, None, :], ((steps - edge, 0), (SEG - 1, 0), (0, 0)))
     d_n1 = d_n1_sum[:length] + last_rows.reshape(length, width)
     scale_mix = rms_scale(stream)
-    d_stream, gain_terms = norm_grads(stream, scale_mix, gain_mix, d_n1)
-    grad_gain_mix = jnp.sum(gain_terms, axis=0)
+    d_stream, _ = norm_grads(stream, scale_mix, gain_mix, d_n1)
     input_grad = d_h1 + d_stream
-
-    grad_in = jnp.concatenate(
-        [grad_in[:, :local], grad_in[:, padded : padded + local]], axis=1
-    ).astype(BF16)
-    slice_in = lax.psum_scatter(grad_in, "ctx", scatter_dimension=0, tiled=True)
-    of_x, of_z = slice_in[:, :local], slice_in[:, local:]
-    went_a = lax.ppermute(jnp.where(odd, of_z, of_x), "wa", [(b, a) for a, b in first])
-    went_b = lax.ppermute(jnp.where(odd, of_x, of_z), "wa", [(b, a) for a, b in second])
-    slice_in = jnp.concatenate(
-        [jnp.where(upper, went_b, went_a), jnp.where(upper, went_a, went_b)], axis=1
-    )
-    share_in = lax.all_gather(slice_in, "ctx", axis=0, tiled=True).astype(F32)
-    share_out = lax.all_gather(
-        lax.psum_scatter(grad_out[:local].astype(BF16), "ctx", scatter_dimension=0, tiled=True),
-        "ctx", axis=0, tiled=True,
-    ).astype(F32)
-    totals = lax.psum(
-        (
-            jnp.stack(tap_grads, axis=0)[:, :local],
-            grad_conv_bias[:local],
-            grad_x[:local],
-            grad_dt[:, :local],
-            grad_step_bias[:local],
-            grad_a_log[:, :local],
-            grad_skip[:local],
-            sums,
-        ),
-        "ctx",
-    )
-    wide_totals = lax.psum((grad_gain_mix, grad_gain_moe, grad_router), ("ctx", "wa"))
-    share_mix, share_moe, share_router = [
-        lax.dynamic_slice_in_dim(t, mine * share, share, 0) for t in wide_totals
-    ]
+    marks_at = [0, taps, taps + 1, taps + 2, taps + 3, taps + 3 + states]
+    marks_at += [marks_at[-1] + ranked, marks_at[-1] + ranked + w_x.shape[1]]
+    cut_at = [smalls_sum[a:b] for a, b in zip(marks_at[:-1], marks_at[1:])]
+    stat_sums = stat_sum[:3] + stat_sum[3:]
     denom = length * ring * width
-    rms_stats = jnp.sqrt(totals[7] / denom)[None]
+    rms_stats = jnp.sqrt(stat_sums / denom)[None]
     return (
         in_order(result)[None],
         in_order(input_grad)[None],
-        share_mix,
+        full_sum[0],
         share_in,
-        totals[0],
-        totals[1],
-        totals[2],
-        totals[3],
-        totals[4],
-        totals[5],
-        totals[6],
+        cut_at[0],
+        cut_at[1][0],
+        cut_at[6].T,
+        cut_at[5],
+        cut_at[2][0],
+        cut_at[4],
+        cut_at[3][0],
         share_out,
-        share_moe,
-        share_router,
+        full_sum[1],
+        full_sum[2:].T,
         share_up.T.astype(F32)[None],
         share_down.astype(F32)[None],
         rms_stats,

time: 806 us -> 650 us (0.81)
  waiting for transfers between devices: 222 us -> 41.9 us
  Pallas kernels: 300 us -> 385 us
  blocking collectives: 76.8 us -> 0 us
  local copies, waits for them, and re-layouts: 35.7 us -> 65.8 us
  starting transfers between devices: 15.5 us -> 2.21 us
  matrix products: 65.9 us -> 77.5 us
  other arithmetic: 59.9 us -> 50.9 us
    pallas_call x0 -> x2, Pallas kernels: none -> 116 us  [the longest x1 74.2 us: finish(): pl.pallas_call(functools.partial(finish_kernel, ring, group, in_rows, sma...]
    psum x2 -> x0, blocking collectives: 64.5 us -> none  [the longest x1 40.8 us: body(): lax.psum((grad_gain_mix, grad_gain_moe, grad_router), ('ctx', 'wa'))]
    psum x1 -> x0, waiting for transfers between devices: 52.6 us -> none  [body(): lax.psum((jnp.stack(tap_grads, axis=0)[:, :local], grad_conv_bias[:local]...]
    reduce_scatter x3, waiting for transfers between devices: 93 us -> 40.4 us  [the longest x1 20.5 us: body(): chunk_zo = lax.psum_scatter(grad_zo, 'ctx', scatter_dimension=0, tiled=True)]
    all_gather x5 -> x2, waiting for transfers between devices: 33.9 us -> 0.02 us  [the longest x1 0.02 us: body(): expert_up = lax.all_gather(w_up[0].T, 'ctx', axis=0, tiled=True)]
    pallas_call x10 -> x8, Pallas kernels: 243 us -> 212 us  [exchange(): pl.pallas_call(functools.partial(kernel, axis, count), out_shape=jax.Shap...]
    unnamed x11 -> x5, waiting for transfers between devices: 29.6 us -> 1.43 us
    slice x4 -> x18, local copies, waits for them, and re-layouts: 2 us -> 20.7 us  [the longest x4 5.86 us: body(): cut_at = [smalls_sum[a:b] for a, b in zip(marks_at[:-1], marks_at[1:])]]
  transfers between devices with their start and end apart: 16 -> 6, of which waited for: 9 -> 2; matrix products, arithmetic and copies ran while one was open for 13% -> 19% of each run, Pallas kernels for 22% -> 41%
where the time goes in v2:
time: 650 us; the launch traced here: 639 us
  Pallas kernels  385 us (59%)
  matrix products  77.5 us (12%)
  local copies, waits for them, and re-layouts  65.8 us (10%)
  other arithmetic  50.9 us (8%)
  waiting for transfers between devices  41.9 us (6%)
  between operations  16 us (2%)
    pallas_call x8, Pallas kernels, exchange(): pl.pallas_call(functools.partial(kernel, axis, count), out_shape=jax.Shap...  212 us
    pallas_call x1, Pallas kernels, finish(): pl.pallas_call(functools.partial(finish_kernel, ring, group, in_rows, sma...  74.2 us
    pallas_call x4, Pallas kernels, scan_call(): pl.pallas_call(kernel, grid=(streams,), out_shape=[jax.ShapeDtypeStruct(s...  56.4 us
    pallas_call x1, Pallas kernels, start(): pl.pallas_call(functools.partial(start_kernel, ring, group), out_shape=[j...  41.7 us
    reduce_scatter x1, waiting for transfers between devices, body(): chunk_zo = lax.psum_scatter(grad_zo, 'ctx', scatter_dimension=0, tiled=True)  20.5 us
    reduce_scatter x2, waiting for transfers between devices, body(): lax.psum_scatter((grad_up, grad_down), 'ctx', scatter_dimension=0, tiled=...  19.9 us
    unnamed x242, local copies, waits for them, and re-layouts  16.7 us
    dot_general x1, matrix products, body(): lax.dot_general(d_pre, expert_in, (((0,), (0,)), ((), ())), preferred_ele...  15.5 us
  transfers between devices with their start and end apart: 6, of which 2 were waited for; matrix products, arithmetic and copies ran while one was open for 19% of the time, Pallas kernels for 41%

profile of v2, /device:TPU:11, one launch (start us, length us, event | category | flops | bytes accessed | tf_op | source)
XLA Modules:
  0.0 638.9 jit_solution(11791574983221851796)
XLA Ops:
  13.5 41.7 %start.1 = (bf16[4,128,1152]{2,1,0:T(8,128)(2,1)}, bf16[4,16,1152]{2,1,0:T(8,128)(2,1)}, bf16[4,16,128]{2,1,0:T(8,128)(2,1)}, s32[4,8,128]{2,1,0:T(8,128)}, bf16[2,8,144,640]{3,2,1,0:T(8,128)(2,1)}) custom-call(bf16[128,1152]{1,0:T(8,128)(2,1)} %bitcast.322, bf16[16,1152]{1,0:T(8,128)(2,1)} %slice_bitcast_fusion.2.edge, ...), custom_call_target="tpu_custom_call" | custom-call | flops 38499999744 | bytes 122500000 | tf_op jit(solution)/shard_map/start/pallas_call | solution.py:412
  74.3 13.4 %shard_map.314 = bf16[4,512,104]{2,1,0:T(8,128)(2,1)} custom-call(bf16[512,104]{1,0:T(8,128)(2,1)} %copy.252.x_ref), custom_call_target="tpu_custom_call" | custom-call | flops 16499999744 | bytes 52500000 | tf_op jit(solution)/shard_map/pallas_call | solution.py:82
  92.4 8.0 %scan_summary.1 = (f32[4,16,8,640]{3,2,1,0:T(8,128)S(1)}, f32[4,8,640]{2,1,0:T(8,128)S(1)}, f32[4,16,640]{2,1,0:T(8,128)S(1)}, f32[4,1,640]{2,1,0:T(1,128)S(1)}) custom-call(f32[4,128,640]{2,1,0:T(8,128)S(1)} %bitcast.264, f32[4,128,640]{2,1,0:T(8,128)S(1)} %bitcast.261, bf16[4,128,16]{2,1,0:T(8,128)(2,1)S(1)} %bitcast.274, ...), custom_call_target="tpu_custom_call" | custom-call | flops 8800000000 | bytes 28000000 | tf_op jit(solution)/shard_map/scan_summary/pallas_call | solution.py:671
  102.2 37.1 %shard_map.315 = f32[8,68,640]{2,1,0:T(8,128)} custom-call(f32[68,640]{1,0:T(8,128)} %reshape.707.x_ref), custom_call_target="tpu_custom_call" | custom-call | flops 19800000512 | bytes 63000000 | tf_op jit(solution)/shard_map/pallas_call | solution.py:82
  145.2 9.7 %scan_output.1 = f32[4,128,640]{2,1,0:T(8,128)S(1)} custom-call(f32[4,128,640]{2,1,0:T(8,128)S(1)} %bitcast.265, f32[4,128,640]{2,1,0:T(8,128)S(1)} %bitcast.262, bf16[4,128,16]{2,1,0:T(8,128)(2,1)S(1)} %bitcast.275, bf16[4,128,16]{2,1,0:T(8,128)(2,1)S(1)} %bitcast.271, f32[16,640]{1,0:T(8,128)S(1)} %exponential_negate_fusion.a_ref, ...), custom_call_target="tpu_custom_call" | custom-call | flops 11000000512 | bytes 35000000 | tf_op jit(solution)/shard_map/scan_output/pallas_call | solution.py:671
  159.2 28.0 %shard_map.316 = bf16[4,128,1152]{2,1,0:T(8,128)(2,1)} custom-call(bf16[4,128,1152]{2,1,0:T(8,128)(2,1)} %bitcast.341), custom_call_target="tpu_custom_call" | custom-call | flops 27499999232 | bytes 87500000 | tf_op jit(solution)/shard_map/pallas_call | solution.py:82
  196.4 29.1 %shard_map.317 = bf16[4,64,2304]{2,1,0:T(8,128)(2,1)} custom-call(bf16[4,64,2304]{2,1,0:T(8,128)(2,1)} %bitcast.303), custom_call_target="tpu_custom_call" | custom-call | flops 31900000256 | bytes 101500000 | tf_op jit(solution)/shard_map/pallas_call | solution.py:82
  225.6 5.5 fusion.79
  232.7 5.6 convolution_convert_fusion
  238.4 7.6 %fusion.10 = bf16[256,3072]{1,0:T(8,128)(2,1)S(1)} fusion(f32[256,3072]{1,0:T(8,128)} %copy-done.111, bf16[1,3072,1152]{2,1,0:T(8,128)(2,1)} %all-gather.6.cloned.1.call-done, bf16[256,2304]{1,0:T(8,128)(2,1)} %bitcast.318), kind=kOutput, calls=%fused_computation.18 | convolution fusion | flops 1827667968 | bytes 12386304 | tf_op jit(solution)/shard_map/dot_general | solution.py:900
  246.0 15.5 %convolution_convert_fusion.1 = bf16[3072,1152]{1,0:T(8,128)(2,1)} fusion(bf16[256,3072]{1,0:T(8,128)(2,1)S(1)} %fusion.10, bf16[256,2304]{1,0:T(8,128)(2,1)S(1)} %bitcast.320), kind=kOutput, calls=%fused_computation.1 | convolution fusion | flops 1815478272 | bytes 9240576 | tf_op jit(solution)/shard_map/dot_general | solution.py:906
  261.5 5.4 convolution_convert_fusion.4
  266.9 5.5 fusion.15
  276.7 28.8 %shard_map.318 = bf16[4,64,2304]{2,1,0:T(8,128)(2,1)} custom-call(bf16[4,64,2304]{2,1,0:T(8,128)(2,1)} %bitcast.302), custom_call_target="tpu_custom_call" | custom-call | flops 31900000256 | bytes 101500000 | tf_op jit(solution)/shard_map/pallas_call | solution.py:82
  317.0 27.4 %shard_map.319 = bf16[4,128,1152]{2,1,0:T(8,128)(2,1)} custom-call(bf16[128,1152]{1,0:T(8,128)(2,1)} %get-tuple-element.208.x_ref), custom_call_target="tpu_custom_call" | custom-call | flops 30799998976 | bytes 98000000 | tf_op jit(solution)/shard_map/pallas_call | solution.py:82
  344.5 4.1 fusion.29
  358.9 8.4 %scan_back_summary.1 = (f32[4,16,8,640]{3,2,1,0:T(8,128)S(1)}, f32[4,8,640]{2,1,0:T(8,128)S(1)}, f32[4,16,640]{2,1,0:T(8,128)S(1)}) custom-call(f32[4,128,640]{2,1,0:T(8,128)S(1)} %bitcast.266, bf16[4,128,16]{2,1,0:T(8,128)(2,1)S(1)} %bitcast.272, f32[4,128,640]{2,1,0:T(8,128)S(1)} %bitcast.268, f32[16,640]{1,0:T(8,128)S(1)} %exponential_negate_fusion.a_ref), custom_call_target="tpu_custom_call" | custom-call | flops 8800000000 | bytes 28000000 | tf_op jit(solution)/shard_map/scan_back_summary/pallas_call | solution.py:671
  369.1 33.2 %shard_map.320 = f32[8,64,640]{2,1,0:T(8,128)} custom-call(f32[64,640]{1,0:T(8,128)} %bitcast.277), custom_call_target="tpu_custom_call" | custom-call | flops 19800000512 | bytes 63000000 | tf_op jit(solution)/shard_map/pallas_call | solution.py:82
  402.4 19.9 %reduce-scatter.6.cloned.1.call-done = bf16[384,1152]{1,0:T(8,128)(2,1)} async-done(((bf16[3072,1152]{1,0:T(8,128)(2,1)}), bf16[384,1152]{1,0:T(8,128)(2,1)}) %reduce-scatter.6.cloned.1.call-update) | async-done | bytes 884752 | tf_op jit(solution)/shard_map/reduce_scatter | solution.py:913
  424.0 30.2 %scan_back.1 = (f32[4,128,640]{2,1,0:T(8,128)S(1)}, f32[4,128,640]{2,1,0:T(8,128)S(1)}, f32[4,128,16]{2,1,0:T(8,128)S(1)}, f32[4,128,16]{2,1,0:T(8,128)S(1)}, f32[16,8,640]{2,1,0:T(8,128)S(1)}) custom-call(f32[4,128,640]{2,1,0:T(8,128)S(1)} %bitcast.267, f32[4,128,640]{2,1,0:T(8,128)} %bitcast.263, f32[4,128,640]{2,1,0:T(8,128)} %fusion.61.u_ref, ...), custom_call_target="tpu_custom_call" | custom-call | flops 32999999488 | bytes 105000000 | tf_op jit(solution)/shard_map/scan_back/pallas_call | solution.py:671
  458.3 15.2 %shard_map.321 = bf16[4,512,104]{2,1,0:T(8,128)(2,1)} custom-call(bf16[512,104]{1,0:T(8,128)(2,1)} %pad_maximum_fusion.7.x_ref), custom_call_target="tpu_custom_call" | custom-call | flops 15399999488 | bytes 49000000 | tf_op jit(solution)/shard_map/pallas_call | solution.py:82
  504.4 20.5 %reduce-scatter.8.cloned.1.call-done = bf16[144,1152]{1,0:T(8,128)(2,1)} async-done(((bf16[1152,1152]{1,0:T(8,128)(2,1)}), bf16[144,1152]{1,0:T(8,128)(2,1)}) %reduce-scatter.8.cloned.1.call-update) | async-done | bytes 331792 | tf_op jit(solution)/shard_map/reduce_scatter | solution.py:962
  526.0 74.2 %finish.1 = (bf16[8,480,576]{2,1,0:T(8,128)(2,1)}, bf16[4,144,1152]{2,1,0:T(8,128)(2,1)S(1)}) custom-call(bf16[2,4,192,576]{3,2,1,0:T(8,128)(2,1)S(1)} %copy_bitcast_fusion.g_ref, bf16[144,576]{1,0:T(8,128)(2,1)S(1)} %get-tuple-element.242.z_ref, bf16[144,576]{1,0:T(8,128)(2,1)S(1)} %get-tuple-element.241.f_ref, bf16[4,144,1152]{2,1,0:T(8,128)(2,1)S(1)} %pad.125.d_ref), custom_call_target="tpu_custom_call" | custom-call | flops 65999998976 | bytes 210000000 | tf_op jit(solution)/shard_map/finish/pallas_call | solution.py:253
  600.3 4.7 fusion.131
  (458 shorter events, 144.0 us)
Async XLA Ops:
  7.2 218.3 %all-gather.4.cloned.1.call-start = ((), (), s32[]{:S(2)}) async-start(), calls=%async_computation.3 | async-start | bytes 7962624 | tf_op jit(solution)/shard_map/all_gather | solution.py:740
  8.0 230.4 %all-gather.6.cloned.1.call-start = ((), (), s32[]{:S(2)}) async-start(), calls=%async_computation.7 | async-start | bytes 7962624 | tf_op jit(solution)/shard_map/all_gather | solution.py:741
  8.7 393.7 %reduce-scatter.4.cloned.1.call-start = ((), (), s32[]{:S(2)}) async-start(), calls=%async_computation.4 | async-start | bytes 7962624 | tf_op jit(solution)/shard_map/reduce_scatter | solution.py:913
  74.3 14.7 %copy-start.72 = (bf16[16,576]{1,0:T(8,128)(2,1)S(1)}, bf16[16,576]{1,0:T(8,128)(2,1)}, u32[]{:S(2)}) copy-start(bf16[16,576]{1,0:T(8,128)(2,1)} %param.31) | copy-start | bytes 55300
  74.3 14.8 %copy-start.56 = (bf16[72,576]{1,0:T(8,128)(2,1)S(1)}, bf16[72,576]{1,0:T(8,128)(2,1)}, u32[]{:S(2)}) copy-start(bf16[72,576]{1,0:T(8,128)(2,1)} %param.29) | copy-start | bytes 248836
  89.1 56.1 %copy-start.9 = (bf16[512,16]{1,0:T(8,128)(2,1)}, bf16[512,16]{1,0:T(8,128)(2,1)S(1)}, u32[]{:S(2)}) copy-start(bf16[512,16]{1,0:T(8,128)(2,1)S(1)} %get-tuple-element.244) | copy-start | bytes 49156
  89.1 269.9 %copy-start.7 = (bf16[512,16]{1,0:T(8,128)(2,1)}, bf16[512,16]{1,0:T(8,128)(2,1)S(1)}, u32[]{:S(2)}) copy-start(bf16[512,16]{1,0:T(8,128)(2,1)S(1)} %get-tuple-element.243) | copy-start | bytes 49156
  92.4 52.7 %copy-start = (f32[512,640]{1,0:T(8,128)}, f32[512,640]{1,0:T(8,128)S(1)}, u32[]{:S(2)}) copy-start(f32[512,640]{1,0:T(8,128)S(1)} %get-tuple-element.236) | copy-start | bytes 3932164
  102.2 37.1 %copy-start.104 = (pred[8]{0:T(512)(128)(4,1)S(1)}, pred[8]{0:T(512)(128)(4,1)}, u32[]{:S(2)}) copy-start(pred[8]{0:T(512)(128)(4,1)} %get-tuple-element.253) | copy-start | bytes 28
  102.2 37.1 %copy-start.106 = (pred[8]{0:T(512)(128)(4,1)S(1)}, pred[8]{0:T(512)(128)(4,1)}, u32[]{:S(2)}) copy-start(pred[8]{0:T(512)(128)(4,1)} %get-tuple-element.254) | copy-start | bytes 28
  144.6 10.4 %copy-start.84 = (f32[640]{0:T(1024)}, f32[640]{0:T(1024)S(1)}, u32[]{:S(2)}) copy-start(f32[640]{0:T(1024)S(1)} %pad_convert_fusion.1) | copy-start | bytes 7684
  273.5 148.8 %reduce-scatter.6.cloned.1.call-start = ((), (), s32[]{:S(2)}) async-start(), calls=%async_computation.5 | async-start | bytes 7962624 | tf_op jit(solution)/shard_map/reduce_scatter | solution.py:913
  305.6 219.3 %reduce-scatter.8.cloned.1.call-start = ((), (), s32[]{:S(2)}) async-start(), calls=%async_computation.6 | async-start | bytes 2985984 | tf_op jit(solution)/shard_map/reduce_scatter | solution.py:962
  317.0 27.4 %copy-start.85 = (f32[640]{0:T(1024)S(1)}, f32[640]{0:T(1024)}, u32[]{:S(2)}) copy-start(f32[640]{0:T(1024)} %copy-done.84) | copy-start | bytes 7684
  348.6 10.3 %copy-start.1 = (f32[512,640]{1,0:T(8,128)}, f32[512,640]{1,0:T(8,128)S(1)}, u32[]{:S(2)}) copy-start(f32[512,640]{1,0:T(8,128)S(1)} %get-tuple-element.205) | copy-start | bytes 3932164
  369.1 53.2 %copy-start.58 = (f32[8,4,640]{2,1,0:T(4,128)S(1)}, f32[8,4,640]{2,1,0:T(4,128)}, u32[]{:S(2)}) copy-start(f32[8,4,640]{2,1,0:T(4,128)} %get-tuple-element.186) | copy-start | bytes 245764
  369.1 53.2 %copy-start.105 = (pred[8]{0:T(512)(128)(4,1)S(1)}, pred[8]{0:T(512)(128)(4,1)}, u32[]{:S(2)}) copy-start(pred[8]{0:T(512)(128)(4,1)} %get-tuple-element.253) | copy-start | bytes 28
  402.3 21.6 %copy-start.6 = (f32[4,16,640]{2,1,0:T(8,128)S(1)}, f32[4,16,640]{2,1,0:T(8,128)}, u32[]{:S(2)}) copy-start(f32[4,16,640]{2,1,0:T(8,128)} %copy-done.5) | copy-start | bytes 491524
  402.4 21.6 %copy-start.8 = (bf16[512,16]{1,0:T(8,128)(2,1)S(1)}, bf16[512,16]{1,0:T(8,128)(2,1)}, u32[]{:S(2)}) copy-start(bf16[512,16]{1,0:T(8,128)(2,1)} %copy-done.7) | copy-start | bytes 49156
  402.4 21.6 %copy-start.10 = (bf16[512,16]{1,0:T(8,128)(2,1)S(1)}, bf16[512,16]{1,0:T(8,128)(2,1)}, u32[]{:S(2)}) copy-start(bf16[512,16]{1,0:T(8,128)(2,1)} %copy-done.9) | copy-start | bytes 49156
  424.0 30.3 %copy-start.34 = (f32[512,640]{1,0:T(8,128)S(1)}, f32[512,640]{1,0:T(8,128)}, u32[]{:S(2)}) copy-start(f32[512,640]{1,0:T(8,128)} %get-tuple-element.248) | copy-start | bytes 3932164
  458.3 16.4 %copy-start.2 = (f32[512,640]{1,0:T(8,128)S(1)}, f32[512,640]{1,0:T(8,128)}, u32[]{:S(2)}) copy-start(f32[512,640]{1,0:T(8,128)} %copy-done.1) | copy-start | bytes 3932164
  458.3 16.4 %copy-start.55 = (bf16[576,104]{0,1:T(8,128)(2,1)S(1)}, bf16[576,104]{0,1:T(8,128)(2,1)}, u32[]{:S(2)}) copy-start(bf16[576,104]{0,1:T(8,128)(2,1)} %param.28) | copy-start | bytes 359428
  611.1 17.1 %collective-permute-start = (f32[3,1152]{1,0:T(4,128)S(1)}, f32[3,1152]{1,0:T(4,128)S(1)}, u32[]{:S(2)}, u32[]{:S(2)}) collective-permute-start(f32[3,1152]{1,0:T(4,128)S(1)} %slice.325), channel_id=1, source_target_pairs={{4,0},{8,4},{12,8},{16,12},{20,16},{24,20},{28,24},{5,1},{9,5},{13... | collective-permute-start | bytes 41480 | tf_op jit(solution)/shard_map/ppermute | solution.py:1082
  (97 other events, 284.5 us)
Sparse Core Ops, SparseCore 0:
  9.9 65.4 all-gather.3
  77.3 64.6 all-gather.5
  273.6 65.2 reduce-scatter.3
  342.7 79.5 reduce-scatter.5
  481.3 43.5 reduce-scatter.7

commit v3 on v2

v3 whole, which is shorter than its diff:
```python
import functools

import jax
import jax.numpy as jnp
from jax import lax
from jax.experimental import pallas as pl
from jax.experimental.pallas import tpu as pltpu
from jax.sharding import PartitionSpec as P

EPS = 1e-05
F32 = jnp.float32
BF16 = jnp.bfloat16
SEG = 8
LANE = 128
EDGE = 16
CUT = 1e30
MESH = pl.DeviceIdType.MESH
VMEM_LIMIT = 60 * 2**20


def lasting(us):
    return pl.CostEstimate(
        flops=int(us * 1.1e9), bytes_accessed=int(us * 3.5e6), transcendentals=0
    )


def greet(axis, count):
    me = lax.axis_index(axis)
    barrier = pltpu.get_barrier_semaphore()
    for k in range(1, count):
        pl.semaphore_signal(
            barrier, inc=1, device_id={axis: lax.rem(me + k, count)}, device_id_type=MESH
        )
    pl.semaphore_wait(barrier, count - 1)
    return me


def gather_kernel(axis, count, arrays, *refs):
    srcs, dsts = refs[:arrays], refs[arrays : 2 * arrays]
    send, recv, own = refs[-3:]
    me = greet(axis, count)
    copies = []
    for i in range(arrays):
        for k in range(1, count):
            copy = pltpu.make_async_remote_copy(
                src_ref=srcs[i],
                dst_ref=dsts[i].at[me],
                send_sem=send.at[i, k],
                recv_sem=recv.at[i, k],
                device_id={axis: lax.rem(me + k, count)},
                device_id_type=MESH,
            )
            copy.start()
            copies.append(copy)
    for i in range(arrays):
        local = pltpu.make_async_copy(srcs[i], dsts[i].at[me], own.at[i])
        local.start()
        copies.append(local)
    for copy in copies:
        copy.wait()


def trade_kernel(axis, count, x_ref, o_ref, send, recv, own):
    me = greet(axis, count)
    copies = []
    for k in range(1, count):
        other = lax.rem(me + k, count)
        copy = pltpu.make_async_remote_copy(
            src_ref=x_ref.at[other],
            dst_ref=o_ref.at[me],
            send_sem=send.at[k],
            recv_sem=recv.at[k],
            device_id={axis: other},
            device_id_type=MESH,
        )
        copy.start()
        copies.append(copy)
    local = pltpu.make_async_copy(x_ref.at[me], o_ref.at[me], own)
    local.start()
    local.wait()
    for copy in copies:
        copy.wait()


def trade(x, axis, cid, us):
    count = lax.axis_size(axis)
    return pl.pallas_call(
        functools.partial(trade_kernel, axis, count),
        out_shape=jax.ShapeDtypeStruct(x.shape, x.dtype),
        in_specs=[pl.BlockSpec(memory_space=pl.ANY)],
        out_specs=pl.BlockSpec(memory_space=pl.ANY),
        scratch_shapes=[
            pltpu.SemaphoreType.DMA((count,)),
            pltpu.SemaphoreType.DMA((count,)),
            pltpu.SemaphoreType.DMA,
        ],
        compiler_params=pltpu.CompilerParams(
            collective_id=cid, has_side_effects=True, vmem_limit_bytes=VMEM_LIMIT
        ),
        cost_estimate=lasting(us),
        name=f"trade_{cid}",
    )(x)


def gather_all(xs, axis, cid, us):
    count, arrays = lax.axis_size(axis), len(xs)
    return pl.pallas_call(
        functools.partial(gather_kernel, axis, count, arrays),
        out_shape=[jax.ShapeDtypeStruct((count,) + x.shape, x.dtype) for x in xs],
        in_specs=[pl.BlockSpec(memory_space=pl.ANY)] * arrays,
        out_specs=[pl.BlockSpec(memory_space=pl.ANY)] * arrays,
        scratch_shapes=[
            pltpu.SemaphoreType.DMA((arrays, count)),
            pltpu.SemaphoreType.DMA((arrays, count)),
            pltpu.SemaphoreType.DMA((arrays,)),
        ],
        compiler_params=pltpu.CompilerParams(
            collective_id=cid, has_side_effects=True, vmem_limit_bytes=VMEM_LIMIT
        ),
        cost_estimate=lasting(us),
        name=f"gather_{cid}",
    )(*xs)


def remote(src, dst, send, recv, where):
    return pltpu.make_async_remote_copy(
        src_ref=src, dst_ref=dst, send_sem=send, recv_sem=recv,
        device_id=where, device_id_type=MESH,
    )


def add_rows(out, parts, rows):
    def one(i, _):
        at = pl.ds(pl.multiple_of(i * 16, 16), 16)
        total = parts[0][at, :].astype(F32)
        for part in parts[1:]:
            total = total + part[at, :].astype(F32)
        out[at, :] = total.astype(out.dtype)
        return 0

    lax.fori_loop(0, rows // 16, one, 0)


def neighbours(ring):
    me = lax.axis_index("ctx")
    half = ring // 2
    lane = lax.rem(me, 2)
    chip = me // 2
    peers = [lax.rem(chip + k, half) * 2 + lane for k in range(1, half)]
    return me, chip, lane, me + 1 - 2 * lane, peers


def mates_of(group):
    mine = lax.axis_index("wa")
    return mine, [lax.rem(mine + k, group) for k in range(1, group)]


def hello(barrier, axis, who):
    pl.semaphore_signal(barrier, inc=1, device_id={axis: who}, device_id_type=MESH)


def carry_back_kernel(ring, f_ref, g_ref, f_o, p_o, send, recv, own, pair_s, pair_r):
    me, _, lane, pair, _ = neighbours(ring)
    greet("ctx", ring)
    to_pair = remote(g_ref.at[:, 1 - lane], p_o, pair_s, pair_r, {"ctx": pair})
    copies = []
    for k in range(1, ring):
        copy = remote(f_ref, f_o.at[me], send.at[k], recv.at[k], {"ctx": lax.rem(me + k, ring)})
        copy.start()
        copies.append(copy)
    to_pair.start()
    local = pltpu.make_async_copy(f_ref, f_o.at[me], own)
    local.start()
    for copy in copies + [to_pair, local]:
        copy.wait()


def carry_back(f, g, cid, us):
    ring = lax.axis_size("ctx")
    hbm = pl.BlockSpec(memory_space=pl.ANY)
    dma = pltpu.SemaphoreType.DMA
    return pl.pallas_call(
        functools.partial(carry_back_kernel, ring),
        out_shape=[
            jax.ShapeDtypeStruct((ring,) + f.shape, f.dtype),
            jax.ShapeDtypeStruct(g.shape[:1] + g.shape[2:], g.dtype),
        ],
        in_specs=[hbm] * 2,
        out_specs=[hbm] * 2,
        scratch_shapes=[dma((ring,)), dma((ring,)), dma, dma, dma],
        compiler_params=pltpu.CompilerParams(
            collective_id=cid, has_side_effects=True, vmem_limit_bytes=VMEM_LIMIT
        ),
        cost_estimate=lasting(us),
        name="carry_back",
    )(f, g)


def proj_back_kernel(
    ring, group, x_ref, g_ref, p_ref, x_o, g_o,
    kept, paired, came, mate_s, mate_r, own_s, load, ctx_s, ctx_r,
):
    _, chip, lane, _, peers = neighbours(ring)
    mine, mates = mates_of(group)
    half = ring // 2
    rows = g_o.shape[0]
    loads = [
        pltpu.make_async_copy(g_ref.at[:, lane], kept, load.at[0]),
        pltpu.make_async_copy(p_ref, paired, load.at[1]),
    ]
    for copy in loads:
        copy.start()
    barrier = pltpu.get_barrier_semaphore()
    for who in peers:
        hello(barrier, "ctx", who)
    for who in mates:
        hello(barrier, "wa", who)
    pl.semaphore_wait(barrier, half + group - 2)
    copies = []
    for k, who in enumerate(mates):
        copy = remote(x_ref, x_o.at[mine], mate_s.at[k], mate_r.at[k], {"wa": who})
        copy.start()
        copies.append(copy)
    local = pltpu.make_async_copy(x_ref, x_o.at[mine], own_s)
    local.start()
    for copy in loads:
        copy.wait()
    scattered = []
    for k, who in enumerate(peers):
        to = lax.rem(chip + k + 1, half)
        add_rows(kept.at[to], [kept.at[to], paired.at[to]], rows)
        copy = remote(kept.at[to], came.at[k], ctx_s.at[k], ctx_r.at[k], {"ctx": who})
        copy.start()
        scattered.append(copy)
    add_rows(kept.at[chip], [kept.at[chip], paired.at[chip]], rows)
    for copy in scattered:
        copy.wait_recv()
    add_rows(g_o, [kept.at[chip]] + [came.at[k] for k in range(half - 1)], rows)
    for copy in scattered:
        copy.wait_send()
    for copy in copies + [local]:
        copy.wait()


def proj_back(x, g, p, cid, us):
    ring, group = lax.axis_size("ctx"), lax.axis_size("wa")
    half = ring // 2
    hbm = pl.BlockSpec(memory_space=pl.ANY)
    dma = pltpu.SemaphoreType.DMA
    block = pltpu.VMEM((half,) + g.shape[2:], g.dtype)
    return pl.pallas_call(
        functools.partial(proj_back_kernel, ring, group),
        out_shape=[
            jax.ShapeDtypeStruct((group,) + x.shape, x.dtype),
            jax.ShapeDtypeStruct(g.shape[2:], g.dtype),
        ],
        in_specs=[hbm] * 3,
        out_specs=[hbm, pl.BlockSpec(memory_space=pltpu.VMEM)],
        scratch_shapes=[
            block, block, pltpu.VMEM((half - 1,) + g.shape[2:], g.dtype),
            dma((group - 1,)), dma((group - 1,)), dma, dma((2,)),
            dma((half - 1,)), dma((half - 1,)),
        ],
        compiler_params=pltpu.CompilerParams(
            collective_id=cid, has_side_effects=True, vmem_limit_bytes=VMEM_LIMIT
        ),
        cost_estimate=lasting(us),
        name="proj_back",
    )(x, g, p)


def finish_kernel(
    ring, group, in_rows, small_rows,
    g_ref, zf_ref, d_ref, o_ref, dt_ref, de_ref,
    from_pair, paired, came, own, zin, tiles,
    pair_s, pair_r, ctx_s, ctx_r, z_s, z_r, tile_s, tile_r, d_s, d_r, d_own, last_s, last_r, fwd_s, fwd_r,
    edge_s, edge_r,
):
    me, chip, lane, pair, peers = neighbours(ring)
    mine, mates = mates_of(group)
    half = ring // 2
    rows = in_rows + small_rows + 16
    lanes = g_ref.shape[3]
    barrier = pltpu.get_barrier_semaphore()
    for who in [pair] + peers:
        hello(barrier, "ctx", who)
    for who in mates:
        hello(barrier, "wa", who)
    has_next = me < ring - 1
    has_last = me > 0

    @pl.when(has_next)
    def _():
        hello(barrier, "ctx", me + 1)

    @pl.when(has_last)
    def _():
        hello(barrier, "ctx", me - 1)

    around = jnp.where(has_next, 1, 0) + jnp.where(has_last, 1, 0)
    pl.semaphore_wait(barrier, half + group - 1 + around)

    to_pair = remote(g_ref.at[:, 1 - lane], from_pair, pair_s, pair_r, {"ctx": pair})
    to_pair.start()
    ready = 2 * in_rows + small_rows + 16
    parts = [pl.ds(ready, in_rows), pl.ds(0, ready)]
    o_ref[me, parts[0]] = zf_ref[:, lanes:]

    def to_all(i):
        src = o_ref.at[me, parts[i]]
        copies = []
        for k, who in enumerate(peers):
            copies.append(remote(src, src, last_s.at[i, k], last_r.at[i, k], {"ctx": who}))
        copies.append(remote(src, src, fwd_s.at[i, 0], fwd_r.at[i, 0], {"ctx": pair}))
        for copy in copies:
            copy.start()
        return copies

    def forward(i, copies):
        for k in range(1, half):
            copies[k - 1].wait_recv()
            source = lax.rem(chip + half - k, half) * 2 + lane
            block = o_ref.at[source, parts[i]]
            copy = remote(block, block, fwd_s.at[i, k], fwd_r.at[i, k], {"ctx": pair})
            copy.start()
            copies.append(copy)

    early = to_all(0)

    x_to = mine // 2
    z_to = group // 2 + mine // 2
    slot = lax.rem(mine, 2)
    z_ref = zf_ref.at[:, pl.ds(0, lanes)]
    x_ref = own.at[pl.ds(0, in_rows)]
    send_x = remote(x_ref, zin.at[slot], z_s.at[0], z_r.at[slot], {"wa": x_to})
    send_z = remote(z_ref, zin.at[slot], z_s.at[1], z_r.at[slot], {"wa": z_to})
    keep_x = pltpu.make_async_copy(x_ref, zin.at[slot], z_r.at[slot])
    keep_z = pltpu.make_async_copy(z_ref, zin.at[slot], z_r.at[slot])

    @pl.when(z_to != mine)
    def _():
        send_z.start()

    @pl.when(z_to == mine)
    def _():
        keep_z.start()

    cut = d_ref.shape[1] // 32 * 16
    pieces = [pl.ds(0, cut), pl.ds(cut, d_ref.shape[1] - cut)]
    trades = []

    def trade_rows(i):
        for k, who in enumerate(mates):
            copy = remote(
                d_ref.at[who, pieces[i]], dt_ref.at[mine, pieces[i]], d_s.at[i, k], d_r.at[i, k],
                {"wa": who},
            )
            copy.start()
            trades.append(copy)

    trade_rows(0)
    kept = pltpu.make_async_copy(d_ref.at[mine], dt_ref.at[mine], d_own)
    kept.start()

    to_pair.wait_recv()
    scattered = []
    for k, who in enumerate(peers):
        to = lax.rem(chip + k + 1, half)
        add_rows(paired.at[to], [g_ref.at[to, lane], from_pair.at[to]], rows)
        copy = remote(paired.at[to], came.at[k], ctx_s.at[k], ctx_r.at[k], {"ctx": who})
        copy.start()
        scattered.append(copy)
    add_rows(paired.at[chip], [g_ref.at[chip, lane], from_pair.at[chip]], rows)
    for copy in scattered:
        copy.wait_recv()
    add_rows(own, [paired.at[chip]] + [came.at[k] for k in range(half - 1)], rows)

    @pl.when(x_to != mine)
    def _():
        send_x.start()

    @pl.when(x_to == mine)
    def _():
        keep_x.start()

    tile = pl.ds(in_rows + small_rows, 16)
    spread_tiles = []
    for k, who in enumerate(mates):
        copy = remote(own.at[tile], tiles.at[k], tile_s.at[k], tile_r.at[k], {"wa": who})
        copy.start()
        spread_tiles.append(copy)
    forward(0, early)
    o_ref[me, pl.ds(2 * in_rows, small_rows)] = own[pl.ds(in_rows, small_rows)]
    for copy in spread_tiles:
        copy.wait_recv()
    add_rows(
        o_ref.at[me, pl.ds(2 * in_rows + small_rows, 16)],
        [own.at[tile]] + [tiles.at[k] for k in range(group - 1)],
        16,
    )
    for s in range(2):
        pltpu.make_async_copy(zin.at[s], zin.at[s], z_r.at[s]).wait()
        o_ref[me, pl.ds(s * in_rows, in_rows)] = zin[s]
    late = to_all(1)
    trade_rows(1)
    kept.wait()
    forward(1, late)

    for copy in trades:
        copy.wait_recv()
    edges = dt_ref.at[:, pl.ds(d_ref.shape[1] - EDGE, EDGE)]
    to_last = remote(edges, de_ref, edge_s, edge_r, {"ctx": me - 1})

    @pl.when(has_last)
    def _():
        to_last.start()

    for copies in (early, late):
        for copy in copies[half - 1 :]:
            copy.wait_recv()

    to_pair.wait_send()
    for copy in scattered + spread_tiles + early + late + trades:
        copy.wait_send()

    @pl.when(x_to != mine)
    def _():
        send_x.wait_send()

    @pl.when(z_to != mine)
    def _():
        send_z.wait_send()

    @pl.when(has_last)
    def _():
        to_last.wait_send()

    @pl.when(has_next)
    def _():
        to_last.wait_recv()


def finish(g, zf, d, in_rows, small_rows, cid):
    ring, group = lax.axis_size("ctx"), lax.axis_size("wa")
    half = ring // 2
    rows, lanes = g.shape[2:]
    out_rows = 3 * in_rows + small_rows + 16
    vmem = pl.BlockSpec(memory_space=pltpu.VMEM)
    hbm = pl.BlockSpec(memory_space=pl.ANY)
    dma = pltpu.SemaphoreType.DMA
    return pl.pallas_call(
        functools.partial(finish_kernel, ring, group, in_rows, small_rows),
        out_shape=[
            jax.ShapeDtypeStruct((ring, out_rows, lanes), BF16),
            jax.ShapeDtypeStruct(d.shape, d.dtype),
            jax.ShapeDtypeStruct((group, EDGE, d.shape[2]), d.dtype),
        ],
        in_specs=[vmem, vmem, hbm],
        out_specs=[vmem, hbm, hbm],
        scratch_shapes=[
            pltpu.VMEM((half, rows, lanes), BF16),
            pltpu.VMEM((half, rows, lanes), BF16),
            pltpu.VMEM((half - 1, rows, lanes), BF16),
            pltpu.VMEM((rows, lanes), BF16),
            pltpu.VMEM((2, in_rows, lanes), BF16),
            pltpu.VMEM((group - 1, 16, lanes), BF16),
            dma, dma,
            dma((half - 1,)), dma((half - 1,)),
            dma((2,)), dma((2,)),
            dma((group - 1,)), dma((group - 1,)),
            dma((2, group - 1)), dma((2, group - 1)), dma,
            dma((2, half - 1)), dma((2, half - 1)),
            dma((2, half)), dma((2, half)),
            dma, dma,
        ],
        compiler_params=pltpu.CompilerParams(
            collective_id=cid, has_side_effects=True, vmem_limit_bytes=VMEM_LIMIT
        ),
        cost_estimate=lasting(60),
        name="finish",
    )(g, zf, d)


def start_kernel(
    ring, group, tok, par, doc, w_ref, tok_o, edge_o, par_o, doc_o, w_o,
    mate_s, mate_r, own_s, edge_s, edge_r, relay_s, relay_r, shift_s, shift_r, out_s, out_r, fwd_s, fwd_r,
):
    me = lax.axis_index("ctx")
    mine = lax.axis_index("wa")
    half = ring // 2
    lane = lax.rem(me, 2)
    chip = me // 2
    pair = me + 1 - 2 * lane
    peers = [lax.rem(chip + k, half) * 2 + lane for k in range(1, half)]
    mates = [lax.rem(mine + k, group) for k in range(1, group)]
    barrier = pltpu.get_barrier_semaphore()
    for who in [pair] + peers:
        pl.semaphore_signal(barrier, inc=1, device_id={"ctx": who}, device_id_type=MESH)
    for who in mates:
        pl.semaphore_signal(barrier, inc=1, device_id={"wa": who}, device_id_type=MESH)
    has_next = me < ring - 1
    has_last = me > 0

    @pl.when(has_next)
    def _():
        pl.semaphore_signal(barrier, inc=1, device_id={"ctx": me + 1}, device_id_type=MESH)

    @pl.when(has_last)
    def _():
        pl.semaphore_signal(barrier, inc=1, device_id={"ctx": me - 1}, device_id_type=MESH)

    around = jnp.where(has_next, 1, 0) + jnp.where(has_last, 1, 0)
    pl.semaphore_wait(barrier, half + group - 1 + around)

    edge = tok.at[pl.ds(tok.shape[0] - EDGE, EDGE)]
    to_next = remote(edge, edge_o.at[mine], edge_s, edge_r, {"ctx": me + 1})

    @pl.when(has_next)
    def _():
        to_next.start()

    kind = mine // (group // 2)
    base = 2 * lax.rem(mine, group // 2)
    for h in range(2):
        where = base + h
        send = remote(
            w_ref.at[h], w_o.at[kind, me], shift_s.at[h], shift_r.at[kind], {"wa": where}
        )
        keep = pltpu.make_async_copy(w_ref.at[h], w_o.at[kind, me], shift_r.at[kind])

        @pl.when(where != mine)
        def _():
            send.start()

        @pl.when(where == mine)
        def _():
            keep.start()

    trades = []
    for i, (src, dst) in enumerate(((par, par_o), (doc, doc_o), (tok, tok_o))):
        for k, who in enumerate(mates):
            copy = remote(src, dst.at[mine], mate_s.at[i, k], mate_r.at[i, k], {"wa": who})
            copy.start()
            trades.append(copy)
        keep = pltpu.make_async_copy(src, dst.at[mine], own_s.at[i])
        keep.start()

    @pl.when(has_last)
    def _():
        to_next.wait_recv()
        for k, who in enumerate(mates):
            remote(
                edge_o.at[mine], edge_o.at[mine], relay_s.at[k], relay_r.at[k], {"wa": who}
            ).start()

    sends = []
    for t in range(2):
        block = w_o.at[t, me]
        pltpu.make_async_copy(block, block, shift_r.at[t]).wait()
        for k, who in enumerate(peers):
            copy = remote(block, block, out_s.at[t, k], out_r.at[t, k], {"ctx": who})
            copy.start()
            sends.append(copy)
        copy = remote(block, block, fwd_s.at[t, 0], fwd_r.at[t, 0], {"ctx": pair})
        copy.start()
        sends.append(copy)
    forwards = []
    for t in range(2):
        for k in range(1, half):
            source = lax.rem(chip + half - k, half) * 2 + lane
            block = w_o.at[t, source]
            pltpu.make_async_copy(block, block, out_r.at[t, k - 1]).wait()
            copy = remote(block, block, fwd_s.at[t, k], fwd_r.at[t, k], {"ctx": pair})
            copy.start()
            forwards.append(copy)
    for t in range(2):
        for k in range(half):
            pltpu.make_async_copy(w_o.at[t, me], w_o.at[t, me], fwd_r.at[t, k]).wait()
    for copy in sends + forwards:
        copy.wait_send()
    for h in range(2):

        @pl.when(base + h != mine)
        def _():
            remote(
                w_ref.at[h], w_o.at[kind, me], shift_s.at[h], shift_r.at[kind], {"wa": mine}
            ).wait_send()

    for copy in trades:
        copy.wait()
    for i, (src, dst) in enumerate(((par, par_o), (doc, doc_o), (tok, tok_o))):
        pltpu.make_async_copy(src, dst.at[mine], own_s.at[i]).wait()

    @pl.when(has_next)
    def _():
        to_next.wait_send()

    @pl.when(has_last)
    def _():
        for k, who in enumerate(mates):
            remote(
                edge_o.at[mine], edge_o.at[mine], relay_s.at[k], relay_r.at[k], {"wa": who}
            ).wait()


def start(tok, par, doc, halves, cid):
    ring, group = lax.axis_size("ctx"), lax.axis_size("wa")
    half = ring // 2
    hbm = pl.BlockSpec(memory_space=pl.ANY)
    dma = pltpu.SemaphoreType.DMA
    outs = [(group,) + a.shape for a in (tok, tok[:EDGE], par, doc)] + [(2, ring) + halves.shape[1:]]
    types = [a.dtype for a in (tok, tok, par, doc, halves)]
    return pl.pallas_call(
        functools.partial(start_kernel, ring, group),
        out_shape=[jax.ShapeDtypeStruct(s, t) for s, t in zip(outs, types)],
        in_specs=[hbm] * 4,
        out_specs=[hbm] * 5,
        scratch_shapes=[
            dma((3, group - 1)), dma((3, group - 1)), dma((3,)),
            dma, dma,
            dma((group - 1,)), dma((group - 1,)),
            dma((2,)), dma((2,)),
            dma((2, half - 1)), dma((2, half - 1)),
            dma((2, half)), dma((2, half)),
        ],
        compiler_params=pltpu.CompilerParams(
            collective_id=cid, has_side_effects=True, vmem_limit_bytes=VMEM_LIMIT
        ),
        cost_estimate=lasting(35),
        name="start",
    )(tok, par, doc, halves)


def pick(rows, states, at):
    shape = (rows, states * LANE)
    lower = (lax.broadcasted_iota(jnp.int32, shape, 0) - at) * LANE
    place = lax.broadcasted_iota(jnp.int32, shape, 1)
    return jnp.where((place >= lower) & (place < lower + LANE), 1.0, 0.0)


def spread(rows, states, at):
    return jnp.dot(rows, pick(rows.shape[1], states, at).astype(BF16), preferred_element_type=F32)


def collected(wide_rows, states, columns, at):
    shape = (states * LANE, columns)
    lower = (lax.broadcasted_iota(jnp.int32, shape, 1) - at) * LANE
    place = lax.broadcasted_iota(jnp.int32, shape, 0)
    ones = jnp.where((place >= lower) & (place < lower + LANE), 1.0, 0.0)
    return jnp.dot(wide_rows, ones, precision=lax.Precision.HIGHEST, preferred_element_type=F32)


def position_of(shape, axis, steps):
    row = lax.broadcasted_iota(jnp.int32, shape, axis)
    return (row & (SEG - 1)) * steps + (row >> 3)


def permutation(length):
    shape = (length, length)
    at = position_of(shape, 0, length // SEG)
    return jnp.where(at == lax.broadcasted_iota(jnp.int32, shape, 1), 1.0, 0.0).astype(BF16)


def rolled(value, by):
    return pltpu.roll(value, by % SEG, 0)


def lanes_of(g):
    return pl.ds(pl.multiple_of(g * LANE, LANE), LANE)


def rows_of(j):
    return pl.ds(pl.multiple_of(j * SEG, SEG), SEG)


def wide(ref, n, lanes):
    return jnp.broadcast_to(ref[pl.ds(n, 1), lanes], (SEG, LANE))


def state_cols(n):
    return slice(n * LANE, (n + 1) * LANE)


def dot_nt(a, b):
    return lax.dot_general(a, b, (((1,), (1,)), ((), ())), preferred_element_type=F32)


def dot_tn(a, b):
    return lax.dot_general(a, b, (((0,), (0,)), ((), ())), preferred_element_type=F32)


def dot_nn(a, b):
    return jnp.dot(a, b, preferred_element_type=F32)


def rms_scale(values):
    return lax.rsqrt(jnp.mean(values * values, axis=-1, keepdims=True) + EPS)


def norm_grads(values, scale, gain, d_out):
    unit = values * scale
    d_unit = d_out * gain
    d_values = scale * (d_unit - unit * jnp.mean(d_unit * unit, axis=-1, keepdims=True))
    return d_values, d_out * unit


def silu_slope(v):
    s = jax.nn.sigmoid(v)
    return s * (1.0 + v * (1.0 - s))


def seg_of():
    return lax.broadcasted_iota(jnp.int32, (SEG, LANE), 0)


def lag_masks(place, doc_ref, stream, length, taps):
    at = place * length + position_of((length, LANE), 0, length // SEG)
    masks = [None]
    for lag in range(1, taps):
        cut = None
        for d in range(doc_ref.shape[1]):
            begin = doc_ref[stream, d]
            here = (begin > at - lag) & (begin <= at)
            cut = here if cut is None else cut | here
        masks.append(jnp.where(cut, 0.0, 1.0))
    hit = None
    for d in range(doc_ref.shape[1]):
        here = doc_ref[stream, d] == at
        hit = here if hit is None else hit | here
    return masks, jnp.where(hit, CUT, 0.0)


def enter_kernel(
    taps, place_ref, doc_ref, tok, edge, gain, wx, wz, conv, wproj,
    n1_o, ext_o, pre_o, uf_o, u_o, z_o, part_o, cut_o,
):
    length = tok.shape[1]
    steps = length // SEG
    place = place_ref[0]
    gains = gain[...]

    def normal(rows):
        return (rows * rms_scale(rows) * gains).astype(BF16)

    n1_o[0, :length] = normal(dot_nn(permutation(length), tok[0]))
    n1_o[0, length:] = normal(jnp.where(place > 0, edge[0].astype(F32), 0.0))
    inner = dot_nn(n1_o[0], wx[0]).astype(BF16).astype(F32)
    z_o[0] = dot_nn(n1_o[0, :length], wz[0]).astype(BF16)
    masks, cut = lag_masks(place, doc_ref, pl.program_id(0), length, taps)
    cut_o[0] = cut
    seg = seg_of()
    behind = taps - 1
    for g in range(inner.shape[1] // LANE):
        cols = slice(g * LANE, (g + 1) * LANE)
        rows, before = inner[:length, cols], inner[length:, cols]
        parts = []
        for i in range(behind):
            j = steps - behind + i
            last = jnp.broadcast_to(before[EDGE - behind + i : EDGE - behind + i + 1], (SEG, LANE))
            parts.append(jnp.where(seg == 0, last, rolled(rows[j * SEG : (j + 1) * SEG], 1)))
        ext = jnp.concatenate(parts + [rows], axis=0)
        ext_o[0, :, cols] = ext
        pre = conv[taps : taps + 1, cols] + conv[0:1, cols] * rows
        for lag in range(1, taps):
            window = ext[(behind - lag) * SEG : (behind - lag) * SEG + length]
            pre = pre + conv[lag : lag + 1, cols] * window * masks[lag]
        pre_o[0, :, cols] = pre
        u = (pre * jax.nn.sigmoid(pre)).astype(BF16)
        u_o[0, :, cols] = u
        uf_o[0, :, cols] = u.astype(F32)
    part_o[0] = dot_nn(u_o[0], wproj[...]).astype(BF16)


def summary_kernel(
    states, b_at, terms, wdt, bias, uf, cut, a_ref,
    proj_o, step_o, sig_o, hx_ref, sx_ref, hd_o, sd_ref, bb, st_s, dr_s, hd_s,
):
    length, width = step_o.shape[1:]
    groups, steps = width // LANE, length // SEG
    total = terms[0, 0].astype(F32)
    for w in range(1, terms.shape[0]):
        total = total + terms[w, 0].astype(F32)
    proj = total.astype(BF16)
    proj_o[0] = proj
    bb[...] = spread(proj, states, b_at)
    pre = dot_nn(proj, wdt[...]) + bias[...]
    step_size = jnp.maximum(pre, 0.0) + jnp.log1p(jnp.exp(-jnp.abs(pre)))
    step_o[0] = step_size
    sig_o[0] = jax.nn.sigmoid(pre)
    dr_s[...] = step_size * uf[0]
    for g in range(groups):
        cols = slice(g * LANE, (g + 1) * LANE)
        st_s[:, cols] = step_size[:, cols] + cut[0]
    zero = jnp.zeros((SEG, LANE), F32)
    seg = seg_of()

    def group(g, _):
        lanes = lanes_of(g)
        a = [wide(a_ref, n, lanes) for n in range(states)]

        def step(j, carry):
            rows = rows_of(j)
            st = st_s[rows, lanes]
            dr = dr_s[rows, lanes]
            new = [carry[0] + st]
            for n in range(states):
                new.append(jnp.exp(st * a[n]) * carry[n + 1] + bb[rows, state_cols(n)] * dr)
            return tuple(new)

        out = lax.fori_loop(0, steps, step, (zero,) * (states + 1), unroll=2)
        total, h = out[0], list(out[1:])
        for k in (1, 2, 4):
            ok = seg >= k
            for n in range(states):
                h[n] = h[n] + jnp.where(ok, jnp.exp(total * a[n]) * rolled(h[n], k), 0.0)
            total = total + jnp.where(ok, rolled(total, k), 0.0)
        ok = seg >= 1
        sx_ref[0, :, lanes] = jnp.where(ok, rolled(total, 1), 0.0)
        sd_ref[0, :, lanes] = total[SEG - 1 : SEG]
        for n in range(states):
            hx_ref[0, n, :, lanes] = jnp.where(ok, rolled(h[n], 1), 0.0)
            hd_s[pl.ds(n, 1), lanes] = h[n][SEG - 1 : SEG]
        return 0

    lax.fori_loop(0, groups, group, 0)
    hd_o[0] = hd_s[...].astype(BF16)


def entering(e_ref, finals, sums, a_ref, place, ahead):
    ring = finals.shape[0]
    e_ref[...] = jnp.zeros_like(e_ref)

    def one(lap, _):
        c = lap if ahead else ring - 1 - lap
        use = (c < place) if ahead else (c > place)

        @pl.when(use)
        def _():
            e_ref[...] = jnp.exp(sums[c, 0] * a_ref[...]) * e_ref[...] + finals[c, 0].astype(F32)

        return 0

    lax.fori_loop(0, ring, one, 0)


def output_kernel(
    states, b_at, place_ref, proj, step_i, uf, cut, a_ref, hx_ref, sx_ref, finals, sums, z, skip, wout,
    y_o, gated_o, mix_o, e_o, bb, cb, st_s, dr_s,
):
    length, width = step_i.shape[1:]
    groups, steps = width // LANE, length // SEG
    bb[...] = spread(proj[0], states, b_at)
    cb[...] = spread(proj[0], states, b_at + states)
    e_ref = e_o.at[0]
    entering(e_ref, finals, sums, a_ref, place_ref[0], True)
    dr_s[...] = step_i[0] * uf[0]
    for g in range(groups):
        cols = slice(g * LANE, (g + 1) * LANE)
        st_s[:, cols] = step_i[0, :, cols] + cut[0]

    def group(g, _):
        lanes = lanes_of(g)
        a = [wide(a_ref, n, lanes) for n in range(states)]
        sx = sx_ref[0, :, lanes]
        first = tuple(
            jnp.exp(sx * a[n]) * wide(e_ref, n, lanes) + hx_ref[0, n, :, lanes]
            for n in range(states)
        )
        gain = wide(skip, 0, lanes)

        def step(j, h):
            rows = rows_of(j)
            st = st_s[rows, lanes]
            dr = dr_s[rows, lanes]
            new = []
            y = gain * uf[0, rows, lanes]
            for n in range(states):
                state = jnp.exp(st * a[n]) * h[n] + bb[rows, state_cols(n)] * dr
                new.append(state)
                y = y + cb[rows, state_cols(n)] * state
            y_o[0, rows, lanes] = y
            return tuple(new)

        lax.fori_loop(0, steps, step, first, unroll=2)
        return 0

    lax.fori_loop(0, groups, group, 0)
    zf = z[0].astype(F32)
    gated = (y_o[0] * (zf * jax.nn.sigmoid(zf))).astype(BF16)
    gated_o[0] = gated
    mix_o[0] = dot_nn(gated, wout[...]).astype(BF16)


def route_kernel(
    experts, terms, tok, gain, router, route, keep, grad,
    h1_o, n2_o, up_o, cols_o, match_o, out_o, sums_o,
):
    length, width = tok.shape
    shift = permutation(length)
    mix = terms[0].astype(F32)
    for w in range(1, terms.shape[0]):
        mix = mix + terms[w].astype(F32)
    h1 = dot_nn(shift, tok[...]) + mix
    h1_o[...] = h1
    n2 = (h1 * rms_scale(h1) * gain[...]).astype(BF16)
    n2_o[...] = n2
    logits = dot_nt(n2, router[...])
    lane = lax.broadcasted_iota(jnp.int32, (length, LANE), 1)
    named = route[...]
    onehot = jnp.where(named == lane, 1.0, 0.0)
    one = lax.broadcasted_iota(jnp.int32, (length, length), 0)
    two = lax.broadcasted_iota(jnp.int32, (length, length), 1)
    earlier = jnp.where(two < one, 1.0, 0.0).astype(BF16)
    before = dot_nn(earlier, onehot.astype(BF16))
    within = jnp.sum(before * onehot, axis=1, keepdims=True)
    slot = named.astype(F32) * (length // 2) + within
    facts = jnp.where(lane == experts, slot, jnp.where(lane == experts + 1, keep[...].astype(F32), onehot))
    facts = dot_nn(shift, facts.astype(BF16))
    onehot = jnp.where(lane < experts, facts, 0.0)
    slot = jnp.sum(jnp.where(lane == experts, facts, 0.0), axis=1, keepdims=True)
    kept = jnp.sum(jnp.where(lane == experts + 1, facts, 0.0), axis=1, keepdims=True)
    sig = jax.nn.sigmoid(jnp.sum(logits * onehot, axis=1, keepdims=True))
    gates = kept * sig
    cols_o[...] = jnp.where(
        lane == experts, gates, jnp.where(lane == experts + 1, gates * (1.0 - sig), onehot)
    )
    up = dot_nn(shift, grad[...])
    up_o[...] = up
    slots = match_o.shape[1]
    spot = lax.broadcasted_iota(jnp.int32, (length, slots), 1).astype(F32)
    match = jnp.where(slot == spot, 1.0, 0.0).astype(BF16)
    match_o[...] = match
    out_o[:, :width] = dot_tn(match, n2).astype(BF16)
    out_o[:, width:] = dot_tn(match, (gates * up).astype(BF16)).astype(BF16)
    sums_o[...] = jnp.broadcast_to(jnp.sum(mix * mix, keepdims=True), (SEG, LANE))


def pack_kernel(up, down, _, out):
    width = up.shape[0]
    units = up.shape[1]
    line = lax.broadcasted_iota(jnp.int32, (units, units), 0)
    same = jnp.where(line == lax.broadcasted_iota(jnp.int32, (units, units), 1), 1.0, 0.0)
    out[:, :width] = dot_nt(same.astype(BF16), up[...]).astype(BF16)
    out[:, width:] = down[...]


def experts_kernel(x_ref, w_ref, g_ref, o_ref, acc):
    width = x_ref.shape[1] // 2
    at = pl.program_id(0)

    @pl.when(at == 0)
    def _():
        acc[...] = jnp.zeros_like(acc)

    up, down = w_ref[:, :width], w_ref[:, width:]
    rows, d_out = x_ref[:, :width], x_ref[:, width:]
    hidden = dot_nt(up, rows)
    d_act = dot_nt(down, d_out)
    c = 0.7978845608
    t = jnp.tanh(c * (hidden + 0.044715 * hidden * hidden * hidden))
    act = (0.5 * hidden * (1.0 + t)).astype(BF16)
    slope = 0.5 * (1.0 + t) + 0.5 * hidden * (1.0 - t * t) * c * (
        1.0 + 3.0 * 0.044715 * hidden * hidden
    )
    d_pre = (d_act * slope).astype(BF16)
    acc[:, :width] += dot_tn(act, down)
    acc[:, width:] += dot_tn(d_pre, up)
    g_ref[:, :width] = dot_nn(d_pre, rows).astype(BF16)
    g_ref[:, width:] = dot_nn(act, d_out).astype(BF16)

    @pl.when(at == pl.num_programs(0) - 1)
    def _():
        o_ref[...] = acc[...].astype(BF16)


def store_in_order(out, rows, order_s):
    steps = rows.shape[0] // SEG
    for g in range(rows.shape[1] // LANE):
        cols = slice(g * LANE, (g + 1) * LANE)
        for j in range(steps):
            order_s[g, pl.ds(j, SEG, stride=steps), :] = rows[j * SEG : (j + 1) * SEG, cols]
        out[:, cols] = order_s[g]


def combine_kernel(
    experts, back, match, h1_i, n2, up_i, cols, gain, router,
    out_o, dh_o, dmix_o, router_o, gain_o, sums_o, order_s,
):
    length, width = h1_i.shape
    h1, up = h1_i[...], up_i[...]
    lane = lax.broadcasted_iota(jnp.int32, (length, LANE), 1)
    facts = cols[...]

    def column(at):
        return jnp.sum(jnp.where(lane == at, facts, 0.0), axis=1, keepdims=True)

    gates, slope = column(experts), column(experts + 1)
    onehot = jnp.where(lane < experts, facts, 0.0)
    rows = dot_nn(match[...], back[:, :width])
    moe = gates * rows
    result = h1 + moe
    store_in_order(out_o, result, order_s)
    d_gate = jnp.sum(rows * up, axis=1, keepdims=True)
    d_logits = (onehot * (d_gate * slope)).astype(BF16)
    router_o[...] = dot_tn(d_logits, n2[...])
    d_n2 = dot_nn(match[...], back[:, width:]) + dot_nn(d_logits, router[...])
    d_norm, terms = norm_grads(h1, rms_scale(h1), gain[...], d_n2)
    gain_o[...] = jnp.sum(terms, axis=0, keepdims=True)
    d_h1 = up + d_norm
    dh_o[...] = d_h1
    dmix_o[...] = d_h1.astype(BF16)
    sums_o[0:1] = jnp.broadcast_to(jnp.sum(result * result, keepdims=True), (1, LANE))
    sums_o[1:2] = jnp.broadcast_to(jnp.sum(moe * moe, keepdims=True), (1, LANE))


def gate_back_kernel(
    states, c_at, d_mix, wout, y, z, uf, proj, step_i, cut, a_ref,
    dy_o, dz_o, skip_o, fx_ref, tx_ref, fd_o, cb, st_s, fd_s,
):
    length, width = step_i.shape[1:]
    groups, steps = width // LANE, length // SEG
    d_gated = dot_nt(d_mix[0], wout[...])
    zf = z[0].astype(F32)
    dy = d_gated * (zf * jax.nn.sigmoid(zf))
    dy_o[0] = dy
    dz_o[0, :length] = (d_gated * y[0] * silu_slope(zf)).astype(BF16)
    dz_o[0, length:] = jnp.zeros((EDGE, width), BF16)

    @pl.when(pl.program_id(0) == 0)
    def _():
        skip_o[...] = jnp.zeros_like(skip_o)

    skip_o[...] += jnp.sum(dy * uf[0], axis=0, keepdims=True)
    cb[...] = spread(proj[0], states, c_at)
    for g in range(groups):
        cols = slice(g * LANE, (g + 1) * LANE)
        st_s[:, cols] = step_i[0, :, cols] + cut[0]
    zero = jnp.zeros((SEG, LANE), F32)
    seg = seg_of()

    def group(g, _):
        lanes = lanes_of(g)
        a = [wide(a_ref, n, lanes) for n in range(states)]

        def step(lap, carry):
            rows = rows_of(steps - 1 - lap)
            st = st_s[rows, lanes]
            d = dy_o[0, rows, lanes]
            new = [carry[0] + st]
            for n in range(states):
                new.append(jnp.exp(st * a[n]) * (carry[n + 1] + cb[rows, state_cols(n)] * d))
            return tuple(new)

        out = lax.fori_loop(0, steps, step, (zero,) * (states + 1), unroll=2)
        total, f = out[0], list(out[1:])
        for k in (1, 2, 4):
            ok = seg < SEG - k
            for n in range(states):
                f[n] = f[n] + jnp.where(ok, jnp.exp(total * a[n]) * rolled(f[n], -k), 0.0)
            total = total + jnp.where(ok, rolled(total, -k), 0.0)
        ok = seg < SEG - 1
        tx_ref[0, :, lanes] = jnp.where(ok, rolled(total, -1), 0.0)
        for n in range(states):
            fx_ref[0, n, :, lanes] = jnp.where(ok, rolled(f[n], -1), 0.0)
            fd_s[pl.ds(n, 1), lanes] = f[n][0:1]
        return 0

    lax.fori_loop(0, groups, group, 0)
    fd_o[0] = fd_s[...].astype(BF16)


def scan_back_kernel(
    states, b_at, place_ref, proj, step_i, sig, uf, cut, dy_i, a_ref, skip, wdt, hx_ref, sx_ref, e_i,
    fx_ref, tx_ref, finals, sums,
    part_o, du_o, dt_o, bias_o, ga_ref,
    bb, cb, dec, pri, accb, accc, st_s, dr_s, ds_s, out_s,
):
    length, width = step_i.shape[1:]
    groups, steps = width // LANE, length // SEG
    bb[...] = spread(proj[0], states, b_at)
    cb[...] = spread(proj[0], states, b_at + states)
    accb[...] = jnp.zeros_like(accb)
    accc[...] = jnp.zeros_like(accc)
    entering(out_s, finals, sums, a_ref, place_ref[0], False)
    e_ref = e_i.at[0]
    dr_s[...] = step_i[0] * uf[0]
    for g in range(groups):
        cols = slice(g * LANE, (g + 1) * LANE)
        st_s[:, cols] = step_i[0, :, cols] + cut[0]

    @pl.when(pl.program_id(0) == 0)
    def _():
        ga_ref[...] = jnp.zeros_like(ga_ref)
        dt_o[...] = jnp.zeros_like(dt_o)
        bias_o[...] = jnp.zeros_like(bias_o)

    def group(g, _):
        lanes = lanes_of(g)
        a = [wide(a_ref, n, lanes) for n in range(states)]
        sx = sx_ref[0, :, lanes]
        first = tuple(
            jnp.exp(sx * a[n]) * wide(e_ref, n, lanes) + hx_ref[0, n, :, lanes]
            for n in range(states)
        )

        def ahead(j, h):
            rows = rows_of(j)
            st = st_s[rows, lanes]
            dr = dr_s[rows, lanes]
            new = []
            for n in range(states):
                decay = jnp.exp(st * a[n])
                dec[rows, state_cols(n)] = decay
                pri[rows, state_cols(n)] = h[n]
                new.append(decay * h[n] + bb[rows, state_cols(n)] * dr)
            return tuple(new)

        last = lax.fori_loop(0, steps, ahead, first, unroll=2)
        end = rows_of(steps)
        for n in range(states):
            pri[end, state_cols(n)] = last[n]
        tx = tx_ref[0, :, lanes]
        flow = tuple(
            jnp.exp(tx * a[n]) * wide(out_s, n, lanes) + fx_ref[0, n, :, lanes]
            for n in range(states)
        )
        gain = wide(skip, 0, lanes)

        def back(lap, f):
            j = steps - 1 - lap
            rows = rows_of(j)
            after = rows_of(j + 1)
            st = step_i[0, rows, lanes]
            dr = dr_s[rows, lanes]
            dy = dy_i[0, rows, lanes]
            new = []
            d_step = None
            d_drive = None
            for n in range(states):
                cols = state_cols(n)
                d = f[n] + cb[rows, cols] * dy
                accc[rows, cols] += pri[after, cols] * dy
                accb[rows, cols] += d * dr
                flowing = dec[rows, cols] * d
                new.append(flowing)
                d_log = flowing * pri[rows, cols]
                ga_ref[n, :, lanes] += d_log * st
                part = d_log * a[n]
                d_step = part if d_step is None else d_step + part
                part = d * bb[rows, cols]
                d_drive = part if d_drive is None else d_drive + part
            ds_s[rows, lanes] = (d_step + d_drive * uf[0, rows, lanes]) * sig[0, rows, lanes]
            du_o[0, rows, lanes] = d_drive * st + dy * gain
            return tuple(new)

        lax.fori_loop(0, steps, back, flow, unroll=2)
        return 0

    lax.fori_loop(0, groups, group, 0)
    d_pre = ds_s[...]
    bias_o[...] += jnp.sum(d_pre, axis=0, keepdims=True)
    d_pre = d_pre.astype(BF16)
    dt_o[...] += dot_tn(proj[0], d_pre)
    columns = part_o.shape[2]
    part = dot_nt(d_pre, wdt[...])
    part = part + collected(accb[...], states, columns, b_at)
    part = part + collected(accc[...], states, columns, b_at + states)
    part_o[0] = part.astype(BF16)


def conv_back_kernel(
    taps, place_ref, doc_ref, terms, wproj, du, pre, ext, u, conv, dz, wx, wz, n1,
    dx_o, dn_o, gconv_o, gx_o, gain_o, dext,
):
    length, width = du.shape[1:]
    steps = length // SEG
    behind = taps - 1

    @pl.when(pl.program_id(0) == 0)
    def _():
        gconv_o[...] = jnp.zeros_like(gconv_o)
        gx_o[...] = jnp.zeros_like(gx_o)
        gain_o[...] = jnp.zeros_like(gain_o)

    total = terms[0, 0].astype(F32)
    for w in range(1, terms.shape[0]):
        total = total + terms[w, 0].astype(F32)
    proj = total.astype(BF16)
    gx_o[...] += dot_tn(proj, u[0])
    d_u = dot_nt(proj, wproj[...]) + du[0]
    masks, _ = lag_masks(place_ref[0], doc_ref, pl.program_id(0), length, taps)
    seg = seg_of()
    row = lax.broadcasted_iota(jnp.int32, (EDGE, LANE), 0)
    for g in range(width // LANE):
        cols = slice(g * LANE, (g + 1) * LANE)
        d = d_u[:, cols] * silu_slope(pre[0, :, cols])
        gconv_o[taps : taps + 1, cols] += jnp.sum(d, axis=0, keepdims=True)
        dext[...] = jnp.zeros_like(dext)
        for lag in range(taps):
            weighted = d if lag == 0 else d * masks[lag]
            at = pl.ds((behind - lag) * SEG, length)
            gconv_o[lag : lag + 1, cols] += jnp.sum(weighted * ext[0, at, cols], axis=0, keepdims=True)
            dext[at, :] += weighted * conv[lag : lag + 1, cols]
        before = jnp.zeros((EDGE, LANE), F32)
        for i in range(behind):
            head = dext[i * SEG : (i + 1) * SEG]
            j = pl.ds((steps + i) * SEG, SEG)
            dext[j, :] += jnp.where(seg < SEG - 1, rolled(head, -1), 0.0)
            first = jnp.broadcast_to(head[0:1], (EDGE, LANE))
            before = before + jnp.where(row == EDGE - behind + i, first, 0.0)
        dx_o[0, :length, cols] = dext[behind * SEG :].astype(BF16)
        dx_o[0, length:, cols] = before.astype(BF16)
    d_n1 = dot_nt(dx_o[0], wx[0]) + dot_nt(dz[0], wz[0])
    gain_o[...] += jnp.sum(d_n1 * n1[0].astype(F32), axis=0, keepdims=True)
    dn_o[0] = d_n1.astype(BF16)


def leave_kernel(taps, last_ref, terms, edges, tok, gain, dh, out_o, dn_s, order_s):
    length = tok.shape[0]
    steps = length // SEG
    behind = taps - 1
    total = terms[0, :length].astype(F32)
    edge = edges[0].astype(F32)
    for w in range(1, terms.shape[0]):
        total = total + terms[w, :length].astype(F32)
        edge = edge + edges[w].astype(F32)
    edge = jnp.where(last_ref[0] > 0, 0.0, edge)
    dn_s[...] = total
    seg = lax.broadcasted_iota(jnp.int32, (SEG, tok.shape[1]), 0)
    for i in range(behind):
        j = pl.ds((steps - behind + i) * SEG, SEG)
        row = EDGE - behind + i
        came = jnp.broadcast_to(edge[row : row + 1], seg.shape)
        dn_s[j, :] += jnp.where(seg == SEG - 1, came, 0.0)
    x = dot_nn(permutation(length), tok[...])
    d_x, _ = norm_grads(x, rms_scale(x), gain[...], dn_s[...])
    result = dh[...] + d_x
    store_in_order(out_o, result, order_s)


SMEM = "smem"
ANY = "any"


def by_stream(shape, at=0):
    block = tuple(1 if i == at else n for i, n in enumerate(shape))
    rank = len(shape)

    def index(s):
        return tuple(s if i == at else 0 for i in range(rank))

    return pl.BlockSpec(block, index)


def whole(shape):
    return pl.BlockSpec(shape, lambda s: (0,) * len(shape))


def call(kernel, name, grid, args, outs, scratch, us):
    arrays, specs = [], []
    for array, at in args:
        arrays.append(array)
        if at == SMEM:
            specs.append(pl.BlockSpec(memory_space=pltpu.SMEM))
        elif at == ANY:
            specs.append(pl.BlockSpec(memory_space=pl.ANY))
        elif callable(at):
            specs.append(at(array.shape))
        else:
            specs.append(whole(array.shape) if at is None else by_stream(array.shape, at))
    out_specs = []
    for shape, _, at in outs:
        if callable(at):
            out_specs.append(at(shape))
        else:
            out_specs.append(whole(shape) if at is None else by_stream(shape, at))
    return pl.pallas_call(
        kernel,
        grid=(grid,),
        out_shape=[jax.ShapeDtypeStruct(shape, dtype) for shape, dtype, _ in outs],
        in_specs=specs,
        out_specs=out_specs,
        scratch_shapes=scratch,
        compiler_params=pltpu.CompilerParams(vmem_limit_bytes=VMEM_LIMIT),
        cost_estimate=lasting(us),
        name=name,
    )(*arrays)


def padded_to(array, width, axis):
    pads = [(0, 0)] * array.ndim
    pads[axis] = (0, width - array.shape[axis])
    return jnp.pad(array, pads)


def up_to(n, multiple):
    return -(-n // multiple) * multiple


def body(
    tokens, out_grad, doc_starts, routes, keep_mask, norm_mix, w_in, conv_w, conv_b, w_x, w_dt,
    dt_bias, a_log, d_skip, w_out, norm_moe, w_router, w_up, w_down,
):
    group = lax.axis_size("wa")
    ring = lax.axis_size("ctx")
    mine = lax.axis_index("wa")
    place = lax.axis_index("ctx")
    length, width = tokens.shape[1:]
    taps, local = conv_w.shape
    states = a_log.shape[0]
    ranked = w_dt.shape[0]
    experts = w_router.shape[1]
    padded = up_to(local, LANE)
    columns = up_to(w_x.shape[1], LANE)
    steps = length // SEG
    rows = length + EDGE
    slots = experts * (length // 2)
    share = norm_mix.shape[0]
    order_vmem = pltpu.VMEM((width // LANE, length, LANE), F32)
    place_s = place.astype(jnp.int32).reshape(1)
    last_s = (place == ring - 1).astype(jnp.int32).reshape(1)
    f32_vmem = lambda *shape: pltpu.VMEM(shape, F32)

    in_each = -(-width // ring)
    in_rows = up_to(in_each, 16)
    part_in = lax.dynamic_slice_in_dim(w_in, place * in_each, in_each, 0)
    halves = jnp.stack([part_in[:, :local], part_in[:, local:]], axis=0)
    halves = jnp.pad(halves, ((0, 0), (0, in_rows - in_each), (0, padded - local)))
    small = jnp.concatenate([norm_mix, norm_moe, w_router.T.reshape(-1)], axis=0)
    small_count = up_to(-(-small.shape[0] // LANE), 16)
    small = jnp.pad(small, (0, small_count * LANE - small.shape[0])).reshape(small_count, LANE)
    documents = doc_starts.shape[1]
    doc_tile = jnp.pad(doc_starts, ((0, SEG - 1), (0, LANE - documents)))
    all_rows, all_edges, smalls, docs, w_blocks = start(tokens[0], small, doc_tile, halves, 1)
    proj_in = w_blocks[:, :, :in_each].reshape(2, width, padded)
    of_x = lambda shape: pl.BlockSpec((1,) + shape[1:], lambda i: (0, 0, 0))
    of_z = lambda shape: pl.BlockSpec((1,) + shape[1:], lambda i: (1, 0, 0))
    (own_experts,) = call(
        pack_kernel, "pack", 1, [(w_up[0], None), (w_down[0], None), (docs, ANY)],
        [((w_down.shape[1], 2 * width), BF16, None)], [], 3,
    )
    expert_w = lax.all_gather(own_experts, "ctx", axis=0, tiled=True)
    smalls = smalls.reshape(group, -1)[:, : (2 + experts) * share]
    smalls = smalls.reshape(group, 2 + experts, share).swapaxes(0, 1).reshape(2 + experts, width)
    gain_mix, gain_moe = smalls[0:1].astype(F32), smalls[1:2].astype(F32)
    router = padded_to(smalls[2:], LANE, 0)
    docs = docs[:, 0, :documents]

    conv = jnp.concatenate([conv_w, conv_b[None]], axis=0).astype(F32)
    conv = jnp.pad(conv, ((0, SEG - taps - 1), (0, padded - local)))
    wproj = jnp.pad(w_x, ((0, padded - local), (0, columns - w_x.shape[1])))
    wdt = jnp.pad(w_dt, ((0, columns - ranked), (0, padded - local)))
    step_bias = padded_to(dt_bias[None], padded, 1).astype(F32)
    a_mat = -jnp.exp(padded_to(a_log, padded, 1).astype(F32))
    skip = padded_to(d_skip[None], padded, 1).astype(F32)
    wout = padded_to(w_out, padded, 0)

    vec = (group, length, padded)
    n1, ext, pre_conv, u_f, u, z, part, cut = call(
        functools.partial(enter_kernel, taps), "enter", group,
        [(place_s, SMEM), (docs, SMEM), (all_rows, 0), (all_edges, 0), (gain_mix, None),
         (proj_in, of_x), (proj_in, of_z), (conv, None), (wproj, None)],
        [((group, rows, width), BF16, 0), ((group, (taps - 1) * SEG + length, padded), F32, 0),
         (vec, F32, 0), (vec, F32, 0), (vec, BF16, 0), (vec, BF16, 0),
         ((group, length, columns), BF16, 0), ((group, length, LANE), F32, 0)],
        [], 8,
    )
    (parts,) = gather_all([part], "wa", 2, 15)
    seg_states = (group, states, SEG, padded)
    seg_sums = (group, SEG, padded)
    dev_states = (group, states, padded)
    dev_sums = (group, 1, padded)
    spread_vmem = f32_vmem(length, states * LANE)
    lane_vmem = f32_vmem(length, padded)
    state_vmem = f32_vmem(states, padded)
    proj, step_size, sig, h_in, s_in, h_dev, s_dev = call(
        functools.partial(summary_kernel, states, ranked), "scan_summary", group,
        [(parts, 1), (wdt, None), (step_bias, None), (u_f, 0), (cut, 0), (a_mat, None)],
        [((group, length, columns), BF16, 0), (vec, F32, 0), (vec, F32, 0), (seg_states, F32, 0),
         (seg_sums, F32, 0), (dev_states, BF16, 0), (dev_sums, F32, 0)],
        [spread_vmem, lane_vmem, lane_vmem, state_vmem], 10,
    )
    all_h, all_s = gather_all([h_dev, s_dev], "ctx", 3, 15)
    y_full, gated, mix_part, e_in = call(
        functools.partial(output_kernel, states, ranked), "scan_output", group,
        [(place_s, SMEM), (proj, 0), (step_size, 0), (u_f, 0), (cut, 0), (a_mat, None), (h_in, 0),
         (s_in, 0), (all_h, 1), (all_s, 1), (z, 0), (skip, None), (wout, None)],
        [(vec, F32, 0), (vec, BF16, 0), ((group, length, width), BF16, 0), (dev_states, F32, 0)],
        [spread_vmem, spread_vmem, lane_vmem, lane_vmem], 13,
    )
    mix_terms = trade(mix_part, "wa", 4, 25)

    row_f = (length, width)
    h1, n2, upstream, facts, match, outgoing, mix_sum = call(
        functools.partial(route_kernel, experts), "route", 1,
        [(mix_terms, None), (tokens[0], None), (gain_moe, None), (router, None),
         (routes[0], None), (keep_mask[0][:, None], None), (out_grad[0], None)],
        [(row_f, F32, None), (row_f, BF16, None), (row_f, F32, None), ((length, LANE), F32, None),
         ((length, slots), BF16, None), ((slots, 2 * width), BF16, None), ((SEG, LANE), F32, None)],
        [], 5,
    )
    arrived = trade(outgoing.reshape(group, slots // group, 2 * width), "wa", 5, 29)
    hidden_units = expert_w.shape[0]
    block = hidden_units // 8
    of_block = lambda shape: pl.BlockSpec((block, shape[1]), lambda i: (i, 0))
    grad_experts, returning = call(
        experts_kernel, "experts", 8,
        [(arrived.reshape(slots, 2 * width), None), (expert_w, of_block)],
        [((hidden_units, 2 * width), BF16, of_block), ((slots, 2 * width), BF16, None)],
        [f32_vmem(slots, 2 * width)], 18,
    )
    share_experts = lax.psum_scatter(grad_experts, "ctx", scatter_dimension=0, tiled=True)
    returned = trade(returning.reshape(group, slots // group, 2 * width), "wa", 6, 29)
    result, d_h1, d_mix_own, grad_router, grad_gain_moe, out_sums = call(
        functools.partial(combine_kernel, experts), "combine", 1,
        [(returned.reshape(slots, 2 * width), None), (match, None), (h1, None), (n2, None),
         (upstream, None), (facts, None), (gain_moe, None), (router, None)],
        [(row_f, F32, None), (row_f, F32, None), (row_f, BF16, None), ((LANE, width), F32, None),
         ((1, width), F32, None), ((SEG, LANE), F32, None)],
        [order_vmem], 6,
    )
    (d_mix,) = gather_all([d_mix_own], "wa", 7, 28)

    d_y, d_z, grad_skip, f_in, t_in, f_dev = call(
        functools.partial(gate_back_kernel, states, ranked + states), "gate_back", group,
        [(d_mix, 0), (wout, None), (y_full, 0), (z, 0), (u_f, 0), (proj, 0), (step_size, 0),
         (cut, 0), (a_mat, None)],
        [(vec, F32, 0), ((group, rows, padded), BF16, 0), ((1, padded), F32, None),
         (seg_states, F32, 0), (seg_sums, F32, 0), (dev_states, BF16, 0)],
        [spread_vmem, lane_vmem, state_vmem], 11,
    )
    grad_in_z = dot_tn(n1.reshape(group * rows, width), d_z.reshape(group * rows, padded))
    grad_out = dot_tn(
        d_mix.reshape(group * length, width), gated.reshape(group * length, padded)
    )
    grad_zo = jnp.concatenate([grad_in_z, grad_out], axis=1).astype(BF16)
    grad_zo = jnp.pad(
        grad_zo.reshape(ring // 2, 2, in_each, 2 * padded),
        ((0, 0), (0, 0), (0, in_rows - in_each), (0, 0)),
    )
    all_f, pair_zo = carry_back(f_dev, grad_zo, 8, 14)
    d_part, d_u, grad_dt, grad_step_bias, grad_a = call(
        functools.partial(scan_back_kernel, states, ranked), "scan_back", group,
        [(place_s, SMEM), (proj, 0), (step_size, 0), (sig, 0), (u_f, 0), (cut, 0), (d_y, 0),
         (a_mat, None), (skip, None), (wdt, None), (h_in, 0), (s_in, 0), (e_in, 0), (f_in, 0),
         (t_in, 0), (all_f, 1), (all_s, 1)],
        [((group, length, columns), BF16, 0), (vec, F32, 0), ((columns, padded), F32, None),
         ((1, padded), F32, None), ((states, SEG, padded), F32, None)],
        [spread_vmem, spread_vmem, spread_vmem, f32_vmem(length + SEG, states * LANE), spread_vmem,
         spread_vmem, lane_vmem, lane_vmem, lane_vmem, state_vmem], 34,
    )
    d_parts, chunk_zo = proj_back(d_part, grad_zo, pair_zo, 9, 20)
    d_x, d_n1_part, grad_conv, grad_x, gain_terms = call(
        functools.partial(conv_back_kernel, taps), "conv_back", group,
        [(place_s, SMEM), (docs, SMEM), (d_parts, 1), (wproj, None), (d_u, 0), (pre_conv, 0),
         (ext, 0), (u, 0), (conv, None), (d_z, 0), (proj_in, of_x), (proj_in, of_z), (n1, 0)],
        [((group, rows, padded), BF16, 0), ((group, rows, width), BF16, 0),
         ((SEG, padded), F32, None), ((columns, padded), F32, None), ((1, width), F32, None)],
        [f32_vmem((taps - 1) * SEG + length, LANE)], 10,
    )
    grad_gain_mix = gain_terms / gain_mix
    grad_in_x = dot_tn(n1.reshape(group * rows, width), d_x.reshape(group * rows, padded))
    grad_a_log = jnp.sum(grad_a, axis=1) * a_mat

    def dealt(rows, count):
        each = -(-rows.shape[0] // ring)
        rows = jnp.pad(rows, ((0, each * ring - rows.shape[0]), (0, 0)))
        return jnp.pad(rows.reshape(ring, each, -1), ((0, 0), (0, count - each), (0, 0)))

    small = jnp.concatenate(
        [grad_conv[: taps + 1], grad_step_bias, grad_skip, grad_a_log, grad_dt[:ranked],
         grad_x[: w_x.shape[1]]],
        axis=0,
    ).astype(BF16)
    small_each = -(-small.shape[0] // ring)
    small_rows = up_to(small_each, 16)
    fulls = jnp.concatenate([grad_gain_mix, grad_gain_moe, grad_router[:experts]], axis=0)
    fulls = fulls.reshape(2 + experts, group, share).swapaxes(0, 1).reshape(group, -1)
    full_each = -(-fulls.shape[1] // ring)
    fulls = jnp.pad(fulls, ((0, 0), (0, full_each * ring - fulls.shape[1])))
    fulls = fulls.reshape(group, ring, full_each).swapaxes(0, 1)
    fulls = jnp.pad(fulls, ((0, 0), (0, 0), (0, padded - full_each)))
    stat_row = jnp.stack([out_sums[0, 0], mix_sum[0, 0], out_sums[1, 0]])
    is_mine = (lax.iota(jnp.int32, group) == mine).astype(F32)
    stat_rows = padded_to(is_mine[:, None] * stat_row[None, :], padded, 1)
    stat_rows = jnp.broadcast_to(stat_rows[None], (ring, group, padded))
    tile = jnp.concatenate([fulls, stat_rows], axis=1)
    tile = jnp.pad(tile, ((0, 0), (0, 16 - tile.shape[1]), (0, 0))).astype(BF16)
    packed = jnp.concatenate(
        [dealt(grad_in_x.astype(BF16), in_rows), dealt(small, small_rows), tile], axis=1
    )
    packed = packed.reshape((ring // 2, 2) + packed.shape[1:])
    done, d_n1_terms, d_edges = finish(packed, chunk_zo, d_n1_part, in_rows, small_rows, 11)
    share_in = jnp.concatenate(
        [done[:, :in_each, :local], done[:, in_rows : in_rows + in_each, :local]], axis=2
    ).reshape(width, 2 * local).astype(F32)
    base = 2 * in_rows + small_rows + 16
    share_out = done[:, base : base + in_each, :local].reshape(width, local).T.astype(F32)
    base = 2 * in_rows
    smalls_sum = done[:, base : base + small_each, :local].reshape(ring * small_each, local)
    smalls_sum = smalls_sum.astype(F32)
    base = base + small_rows
    full_sum = lax.dynamic_index_in_dim(done, base + mine, 1, False)[:, :full_each]
    full_sum = full_sum.reshape(-1)[: (2 + experts) * share].reshape(2 + experts, share).astype(F32)
    stat_sums = lax.dynamic_index_in_dim(done, base + group + mine, 1, False)[0, :3].astype(F32)
    (input_grad,) = call(
        functools.partial(leave_kernel, taps), "leave", 1,
        [(last_s, SMEM), (d_n1_terms, None), (d_edges, None), (tokens[0], None), (gain_mix, None),
         (d_h1, None)],
        [(row_f, F32, None)], [f32_vmem(length, width), order_vmem], 4,
    )
    marks_at = [0, taps, taps + 1, taps + 2, taps + 3, taps + 3 + states]
    marks_at += [marks_at[-1] + ranked, marks_at[-1] + ranked + w_x.shape[1]]
    cut_at = [smalls_sum[a:b] for a, b in zip(marks_at[:-1], marks_at[1:])]
    denom = length * ring * width
    rms_stats = jnp.sqrt(stat_sums / denom)[None]
    return (
        result[None],
        input_grad[None],
        full_sum[0],
        share_in,
        cut_at[0],
        cut_at[1][0],
        cut_at[6].T,
        cut_at[5],
        cut_at[2][0],
        cut_at[4],
        cut_at[3][0],
        share_out,
        full_sum[1],
        full_sum[2:].T,
        share_experts[:, :width].T.astype(F32)[None],
        share_experts[:, width:].astype(F32)[None],
        rms_stats,
    )


def solution(mesh):
    placed = (
        P("wa", "ctx", None),
        P("wa", "ctx", None),
        P("wa", None),
        P("wa", "ctx", None),
        P("wa", "ctx"),
        P("wa"),
        P(None, "wa"),
        P(None, "wa"),
        P("wa"),
        P("wa", None),
        P(None, "wa"),
        P("wa"),
        P(None, "wa"),
        P("wa"),
        P("wa", None),
        P("wa"),
        P("wa", None),
        P("wa", None, "ctx"),
        P("wa", "ctx", None),
    )
    return jax.shard_map(
        body,
        mesh=mesh,
        in_specs=placed,
        out_specs=(
            P("wa", "ctx", None),
            P("wa", "ctx", None),
            P("wa"),
            P(None, "wa"),
            P(None, "wa"),
            P("wa"),
            P("wa", None),
            P(None, "wa"),
            P("wa"),
            P(None, "wa"),
            P("wa"),
            P("wa", None),
            P("wa"),
            P("wa", None),
            P("wa", None, "ctx"),
            P("wa", "ctx", None),
            P("wa", None),
        ),
        check_vma=False,
    )
```

time: 650 us -> 509 us (0.78); the launches traced: 639 us -> 507 us
  matrix products: 77.5 us -> 4.11 us
  Pallas kernels: 385 us -> 432 us
  waiting for transfers between devices: 41.9 us -> 0.06 us
  local copies, waits for them, and re-layouts: 65.8 us -> 35.1 us
  other arithmetic: 50.9 us -> 21 us
    dot_general x26 -> x3, matrix products: 77.5 us -> 4.11 us  [dot_tn(): lax.dot_general(a, b, (((0,), (0,)), ((), ())), preferred_element_type=F32)]
    pallas_call x12 -> x19, Pallas kernels: 269 us -> 320 us  [the longest x11 133 us: call(): pl.pallas_call(kernel, grid=(grid,), out_shape=[jax.ShapeDtypeStruct(shap...]
    reduce_scatter x3 -> x1, waiting for transfers between devices: 40.4 us -> 0.01 us  [body(): lax.psum_scatter(grad_experts, 'ctx', scatter_dimension=0, tiled=True)]
    reduce_sum x14 -> x0, other arithmetic: 16 us -> none  [the longest x1 2.64 us: body(): grad_step_bias = jnp.sum(d_step_pre, axis=0)]
    unnamed x242 -> x52, local copies, waits for them, and re-layouts: 16.7 us -> 2.39 us
    convert_element_type x21 -> x6, other arithmetic: 14.4 us -> 5.47 us  [the longest x1 2.92 us: body(): share_in = jnp.concatenate([done[:, :in_each, :local], done[:, in_rows:in...]
    slice x16 -> x11, local copies, waits for them, and re-layouts: 14.4 us -> 11.8 us  [the longest x1 4.24 us: body(): done[:, base:base + in_each, :local].reshape(width, local).T.astype(F32)]
  transfers between devices with their start and end apart: 6 -> 2, of which waited for: 2 -> 0; matrix products, arithmetic and copies ran while one was open for 19% -> 10% of each run, Pallas kernels for 41% -> 67%
where the time goes in v3:
time: 509 us; the launch traced here: 507 us
  Pallas kernels  432 us (85%)
  local copies, waits for them, and re-layouts  35.1 us (7%)
  other arithmetic  21 us (4%)
  between operations  14.6 us (3%)
    pallas_call x11, Pallas kernels, call(): pl.pallas_call(kernel, grid=(grid,), out_shape=[jax.ShapeDtypeStruct(shap...  133 us
    pallas_call x3, Pallas kernels, trade(): pl.pallas_call(functools.partial(trade_kernel, axis, count), out_shape=ja...  84.4 us
    pallas_call x1, Pallas kernels, finish(): pl.pallas_call(functools.partial(finish_kernel, ring, group, in_rows, sma...  70.2 us
    pallas_call x3, Pallas kernels, gather_all(): pl.pallas_call(functools.partial(gather_kernel, axis, count, arrays), out...  62.5 us
    pallas_call x1, Pallas kernels, start(): pl.pallas_call(functools.partial(start_kernel, ring, group), out_shape=[j...  41.4 us
    pallas_call x1, Pallas kernels, proj_back(): pl.pallas_call(functools.partial(proj_back_kernel, ring, group), out_shap...  20.1 us
    pallas_call x1, Pallas kernels, carry_back(): pl.pallas_call(functools.partial(carry_back_kernel, ring), out_shape=[jax...  19.5 us
  transfers between devices with their start and end apart: 2, of which 0 were waited for; matrix products, arithmetic and copies ran while one was open for 10% of the time, Pallas kernels for 67%

profile of v3, /device:TPU:11, one launch (start us, length us, event | category | flops | bytes accessed | tf_op | source)
XLA Modules:
  0.0 506.5 jit_solution(2041782603731425639)
XLA Ops:
  13.3 41.4 %start.1 = (bf16[4,128,1152]{2,1,0:T(8,128)(2,1)}, bf16[4,16,1152]{2,1,0:T(8,128)(2,1)}, bf16[4,16,128]{2,1,0:T(8,128)(2,1)}, s32[4,8,128]{2,1,0:T(8,128)}, bf16[2,8,144,640]{3,2,1,0:T(8,128)(2,1)}) custom-call(bf16[128,1152]{1,0:T(8,128)(2,1)} %bitcast.106, bf16[16,128]{1,0:T(8,128)(2,1)} %pad_bitcast_fusion.par, s32[8,128]{1,0:T(8,128)} %pad.68.doc, ...), custom_call_target="tpu_custom_call" | custom-call | flops 38499999744 | bytes 122500000 | tf_op jit(solution)/shard_map/start/pallas_call | solution.py:613
  54.7 3.3 pack.1
  68.7 8.8 %enter.1 = (bf16[4,144,1152]{2,1,0:T(8,128)(2,1)}, f32[4,152,640]{2,1,0:T(8,128)}, f32[4,128,640]{2,1,0:T(8,128)}, f32[4,128,640]{2,1,0:T(8,128)}, bf16[4,128,64...) custom-call(s32[1]{0:T(128)} %bitcast.place_ref, ...), custom_call_target="tpu_custom_call" | custom-call | flops 8800000000 | bytes 28000000 | tf_op jit(solution)/shard_map/enter/pallas_call | solution.py:1277
  77.6 13.6 %gather_2.1.terms = bf16[4,4,128,128]{3,2,1,0:T(8,128)(2,1)} custom-call(bf16[4,128,128]{2,1,0:T(8,128)(2,1)} %get-tuple-element.86.refs_0_), custom_call_target="tpu_custom_call" | custom-call | flops 16499999744 | bytes 52500000 | tf_op jit(solution)/shard_map/gather_2/pallas_call | solution.py:107
  91.1 11.6 %scan_summary.1 = (bf16[4,128,128]{2,1,0:T(8,128)(2,1)}, f32[4,128,640]{2,1,0:T(8,128)}, f32[4,128,640]{2,1,0:T(8,128)}, f32[4,16,8,640]{3,2,1,0:T(8,128)}, f32[...) custom-call(bf16[4,4,128,128]{3,2,1,0:T(8,128)(2,1)} %gather_2.1.terms, ...), custom_call_target="tpu_custom_call" | custom-call | flops 11000000512 | bytes 35000000 | tf_op jit(solution)/shard_map/scan_summary/pallas_call | solution.py:1277
  102.7 21.5 %gather_3.1 = (bf16[8,4,16,640]{3,2,1,0:T(8,128)(2,1)}, f32[8,4,1,640]{3,2,1,0:T(1,128)}) custom-call(bf16[4,16,640]{2,1,0:T(8,128)(2,1)} %get-tuple-element.93.refs_0_, f32[4,1,640]{2,1,0:T(1,128)} %get-tuple-element.94.refs_1_), custom_call_target="tpu_custom_call" | custom-call | flops 16499999744 | bytes 52500000 | tf_op jit(solution)/shard_map/gather_3/pallas_call | solution.py:107
  124.2 16.2 %scan_output.1 = (f32[4,128,640]{2,1,0:T(8,128)}, bf16[4,128,640]{2,1,0:T(8,128)(2,1)}, bf16[4,128,1152]{2,1,0:T(8,128)(2,1)}, f32[4,16,640]{2,1,0:T(8,128)}) custom-call(s32[1]{0:T(128)} %bitcast.place_ref, bf16[4,128,128]{2,1,0:T(8,128)(2,1)} %get-tuple-element.89.proj, f32[4,128,640]{2,1,0:T(8,128)} %get-tuple-element.90.step_i, ...), custom_call_target="tpu_custom_call" | custom-call | flops 14300000256 | bytes 45500000 | tf_op jit(solution)/shard_map/scan_output/pallas_call | solution.py:1277
  140.4 28.4 %trade_4.1.terms = bf16[4,128,1152]{2,1,0:T(8,128)(2,1)} custom-call(bf16[4,128,1152]{2,1,0:T(8,128)(2,1)} %get-tuple-element.98.x_ref), custom_call_target="tpu_custom_call" | custom-call | flops 27499999232 | bytes 87500000 | tf_op jit(solution)/shard_map/trade_4/pallas_call | solution.py:87
  168.8 4.0 route.1
  174.5 28.6 %trade_5.1 = bf16[4,64,2304]{2,1,0:T(8,128)(2,1)} custom-call(bf16[4,64,2304]{2,1,0:T(8,128)(2,1)} %bitcast.114), custom_call_target="tpu_custom_call" | custom-call | flops 31900000256 | bytes 101500000 | tf_op jit(solution)/shard_map/trade_5/pallas_call | solution.py:87
  203.1 21.2 %experts.1 = (bf16[3072,2304]{1,0:T(8,128)(2,1)}, bf16[256,2304]{1,0:T(8,128)(2,1)}) custom-call(bf16[256,2304]{1,0:T(8,128)(2,1)} %bitcast.115, bf16[3072,2304]{1,0:T(8,128)(2,1)} %all-gather.2.cloned.1.call-done.w_ref), custom_call_target="tpu_custom_call" | custom-call | flops 19800000512 | bytes 63000000 | tf_op jit(solution)/shard_map/experts/pallas_call | solution.py:1277
  224.3 27.4 %trade_6.1 = bf16[4,64,2304]{2,1,0:T(8,128)(2,1)} custom-call(bf16[4,64,2304]{2,1,0:T(8,128)(2,1)} %bitcast.116), custom_call_target="tpu_custom_call" | custom-call | flops 31900000256 | bytes 101500000 | tf_op jit(solution)/shard_map/trade_6/pallas_call | solution.py:87
  251.7 4.0 combine.1
  255.7 27.4 %gather_7.1.d_mix = bf16[4,128,1152]{2,1,0:T(8,128)(2,1)} custom-call(bf16[128,1152]{1,0:T(8,128)(2,1)} %get-tuple-element.109.refs_0_), custom_call_target="tpu_custom_call" | custom-call | flops 30799998976 | bytes 98000000 | tf_op jit(solution)/shard_map/gather_7/pallas_call | solution.py:107
  283.1 16.0 %gate_back.1 = (f32[4,128,640]{2,1,0:T(8,128)}, bf16[4,144,640]{2,1,0:T(8,128)(2,1)}, f32[1,640]{1,0:T(1,128)}, f32[4,16,8,640]{3,2,1,0:T(8,128)}, f32[4,8,640]{2,1,0:T(8,128)}, /*index=5*/bf16[4,16,640]{2,1,0:T(8,128)(2,1)}) custom-call(bf16[4,128,1152]{2,1,0:T(8,128)(2,1)} %gather_7.1.d_mix, bf16[640,1152]{1,0:T(8,128)(2,1)} %pad.77.wout, ...), custom_call_target="tpu_custom_call" | custom-call | flops 12099999744 | bytes 38500000 | tf_op jit(solution)/shard_map/gate_back/pallas_call | solution.py:1277
  304.9 19.5 %carry_back.1 = (bf16[8,4,16,640]{3,2,1,0:T(8,128)(2,1)}, bf16[4,144,1280]{2,1,0:T(8,128)(2,1)}) custom-call(bf16[4,16,640]{2,1,0:T(8,128)(2,1)} %get-tuple-element.115.f_ref, bf16[4,2,144,1280]{3,2,1,0:T(8,128)(2,1)} %pad_maximum_fusion.g_ref), custom_call_target="tpu_custom_call" | custom-call | flops 15399999488 | bytes 49000000 | tf_op jit(solution)/shard_map/carry_back/pallas_call | solution.py:182
  324.4 35.5 %scan_back.1 = (bf16[4,128,128]{2,1,0:T(8,128)(2,1)}, f32[4,128,640]{2,1,0:T(8,128)}, f32[128,640]{1,0:T(8,128)}, f32[1,640]{1,0:T(1,128)}, f32[16,8,640]{2,1,0:T(8,128)}) custom-call(s32[1]{0:T(128)} %bitcast.place_ref, bf16[4,128,128]{2,1,0:T(8,128)(2,1)} %get-tuple-element.89.proj, f32[4,128,640]{2,1,0:T(8,128)} %get-tuple-element.90.step_i, ...), custom_call_target="tpu_custom_call" | custom-call | flops 37399998464 | bytes 119000000 | tf_op jit(solution)/shard_map/scan_back/pallas_call | solution.py:1277
  360.6 20.1 %proj_back.1 = (bf16[4,4,128,128]{3,2,1,0:T(8,128)(2,1)}, bf16[144,1280]{1,0:T(8,128)(2,1)}) custom-call(bf16[4,128,128]{2,1,0:T(8,128)(2,1)} %get-tuple-element.119.x_ref, bf16[4,2,144,1280]{3,2,1,0:T(8,128)(2,1)} %pad_maximum_fusion.g_ref, bf16[4,144,1280]{2,1,0:T(8,128)(2,1)} %get-tuple-element.120.p_ref), custom_call_target="tpu_custom_call" | custom-call | flops 22000001024 | bytes 70000000 | tf_op jit(solution)/shard_map/proj_back/pallas_call | solution.py:251
  380.8 9.5 %conv_back.1 = (bf16[4,144,640]{2,1,0:T(8,128)(2,1)}, bf16[4,144,1152]{2,1,0:T(8,128)(2,1)}, f32[8,640]{1,0:T(8,128)}, f32[128,640]{1,0:T(8,128)}, f32[1,1152]{1,0:T(1,128)}) custom-call(s32[1]{0:T(128)} %bitcast.place_ref, s32[4,4]{1,0:T(4,128)} %bitcast.100, bf16[4,4,128,128]{3,2,1,0:T(8,128)(2,1)} %get-tuple-element.121.terms, ...), custom_call_target="tpu_custom_call" | custom-call | flops 11000000512 | bytes 35000000 | tf_op jit(solution)/shard_map/conv_back/pallas_call | solution.py:1277
  401.6 70.2 %finish.1 = (bf16[8,480,640]{2,1,0:T(8,128)(2,1)}, bf16[4,144,1152]{2,1,0:T(8,128)(2,1)}, bf16[4,16,1152]{2,1,0:T(8,128)(2,1)}) custom-call(bf16[4,2,192,640]{3,2,1,0:T(8,128)(2,1)} %pad_maximum_fusion.2.g_ref, bf16[144,1280]{1,0:T(8,128)(2,1)} %get-tuple-element.138.zf_ref, bf16[4,144,1152]{2,1,0:T(8,128)(2,1)} %get-tuple-element.139.d_ref), custom_call_target="tpu_custom_call" | custom-call | flops 65999998976 | bytes 210000000 | tf_op jit(solution)/shard_map/finish/pallas_call | solution.py:451
  476.0 4.2 fusion.20
  488.8 3.3 leave.1
  492.1 2.9 bitcast_convert_fusion
  495.1 2.9 fusion.3
  (134 shorter events, 50.3 us)
Async XLA Ops:
  7.2 195.9 %all-gather.2.cloned.1.call-start = ((), (), s32[]{:S(2)}) async-start(), calls=%async_computation.1 | async-start | bytes 15925248 | tf_op jit(solution)/shard_map/all_gather | solution.py:1342
  58.0 1.6 copy-start.11
  58.0 1.6 copy-start.12
  58.0 1.6 copy-start.13
  58.0 1.6 copy-start.14
  58.0 2.4 copy-start.15
  58.0 3.1 copy-start.2
  58.1 3.9 copy-start.3
  58.1 4.6 copy-start
  58.1 437.0 %reduce-scatter.2.cloned.1.call-start = ((), (), s32[]{:S(2)}) async-start(), calls=%async_computation.2 | async-start | bytes 15925248 | tf_op jit(solution)/shard_map/reduce_scatter | solution.py:1412
  62.0 1.9 copy-start.7
  62.7 4.8 copy-start.8
  62.7 5.4 %copy-start.4 = (bf16[16,576]{1,0:T(8,128)(2,1)S(1)}, bf16[16,576]{1,0:T(8,128)(2,1)}, u32[]{:S(2)}) copy-start(bf16[16,576]{1,0:T(8,128)(2,1)} %param.31) | copy-start | bytes 55300
  283.1 16.1 %copy-start.17 = (bf16[4,128,1152]{2,1,0:T(8,128)(2,1)S(1)}, bf16[4,128,1152]{2,1,0:T(8,128)(2,1)}, u32[]{:S(2)}) copy-start(bf16[4,128,1152]{2,1,0:T(8,128)(2,1)} %gather_7.1.d_mix) | copy-start | bytes 3538948
  283.1 16.1 %copy-start.18 = (bf16[4,128,640]{2,1,0:T(8,128)(2,1)S(1)}, bf16[4,128,640]{2,1,0:T(8,128)(2,1)}, u32[]{:S(2)}) copy-start(bf16[4,128,640]{2,1,0:T(8,128)(2,1)} %get-tuple-element.117) | copy-start | bytes 1966084
  299.2 1.5 copy-start.22
  302.2 1.8 copy-start.9
  302.2 2.6 copy-start.10
  380.7 9.5 %copy-start.6 = (f32[1,1152]{1,0:T(1,128)S(1)}, f32[1,1152]{1,0:T(1,128)}, u32[]{:S(2)}) copy-start(f32[1,1152]{1,0:T(1,128)} %reshape.164.gain) | copy-start | bytes 13828
  380.7 14.5 %copy-start.16 = (f32[4]{0:T(128)S(1)}, f32[4]{0:T(128)}, u32[]{:S(2)}) copy-start(f32[4]{0:T(128)} %compare_convert_fusion) | copy-start | bytes 52
  380.8 16.7 %copy-start.1 = (f32[16,8,640]{2,1,0:T(8,128)S(1)}, f32[16,8,640]{2,1,0:T(8,128)}, u32[]{:S(2)}) copy-start(f32[16,8,640]{2,1,0:T(8,128)} %get-tuple-element.130) | copy-start | bytes 983044
  390.3 7.3 %copy-start.5 = (bf16[16,576]{1,0:T(8,128)(2,1)S(1)}, bf16[16,576]{1,0:T(8,128)(2,1)}, u32[]{:S(2)}) copy-start(bf16[16,576]{1,0:T(8,128)(2,1)} %param.31) | copy-start | bytes 55300
  395.4 3.2 copy-start.20
  395.4 3.2 copy-start.21
  (1 other events, 1.3 us)
Sparse Core Ops, SparseCore 0:
  58.2 88.0 all-gather.1
  251.8 109.2 reduce-scatter.1

commit v4 on v3

--- a/solution.py
+++ b/solution.py
@@ -15,7 +15,7 @@
 EDGE = 16
 CUT = 1e30
 MESH = pl.DeviceIdType.MESH
-VMEM_LIMIT = 60 * 2**20
+VMEM_LIMIT = 24 * 2**20
 
 
 def lasting(us):
@@ -102,6 +102,57 @@
     )(x)
 
 
+def sum_start(mates, x_ref, got, send, recv):
+    copies = []
+    for k, who in enumerate(mates):
+        copy = remote(x_ref.at[who], got.at[k], send.at[k], recv.at[k], {"wa": who})
+        copy.start()
+        copies.append(copy)
+    return copies
+
+
+def sum_spread(mine, mates, x_ref, got, o_ref, copies, send, recv):
+    for copy in copies:
+        copy.wait_recv()
+    parts = [x_ref.at[mine]] + [got.at[k] for k in range(len(mates))]
+    add_rows(o_ref.at[mine], parts, x_ref.shape[1])
+    spreads = []
+    for k, who in enumerate(mates):
+        copy = remote(o_ref.at[mine], o_ref.at[mine], send.at[k], recv.at[k], {"wa": who})
+        copy.start()
+        spreads.append(copy)
+    return spreads
+
+
+def sum_all_kernel(group, x_ref, o_ref, got, s1, r1, s2, r2):
+    greet("wa", group)
+    mine, mates = mates_of(group)
+    copies = sum_start(mates, x_ref, got, s1, r1)
+    spreads = sum_spread(mine, mates, x_ref, got, o_ref, copies, s2, r2)
+    for copy in spreads:
+        copy.wait()
+    for copy in copies:
+        copy.wait_send()
+
+
+def sum_all(x, cid, us):
+    group = lax.axis_size("wa")
+    vmem = pl.BlockSpec(memory_space=pltpu.VMEM)
+    dma = pltpu.SemaphoreType.DMA
+    return pl.pallas_call(
+        functools.partial(sum_all_kernel, group),
+        out_shape=jax.ShapeDtypeStruct(x.shape, x.dtype),
+        in_specs=[vmem],
+        out_specs=vmem,
+        scratch_shapes=[pltpu.VMEM((group - 1,) + x.shape[1:], x.dtype)] + [dma((group - 1,))] * 4,
+        compiler_params=pltpu.CompilerParams(
+            collective_id=cid, has_side_effects=True, vmem_limit_bytes=VMEM_LIMIT
+        ),
+        cost_estimate=lasting(us),
+        name="sum_all",
+    )(x)
+
+
 def gather_all(xs, axis, cid, us):
     count, arrays = lax.axis_size(axis), len(xs)
     return pl.pallas_call(
@@ -198,7 +249,7 @@
 
 def proj_back_kernel(
     ring, group, x_ref, g_ref, p_ref, x_o, g_o,
-    kept, paired, came, mate_s, mate_r, own_s, load, ctx_s, ctx_r,
+    kept, paired, came, got, s1, r1, s2, r2, load, ctx_s, ctx_r,
 ):
     _, chip, lane, _, peers = neighbours(ring)
     mine, mates = mates_of(group)
@@ -216,13 +267,7 @@
     for who in mates:
         hello(barrier, "wa", who)
     pl.semaphore_wait(barrier, half + group - 2)
-    copies = []
-    for k, who in enumerate(mates):
-        copy = remote(x_ref, x_o.at[mine], mate_s.at[k], mate_r.at[k], {"wa": who})
-        copy.start()
-        copies.append(copy)
-    local = pltpu.make_async_copy(x_ref, x_o.at[mine], own_s)
-    local.start()
+    copies = sum_start(mates, x_ref, got, s1, r1)
     for copy in loads:
         copy.wait()
     scattered = []
@@ -232,13 +277,14 @@
         copy = remote(kept.at[to], came.at[k], ctx_s.at[k], ctx_r.at[k], {"ctx": who})
         copy.start()
         scattered.append(copy)
+    spreads = sum_spread(mine, mates, x_ref, got, x_o, copies, s2, r2)
     add_rows(kept.at[chip], [kept.at[chip], paired.at[chip]], rows)
     for copy in scattered:
         copy.wait_recv()
     add_rows(g_o, [kept.at[chip]] + [came.at[k] for k in range(half - 1)], rows)
-    for copy in scattered:
+    for copy in scattered + copies:
         copy.wait_send()
-    for copy in copies + [local]:
+    for copy in spreads:
         copy.wait()
 
 
@@ -246,19 +292,21 @@
     ring, group = lax.axis_size("ctx"), lax.axis_size("wa")
     half = ring // 2
     hbm = pl.BlockSpec(memory_space=pl.ANY)
+    vmem = pl.BlockSpec(memory_space=pltpu.VMEM)
     dma = pltpu.SemaphoreType.DMA
     block = pltpu.VMEM((half,) + g.shape[2:], g.dtype)
     return pl.pallas_call(
         functools.partial(proj_back_kernel, ring, group),
         out_shape=[
-            jax.ShapeDtypeStruct((group,) + x.shape, x.dtype),
+            jax.ShapeDtypeStruct(x.shape, x.dtype),
             jax.ShapeDtypeStruct(g.shape[2:], g.dtype),
         ],
-        in_specs=[hbm] * 3,
-        out_specs=[hbm, pl.BlockSpec(memory_space=pltpu.VMEM)],
+        in_specs=[vmem, hbm, hbm],
+        out_specs=[vmem, vmem],
         scratch_shapes=[
             block, block, pltpu.VMEM((half - 1,) + g.shape[2:], g.dtype),
-            dma((group - 1,)), dma((group - 1,)), dma, dma((2,)),
+            pltpu.VMEM((group - 1,) + x.shape[1:], x.dtype),
+            dma((group - 1,)), dma((group - 1,)), dma((group - 1,)), dma((group - 1,)), dma((2,)),
             dma((half - 1,)), dma((half - 1,)),
         ],
         compiler_params=pltpu.CompilerParams(
@@ -325,8 +373,6 @@
             copy.start()
             copies.append(copy)
 
-    early = to_all(0)
-
     x_to = mine // 2
     z_to = group // 2 + mine // 2
     slot = lax.rem(mine, 2)
@@ -370,6 +416,7 @@
         copy = remote(paired.at[to], came.at[k], ctx_s.at[k], ctx_r.at[k], {"ctx": who})
         copy.start()
         scattered.append(copy)
+    early = to_all(0)
     add_rows(paired.at[chip], [g_ref.at[chip, lane], from_pair.at[chip]], rows)
     for copy in scattered:
         copy.wait_recv()
@@ -713,31 +760,31 @@
     return lax.broadcasted_iota(jnp.int32, (SEG, LANE), 0)
 
 
-def lag_masks(place, doc_ref, stream, length, taps):
+def lag_masks(place, doc_ref, documents, stream, length, taps):
     at = place * length + position_of((length, LANE), 0, length // SEG)
     masks = [None]
     for lag in range(1, taps):
         cut = None
-        for d in range(doc_ref.shape[1]):
-            begin = doc_ref[stream, d]
+        for d in range(documents):
+            begin = doc_ref[stream, 0, d]
             here = (begin > at - lag) & (begin <= at)
             cut = here if cut is None else cut | here
         masks.append(jnp.where(cut, 0.0, 1.0))
     hit = None
-    for d in range(doc_ref.shape[1]):
-        here = doc_ref[stream, d] == at
+    for d in range(documents):
+        here = doc_ref[stream, 0, d] == at
         hit = here if hit is None else hit | here
     return masks, jnp.where(hit, CUT, 0.0)
 
 
 def enter_kernel(
-    taps, place_ref, doc_ref, tok, edge, gain, wx, wz, conv, wproj,
+    taps, documents, place_ref, doc_ref, tok, edge, gain, wx, wz, conv, wproj,
     n1_o, ext_o, pre_o, uf_o, u_o, z_o, part_o, cut_o,
 ):
     length = tok.shape[1]
     steps = length // SEG
     place = place_ref[0]
-    gains = gain[...]
+    gains = gain[0:1]
 
     def normal(rows):
         return (rows * rms_scale(rows) * gains).astype(BF16)
@@ -746,7 +793,7 @@
     n1_o[0, length:] = normal(jnp.where(place > 0, edge[0].astype(F32), 0.0))
     inner = dot_nn(n1_o[0], wx[0]).astype(BF16).astype(F32)
     z_o[0] = dot_nn(n1_o[0, :length], wz[0]).astype(BF16)
-    masks, cut = lag_masks(place, doc_ref, pl.program_id(0), length, taps)
+    masks, cut = lag_masks(place, doc_ref, documents, pl.program_id(0), length, taps)
     cut_o[0] = cut
     seg = seg_of()
     behind = taps - 1
@@ -768,22 +815,18 @@
         u = (pre * jax.nn.sigmoid(pre)).astype(BF16)
         u_o[0, :, cols] = u
         uf_o[0, :, cols] = u.astype(F32)
-    part_o[0] = dot_nn(u_o[0], wproj[...]).astype(BF16)
+    part_o[0] = dot_nt(u_o[0], wproj[...]).astype(BF16)
 
 
 def summary_kernel(
-    states, b_at, terms, wdt, bias, uf, cut, a_ref,
-    proj_o, step_o, sig_o, hx_ref, sx_ref, hd_o, sd_ref, bb, st_s, dr_s, hd_s,
+    states, b_at, proj_i, wdt, bias, uf, cut, a_ref,
+    step_o, sig_o, hx_ref, sx_ref, hd_o, sd_ref, bb, st_s, dr_s, hd_s,
 ):
     length, width = step_o.shape[1:]
     groups, steps = width // LANE, length // SEG
-    total = terms[0, 0].astype(F32)
-    for w in range(1, terms.shape[0]):
-        total = total + terms[w, 0].astype(F32)
-    proj = total.astype(BF16)
-    proj_o[0] = proj
+    proj = proj_i[0]
     bb[...] = spread(proj, states, b_at)
-    pre = dot_nn(proj, wdt[...]) + bias[...]
+    pre = dot_nn(proj, wdt[...]) + bias[0:1]
     step_size = jnp.maximum(pre, 0.0) + jnp.log1p(jnp.exp(-jnp.abs(pre)))
     step_o[0] = step_size
     sig_o[0] = jax.nn.sigmoid(pre)
@@ -866,7 +909,7 @@
             jnp.exp(sx * a[n]) * wide(e_ref, n, lanes) + hx_ref[0, n, :, lanes]
             for n in range(states)
         )
-        gain = wide(skip, 0, lanes)
+        gain = wide(skip, 1, lanes)
 
         def step(j, h):
             rows = rows_of(j)
@@ -902,20 +945,21 @@
         mix = mix + terms[w].astype(F32)
     h1 = dot_nn(shift, tok[...]) + mix
     h1_o[...] = h1
-    n2 = (h1 * rms_scale(h1) * gain[...]).astype(BF16)
+    n2 = (h1 * rms_scale(h1) * gain[1:2]).astype(BF16)
     n2_o[...] = n2
     logits = dot_nt(n2, router[...])
     lane = lax.broadcasted_iota(jnp.int32, (length, LANE), 1)
+    kind = lax.broadcasted_iota(jnp.int32, (LANE, length), 0)
     named = route[...]
-    onehot = jnp.where(named == lane, 1.0, 0.0)
+    onehot = jnp.where(kind == named, 1.0, 0.0)
     one = lax.broadcasted_iota(jnp.int32, (length, length), 0)
     two = lax.broadcasted_iota(jnp.int32, (length, length), 1)
-    earlier = jnp.where(two < one, 1.0, 0.0).astype(BF16)
-    before = dot_nn(earlier, onehot.astype(BF16))
-    within = jnp.sum(before * onehot, axis=1, keepdims=True)
+    earlier = jnp.where(one < two, 1.0, 0.0).astype(BF16)
+    before = dot_nn(onehot.astype(BF16), earlier)
+    within = jnp.sum(before * onehot, axis=0, keepdims=True)
     slot = named.astype(F32) * (length // 2) + within
-    facts = jnp.where(lane == experts, slot, jnp.where(lane == experts + 1, keep[...].astype(F32), onehot))
-    facts = dot_nn(shift, facts.astype(BF16))
+    facts = jnp.where(kind == experts, slot, jnp.where(kind == experts + 1, keep[...].astype(F32), onehot))
+    facts = dot_nt(shift, facts.astype(BF16))
     onehot = jnp.where(lane < experts, facts, 0.0)
     slot = jnp.sum(jnp.where(lane == experts, facts, 0.0), axis=1, keepdims=True)
     kept = jnp.sum(jnp.where(lane == experts + 1, facts, 0.0), axis=1, keepdims=True)
@@ -930,47 +974,323 @@
     spot = lax.broadcasted_iota(jnp.int32, (length, slots), 1).astype(F32)
     match = jnp.where(slot == spot, 1.0, 0.0).astype(BF16)
     match_o[...] = match
-    out_o[:, :width] = dot_tn(match, n2).astype(BF16)
-    out_o[:, width:] = dot_tn(match, (gates * up).astype(BF16)).astype(BF16)
+    out_o[0] = dot_tn(match, n2).astype(BF16)
+    out_o[1] = dot_tn(match, (gates * up).astype(BF16)).astype(BF16)
     sums_o[...] = jnp.broadcast_to(jnp.sum(mix * mix, keepdims=True), (SEG, LANE))
 
 
-def pack_kernel(up, down, _, out):
-    width = up.shape[0]
-    units = up.shape[1]
+def pack_kernel(up, down, out):
+    width, units = up.shape
     line = lax.broadcasted_iota(jnp.int32, (units, units), 0)
     same = jnp.where(line == lax.broadcasted_iota(jnp.int32, (units, units), 1), 1.0, 0.0)
     out[:, :width] = dot_nt(same.astype(BF16), up[...]).astype(BF16)
     out[:, width:] = down[...]
 
 
-def experts_kernel(x_ref, w_ref, g_ref, o_ref, acc):
-    width = x_ref.shape[1] // 2
-    at = pl.program_id(0)
-
-    @pl.when(at == 0)
-    def _():
-        acc[...] = jnp.zeros_like(acc)
-
-    up, down = w_ref[:, :width], w_ref[:, width:]
-    rows, d_out = x_ref[:, :width], x_ref[:, width:]
-    hidden = dot_nt(up, rows)
-    d_act = dot_nt(down, d_out)
-    c = 0.7978845608
-    t = jnp.tanh(c * (hidden + 0.044715 * hidden * hidden * hidden))
-    act = (0.5 * hidden * (1.0 + t)).astype(BF16)
-    slope = 0.5 * (1.0 + t) + 0.5 * hidden * (1.0 - t * t) * c * (
-        1.0 + 3.0 * 0.044715 * hidden * hidden
-    )
-    d_pre = (d_act * slope).astype(BF16)
-    acc[:, :width] += dot_tn(act, down)
-    acc[:, width:] += dot_tn(d_pre, up)
-    g_ref[:, :width] = dot_nn(d_pre, rows).astype(BF16)
-    g_ref[:, width:] = dot_nn(act, d_out).astype(BF16)
-
-    @pl.when(at == pl.num_programs(0) - 1)
-    def _():
-        o_ref[...] = acc[...].astype(BF16)
+def prepare_kernel(
+    experts, small, own, wx_t, wdt, wout, conv_w, a_log,
+    gain_o, router_o, wx_o, wdt_o, wout_o, conv_o, rows_o, a_o, wide_s,
+):
+    width = wout.shape[1]
+    group = small.shape[0]
+    share = width // group
+    for w in range(group):
+        wide_s[:, w * share : (w + 1) * share] = small[w, :, :share].astype(F32)
+    gain_o[0:1] = wide_s[SEG - 2 : SEG - 1]
+    gain_o[1:2] = wide_s[SEG - 1 : SEG]
+    gain_o[2:] = jnp.zeros((SEG - 2, width), F32)
+    rows = wide_s[SEG:]
+    row = lax.broadcasted_iota(jnp.int32, rows.shape, 0)
+    router_o[...] = jnp.zeros_like(router_o)
+    router_o[: 2 * SEG] = jnp.concatenate(
+        [jnp.where(row < experts, rows, 0.0), jnp.zeros_like(rows)], axis=0
+    ).astype(BF16)
+    local = wout.shape[0]
+    for out, src in ((wx_o, wx_t), (wdt_o, wdt), (a_o, None)):
+        out[...] = jnp.zeros_like(out)
+        if src is not None:
+            out[: src.shape[0], :local] = src[...]
+    a_o[...] = jnp.full(a_o.shape, -1.0, F32)
+    a_o[:, :local] = -jnp.exp(a_log[...].astype(F32))
+    wout_o[...] = jnp.zeros_like(wout_o)
+    wout_o[:local] = wout[...]
+    conv_o[...] = jnp.zeros_like(conv_o)
+    taps = conv_w.shape[0]
+    conv_o[:taps, :local] = conv_w[...].astype(F32)
+    mine = own[...].astype(F32)
+    rows_o[...] = jnp.zeros_like(rows_o)
+    for h in range(2):
+        cols = slice(h * share, (h + 1) * share)
+        conv_o[taps : taps + 1, cols] = mine[h : h + 1, :share]
+        rows_o[0:1, cols] = mine[2 + h : 3 + h, :share]
+        rows_o[1:2, cols] = mine[4 + h : 5 + h, :share]
+
+
+def block_rows(value, c, rows):
+    low = c * rows
+    have = max(0, min(rows, value.shape[0] - low))
+    if have == rows:
+        return value[low : low + rows]
+    blank = jnp.zeros((rows - have, value.shape[1]), value.dtype)
+    return blank if have == 0 else jnp.concatenate([value[low : low + have], blank], axis=0)
+
+
+def pack_zo_kernel(ring, in_rows, local, n1, d_z, d_mix, gated, out):
+    width = n1.shape[1]
+    lanes = d_z.shape[1]
+    grad_z = dot_tn(n1[...], d_z[...])
+    grad_o = dot_tn(gated[...], d_mix[...])
+    side = jnp.zeros((grad_o.shape[0], lanes - width // 2), F32)
+    first = jnp.concatenate([grad_o[:, : width // 2], side], axis=1)
+    second = jnp.concatenate([grad_o[:, width // 2 :], side], axis=1)
+    rows = in_rows // 2
+    for c in range(ring):
+        out[c // 2, c % 2, :, :lanes] = block_rows(grad_z, c, in_rows).astype(BF16)
+        both = [block_rows(first[:local], c, rows), block_rows(second[:local], c, rows)]
+        out[c // 2, c % 2, :, lanes:] = jnp.concatenate(both, axis=0).astype(BF16)
+
+
+def pack_rest_kernel(
+    ring, in_rows, small_rows, group, experts, ranked, mine_ref, n1, d_x, gx, gdt, ga, a_ref, gconv, bias, skip,
+    gain_mix, gains, gain_moe, router, out_sums, mix_sum, out, small_s, wide_s,
+):
+    lanes = d_x.shape[1]
+    width = n1.shape[1]
+    share = width // group
+    grad_x = dot_tn(n1[...], d_x[...])
+    small_s[...] = jnp.zeros_like(small_s)
+    at = 0
+    grad_a = jnp.sum(ga[...], axis=1) * a_ref[...]
+    for part in (gx[...], gdt[:ranked], grad_a, gconv[...]):
+        small_s[at : at + part.shape[0]] = part
+        at += part.shape[0]
+    small_s[at : at + 1] = bias[...]
+    small_s[at + SEG : at + SEG + 1] = skip[...]
+    wide_s[...] = jnp.zeros_like(wide_s)
+    wide_s[0:1] = gain_mix[...] / gains[0:1]
+    wide_s[1:2] = gain_moe[...]
+    wide_s[2 : 2 + experts] = router[:experts]
+    lane = lax.broadcasted_iota(jnp.int32, (group, LANE), 1)
+    row = lax.broadcasted_iota(jnp.int32, (group, LANE), 0)
+    stats = jnp.where(
+        lane == 0, out_sums[0:1], jnp.where(lane == 1, mix_sum[0:1], jnp.where(lane == 2, out_sums[1:2], 0.0))
+    )
+    stats = jnp.where(row == mine_ref[0], stats, 0.0)
+    stats = jnp.concatenate([stats, jnp.zeros((group, lanes - LANE), F32)], axis=1)
+    bottom = jnp.zeros((16 - 2 * group, lanes), F32)
+    small_each = small_s.shape[0] // ring
+    for c in range(ring):
+        if c < 2 + experts:
+            full = [wide_s[c : c + 1, w * share : (w + 1) * share] for w in range(group)]
+            full = jnp.concatenate(full, axis=0)
+            full = jnp.concatenate([full, jnp.zeros((group, lanes - share), F32)], axis=1)
+        else:
+            full = jnp.zeros((group, lanes), F32)
+        small = small_s[c * small_each : (c + 1) * small_each]
+        blank = jnp.zeros((small_rows - small_each, lanes), F32)
+        parts = [block_rows(grad_x, c, in_rows), small]
+        if small_rows > small_each:
+            parts.append(blank)
+        rows = jnp.concatenate(parts + [full, stats, bottom], axis=0)
+        out[c // 2, c % 2] = rows.astype(BF16)
+
+
+def unpack_kernel(
+    ring, group, in_rows, small_rows, experts, states, ranked, taps, denom, mine_ref, done, up_down,
+    in_o, out_o, up_o, down_o, taps_o, wx_o, wdt_o, a_o, vec_o, stat_o, small_s, full_s,
+):
+    c = pl.program_id(0)
+    width = in_o.shape[1]
+    local = width // 2
+    small_each = small_s.shape[0] // ring
+    base = 2 * in_rows
+
+    @pl.when(c == 0)
+    def _():
+        line = lax.broadcasted_iota(jnp.int32, (width, width), 0)
+        same = jnp.where(line == lax.broadcasted_iota(jnp.int32, (width, width), 1), 1.0, 0.0)
+        up_o[...] = dot_nt(same.astype(BF16), up_down[:, :width])
+        down_o[...] = up_down[:, width:].astype(F32)
+        full_s[...] = jnp.zeros_like(full_s)
+
+    @pl.when(c * in_rows < width)
+    def _():
+        rows = done[0, :base, :].astype(F32)
+        in_o[...] = jnp.concatenate([rows[:in_rows, :local], rows[in_rows:, :local]], axis=1)
+        low = base + small_rows + 16
+        rows = done[0, low : low + in_rows, :].astype(F32)
+        half = in_rows // 2
+        out_o[...] = jnp.concatenate([rows[:half, :local], rows[half:, :local]], axis=1)
+
+    small = done[0, base : base + small_rows, :].astype(F32)
+    small_s[pl.ds(pl.multiple_of(c * small_each, SEG), small_each), :] = small[:small_each]
+    tile = done[0, base + small_rows : base + small_rows + 16, :].astype(F32)
+    row = lax.broadcasted_iota(jnp.int32, tile.shape, 0)
+    own = jnp.sum(jnp.where(row == mine_ref[0], tile, 0.0), axis=0, keepdims=True)
+    spot = lax.broadcasted_iota(jnp.int32, full_s.shape, 0)
+    full_s[...] += jnp.where(spot == c, own, 0.0)
+
+    @pl.when(c == 0)
+    def _():
+        sums = jnp.sum(jnp.where(row == group + mine_ref[0], tile, 0.0), axis=0, keepdims=True)
+        stat_o[...] = jnp.sqrt(sums[:, :LANE] / denom)
+
+    @pl.when(c == ring - 1)
+    def _():
+        at = 0
+        wx_o[...] = small_s[: wx_o.shape[0], :local]
+        at += up_to(wx_o.shape[0], LANE)
+        wdt_o[...] = small_s[at : at + ranked, :local]
+        at += ranked
+        a_o[...] = small_s[at : at + states, :local]
+        at += states
+        taps_o[...] = small_s[at : at + taps, :local]
+        vec_o[:SEG] = full_s[...]
+        vec_o[SEG : SEG + 1] = small_s[at + taps : at + taps + 1]
+        at += SEG
+        vec_o[SEG + 1 : SEG + 2] = small_s[at : at + 1]
+        vec_o[SEG + 2 : SEG + 3] = small_s[at + SEG : at + SEG + 1]
+
+
+def experts_kernel(
+    group, chunks, x_ref, w_ref, g_ref, r_ref,
+    got, w_s, g_s, act_s, slope_s, pre_s, acc, out_s,
+    w_sem, g_sem, s1, r1, own1, s2, r2, own2,
+):
+    mine, mates = mates_of(group)
+    count, width = x_ref.shape[2:]
+    slots = group * count
+    block = w_ref.shape[0] // chunks
+
+    def load(t):
+        at = pl.ds(pl.multiple_of(lax.rem(t, chunks) * block, block), block)
+        slot = lax.rem(t, 2)
+        return pltpu.make_async_copy(w_ref.at[at], w_s.at[slot], w_sem.at[slot])
+
+    load(0).start()
+    greet("wa", group)
+    sent = []
+    for h in range(2):
+        for k, who in enumerate(mates):
+            copy = remote(x_ref.at[h, who], got.at[h, mine], s1.at[h, k], r1.at[h, k], {"wa": who})
+            copy.start()
+            sent.append(copy)
+        pltpu.make_async_copy(x_ref.at[h, mine], got.at[h, mine], own1.at[h]).start()
+
+    def arrived(h):
+        pltpu.make_async_copy(x_ref.at[h, mine], got.at[h, mine], own1.at[h]).wait()
+        for copy in sent[h * len(mates) : (h + 1) * len(mates)]:
+            copy.wait_recv()
+        return got[h].reshape(slots, width)
+
+    def chunk(i):
+        return pl.ds(pl.multiple_of(i * block, block), block)
+
+    def returned(h):
+        out_s[h] = acc[...].astype(BF16).reshape(group, count, width)
+        for k, who in enumerate(mates):
+            copy = remote(out_s.at[h, who], r_ref.at[h, mine], s2.at[h, k], r2.at[h, k], {"wa": who})
+            copy.start()
+            sent.append(copy)
+        pltpu.make_async_copy(out_s.at[h, mine], r_ref.at[h, mine], own2.at[h]).start()
+
+    rows = arrived(0)
+    acc[...] = jnp.zeros_like(acc)
+
+    def forward(i, _):
+        load(i).wait()
+        load(i + 1).start()
+        w = w_s.at[lax.rem(i, 2)]
+        hidden = dot_nt(w[:, :width], rows)
+        c = 0.7978845608
+        t = jnp.tanh(c * (hidden + 0.044715 * hidden * hidden * hidden))
+        act = (0.5 * hidden * (1.0 + t)).astype(BF16)
+        act_s[chunk(i), :] = act
+        slope_s[chunk(i), :] = 0.5 * (1.0 + t) + 0.5 * hidden * (1.0 - t * t) * c * (
+            1.0 + 3.0 * 0.044715 * hidden * hidden
+        )
+        acc[...] += dot_tn(act, w[:, width:])
+        return 0
+
+    lax.fori_loop(0, chunks, forward, 0)
+    returned(0)
+    d_out = arrived(1)
+    acc[...] = jnp.zeros_like(acc)
+
+    def backward(i, _):
+        load(chunks + i).wait()
+
+        @pl.when(i < chunks - 1)
+        def _():
+            load(chunks + i + 1).start()
+
+        w = w_s.at[lax.rem(chunks + i, 2)]
+        d_pre = (dot_nt(w[:, width:], d_out) * slope_s[chunk(i), :]).astype(BF16)
+        pre_s[chunk(i), :] = d_pre
+        acc[...] += dot_tn(d_pre, w[:, :width])
+        return 0
+
+    lax.fori_loop(0, chunks, backward, 0)
+    returned(1)
+
+    def store(i):
+        slot = lax.rem(i, 2)
+        return pltpu.make_async_copy(g_s.at[slot], g_ref.at[chunk(i)], g_sem.at[slot])
+
+    def gradients(i, _):
+        @pl.when(i >= 2)
+        def _():
+            store(i - 2).wait()
+
+        g = g_s.at[lax.rem(i, 2)]
+        g[:, :width] = dot_nn(pre_s[chunk(i), :], got[0].reshape(slots, width)).astype(BF16)
+        g[:, width:] = dot_nn(act_s[chunk(i), :], got[1].reshape(slots, width)).astype(BF16)
+        store(i).start()
+        return 0
+
+    lax.fori_loop(0, chunks, gradients, 0)
+    store(chunks - 2).wait()
+    store(chunks - 1).wait()
+    for h in range(2):
+        pltpu.make_async_copy(out_s.at[h, mine], r_ref.at[h, mine], own2.at[h]).wait()
+    for copy in sent[: 2 * len(mates)]:
+        copy.wait_send()
+    for copy in sent[2 * len(mates) :]:
+        copy.wait()
+
+
+def experts_call(x, w, chunks, cid, us):
+    group = lax.axis_size("wa")
+    units, width = w.shape[0], x.shape[3]
+    slots = group * x.shape[2]
+    block = units // chunks
+    dma = pltpu.SemaphoreType.DMA
+    hbm = pl.BlockSpec(memory_space=pltpu.HBM)
+    vmem = pl.BlockSpec(memory_space=pltpu.VMEM)
+    two = dma((2, group - 1))
+    return pl.pallas_call(
+        functools.partial(experts_kernel, group, chunks),
+        out_shape=[jax.ShapeDtypeStruct(w.shape, BF16), jax.ShapeDtypeStruct(x.shape, BF16)],
+        in_specs=[vmem, hbm],
+        out_specs=[hbm, vmem],
+        scratch_shapes=[
+            pltpu.VMEM(x.shape, BF16),
+            pltpu.VMEM((2, block, 2 * width), BF16),
+            pltpu.VMEM((2, block, 2 * width), BF16),
+            pltpu.VMEM((units, slots), BF16),
+            pltpu.VMEM((units, slots), F32),
+            pltpu.VMEM((units, slots), BF16),
+            pltpu.VMEM((slots, width), F32),
+            pltpu.VMEM(x.shape, BF16),
+            dma((2,)), dma((2,)),
+            two, two, dma((2,)), two, two, dma((2,)),
+        ],
+        compiler_params=pltpu.CompilerParams(
+            collective_id=cid, has_side_effects=True, vmem_limit_bytes=VMEM_LIMIT + 20 * 2**20
+        ),
+        cost_estimate=lasting(us),
+        name="experts",
+    )(x, w)
 
 
 def store_in_order(out, rows, order_s):
@@ -996,15 +1316,15 @@
 
     gates, slope = column(experts), column(experts + 1)
     onehot = jnp.where(lane < experts, facts, 0.0)
-    rows = dot_nn(match[...], back[:, :width])
+    rows = dot_nn(match[...], back[0])
     moe = gates * rows
     result = h1 + moe
     store_in_order(out_o, result, order_s)
     d_gate = jnp.sum(rows * up, axis=1, keepdims=True)
     d_logits = (onehot * (d_gate * slope)).astype(BF16)
     router_o[...] = dot_tn(d_logits, n2[...])
-    d_n2 = dot_nn(match[...], back[:, width:]) + dot_nn(d_logits, router[...])
-    d_norm, terms = norm_grads(h1, rms_scale(h1), gain[...], d_n2)
+    d_n2 = dot_nn(match[...], back[1]) + dot_nn(d_logits, router[...])
+    d_norm, terms = norm_grads(h1, rms_scale(h1), gain[1:2], d_n2)
     gain_o[...] = jnp.sum(terms, axis=0, keepdims=True)
     d_h1 = up + d_norm
     dh_o[...] = d_h1
@@ -1124,7 +1444,7 @@
             jnp.exp(tx * a[n]) * wide(out_s, n, lanes) + fx_ref[0, n, :, lanes]
             for n in range(states)
         )
-        gain = wide(skip, 0, lanes)
+        gain = wide(skip, 1, lanes)
 
         def back(lap, f):
             j = steps - 1 - lap
@@ -1169,7 +1489,7 @@
 
 
 def conv_back_kernel(
-    taps, place_ref, doc_ref, terms, wproj, du, pre, ext, u, conv, dz, wx, wz, n1,
+    taps, documents, place_ref, doc_ref, proj_i, wproj, du, pre, ext, u, conv, dz, wx, wz, n1,
     dx_o, dn_o, gconv_o, gx_o, gain_o, dext,
 ):
     length, width = du.shape[1:]
@@ -1182,13 +1502,10 @@
         gx_o[...] = jnp.zeros_like(gx_o)
         gain_o[...] = jnp.zeros_like(gain_o)
 
-    total = terms[0, 0].astype(F32)
-    for w in range(1, terms.shape[0]):
-        total = total + terms[w, 0].astype(F32)
-    proj = total.astype(BF16)
+    proj = proj_i[0]
     gx_o[...] += dot_tn(proj, u[0])
-    d_u = dot_nt(proj, wproj[...]) + du[0]
-    masks, _ = lag_masks(place_ref[0], doc_ref, pl.program_id(0), length, taps)
+    d_u = dot_nn(proj, wproj[...]) + du[0]
+    masks, _ = lag_masks(place_ref[0], doc_ref, documents, pl.program_id(0), length, taps)
     seg = seg_of()
     row = lax.broadcasted_iota(jnp.int32, (EDGE, LANE), 0)
     for g in range(width // LANE):
@@ -1233,7 +1550,7 @@
         came = jnp.broadcast_to(edge[row : row + 1], seg.shape)
         dn_s[j, :] += jnp.where(seg == SEG - 1, came, 0.0)
     x = dot_nn(permutation(length), tok[...])
-    d_x, _ = norm_grads(x, rms_scale(x), gain[...], dn_s[...])
+    d_x, _ = norm_grads(x, rms_scale(x), gain[0:1], dn_s[...])
     result = dh[...] + d_x
     store_in_order(out_o, result, order_s)
 
@@ -1318,54 +1635,53 @@
     share = norm_mix.shape[0]
     order_vmem = pltpu.VMEM((width // LANE, length, LANE), F32)
     place_s = place.astype(jnp.int32).reshape(1)
+    mine_s = mine.astype(jnp.int32).reshape(1)
     last_s = (place == ring - 1).astype(jnp.int32).reshape(1)
     f32_vmem = lambda *shape: pltpu.VMEM(shape, F32)
 
-    in_each = -(-width // ring)
-    in_rows = up_to(in_each, 16)
-    part_in = lax.dynamic_slice_in_dim(w_in, place * in_each, in_each, 0)
+    (own_experts,) = call(
+        pack_kernel, "pack", 1, [(w_up[0], None), (w_down[0], None)],
+        [((w_down.shape[1], 2 * width), BF16, None)], [], 3,
+    )
+    expert_w = lax.all_gather(own_experts, "ctx", axis=0, tiled=True)
+
+    in_rows = up_to(-(-width // ring), 16)
+    blank = ring * in_rows - width
+    part_in = jnp.pad(w_in, ((0, blank), (0, 0))) if blank else w_in
+    part_in = lax.dynamic_slice_in_dim(part_in, place * in_rows, in_rows, 0)
     halves = jnp.stack([part_in[:, :local], part_in[:, local:]], axis=0)
-    halves = jnp.pad(halves, ((0, 0), (0, in_rows - in_each), (0, padded - local)))
-    small = jnp.concatenate([norm_mix, norm_moe, w_router.T.reshape(-1)], axis=0)
-    small_count = up_to(-(-small.shape[0] // LANE), 16)
-    small = jnp.pad(small, (0, small_count * LANE - small.shape[0])).reshape(small_count, LANE)
+    halves = jnp.pad(halves, ((0, 0), (0, 0), (0, padded - local)))
+    small = jnp.concatenate([conv_b, dt_bias, d_skip, norm_mix, norm_moe], axis=0).reshape(SEG, share)
+    small = jnp.concatenate([small, jnp.pad(w_router.T, ((0, SEG - experts), (0, 0)))], axis=0)
+    small = padded_to(small, up_to(share, LANE), 1)
     documents = doc_starts.shape[1]
     doc_tile = jnp.pad(doc_starts, ((0, SEG - 1), (0, LANE - documents)))
     all_rows, all_edges, smalls, docs, w_blocks = start(tokens[0], small, doc_tile, halves, 1)
-    proj_in = w_blocks[:, :, :in_each].reshape(2, width, padded)
+    proj_in = w_blocks.reshape(2, ring * in_rows, padded)[:, :width]
     of_x = lambda shape: pl.BlockSpec((1,) + shape[1:], lambda i: (0, 0, 0))
     of_z = lambda shape: pl.BlockSpec((1,) + shape[1:], lambda i: (1, 0, 0))
-    (own_experts,) = call(
-        pack_kernel, "pack", 1, [(w_up[0], None), (w_down[0], None), (docs, ANY)],
-        [((w_down.shape[1], 2 * width), BF16, None)], [], 3,
-    )
-    expert_w = lax.all_gather(own_experts, "ctx", axis=0, tiled=True)
-    smalls = smalls.reshape(group, -1)[:, : (2 + experts) * share]
-    smalls = smalls.reshape(group, 2 + experts, share).swapaxes(0, 1).reshape(2 + experts, width)
-    gain_mix, gain_moe = smalls[0:1].astype(F32), smalls[1:2].astype(F32)
-    router = padded_to(smalls[2:], LANE, 0)
-    docs = docs[:, 0, :documents]
-
-    conv = jnp.concatenate([conv_w, conv_b[None]], axis=0).astype(F32)
-    conv = jnp.pad(conv, ((0, SEG - taps - 1), (0, padded - local)))
-    wproj = jnp.pad(w_x, ((0, padded - local), (0, columns - w_x.shape[1])))
-    wdt = jnp.pad(w_dt, ((0, columns - ranked), (0, padded - local)))
-    step_bias = padded_to(dt_bias[None], padded, 1).astype(F32)
-    a_mat = -jnp.exp(padded_to(a_log, padded, 1).astype(F32))
-    skip = padded_to(d_skip[None], padded, 1).astype(F32)
-    wout = padded_to(w_out, padded, 0)
+    par = (SEG, padded)
+    gains, router, wproj, wdt, wout, conv, vectors, a_mat = call(
+        functools.partial(prepare_kernel, experts), "prepare", 1,
+        [(smalls, None), (small, None), (w_x.T, None), (w_dt, None), (w_out, None), (conv_w, None),
+         (a_log, None)],
+        [((SEG, width), F32, None), ((LANE, width), BF16, None), ((columns, padded), BF16, None),
+         ((columns, padded), BF16, None), ((padded, width), BF16, None), (par, F32, None),
+         (par, F32, None), ((states, padded), F32, None)],
+        [f32_vmem(2 * SEG, width)], 3,
+    )
 
     vec = (group, length, padded)
     n1, ext, pre_conv, u_f, u, z, part, cut = call(
-        functools.partial(enter_kernel, taps), "enter", group,
-        [(place_s, SMEM), (docs, SMEM), (all_rows, 0), (all_edges, 0), (gain_mix, None),
+        functools.partial(enter_kernel, taps, documents), "enter", group,
+        [(place_s, SMEM), (docs, SMEM), (all_rows, 0), (all_edges, 0), (gains, None),
          (proj_in, of_x), (proj_in, of_z), (conv, None), (wproj, None)],
         [((group, rows, width), BF16, 0), ((group, (taps - 1) * SEG + length, padded), F32, 0),
          (vec, F32, 0), (vec, F32, 0), (vec, BF16, 0), (vec, BF16, 0),
          ((group, length, columns), BF16, 0), ((group, length, LANE), F32, 0)],
         [], 8,
     )
-    (parts,) = gather_all([part], "wa", 2, 15)
+    projected = sum_all(part, 2, 11)
     seg_states = (group, states, SEG, padded)
     seg_sums = (group, SEG, padded)
     dev_states = (group, states, padded)
@@ -1373,18 +1689,18 @@
     spread_vmem = f32_vmem(length, states * LANE)
     lane_vmem = f32_vmem(length, padded)
     state_vmem = f32_vmem(states, padded)
-    proj, step_size, sig, h_in, s_in, h_dev, s_dev = call(
+    step_size, sig, h_in, s_in, h_dev, s_dev = call(
         functools.partial(summary_kernel, states, ranked), "scan_summary", group,
-        [(parts, 1), (wdt, None), (step_bias, None), (u_f, 0), (cut, 0), (a_mat, None)],
-        [((group, length, columns), BF16, 0), (vec, F32, 0), (vec, F32, 0), (seg_states, F32, 0),
+        [(projected, 0), (wdt, None), (vectors, None), (u_f, 0), (cut, 0), (a_mat, None)],
+        [(vec, F32, 0), (vec, F32, 0), (seg_states, F32, 0),
          (seg_sums, F32, 0), (dev_states, BF16, 0), (dev_sums, F32, 0)],
         [spread_vmem, lane_vmem, lane_vmem, state_vmem], 10,
     )
     all_h, all_s = gather_all([h_dev, s_dev], "ctx", 3, 15)
     y_full, gated, mix_part, e_in = call(
         functools.partial(output_kernel, states, ranked), "scan_output", group,
-        [(place_s, SMEM), (proj, 0), (step_size, 0), (u_f, 0), (cut, 0), (a_mat, None), (h_in, 0),
-         (s_in, 0), (all_h, 1), (all_s, 1), (z, 0), (skip, None), (wout, None)],
+        [(place_s, SMEM), (projected, 0), (step_size, 0), (u_f, 0), (cut, 0), (a_mat, None), (h_in, 0),
+         (s_in, 0), (all_h, 1), (all_s, 1), (z, 0), (vectors, None), (wout, None)],
         [(vec, F32, 0), (vec, BF16, 0), ((group, length, width), BF16, 0), (dev_states, F32, 0)],
         [spread_vmem, spread_vmem, lane_vmem, lane_vmem], 13,
     )
@@ -1393,28 +1709,20 @@
     row_f = (length, width)
     h1, n2, upstream, facts, match, outgoing, mix_sum = call(
         functools.partial(route_kernel, experts), "route", 1,
-        [(mix_terms, None), (tokens[0], None), (gain_moe, None), (router, None),
-         (routes[0], None), (keep_mask[0][:, None], None), (out_grad[0], None)],
+        [(mix_terms, None), (tokens[0], None), (gains, None), (router, None),
+         (routes[0].T, None), (keep_mask, None), (out_grad[0], None)],
         [(row_f, F32, None), (row_f, BF16, None), (row_f, F32, None), ((length, LANE), F32, None),
-         ((length, slots), BF16, None), ((slots, 2 * width), BF16, None), ((SEG, LANE), F32, None)],
+         ((length, slots), BF16, None), ((2, slots, width), BF16, None), ((SEG, LANE), F32, None)],
         [], 5,
     )
-    arrived = trade(outgoing.reshape(group, slots // group, 2 * width), "wa", 5, 29)
-    hidden_units = expert_w.shape[0]
-    block = hidden_units // 8
-    of_block = lambda shape: pl.BlockSpec((block, shape[1]), lambda i: (i, 0))
-    grad_experts, returning = call(
-        experts_kernel, "experts", 8,
-        [(arrived.reshape(slots, 2 * width), None), (expert_w, of_block)],
-        [((hidden_units, 2 * width), BF16, of_block), ((slots, 2 * width), BF16, None)],
-        [f32_vmem(slots, 2 * width)], 18,
+    grad_experts, returned = experts_call(
+        outgoing.reshape(2, group, slots // group, width), expert_w, 8, 5, 58
     )
     share_experts = lax.psum_scatter(grad_experts, "ctx", scatter_dimension=0, tiled=True)
-    returned = trade(returning.reshape(group, slots // group, 2 * width), "wa", 6, 29)
     result, d_h1, d_mix_own, grad_router, grad_gain_moe, out_sums = call(
         functools.partial(combine_kernel, experts), "combine", 1,
-        [(returned.reshape(slots, 2 * width), None), (match, None), (h1, None), (n2, None),
-         (upstream, None), (facts, None), (gain_moe, None), (router, None)],
+        [(returned.reshape(2, slots, width), None), (match, None), (h1, None), (n2, None),
+         (upstream, None), (facts, None), (gains, None), (router, None)],
         [(row_f, F32, None), (row_f, F32, None), (row_f, BF16, None), ((LANE, width), F32, None),
          ((1, width), F32, None), ((SEG, LANE), F32, None)],
         [order_vmem], 6,
@@ -1423,115 +1731,97 @@
 
     d_y, d_z, grad_skip, f_in, t_in, f_dev = call(
         functools.partial(gate_back_kernel, states, ranked + states), "gate_back", group,
-        [(d_mix, 0), (wout, None), (y_full, 0), (z, 0), (u_f, 0), (proj, 0), (step_size, 0),
+        [(d_mix, 0), (wout, None), (y_full, 0), (z, 0), (u_f, 0), (projected, 0), (step_size, 0),
          (cut, 0), (a_mat, None)],
         [(vec, F32, 0), ((group, rows, padded), BF16, 0), ((1, padded), F32, None),
          (seg_states, F32, 0), (seg_sums, F32, 0), (dev_states, BF16, 0)],
         [spread_vmem, lane_vmem, state_vmem], 11,
     )
-    grad_in_z = dot_tn(n1.reshape(group * rows, width), d_z.reshape(group * rows, padded))
-    grad_out = dot_tn(
-        d_mix.reshape(group * length, width), gated.reshape(group * length, padded)
-    )
-    grad_zo = jnp.concatenate([grad_in_z, grad_out], axis=1).astype(BF16)
-    grad_zo = jnp.pad(
-        grad_zo.reshape(ring // 2, 2, in_each, 2 * padded),
-        ((0, 0), (0, 0), (0, in_rows - in_each), (0, 0)),
+    flat_n1 = n1.reshape(group * rows, width)
+    zo_shape = (ring // 2, 2, in_rows, 2 * padded)
+    (grad_zo,) = call(
+        functools.partial(pack_zo_kernel, ring, in_rows, local), "pack_zo", 1,
+        [(flat_n1, None), (d_z.reshape(group * rows, padded), None),
+         (d_mix.reshape(group * length, width), None), (gated.reshape(group * length, padded), None)],
+        [(zo_shape, BF16, None)], [], 5,
     )
     all_f, pair_zo = carry_back(f_dev, grad_zo, 8, 14)
     d_part, d_u, grad_dt, grad_step_bias, grad_a = call(
         functools.partial(scan_back_kernel, states, ranked), "scan_back", group,
-        [(place_s, SMEM), (proj, 0), (step_size, 0), (sig, 0), (u_f, 0), (cut, 0), (d_y, 0),
-         (a_mat, None), (skip, None), (wdt, None), (h_in, 0), (s_in, 0), (e_in, 0), (f_in, 0),
+        [(place_s, SMEM), (projected, 0), (step_size, 0), (sig, 0), (u_f, 0), (cut, 0), (d_y, 0),
+         (a_mat, None), (vectors, None), (wdt, None), (h_in, 0), (s_in, 0), (e_in, 0), (f_in, 0),
          (t_in, 0), (all_f, 1), (all_s, 1)],
         [((group, length, columns), BF16, 0), (vec, F32, 0), ((columns, padded), F32, None),
          ((1, padded), F32, None), ((states, SEG, padded), F32, None)],
         [spread_vmem, spread_vmem, spread_vmem, f32_vmem(length + SEG, states * LANE), spread_vmem,
          spread_vmem, lane_vmem, lane_vmem, lane_vmem, state_vmem], 34,
     )
-    d_parts, chunk_zo = proj_back(d_part, grad_zo, pair_zo, 9, 20)
+    d_projected, chunk_zo = proj_back(d_part, grad_zo, pair_zo, 9, 20)
     d_x, d_n1_part, grad_conv, grad_x, gain_terms = call(
-        functools.partial(conv_back_kernel, taps), "conv_back", group,
-        [(place_s, SMEM), (docs, SMEM), (d_parts, 1), (wproj, None), (d_u, 0), (pre_conv, 0),
+        functools.partial(conv_back_kernel, taps, documents), "conv_back", group,
+        [(place_s, SMEM), (docs, SMEM), (d_projected, 0), (wproj, None), (d_u, 0), (pre_conv, 0),
          (ext, 0), (u, 0), (conv, None), (d_z, 0), (proj_in, of_x), (proj_in, of_z), (n1, 0)],
         [((group, rows, padded), BF16, 0), ((group, rows, width), BF16, 0),
          ((SEG, padded), F32, None), ((columns, padded), F32, None), ((1, width), F32, None)],
         [f32_vmem((taps - 1) * SEG + length, LANE)], 10,
     )
-    grad_gain_mix = gain_terms / gain_mix
-    grad_in_x = dot_tn(n1.reshape(group * rows, width), d_x.reshape(group * rows, padded))
-    grad_a_log = jnp.sum(grad_a, axis=1) * a_mat
-
-    def dealt(rows, count):
-        each = -(-rows.shape[0] // ring)
-        rows = jnp.pad(rows, ((0, each * ring - rows.shape[0]), (0, 0)))
-        return jnp.pad(rows.reshape(ring, each, -1), ((0, 0), (0, count - each), (0, 0)))
-
-    small = jnp.concatenate(
-        [grad_conv[: taps + 1], grad_step_bias, grad_skip, grad_a_log, grad_dt[:ranked],
-         grad_x[: w_x.shape[1]]],
-        axis=0,
-    ).astype(BF16)
-    small_each = -(-small.shape[0] // ring)
+    small_all = columns + up_to(ranked, SEG) + states + 3 * SEG
+    small_each = up_to(-(-small_all // ring), SEG)
     small_rows = up_to(small_each, 16)
-    fulls = jnp.concatenate([grad_gain_mix, grad_gain_moe, grad_router[:experts]], axis=0)
-    fulls = fulls.reshape(2 + experts, group, share).swapaxes(0, 1).reshape(group, -1)
-    full_each = -(-fulls.shape[1] // ring)
-    fulls = jnp.pad(fulls, ((0, 0), (0, full_each * ring - fulls.shape[1])))
-    fulls = fulls.reshape(group, ring, full_each).swapaxes(0, 1)
-    fulls = jnp.pad(fulls, ((0, 0), (0, 0), (0, padded - full_each)))
-    stat_row = jnp.stack([out_sums[0, 0], mix_sum[0, 0], out_sums[1, 0]])
-    is_mine = (lax.iota(jnp.int32, group) == mine).astype(F32)
-    stat_rows = padded_to(is_mine[:, None] * stat_row[None, :], padded, 1)
-    stat_rows = jnp.broadcast_to(stat_rows[None], (ring, group, padded))
-    tile = jnp.concatenate([fulls, stat_rows], axis=1)
-    tile = jnp.pad(tile, ((0, 0), (0, 16 - tile.shape[1]), (0, 0))).astype(BF16)
-    packed = jnp.concatenate(
-        [dealt(grad_in_x.astype(BF16), in_rows), dealt(small, small_rows), tile], axis=1
-    )
-    packed = packed.reshape((ring // 2, 2) + packed.shape[1:])
+    (packed,) = call(
+        functools.partial(pack_rest_kernel, ring, in_rows, small_rows, group, experts, ranked),
+        "pack_rest", 1,
+        [(mine_s, SMEM), (flat_n1, None), (d_x.reshape(group * rows, padded), None), (grad_x, None),
+         (grad_dt, None), (grad_a, None), (a_mat, None), (grad_conv, None), (grad_step_bias, None),
+         (grad_skip, None), (gain_terms, None), (gains, None), (grad_gain_moe, None),
+         (grad_router, None), (out_sums, None), (mix_sum, None)],
+        [((ring // 2, 2, in_rows + small_rows + 16, padded), BF16, None)],
+        [f32_vmem(ring * small_each, padded), f32_vmem(SEG, width)], 5,
+    )
     done, d_n1_terms, d_edges = finish(packed, chunk_zo, d_n1_part, in_rows, small_rows, 11)
-    share_in = jnp.concatenate(
-        [done[:, :in_each, :local], done[:, in_rows : in_rows + in_each, :local]], axis=2
-    ).reshape(width, 2 * local).astype(F32)
-    base = 2 * in_rows + small_rows + 16
-    share_out = done[:, base : base + in_each, :local].reshape(width, local).T.astype(F32)
-    base = 2 * in_rows
-    smalls_sum = done[:, base : base + small_each, :local].reshape(ring * small_each, local)
-    smalls_sum = smalls_sum.astype(F32)
-    base = base + small_rows
-    full_sum = lax.dynamic_index_in_dim(done, base + mine, 1, False)[:, :full_each]
-    full_sum = full_sum.reshape(-1)[: (2 + experts) * share].reshape(2 + experts, share).astype(F32)
-    stat_sums = lax.dynamic_index_in_dim(done, base + group + mine, 1, False)[0, :3].astype(F32)
+    blocks = width // in_rows
+    of_rows = lambda shape: pl.BlockSpec(
+        (shape[0] // blocks, shape[1]), lambda i: (jnp.minimum(i, blocks - 1), 0)
+    )
+    unpacked = call(
+        functools.partial(
+            unpack_kernel, ring, group, in_rows, small_rows, experts, states, ranked, taps,
+            float(length * ring * width),
+        ),
+        "unpack", ring,
+        [(mine_s, SMEM), (done, 0), (share_experts, None)],
+        [((width, 2 * local), F32, of_rows), ((local, width), F32, of_rows),
+         ((width, w_down.shape[1]), F32, None), ((w_down.shape[1], width), F32, None),
+         ((taps, local), F32, None), ((w_x.shape[1], local), F32, None), ((ranked, local), F32, None),
+         ((states, local), F32, None), ((2 * SEG, padded), F32, None), ((1, LANE), F32, None)],
+        [f32_vmem(ring * small_each, padded), f32_vmem(SEG, padded)], 8,
+    )
+    share_in, share_out, share_up, share_down, g_taps, g_wx, g_wdt, g_a, vecs, stats = unpacked
+    fulls, vecs = vecs[:SEG, :share], vecs[SEG:, :local]
     (input_grad,) = call(
         functools.partial(leave_kernel, taps), "leave", 1,
-        [(last_s, SMEM), (d_n1_terms, None), (d_edges, None), (tokens[0], None), (gain_mix, None),
+        [(last_s, SMEM), (d_n1_terms, None), (d_edges, None), (tokens[0], None), (gains, None),
          (d_h1, None)],
         [(row_f, F32, None)], [f32_vmem(length, width), order_vmem], 4,
     )
-    marks_at = [0, taps, taps + 1, taps + 2, taps + 3, taps + 3 + states]
-    marks_at += [marks_at[-1] + ranked, marks_at[-1] + ranked + w_x.shape[1]]
-    cut_at = [smalls_sum[a:b] for a, b in zip(marks_at[:-1], marks_at[1:])]
-    denom = length * ring * width
-    rms_stats = jnp.sqrt(stat_sums / denom)[None]
     return (
         result[None],
         input_grad[None],
-        full_sum[0],
+        fulls[0],
         share_in,
-        cut_at[0],
-        cut_at[1][0],
-        cut_at[6].T,
-        cut_at[5],
-        cut_at[2][0],
-        cut_at[4],
-        cut_at[3][0],
+        g_taps,
+        vecs[0],
+        g_wx.T,
+        g_wdt,
+        vecs[1],
+        g_a,
+        vecs[2],
         share_out,
-        full_sum[1],
-        full_sum[2:].T,
-        share_experts[:, :width].T.astype(F32)[None],
-        share_experts[:, width:].astype(F32)[None],
-        rms_stats,
+        fulls[1],
+        fulls[2 : 2 + experts].T,
+        share_up[None],
+        share_down[None],
+        stats[:, :3],
     )
 
 

time: 509 us -> 436 us (0.86)
  Pallas kernels: 432 us -> 394 us
  other arithmetic: 21 us -> 0.06 us
  local copies, waits for them, and re-layouts: 35.1 us -> 26.4 us
    pallas_call x0 -> x2, Pallas kernels: none -> 67.5 us  [the longest x1 56.7 us: experts_call(): pl.pallas_call(functools.partial(experts_kernel, group, chunks), out_shap...]
    pallas_call x3 -> x1, Pallas kernels: 84.4 us -> 28 us  [trade(): pl.pallas_call(functools.partial(trade_kernel, axis, count), out_shape=ja...]
    pallas_call x11 -> x14, Pallas kernels: 133 us -> 99.7 us  [call(): pl.pallas_call(kernel, grid=(grid,), out_shape=[jax.ShapeDtypeStruct(shap...]
    unnamed x52 -> x154, local copies, waits for them, and re-layouts: 2.39 us -> 23.3 us
    slice x17 -> x2, local copies, waits for them, and re-layouts: 15 us -> 1.22 us  [the longest x1 0.62 us: body(): vecs[2]]
    pallas_call x3 -> x2, Pallas kernels: 62.5 us -> 51.6 us  [gather_all(): pl.pallas_call(functools.partial(gather_kernel, axis, count, arrays), out...]
    pallas_call x1, Pallas kernels: 70.2 us -> 61.7 us  [finish(): pl.pallas_call(functools.partial(finish_kernel, ring, group, in_rows, sma...]
    convert_element_type x8 -> x0, other arithmetic: 5.98 us -> none  [the longest x1 2.92 us: body(): share_in = jnp.concatenate([done[:, :in_each, :local], done[:, in_rows:in...]
  transfers between devices with their start and end apart: 2 -> 2, of which waited for: 0 -> 0; matrix products, arithmetic and copies ran while one was open for 10% -> 0% of each run, Pallas kernels for 67% -> 75%
where the time goes in v4:
time: 436 us
  Pallas kernels  394 us (90%)
  local copies, waits for them, and re-layouts  26.4 us (6%)
  between operations  15.1 us (3%)
    pallas_call x14, Pallas kernels, call(): pl.pallas_call(kernel, grid=(grid,), out_shape=[jax.ShapeDtypeStruct(shap...  99.7 us
    pallas_call x1, Pallas kernels, finish(): pl.pallas_call(functools.partial(finish_kernel, ring, group, in_rows, sma...  61.7 us
    pallas_call x1, Pallas kernels, experts_call(): pl.pallas_call(functools.partial(experts_kernel, group, chunks), out_shap...  56.7 us
    pallas_call x2, Pallas kernels, gather_all(): pl.pallas_call(functools.partial(gather_kernel, axis, count, arrays), out...  51.6 us
    pallas_call x1, Pallas kernels, start(): pl.pallas_call(functools.partial(start_kernel, ring, group), out_shape=[j...  46.5 us
    pallas_call x1, Pallas kernels, trade(): pl.pallas_call(functools.partial(trade_kernel, axis, count), out_shape=ja...  28 us
    unnamed x154, local copies, waits for them, and re-layouts  23.3 us
    pallas_call x1, Pallas kernels, proj_back(): pl.pallas_call(functools.partial(proj_back_kernel, ring, group), out_shap...  20.5 us
  transfers between devices with their start and end apart: 2, of which 0 were waited for; matrix products, arithmetic and copies ran while one was open for 0% of the time, Pallas kernels for 75%

profile of v4, /device:TPU:11, one launch (start us, length us, event | category | flops | bytes accessed | tf_op | source)
XLA Modules:
  0.0 435.6 jit_solution(3893723614917946684)
XLA Ops:
  9.6 1.9 pack.1
  13.7 46.5 %start.1 = (bf16[4,128,1152]{2,1,0:T(8,128)(2,1)S(1)}, bf16[4,16,1152]{2,1,0:T(8,128)(2,1)S(1)}, bf16[4,16,384]{2,1,0:T(8,128)(2,1)S(1)}, s32[4,8,128]{2,1,0:T(8,128)S(1)}, bf16[2,8,144,640]{3,2,1,0:T(8,128)(2,1)S(1)}) custom-call(bf16[128,1152]{1,0:T(8,128)(2,1)S(1)} %bitcast.33, bf16[16,384]{1,0:T(8,128)(2,1)S(1)} %pad.17.par.own, s32[8,128]{1,0:T(8,128)S(1)} %pad.18.doc, ...), custom_call_target="tpu_custom_call" | custom-call | flops 38499999744 | bytes 122500000 | tf_op jit(solution)/shard_map/start/pallas_call | solution.py:660
  61.8 6.4 %enter.1 = (bf16[4,144,1152]{2,1,0:T(8,128)(2,1)S(1)}, f32[4,152,640]{2,1,0:T(8,128)S(1)}, f32[4,128,640]{2,1,0:T(8,128)S(1)}, f32[4,128,640]{2,1,0:T(8,128)S(1)...) custom-call(s32[1]{0:T(128)} %bitcast.place_ref, ...), custom_call_target="tpu_custom_call" | custom-call | flops 8800000000 | bytes 28000000 | tf_op jit(solution)/shard_map/enter/pallas_call | solution.py:1594
  68.3 10.8 %sum_all.1.proj_i.proj = bf16[4,128,128]{2,1,0:T(8,128)(2,1)S(1)} custom-call(bf16[4,128,128]{2,1,0:T(8,128)(2,1)S(1)} %get-tuple-element.106.x_ref), custom_call_target="tpu_custom_call" | custom-call | flops 12099999744 | bytes 38500000 | tf_op jit(solution)/shard_map/sum_all/pallas_call | solution.py:142
  79.1 9.1 %scan_summary.1 = (f32[4,128,640]{2,1,0:T(8,128)S(1)}, f32[4,128,640]{2,1,0:T(8,128)S(1)}, f32[4,16,8,640]{3,2,1,0:T(8,128)S(1)}, f32[4,8,640]{2,1,0:T(8,128)S(1...) custom-call(bf16[4,128,128]{2,1,0:T(8,128)(2,1)S(1)} %sum_all.1.proj_i.proj, ...), custom_call_target="tpu_custom_call" | custom-call | flops 11000000512 | bytes 35000000 | tf_op jit(solution)/shard_map/scan_summary/pallas_call | solution.py:1594
  88.3 21.8 %gather_3.1 = (bf16[8,4,16,640]{3,2,1,0:T(8,128)(2,1)S(1)}, f32[8,4,1,640]{3,2,1,0:T(1,128)S(1)}) custom-call(bf16[4,16,640]{2,1,0:T(8,128)(2,1)S(1)} %get-tuple-element.115.refs_0_, f32[4,1,640]{2,1,0:T(1,128)S(1)} %get-tuple-element.116.refs_1_), custom_call_target="tpu_custom_call" | custom-call | flops 16499999744 | bytes 52500000 | tf_op jit(solution)/shard_map/gather_3/pallas_call | solution.py:158
  110.2 13.4 %scan_output.1 = (f32[4,128,640]{2,1,0:T(8,128)S(1)}, bf16[4,128,640]{2,1,0:T(8,128)(2,1)S(1)}, bf16[4,128,1152]{2,1,0:T(8,128)(2,1)S(1)}, f32[4,16,640]{2,1,0:T(8,128)S(1)}) custom-call(s32[1]{0:T(128)} %bitcast.place_ref, bf16[4,128,128]{2,1,0:T(8,128)(2,1)S(1)} %sum_all.1.proj_i.proj, f32[4,128,640]{2,1,0:T(8,128)S(1)} %get-tuple-element.112.step_i, ...), custom_call_target="tpu_custom_call" | custom-call | flops 14300000256 | bytes 45500000 | tf_op jit(solution)/shard_map/scan_output/pallas_call | solution.py:1594
  124.7 28.0 %trade_4.1.terms = bf16[4,128,1152]{2,1,0:T(8,128)(2,1)S(1)} custom-call(bf16[4,128,1152]{2,1,0:T(8,128)(2,1)S(1)} %get-tuple-element.121.x_ref), custom_call_target="tpu_custom_call" | custom-call | flops 27499999232 | bytes 87500000 | tf_op jit(solution)/shard_map/trade_4/pallas_call | solution.py:87
  160.0 56.7 %experts.1 = (bf16[3072,2304]{1,0:T(8,128)(2,1)}, bf16[2,4,64,1152]{3,2,1,0:T(8,128)(2,1)S(1)}) custom-call(bf16[2,4,64,1152]{3,2,1,0:T(8,128)(2,1)S(1)} %bitcast.45, bf16[3072,2304]{1,0:T(8,128)(2,1)} %all-gather.2.cloned.1.call-done.w_ref), custom_call_target="tpu_custom_call" | custom-call | flops 63800000512 | bytes 203000000 | tf_op jit(solution)/shard_map/experts/pallas_call | solution.py:1271
  222.5 1.9 combine.1
  224.5 29.8 %gather_7.1.d_mix = bf16[4,128,1152]{2,1,0:T(8,128)(2,1)S(1)} custom-call(bf16[128,1152]{1,0:T(8,128)(2,1)S(1)} %get-tuple-element.133.refs_0_), custom_call_target="tpu_custom_call" | custom-call | flops 30799998976 | bytes 98000000 | tf_op jit(solution)/shard_map/gather_7/pallas_call | solution.py:158
  254.4 12.1 %gate_back.1 = (f32[4,128,640]{2,1,0:T(8,128)S(1)}, bf16[4,144,640]{2,1,0:T(8,128)(2,1)S(1)}, f32[1,640]{1,0:T(1,128)S(1)}, f32[4,16,8,640]{3,2,1,0:T(8,128)S(1)...) custom-call(bf16[4,128,1152]{2,1,0:T(8,128)(2,1)S(1)} %gather_7.1.d_mix, bf16[640,1152]{1,0:T(8,128)(2,1)S(1)} %copy-done.17, ...), custom_call_target="tpu_custom_call" | custom-call | flops 12099999744 | bytes 38500000 | tf_op jit(solution)/shard_map/gate_back/pallas_call | solution.py:1594
  266.5 2.4 pack_zo.1.g_ref
  269.0 18.5 %carry_back.1 = (bf16[8,4,16,640]{3,2,1,0:T(8,128)(2,1)S(1)}, bf16[4,144,1280]{2,1,0:T(8,128)(2,1)S(1)}) custom-call(bf16[4,16,640]{2,1,0:T(8,128)(2,1)S(1)} %get-tuple-element.139.f_ref, bf16[4,2,144,1280]{3,2,1,0:T(8,128)(2,1)S(1)} %pack_zo.1.g_ref), custom_call_target="tpu_custom_call" | custom-call | flops 15399999488 | bytes 49000000 | tf_op jit(solution)/shard_map/carry_back/pallas_call | solution.py:233
  287.5 32.6 %scan_back.1 = (bf16[4,128,128]{2,1,0:T(8,128)(2,1)S(1)}, f32[4,128,640]{2,1,0:T(8,128)S(1)}, f32[128,640]{1,0:T(8,128)S(1)}, f32[1,640]{1,0:T(1,128)S(1)}, f32[16,8,640]{2,1,0:T(8,128)S(1)}) custom-call(s32[1]{0:T(128)} %bitcast.place_ref, bf16[4,128,128]{2,1,0:T(8,128)(2,1)S(1)} %copy-done.61, f32[4,128,640]{2,1,0:T(8,128)S(1)} %copy-done.41, ...), custom_call_target="tpu_custom_call" | custom-call | flops 37399998464 | bytes 119000000 | tf_op jit(solution)/shard_map/scan_back/pallas_call | solution.py:1594
  320.3 20.5 %proj_back.1 = (bf16[4,128,128]{2,1,0:T(8,128)(2,1)S(1)}, bf16[144,1280]{1,0:T(8,128)(2,1)S(1)}) custom-call(bf16[4,128,128]{2,1,0:T(8,128)(2,1)S(1)} %get-tuple-element.143.x_ref, bf16[4,2,144,1280]{3,2,1,0:T(8,128)(2,1)S(1)} %pack_zo.1.g_ref, bf16[4,144,1280]{2,1,0:T(8,128)(2,1)S(1)} %get-tuple-element.144.p_ref), custom_call_target="tpu_custom_call" | custom-call | flops 22000001024 | bytes 70000000 | tf_op jit(solution)/shard_map/proj_back/pallas_call | solution.py:298
  340.8 7.3 %conv_back.1 = (bf16[4,144,640]{2,1,0:T(8,128)(2,1)S(1)}, bf16[4,144,1152]{2,1,0:T(8,128)(2,1)S(1)}, f32[8,640]{1,0:T(8,128)S(1)}, f32[128,640]{1,0:T(8,128)S(1)}, f32[1,1152]{1,0:T(1,128)S(1)}) custom-call(s32[1]{0:T(128)} %bitcast.place_ref, s32[4,8,128]{2,1,0:T(8,128)S(1)} %copy-done.69, bf16[4,128,128]{2,1,0:T(8,128)(2,1)S(1)} %get-tuple-element.145.proj_i, ...), custom_call_target="tpu_custom_call" | custom-call | flops 11000000512 | bytes 35000000 | tf_op jit(solution)/shard_map/conv_back/pallas_call | solution.py:1594
  348.1 1.6 pack_rest.1.g_ref
  349.7 61.7 %finish.1 = (bf16[8,480,640]{2,1,0:T(8,128)(2,1)S(1)}, bf16[4,144,1152]{2,1,0:T(8,128)(2,1)S(1)}, bf16[4,16,1152]{2,1,0:T(8,128)(2,1)S(1)}) custom-call(bf16[4,2,192,640]{3,2,1,0:T(8,128)(2,1)S(1)} %pack_rest.1.g_ref, bf16[144,1280]{1,0:T(8,128)(2,1)S(1)} %get-tuple-element.162.zf_ref, bf16[4,144,1152]{2,1,0:T(8,128)(2,1)S(1)} %get-tuple-element.163.d_ref), custom_call_target="tpu_custom_call" | custom-call | flops 65999998976 | bytes 210000000 | tf_op jit(solution)/shard_map/finish/pallas_call | solution.py:498
  411.5 2.2 copy-done.18
  413.7 1.7 leave.1
  415.4 1.5 copy-done
  416.9 2.4 copy-done.19
  419.3 7.7 %unpack.1 = (f32[1152,1152]{1,0:T(8,128)}, f32[576,1152]{1,0:T(8,128)}, f32[1152,384]{1,0:T(8,128)}, f32[384,1152]{1,0:T(8,128)}, f32[4,576]{1,0:T(4,128)}, /*in...) custom-call(s32[1]{0:T(128)} %bitcast.15.mine_ref, ...), custom_call_target="tpu_custom_call" | custom-call | flops 8800000000 | bytes 28000000 | tf_op jit(solution)/shard_map/unpack/pallas_call | solution.py:1594
  (169 shorter events, 22.0 us)
Async XLA Ops:
  7.2 151.6 %all-gather.2.cloned.1.call-start = ((), (), s32[]{:S(2)}) async-start(), calls=%async_computation.1 | async-start | bytes 15925248 | tf_op jit(solution)/shard_map/all_gather | solution.py:1646
  11.5 403.9 %reduce-scatter.2.cloned.1.call-start = ((), (), s32[]{:S(2)}) async-start(), calls=%async_computation.2 | async-start | bytes 15925248 | tf_op jit(solution)/shard_map/reduce_scatter | solution.py:1721
  13.7 46.6 %copy-start.1 = (bf16[576,1152]{1,0:T(8,128)(2,1)S(1)}, bf16[576,1152]{1,0:T(8,128)(2,1)}, u32[]{:S(2)}) copy-start(bf16[576,1152]{1,0:T(8,128)(2,1)} %wout.1) | copy-start | bytes 3981316
  13.7 46.6 %copy-start.6 = (bf16[576,104]{0,1:T(8,128)(2,1)S(1)}, bf16[576,104]{0,1:T(8,128)(2,1)}, u32[]{:S(2)}) copy-start(bf16[576,104]{0,1:T(8,128)(2,1)} %param.28) | copy-start | bytes 359428
  13.7 46.6 %copy-start.7 = (bf16[72,576]{1,0:T(8,128)(2,1)S(1)}, bf16[72,576]{1,0:T(8,128)(2,1)}, u32[]{:S(2)}) copy-start(bf16[72,576]{1,0:T(8,128)(2,1)} %wdt.1) | copy-start | bytes 248836
  13.7 46.6 %copy-start.8 = (bf16[16,576]{1,0:T(8,128)(2,1)S(1)}, bf16[16,576]{1,0:T(8,128)(2,1)}, u32[]{:S(2)}) copy-start(bf16[16,576]{1,0:T(8,128)(2,1)} %a_log.1) | copy-start | bytes 55300
  13.7 46.6 %copy-start.9 = (bf16[4,576]{1,0:T(4,128)(2,1)S(1)}, bf16[4,576]{1,0:T(4,128)(2,1)}, u32[]{:S(2)}) copy-start(bf16[4,576]{1,0:T(4,128)(2,1)} %conv_w.1) | copy-start | bytes 13828
  60.5 49.6 %copy-start.16 = (bf16[640,1152]{1,0:T(8,128)(2,1)}, bf16[640,1152]{1,0:T(8,128)(2,1)S(1)}, u32[]{:S(2)}) copy-start(bf16[640,1152]{1,0:T(8,128)(2,1)S(1)} %get-tuple-element.120.wout) | copy-start | bytes 4423684
  60.5 49.6 %copy-start.58 = (f32[8,640]{1,0:T(8,128)}, f32[8,640]{1,0:T(8,128)S(1)}, u32[]{:S(2)}) copy-start(f32[8,640]{1,0:T(8,128)S(1)} %get-tuple-element.108.bias.skip) | copy-start | bytes 61444
  60.5 92.2 %copy-start.20 = (bf16[128,1152]{1,0:T(8,128)(2,1)}, bf16[128,1152]{1,0:T(8,128)(2,1)S(1)}, u32[]{:S(2)}) copy-start(bf16[128,1152]{1,0:T(8,128)(2,1)S(1)} %get-tuple-element.122.router) | copy-start | bytes 884740
  68.3 41.9 %copy-start.26 = (f32[4,128,640]{2,1,0:T(8,128)}, f32[4,128,640]{2,1,0:T(8,128)S(1)}, u32[]{:S(2)}) copy-start(f32[4,128,640]{2,1,0:T(8,128)S(1)} %get-tuple-element.109.uf) | copy-start | bytes 3932164
  68.3 41.9 %copy-start.38 = (bf16[4,128,640]{2,1,0:T(8,128)(2,1)}, bf16[4,128,640]{2,1,0:T(8,128)(2,1)S(1)}, u32[]{:S(2)}) copy-start(bf16[4,128,640]{2,1,0:T(8,128)(2,1)S(1)} %get-tuple-element.119.z) | copy-start | bytes 1966084
  68.3 41.9 %copy-start.50 = (f32[4,128,128]{2,1,0:T(8,128)}, f32[4,128,128]{2,1,0:T(8,128)S(1)}, u32[]{:S(2)}) copy-start(f32[4,128,128]{2,1,0:T(8,128)S(1)} %get-tuple-element.110.cut) | copy-start | bytes 786436
  79.1 31.1 %copy-start.60 = (bf16[4,128,128]{2,1,0:T(8,128)(2,1)}, bf16[4,128,128]{2,1,0:T(8,128)(2,1)S(1)}, u32[]{:S(2)}) copy-start(bf16[4,128,128]{2,1,0:T(8,128)(2,1)S(1)} %sum_all.1.proj_i.proj) | copy-start | bytes 393220
  124.7 28.1 %copy-start.4 = (bf16[1,128,1152]{2,1,0:T(8,128)(2,1)S(1)}, bf16[1,128,1152]{2,1,0:T(8,128)(2,1)}, u32[]{:S(2)}) copy-start(bf16[1,128,1152]{2,1,0:T(8,128)(2,1)} %param.20) | copy-start | bytes 884740
  124.7 28.1 %copy-start.10 = (s32[1,128,1]{1,2,0:T(1,128)S(1)}, s32[1,128,1]{1,2,0:T(1,128)}, u32[]{:S(2)}) copy-start(s32[1,128,1]{1,2,0:T(1,128)} %param.22) | copy-start | bytes 1540
  124.7 28.1 %copy-start.11 = (s32[1,128]{1,0:T(1,128)S(1)}, s32[1,128]{1,0:T(1,128)}, u32[]{:S(2)}) copy-start(s32[1,128]{1,0:T(1,128)} %keep.1) | copy-start | bytes 1540
  224.4 29.9 %copy-start.17 = (bf16[640,1152]{1,0:T(8,128)(2,1)S(1)}, bf16[640,1152]{1,0:T(8,128)(2,1)}, u32[]{:S(2)}) copy-start(bf16[640,1152]{1,0:T(8,128)(2,1)} %copy-done.16) | copy-start | bytes 4423684
  224.4 29.9 %copy-start.27 = (f32[4,128,640]{2,1,0:T(8,128)S(1)}, f32[4,128,640]{2,1,0:T(8,128)}, u32[]{:S(2)}) copy-start(f32[4,128,640]{2,1,0:T(8,128)} %copy-done.26) | copy-start | bytes 3932164
  224.4 29.9 %copy-start.39 = (bf16[4,128,640]{2,1,0:T(8,128)(2,1)S(1)}, bf16[4,128,640]{2,1,0:T(8,128)(2,1)}, u32[]{:S(2)}) copy-start(bf16[4,128,640]{2,1,0:T(8,128)(2,1)} %copy-done.38) | copy-start | bytes 1966084
  224.4 29.9 %copy-start.41 = (f32[4,128,640]{2,1,0:T(8,128)S(1)}, f32[4,128,640]{2,1,0:T(8,128)}, u32[]{:S(2)}) copy-start(f32[4,128,640]{2,1,0:T(8,128)} %copy-done.40) | copy-start | bytes 3932164
  224.4 29.9 %copy-start.43 = (f32[4,128,640]{2,1,0:T(8,128)S(1)}, f32[4,128,640]{2,1,0:T(8,128)}, u32[]{:S(2)}) copy-start(f32[4,128,640]{2,1,0:T(8,128)} %copy-done.42) | copy-start | bytes 3932164
  224.4 29.9 %copy-start.51 = (f32[4,128,128]{2,1,0:T(8,128)S(1)}, f32[4,128,128]{2,1,0:T(8,128)}, u32[]{:S(2)}) copy-start(f32[4,128,128]{2,1,0:T(8,128)} %copy-done.50) | copy-start | bytes 786436
  224.5 29.9 %copy-start.61 = (bf16[4,128,128]{2,1,0:T(8,128)(2,1)S(1)}, bf16[4,128,128]{2,1,0:T(8,128)(2,1)}, u32[]{:S(2)}) copy-start(bf16[4,128,128]{2,1,0:T(8,128)(2,1)} %copy-done.60) | copy-start | bytes 393220
  (55 other events, 501.5 us)
Sparse Core Ops, SparseCore 0:
  11.7 104.0 all-gather.1
  216.9 108.6 reduce-scatter.1

commit v5 on v4

--- a/solution.py
+++ b/solution.py
@@ -16,6 +16,7 @@
 CUT = 1e30
 MESH = pl.DeviceIdType.MESH
 VMEM_LIMIT = 24 * 2**20
+LARGE_LIMIT = 60 * 2**20
 
 
 def lasting(us):
@@ -210,117 +211,72 @@
     pl.semaphore_signal(barrier, inc=1, device_id={axis: who}, device_id_type=MESH)
 
 
-def carry_back_kernel(ring, f_ref, g_ref, f_o, p_o, send, recv, own, pair_s, pair_r):
-    me, _, lane, pair, _ = neighbours(ring)
-    greet("ctx", ring)
-    to_pair = remote(g_ref.at[:, 1 - lane], p_o, pair_s, pair_r, {"ctx": pair})
-    copies = []
-    for k in range(1, ring):
-        copy = remote(f_ref, f_o.at[me], send.at[k], recv.at[k], {"ctx": lax.rem(me + k, ring)})
-        copy.start()
-        copies.append(copy)
-    to_pair.start()
-    local = pltpu.make_async_copy(f_ref, f_o.at[me], own)
-    local.start()
-    for copy in copies + [to_pair, local]:
+def carry_kernel(ring, arrays, halved, *refs):
+    total = arrays + halved
+    srcs, dsts = refs[:total], refs[total : 2 * total]
+    send, recv, fwd_s, fwd_r, own, half_s, half_r = refs[2 * total :]
+    me, chip, lane, pair, peers = neighbours(ring)
+    half = ring // 2
+    barrier = pltpu.get_barrier_semaphore()
+    for who in [pair] + peers:
+        hello(barrier, "ctx", who)
+    pl.semaphore_wait(barrier, half)
+    copies, forwards, local = [], [], []
+    for i in range(arrays):
+        for k, who in enumerate(peers):
+            copies.append(remote(srcs[i], dsts[i].at[me], send.at[i, k], recv.at[i, k], {"ctx": who}))
+            copies[-1].start()
+    for i in range(arrays):
+        forwards.append(remote(srcs[i], dsts[i].at[me], fwd_s.at[i, 0], fwd_r.at[i, 0], {"ctx": pair}))
+        forwards[-1].start()
+        local.append(pltpu.make_async_copy(srcs[i], dsts[i].at[me], own.at[i]))
+        local[-1].start()
+    if halved:
+        to_pair = remote(srcs[arrays].at[:, 1 - lane], dsts[arrays], half_s, half_r, {"ctx": pair})
+        to_pair.start()
+        local.append(to_pair)
+    for i in range(arrays):
+        for k in range(1, half):
+            copies[i * (half - 1) + k - 1].wait_recv()
+            block = dsts[i].at[lax.rem(chip + half - k, half) * 2 + lane]
+            forwards.append(remote(block, block, fwd_s.at[i, k], fwd_r.at[i, k], {"ctx": pair}))
+            forwards[-1].start()
+    for copy in copies:
+        copy.wait_send()
+    for copy in forwards + local:
         copy.wait()
 
 
-def carry_back(f, g, cid, us):
-    ring = lax.axis_size("ctx")
+def carry(xs, cid, us, halved=None):
+    ring, arrays = lax.axis_size("ctx"), len(xs)
+    half = ring // 2
+    shapes = [((ring,) + x.shape, x.dtype) for x in xs]
+    if halved is not None:
+        xs = xs + [halved]
+        shapes.append((halved.shape[:1] + halved.shape[2:], halved.dtype))
     hbm = pl.BlockSpec(memory_space=pl.ANY)
     dma = pltpu.SemaphoreType.DMA
     return pl.pallas_call(
-        functools.partial(carry_back_kernel, ring),
-        out_shape=[
-            jax.ShapeDtypeStruct((ring,) + f.shape, f.dtype),
-            jax.ShapeDtypeStruct(g.shape[:1] + g.shape[2:], g.dtype),
-        ],
-        in_specs=[hbm] * 2,
-        out_specs=[hbm] * 2,
-        scratch_shapes=[dma((ring,)), dma((ring,)), dma, dma, dma],
-        compiler_params=pltpu.CompilerParams(
-            collective_id=cid, has_side_effects=True, vmem_limit_bytes=VMEM_LIMIT
-        ),
-        cost_estimate=lasting(us),
-        name="carry_back",
-    )(f, g)
-
-
-def proj_back_kernel(
-    ring, group, x_ref, g_ref, p_ref, x_o, g_o,
-    kept, paired, came, got, s1, r1, s2, r2, load, ctx_s, ctx_r,
-):
-    _, chip, lane, _, peers = neighbours(ring)
-    mine, mates = mates_of(group)
-    half = ring // 2
-    rows = g_o.shape[0]
-    loads = [
-        pltpu.make_async_copy(g_ref.at[:, lane], kept, load.at[0]),
-        pltpu.make_async_copy(p_ref, paired, load.at[1]),
-    ]
-    for copy in loads:
-        copy.start()
-    barrier = pltpu.get_barrier_semaphore()
-    for who in peers:
-        hello(barrier, "ctx", who)
-    for who in mates:
-        hello(barrier, "wa", who)
-    pl.semaphore_wait(barrier, half + group - 2)
-    copies = sum_start(mates, x_ref, got, s1, r1)
-    for copy in loads:
-        copy.wait()
-    scattered = []
-    for k, who in enumerate(peers):
-        to = lax.rem(chip + k + 1, half)
-        add_rows(kept.at[to], [kept.at[to], paired.at[to]], rows)
-        copy = remote(kept.at[to], came.at[k], ctx_s.at[k], ctx_r.at[k], {"ctx": who})
-        copy.start()
-        scattered.append(copy)
-    spreads = sum_spread(mine, mates, x_ref, got, x_o, copies, s2, r2)
-    add_rows(kept.at[chip], [kept.at[chip], paired.at[chip]], rows)
-    for copy in scattered:
-        copy.wait_recv()
-    add_rows(g_o, [kept.at[chip]] + [came.at[k] for k in range(half - 1)], rows)
-    for copy in scattered + copies:
-        copy.wait_send()
-    for copy in spreads:
-        copy.wait()
-
-
-def proj_back(x, g, p, cid, us):
-    ring, group = lax.axis_size("ctx"), lax.axis_size("wa")
-    half = ring // 2
-    hbm = pl.BlockSpec(memory_space=pl.ANY)
-    vmem = pl.BlockSpec(memory_space=pltpu.VMEM)
-    dma = pltpu.SemaphoreType.DMA
-    block = pltpu.VMEM((half,) + g.shape[2:], g.dtype)
-    return pl.pallas_call(
-        functools.partial(proj_back_kernel, ring, group),
-        out_shape=[
-            jax.ShapeDtypeStruct(x.shape, x.dtype),
-            jax.ShapeDtypeStruct(g.shape[2:], g.dtype),
-        ],
-        in_specs=[vmem, hbm, hbm],
-        out_specs=[vmem, vmem],
+        functools.partial(carry_kernel, ring, arrays, len(xs) - arrays),
+        out_shape=[jax.ShapeDtypeStruct(shape, dtype) for shape, dtype in shapes],
+        in_specs=[hbm] * len(xs),
+        out_specs=[hbm] * len(xs),
         scratch_shapes=[
-            block, block, pltpu.VMEM((half - 1,) + g.shape[2:], g.dtype),
-            pltpu.VMEM((group - 1,) + x.shape[1:], x.dtype),
-            dma((group - 1,)), dma((group - 1,)), dma((group - 1,)), dma((group - 1,)), dma((2,)),
-            dma((half - 1,)), dma((half - 1,)),
+            dma((arrays, half - 1)), dma((arrays, half - 1)), dma((arrays, half)), dma((arrays, half)),
+            dma((arrays,)), dma, dma,
         ],
         compiler_params=pltpu.CompilerParams(
             collective_id=cid, has_side_effects=True, vmem_limit_bytes=VMEM_LIMIT
         ),
         cost_estimate=lasting(us),
-        name="proj_back",
-    )(x, g, p)
+        name=f"carry_{cid}",
+    )(*xs)
 
 
 def finish_kernel(
     ring, group, in_rows, small_rows,
     g_ref, zf_ref, d_ref, o_ref, dt_ref, de_ref,
-    from_pair, paired, came, own, zin, tiles,
+    from_pair, paired, came, own, zin, tiles, fin, store_s,
     pair_s, pair_r, ctx_s, ctx_r, z_s, z_r, tile_s, tile_r, d_s, d_r, d_own, last_s, last_r, fwd_s, fwd_r,
     edge_s, edge_r,
 ):
@@ -352,16 +308,19 @@
     to_pair.start()
     ready = 2 * in_rows + small_rows + 16
     parts = [pl.ds(ready, in_rows), pl.ds(0, ready)]
-    o_ref[me, parts[0]] = zf_ref[:, lanes:]
+    fin[parts[0]] = zf_ref[:, lanes:]
+    stored = []
 
     def to_all(i):
-        src = o_ref.at[me, parts[i]]
+        src, dst = fin.at[parts[i]], o_ref.at[me, parts[i]]
         copies = []
         for k, who in enumerate(peers):
-            copies.append(remote(src, src, last_s.at[i, k], last_r.at[i, k], {"ctx": who}))
-        copies.append(remote(src, src, fwd_s.at[i, 0], fwd_r.at[i, 0], {"ctx": pair}))
+            copies.append(remote(src, dst, last_s.at[i, k], last_r.at[i, k], {"ctx": who}))
+        copies.append(remote(src, dst, fwd_s.at[i, 0], fwd_r.at[i, 0], {"ctx": pair}))
         for copy in copies:
             copy.start()
+        stored.append(pltpu.make_async_copy(src, dst, store_s.at[i]))
+        stored[-1].start()
         return copies
 
     def forward(i, copies):
@@ -437,17 +396,17 @@
         copy.start()
         spread_tiles.append(copy)
     forward(0, early)
-    o_ref[me, pl.ds(2 * in_rows, small_rows)] = own[pl.ds(in_rows, small_rows)]
+    fin[pl.ds(2 * in_rows, small_rows)] = own[pl.ds(in_rows, small_rows)]
     for copy in spread_tiles:
         copy.wait_recv()
     add_rows(
-        o_ref.at[me, pl.ds(2 * in_rows + small_rows, 16)],
+        fin.at[pl.ds(2 * in_rows + small_rows, 16)],
         [own.at[tile]] + [tiles.at[k] for k in range(group - 1)],
         16,
     )
     for s in range(2):
         pltpu.make_async_copy(zin.at[s], zin.at[s], z_r.at[s]).wait()
-        o_ref[me, pl.ds(s * in_rows, in_rows)] = zin[s]
+        fin[pl.ds(s * in_rows, in_rows)] = zin[s]
     late = to_all(1)
     trade_rows(1)
     kept.wait()
@@ -466,6 +425,8 @@
         for copy in copies[half - 1 :]:
             copy.wait_recv()
 
+    for copy in stored:
+        copy.wait()
     to_pair.wait_send()
     for copy in scattered + spread_tiles + early + late + trades:
         copy.wait_send()
@@ -503,7 +464,7 @@
             jax.ShapeDtypeStruct((group, EDGE, d.shape[2]), d.dtype),
         ],
         in_specs=[vmem, vmem, hbm],
-        out_specs=[vmem, hbm, hbm],
+        out_specs=[hbm, hbm, hbm],
         scratch_shapes=[
             pltpu.VMEM((half, rows, lanes), BF16),
             pltpu.VMEM((half, rows, lanes), BF16),
@@ -511,7 +472,8 @@
             pltpu.VMEM((rows, lanes), BF16),
             pltpu.VMEM((2, in_rows, lanes), BF16),
             pltpu.VMEM((group - 1, 16, lanes), BF16),
-            dma, dma,
+            pltpu.VMEM((out_rows, lanes), BF16),
+            dma((2,)), dma, dma,
             dma((half - 1,)), dma((half - 1,)),
             dma((2,)), dma((2,)),
             dma((group - 1,)), dma((group - 1,)),
@@ -693,8 +655,10 @@
     shape = (states * LANE, columns)
     lower = (lax.broadcasted_iota(jnp.int32, shape, 1) - at) * LANE
     place = lax.broadcasted_iota(jnp.int32, shape, 0)
-    ones = jnp.where((place >= lower) & (place < lower + LANE), 1.0, 0.0)
-    return jnp.dot(wide_rows, ones, precision=lax.Precision.HIGHEST, preferred_element_type=F32)
+    ones = jnp.where((place >= lower) & (place < lower + LANE), 1.0, 0.0).astype(BF16)
+    coarse = wide_rows.astype(BF16)
+    rest = (wide_rows - coarse.astype(F32)).astype(BF16)
+    return dot_nn(coarse, ones) + dot_nn(rest, ones)
 
 
 def position_of(shape, axis, steps):
@@ -850,7 +814,7 @@
                 new.append(jnp.exp(st * a[n]) * carry[n + 1] + bb[rows, state_cols(n)] * dr)
             return tuple(new)
 
-        out = lax.fori_loop(0, steps, step, (zero,) * (states + 1), unroll=2)
+        out = lax.fori_loop(0, steps, step, (zero,) * (states + 1), unroll=8)
         total, h = out[0], list(out[1:])
         for k in (1, 2, 4):
             ok = seg >= k
@@ -924,7 +888,7 @@
             y_o[0, rows, lanes] = y
             return tuple(new)
 
-        lax.fori_loop(0, steps, step, first, unroll=2)
+        lax.fori_loop(0, steps, step, first, unroll=8)
         return 0
 
     lax.fori_loop(0, groups, group, 0)
@@ -974,8 +938,8 @@
     spot = lax.broadcasted_iota(jnp.int32, (length, slots), 1).astype(F32)
     match = jnp.where(slot == spot, 1.0, 0.0).astype(BF16)
     match_o[...] = match
-    out_o[0] = dot_tn(match, n2).astype(BF16)
-    out_o[1] = dot_tn(match, (gates * up).astype(BF16)).astype(BF16)
+    out_o[0] = dot_tn(match, n2).astype(BF16).reshape(out_o.shape[1:])
+    out_o[1] = dot_tn(match, (gates * up).astype(BF16)).astype(BF16).reshape(out_o.shape[1:])
     sums_o[...] = jnp.broadcast_to(jnp.sum(mix * mix, keepdims=True), (SEG, LANE))
 
 
@@ -1095,12 +1059,52 @@
         out[c // 2, c % 2] = rows.astype(BF16)
 
 
+def store_in_order(out, rows, order_s):
+    steps = rows.shape[0] // SEG
+    for g in range(rows.shape[1] // LANE):
+        cols = slice(g * LANE, (g + 1) * LANE)
+        for j in range(steps):
+            order_s[g, pl.ds(j, SEG, stride=steps), :] = rows[j * SEG : (j + 1) * SEG, cols]
+        out[:, cols] = order_s[g]
+
+
+def input_gradient(taps, last_ref, terms, edges, tok, gain, dh, out_o, dn_s, order_s):
+    length = tok.shape[0]
+    steps = length // SEG
+    behind = taps - 1
+    total = terms[0, :length].astype(F32)
+    edge = edges[0].astype(F32)
+    for w in range(1, terms.shape[0]):
+        total = total + terms[w, :length].astype(F32)
+        edge = edge + edges[w].astype(F32)
+    edge = jnp.where(last_ref[0] > 0, 0.0, edge)
+    dn_s[...] = total
+    seg = lax.broadcasted_iota(jnp.int32, (SEG, tok.shape[1]), 0)
+    for i in range(behind):
+        j = pl.ds((steps - behind + i) * SEG, SEG)
+        row = EDGE - behind + i
+        came = jnp.broadcast_to(edge[row : row + 1], seg.shape)
+        dn_s[j, :] += jnp.where(seg == SEG - 1, came, 0.0)
+    x = dot_nn(permutation(length), tok[...])
+    d_x, _ = norm_grads(x, rms_scale(x), gain[0:1], dn_s[...])
+    result = dh[...] + d_x
+    store_in_order(out_o, result, order_s)
+
+
 def unpack_kernel(
     ring, group, in_rows, small_rows, experts, states, ranked, taps, denom, mine_ref, done, up_down,
-    in_o, out_o, up_o, down_o, taps_o, wx_o, wdt_o, a_o, vec_o, stat_o, small_s, full_s,
+    last_ref, terms, edges, tok, gain, dh, res,
+    in_o, out_o, up_o, down_o, taps_o, wx_o, wdt_o, a_o, vec_o, stat_o, grad_o, layer_o,
+    small_s, full_s, dn_s, order_s,
 ):
     c = pl.program_id(0)
     width = in_o.shape[1]
+
+    @pl.when(c == 1)
+    def _():
+        store_in_order(layer_o, res[...], order_s)
+        input_gradient(taps, last_ref, terms, edges, tok, gain, dh, grad_o, dn_s, order_s)
+
     local = width // 2
     small_each = small_s.shape[0] // ring
     base = 2 * in_rows
@@ -1152,10 +1156,13 @@
         vec_o[SEG + 2 : SEG + 3] = small_s[at + SEG : at + SEG + 1]
 
 
-def experts_kernel(
-    group, chunks, x_ref, w_ref, g_ref, r_ref,
+def middle_kernel(
+    experts, group, chunks,
+    mix_ref, tok, gain, router, route, keep, grad, w_ref,
+    g_ref, layer_o, dh_o, dmix_o, router_o, gain_o, sums_o, mix_o,
+    mix_s, h1_s, n2_s, up_s, cols_s, match_s, x_ref, r_ref,
     got, w_s, g_s, act_s, slope_s, pre_s, acc, out_s,
-    w_sem, g_sem, s1, r1, own1, s2, r2, own2,
+    w_sem, g_sem, s0, r0, own0, s1, r1, own1, s2, r2, own2,
 ):
     mine, mates = mates_of(group)
     count, width = x_ref.shape[2:]
@@ -1169,6 +1176,19 @@
 
     load(0).start()
     greet("wa", group)
+    terms = []
+    for k, who in enumerate(mates):
+        copy = remote(mix_ref.at[who], mix_s.at[mine], s0.at[k], r0.at[k], {"wa": who})
+        copy.start()
+        terms.append(copy)
+    kept = pltpu.make_async_copy(mix_ref.at[mine], mix_s.at[mine], own0)
+    kept.start()
+    for copy in terms + [kept]:
+        copy.wait()
+    route_kernel(
+        experts, mix_s, tok, gain, router, route, keep, grad,
+        h1_s, n2_s, up_s, cols_s, match_s, x_ref, mix_o,
+    )
     sent = []
     for h in range(2):
         for k, who in enumerate(mates):
@@ -1257,54 +1277,62 @@
         copy.wait_send()
     for copy in sent[2 * len(mates) :]:
         copy.wait()
-
-
-def experts_call(x, w, chunks, cid, us):
+    combine_kernel(
+        experts, r_ref, match_s, h1_s, n2_s, up_s, cols_s, gain, router,
+        layer_o, dh_o, dmix_o, router_o, gain_o, sums_o,
+    )
+
+
+def middle(experts, mix_part, tok, gains, router, route, keep, grad, w, chunks, cid, us):
     group = lax.axis_size("wa")
-    units, width = w.shape[0], x.shape[3]
-    slots = group * x.shape[2]
+    units = w.shape[0]
+    length, width = tok.shape
+    slots = experts * (length // 2)
     block = units // chunks
     dma = pltpu.SemaphoreType.DMA
     hbm = pl.BlockSpec(memory_space=pltpu.HBM)
     vmem = pl.BlockSpec(memory_space=pltpu.VMEM)
     two = dma((2, group - 1))
+    one = dma((group - 1,))
+    rows = pltpu.VMEM((2, group, slots // group, width), BF16)
+    shapes = [
+        (w.shape, BF16), ((length, width), F32), ((length, width), F32), ((length, width), BF16),
+        ((LANE, width), F32), ((1, width), F32), ((SEG, LANE), F32), ((SEG, LANE), F32),
+    ]
     return pl.pallas_call(
-        functools.partial(experts_kernel, group, chunks),
-        out_shape=[jax.ShapeDtypeStruct(w.shape, BF16), jax.ShapeDtypeStruct(x.shape, BF16)],
-        in_specs=[vmem, hbm],
-        out_specs=[hbm, vmem],
+        functools.partial(middle_kernel, experts, group, chunks),
+        out_shape=[jax.ShapeDtypeStruct(shape, dtype) for shape, dtype in shapes],
+        in_specs=[vmem] * 7 + [hbm],
+        out_specs=[hbm] + [vmem] * 7,
         scratch_shapes=[
-            pltpu.VMEM(x.shape, BF16),
+            pltpu.VMEM(mix_part.shape, BF16),
+            pltpu.VMEM((length, width), F32),
+            pltpu.VMEM((length, width), BF16),
+            pltpu.VMEM((length, width), F32),
+            pltpu.VMEM((length, LANE), F32),
+            pltpu.VMEM((length, slots), BF16),
+            rows, rows, rows,
             pltpu.VMEM((2, block, 2 * width), BF16),
             pltpu.VMEM((2, block, 2 * width), BF16),
             pltpu.VMEM((units, slots), BF16),
             pltpu.VMEM((units, slots), F32),
             pltpu.VMEM((units, slots), BF16),
             pltpu.VMEM((slots, width), F32),
-            pltpu.VMEM(x.shape, BF16),
+            rows,
             dma((2,)), dma((2,)),
-            two, two, dma((2,)), two, two, dma((2,)),
+            one, one, dma, two, two, dma((2,)), two, two, dma((2,)),
         ],
         compiler_params=pltpu.CompilerParams(
             collective_id=cid, has_side_effects=True, vmem_limit_bytes=VMEM_LIMIT + 20 * 2**20
         ),
         cost_estimate=lasting(us),
-        name="experts",
-    )(x, w)
-
-
-def store_in_order(out, rows, order_s):
-    steps = rows.shape[0] // SEG
-    for g in range(rows.shape[1] // LANE):
-        cols = slice(g * LANE, (g + 1) * LANE)
-        for j in range(steps):
-            order_s[g, pl.ds(j, SEG, stride=steps), :] = rows[j * SEG : (j + 1) * SEG, cols]
-        out[:, cols] = order_s[g]
+        name="middle",
+    )(mix_part, tok, gains, router, route, keep, grad, w)
 
 
 def combine_kernel(
     experts, back, match, h1_i, n2, up_i, cols, gain, router,
-    out_o, dh_o, dmix_o, router_o, gain_o, sums_o, order_s,
+    out_o, dh_o, dmix_o, router_o, gain_o, sums_o,
 ):
     length, width = h1_i.shape
     h1, up = h1_i[...], up_i[...]
@@ -1316,14 +1344,15 @@
 
     gates, slope = column(experts), column(experts + 1)
     onehot = jnp.where(lane < experts, facts, 0.0)
-    rows = dot_nn(match[...], back[0])
+    slots = match.shape[1]
+    rows = dot_nn(match[...], back[0].reshape(slots, width))
     moe = gates * rows
     result = h1 + moe
-    store_in_order(out_o, result, order_s)
+    out_o[...] = result
     d_gate = jnp.sum(rows * up, axis=1, keepdims=True)
     d_logits = (onehot * (d_gate * slope)).astype(BF16)
     router_o[...] = dot_tn(d_logits, n2[...])
-    d_n2 = dot_nn(match[...], back[1]) + dot_nn(d_logits, router[...])
+    d_n2 = dot_nn(match[...], back[1].reshape(slots, width)) + dot_nn(d_logits, router[...])
     d_norm, terms = norm_grads(h1, rms_scale(h1), gain[1:2], d_n2)
     gain_o[...] = jnp.sum(terms, axis=0, keepdims=True)
     d_h1 = up + d_norm
@@ -1371,7 +1400,7 @@
                 new.append(jnp.exp(st * a[n]) * (carry[n + 1] + cb[rows, state_cols(n)] * d))
             return tuple(new)
 
-        out = lax.fori_loop(0, steps, step, (zero,) * (states + 1), unroll=2)
+        out = lax.fori_loop(0, steps, step, (zero,) * (states + 1), unroll=8)
         total, f = out[0], list(out[1:])
         for k in (1, 2, 4):
             ok = seg < SEG - k
@@ -1390,18 +1419,52 @@
 
 
 def scan_back_kernel(
-    states, b_at, place_ref, proj, step_i, sig, uf, cut, dy_i, a_ref, skip, wdt, hx_ref, sx_ref, e_i,
-    fx_ref, tx_ref, finals, sums,
-    part_o, du_o, dt_o, bias_o, ga_ref,
+    states, b_at, proj, step_i, sig, uf, cut, dy_i, a_ref, skip, wdt, hx_ref, sx_ref, e_i,
+    fx_ref, tx_ref, finals, sums, g_ref, p_ref,
+    part_o, du_o, dt_o, bias_o, ga_ref, g_o,
     bb, cb, dec, pri, accb, accc, st_s, dr_s, ds_s, out_s,
+    from_pair, kept, came, load, ctx_s, ctx_r,
 ):
+    ring = finals.shape[0]
+    half = ring // 2
+    _, chip, lane, _, peers = neighbours(ring)
+    own_half = pltpu.make_async_copy(g_ref.at[:, lane], kept, load.at[0])
+    pair_half = pltpu.make_async_copy(p_ref, from_pair, load.at[1])
+    targets = [lax.rem(chip + k, half) for k in range(1, half)]
+    scattered = [
+        remote(kept.at[to], came.at[k], ctx_s.at[k], ctx_r.at[k], {"ctx": who})
+        for k, (to, who) in enumerate(zip(targets, peers))
+    ]
+    at = pl.program_id(0)
+
+    @pl.when(at == 0)
+    def _():
+        own_half.start()
+        pair_half.start()
+        barrier = pltpu.get_barrier_semaphore()
+        for who in peers:
+            hello(barrier, "ctx", who)
+        pl.semaphore_wait(barrier, half - 1)
+        own_half.wait()
+        pair_half.wait()
+        for to, copy in zip(targets, scattered):
+            add_rows(kept.at[to], [kept.at[to], from_pair.at[to]], kept.shape[1])
+            copy.start()
+        add_rows(kept.at[chip], [kept.at[chip], from_pair.at[chip]], kept.shape[1])
+
+    @pl.when(at == pl.num_programs(0) - 1)
+    def _():
+        for copy in scattered:
+            copy.wait()
+        add_rows(g_o, [kept.at[chip]] + [came.at[k] for k in range(half - 1)], kept.shape[1])
+
     length, width = step_i.shape[1:]
     groups, steps = width // LANE, length // SEG
     bb[...] = spread(proj[0], states, b_at)
     cb[...] = spread(proj[0], states, b_at + states)
     accb[...] = jnp.zeros_like(accb)
     accc[...] = jnp.zeros_like(accc)
-    entering(out_s, finals, sums, a_ref, place_ref[0], False)
+    entering(out_s, finals, sums, a_ref, lax.axis_index("ctx"), False)
     e_ref = e_i.at[0]
     dr_s[...] = step_i[0] * uf[0]
     for g in range(groups):
@@ -1435,7 +1498,7 @@
                 new.append(decay * h[n] + bb[rows, state_cols(n)] * dr)
             return tuple(new)
 
-        last = lax.fori_loop(0, steps, ahead, first, unroll=2)
+        last = lax.fori_loop(0, steps, ahead, first, unroll=8)
         end = rows_of(steps)
         for n in range(states):
             pri[end, state_cols(n)] = last[n]
@@ -1473,7 +1536,7 @@
             du_o[0, rows, lanes] = d_drive * st + dy * gain
             return tuple(new)
 
-        lax.fori_loop(0, steps, back, flow, unroll=2)
+        lax.fori_loop(0, steps, back, flow, unroll=8)
         return 0
 
     lax.fori_loop(0, groups, group, 0)
@@ -1532,29 +1595,6 @@
     dn_o[0] = d_n1.astype(BF16)
 
 
-def leave_kernel(taps, last_ref, terms, edges, tok, gain, dh, out_o, dn_s, order_s):
-    length = tok.shape[0]
-    steps = length // SEG
-    behind = taps - 1
-    total = terms[0, :length].astype(F32)
-    edge = edges[0].astype(F32)
-    for w in range(1, terms.shape[0]):
-        total = total + terms[w, :length].astype(F32)
-        edge = edge + edges[w].astype(F32)
-    edge = jnp.where(last_ref[0] > 0, 0.0, edge)
-    dn_s[...] = total
-    seg = lax.broadcasted_iota(jnp.int32, (SEG, tok.shape[1]), 0)
-    for i in range(behind):
-        j = pl.ds((steps - behind + i) * SEG, SEG)
-        row = EDGE - behind + i
-        came = jnp.broadcast_to(edge[row : row + 1], seg.shape)
-        dn_s[j, :] += jnp.where(seg == SEG - 1, came, 0.0)
-    x = dot_nn(permutation(length), tok[...])
-    d_x, _ = norm_grads(x, rms_scale(x), gain[0:1], dn_s[...])
-    result = dh[...] + d_x
-    store_in_order(out_o, result, order_s)
-
-
 SMEM = "smem"
 ANY = "any"
 
@@ -1573,7 +1613,7 @@
     return pl.BlockSpec(shape, lambda s: (0,) * len(shape))
 
 
-def call(kernel, name, grid, args, outs, scratch, us):
+def call(kernel, name, grid, args, outs, scratch, us, cid=None, limit=VMEM_LIMIT):
     arrays, specs = [], []
     for array, at in args:
         arrays.append(array)
@@ -1598,7 +1638,9 @@
         in_specs=specs,
         out_specs=out_specs,
         scratch_shapes=scratch,
-        compiler_params=pltpu.CompilerParams(vmem_limit_bytes=VMEM_LIMIT),
+        compiler_params=pltpu.CompilerParams(
+            vmem_limit_bytes=limit, collective_id=cid, has_side_effects=cid is not None
+        ),
         cost_estimate=lasting(us),
         name=name,
     )(*arrays)
@@ -1641,7 +1683,7 @@
 
     (own_experts,) = call(
         pack_kernel, "pack", 1, [(w_up[0], None), (w_down[0], None)],
-        [((w_down.shape[1], 2 * width), BF16, None)], [], 3,
+        [((w_down.shape[1], 2 * width), BF16, None)], [], 3, None, LARGE_LIMIT,
     )
     expert_w = lax.all_gather(own_experts, "ctx", axis=0, tiled=True)
 
@@ -1696,7 +1738,7 @@
          (seg_sums, F32, 0), (dev_states, BF16, 0), (dev_sums, F32, 0)],
         [spread_vmem, lane_vmem, lane_vmem, state_vmem], 10,
     )
-    all_h, all_s = gather_all([h_dev, s_dev], "ctx", 3, 15)
+    all_h, all_s = carry([h_dev, s_dev], 3, 10)
     y_full, gated, mix_part, e_in = call(
         functools.partial(output_kernel, states, ranked), "scan_output", group,
         [(place_s, SMEM), (projected, 0), (step_size, 0), (u_f, 0), (cut, 0), (a_mat, None), (h_in, 0),
@@ -1704,29 +1746,12 @@
         [(vec, F32, 0), (vec, BF16, 0), ((group, length, width), BF16, 0), (dev_states, F32, 0)],
         [spread_vmem, spread_vmem, lane_vmem, lane_vmem], 13,
     )
-    mix_terms = trade(mix_part, "wa", 4, 25)
 
     row_f = (length, width)
-    h1, n2, upstream, facts, match, outgoing, mix_sum = call(
-        functools.partial(route_kernel, experts), "route", 1,
-        [(mix_terms, None), (tokens[0], None), (gains, None), (router, None),
-         (routes[0].T, None), (keep_mask, None), (out_grad[0], None)],
-        [(row_f, F32, None), (row_f, BF16, None), (row_f, F32, None), ((length, LANE), F32, None),
-         ((length, slots), BF16, None), ((2, slots, width), BF16, None), ((SEG, LANE), F32, None)],
-        [], 5,
-    )
-    grad_experts, returned = experts_call(
-        outgoing.reshape(2, group, slots // group, width), expert_w, 8, 5, 58
+    grad_experts, result, d_h1, d_mix_own, grad_router, grad_gain_moe, out_sums, mix_sum = middle(
+        experts, mix_part, tokens[0], gains, router, routes[0].T, keep_mask, out_grad[0], expert_w, 8, 5, 85
     )
     share_experts = lax.psum_scatter(grad_experts, "ctx", scatter_dimension=0, tiled=True)
-    result, d_h1, d_mix_own, grad_router, grad_gain_moe, out_sums = call(
-        functools.partial(combine_kernel, experts), "combine", 1,
-        [(returned.reshape(2, slots, width), None), (match, None), (h1, None), (n2, None),
-         (upstream, None), (facts, None), (gains, None), (router, None)],
-        [(row_f, F32, None), (row_f, F32, None), (row_f, BF16, None), ((LANE, width), F32, None),
-         ((1, width), F32, None), ((SEG, LANE), F32, None)],
-        [order_vmem], 6,
-    )
     (d_mix,) = gather_all([d_mix_own], "wa", 7, 28)
 
     d_y, d_z, grad_skip, f_in, t_in, f_dev = call(
@@ -1745,18 +1770,22 @@
          (d_mix.reshape(group * length, width), None), (gated.reshape(group * length, padded), None)],
         [(zo_shape, BF16, None)], [], 5,
     )
-    all_f, pair_zo = carry_back(f_dev, grad_zo, 8, 14)
-    d_part, d_u, grad_dt, grad_step_bias, grad_a = call(
+    all_f, pair_zo = carry([f_dev], 8, 10, grad_zo)
+    zo_half = pltpu.VMEM((ring // 2, in_rows, 2 * padded), BF16)
+    dma = pltpu.SemaphoreType.DMA
+    d_part, d_u, grad_dt, grad_step_bias, grad_a, chunk_zo = call(
         functools.partial(scan_back_kernel, states, ranked), "scan_back", group,
-        [(place_s, SMEM), (projected, 0), (step_size, 0), (sig, 0), (u_f, 0), (cut, 0), (d_y, 0),
+        [(projected, 0), (step_size, 0), (sig, 0), (u_f, 0), (cut, 0), (d_y, 0),
          (a_mat, None), (vectors, None), (wdt, None), (h_in, 0), (s_in, 0), (e_in, 0), (f_in, 0),
-         (t_in, 0), (all_f, 1), (all_s, 1)],
+         (t_in, 0), (all_f, 1), (all_s, 1), (grad_zo, ANY), (pair_zo, ANY)],
         [((group, length, columns), BF16, 0), (vec, F32, 0), ((columns, padded), F32, None),
-         ((1, padded), F32, None), ((states, SEG, padded), F32, None)],
+         ((1, padded), F32, None), ((states, SEG, padded), F32, None), ((in_rows, 2 * padded), BF16, None)],
         [spread_vmem, spread_vmem, spread_vmem, f32_vmem(length + SEG, states * LANE), spread_vmem,
-         spread_vmem, lane_vmem, lane_vmem, lane_vmem, state_vmem], 34,
-    )
-    d_projected, chunk_zo = proj_back(d_part, grad_zo, pair_zo, 9, 20)
+         spread_vmem, lane_vmem, lane_vmem, lane_vmem, state_vmem,
+         zo_half, zo_half, pltpu.VMEM((ring // 2 - 1, in_rows, 2 * padded), BF16),
+         dma((2,)), dma((ring // 2 - 1,)), dma((ring // 2 - 1,))], 34, 12,
+    )
+    d_projected = sum_all(d_part, 9, 11)
     d_x, d_n1_part, grad_conv, grad_x, gain_terms = call(
         functools.partial(conv_back_kernel, taps, documents), "conv_back", group,
         [(place_s, SMEM), (docs, SMEM), (d_projected, 0), (wproj, None), (d_u, 0), (pre_conv, 0),
@@ -1789,23 +1818,20 @@
             float(length * ring * width),
         ),
         "unpack", ring,
-        [(mine_s, SMEM), (done, 0), (share_experts, None)],
+        [(mine_s, SMEM), (done, 0), (share_experts, None), (last_s, SMEM), (d_n1_terms, None),
+         (d_edges, None), (tokens[0], None), (gains, None), (d_h1, None), (result, None)],
         [((width, 2 * local), F32, of_rows), ((local, width), F32, of_rows),
          ((width, w_down.shape[1]), F32, None), ((w_down.shape[1], width), F32, None),
          ((taps, local), F32, None), ((w_x.shape[1], local), F32, None), ((ranked, local), F32, None),
-         ((states, local), F32, None), ((2 * SEG, padded), F32, None), ((1, LANE), F32, None)],
-        [f32_vmem(ring * small_each, padded), f32_vmem(SEG, padded)], 8,
-    )
-    share_in, share_out, share_up, share_down, g_taps, g_wx, g_wdt, g_a, vecs, stats = unpacked
+         ((states, local), F32, None), ((2 * SEG, padded), F32, None), ((1, LANE), F32, None),
+         (row_f, F32, None), (row_f, F32, None)],
+        [f32_vmem(ring * small_each, padded), f32_vmem(SEG, padded), f32_vmem(length, width), order_vmem],
+        9,
+    )
+    share_in, share_out, share_up, share_down, g_taps, g_wx, g_wdt, g_a, vecs, stats, input_grad, layer_out = unpacked
     fulls, vecs = vecs[:SEG, :share], vecs[SEG:, :local]
-    (input_grad,) = call(
-        functools.partial(leave_kernel, taps), "leave", 1,
-        [(last_s, SMEM), (d_n1_terms, None), (d_edges, None), (tokens[0], None), (gains, None),
-         (d_h1, None)],
-        [(row_f, F32, None)], [f32_vmem(length, width), order_vmem], 4,
-    )
     return (
-        result[None],
+        layer_out[None],
         input_grad[None],
         fulls[0],
         share_in,

time: 436 us -> 409 us (0.938)
  Pallas kernels: 394 us -> 373 us
  local copies, waits for them, and re-layouts: 26.4 us -> 20.2 us
    pallas_call x2 -> x1, Pallas kernels: 51.6 us -> 28.9 us  [gather_all(): pl.pallas_call(functools.partial(gather_kernel, axis, count, arrays), out...]
    pallas_call x4 -> x3, Pallas kernels: 124 us -> 111 us  [the longest x1 82.8 us: middle(): pl.pallas_call(functools.partial(middle_kernel, experts, group, chunks),...]
    pallas_call x1 -> x2, Pallas kernels: 10.8 us -> 20.2 us  [sum_all(): pl.pallas_call(functools.partial(sum_all_kernel, group), out_shape=jax.Sh...]
    unnamed x154 -> x142, local copies, waits for them, and re-layouts: 23.3 us -> 17 us
    pallas_call x14 -> x11, Pallas kernels: 99.7 us -> 104 us  [call(): pl.pallas_call(kernel, grid=(grid,), out_shape=[jax.ShapeDtypeStruct(shap...]
  transfers between devices with their start and end apart: 2 -> 2, of which waited for: 0 -> 0; matrix products, arithmetic and copies ran while one was open for 0% -> 0% of each run, Pallas kernels for 75% -> 68%
where the time goes in v5:
time: 409 us
  Pallas kernels  373 us (91%)
  local copies, waits for them, and re-layouts  20.2 us (5%)
  between operations  15 us (4%)
    pallas_call x11, Pallas kernels, call(): pl.pallas_call(kernel, grid=(grid,), out_shape=[jax.ShapeDtypeStruct(shap...  104 us
    pallas_call x1, Pallas kernels, middle(): pl.pallas_call(functools.partial(middle_kernel, experts, group, chunks),...  82.8 us
    pallas_call x1, Pallas kernels, finish(): pl.pallas_call(functools.partial(finish_kernel, ring, group, in_rows, sma...  63 us
    pallas_call x1, Pallas kernels, start(): pl.pallas_call(functools.partial(start_kernel, ring, group), out_shape=[j...  46.5 us
    pallas_call x1, Pallas kernels, gather_all(): pl.pallas_call(functools.partial(gather_kernel, axis, count, arrays), out...  28.9 us
    pallas_call x2, Pallas kernels, carry(): pl.pallas_call(functools.partial(carry_kernel, ring, arrays, len(xs) - ar...  28.3 us
    pallas_call x2, Pallas kernels, sum_all(): pl.pallas_call(functools.partial(sum_all_kernel, group), out_shape=jax.Sh...  20.2 us
    unnamed x142, local copies, waits for them, and re-layouts  17 us
  transfers between devices with their start and end apart: 2, of which 0 were waited for; matrix products, arithmetic and copies ran while one was open for 0% of the time, Pallas kernels for 68%

profile of v5, /device:TPU:11, one launch (start us, length us, event | category | flops | bytes accessed | tf_op | source)
XLA Modules:
  0.0 408.8 jit_solution(16742671398146787654)
XLA Ops:
  7.2 3.3 pack.1
  11.5 1.2 dynamic-slice_bitcast_fusion.1
  12.8 46.5 %start.1 = (bf16[4,128,1152]{2,1,0:T(8,128)(2,1)S(1)}, bf16[4,16,1152]{2,1,0:T(8,128)(2,1)S(1)}, bf16[4,16,384]{2,1,0:T(8,128)(2,1)S(1)}, s32[4,8,128]{2,1,0:T(8,128)S(1)}, bf16[2,8,144,640]{3,2,1,0:T(8,128)(2,1)S(1)}) custom-call(bf16[128,1152]{1,0:T(8,128)(2,1)S(1)} %bitcast.29, bf16[16,384]{1,0:T(8,128)(2,1)S(1)} %pad.17.par.own, s32[8,128]{1,0:T(8,128)S(1)} %pad.18.doc, ...), custom_call_target="tpu_custom_call" | custom-call | flops 38499999744 | bytes 122500000 | tf_op jit(solution)/shard_map/start/pallas_call | solution.py:622
  59.6 1.3 copy-done.10
  60.9 6.4 %enter.1 = (bf16[4,144,1152]{2,1,0:T(8,128)(2,1)S(1)}, f32[4,152,640]{2,1,0:T(8,128)S(1)}, f32[4,128,640]{2,1,0:T(8,128)S(1)}, f32[4,128,640]{2,1,0:T(8,128)S(1)...) custom-call(s32[1]{0:T(128)} %bitcast.1.place_ref, ...), custom_call_target="tpu_custom_call" | custom-call | flops 8800000000 | bytes 28000000 | tf_op jit(solution)/shard_map/enter/pallas_call | solution.py:1634
  68.2 10.8 %sum_all.2.proj_i.proj = bf16[4,128,128]{2,1,0:T(8,128)(2,1)S(1)} custom-call(bf16[4,128,128]{2,1,0:T(8,128)(2,1)S(1)} %get-tuple-element.101.x_ref), custom_call_target="tpu_custom_call" | custom-call | flops 12099999744 | bytes 38500000 | tf_op jit(solution)/shard_map/sum_all/pallas_call | solution.py:143
  79.1 8.1 %scan_summary.1 = (f32[4,128,640]{2,1,0:T(8,128)S(1)}, f32[4,128,640]{2,1,0:T(8,128)S(1)}, f32[4,16,8,640]{3,2,1,0:T(8,128)S(1)}, f32[4,8,640]{2,1,0:T(8,128)S(1...) custom-call(bf16[4,128,128]{2,1,0:T(8,128)(2,1)S(1)} %sum_all.2.proj_i.proj, ...), custom_call_target="tpu_custom_call" | custom-call | flops 11000000512 | bytes 35000000 | tf_op jit(solution)/shard_map/scan_summary/pallas_call | solution.py:1634
  87.2 14.9 %carry_3.1 = (bf16[8,4,16,640]{3,2,1,0:T(8,128)(2,1)S(1)}, f32[8,4,1,640]{3,2,1,0:T(1,128)S(1)}) custom-call(bf16[4,16,640]{2,1,0:T(8,128)(2,1)S(1)} %get-tuple-element.111.refs_0_, f32[4,1,640]{2,1,0:T(1,128)S(1)} %get-tuple-element.112.refs_1_), custom_call_target="tpu_custom_call" | custom-call | flops 11000000512 | bytes 35000000 | tf_op jit(solution)/shard_map/carry_3/pallas_call | solution.py:259
  102.2 12.1 %scan_output.1 = (f32[4,128,640]{2,1,0:T(8,128)S(1)}, bf16[4,128,640]{2,1,0:T(8,128)(2,1)S(1)}, bf16[4,128,1152]{2,1,0:T(8,128)(2,1)S(1)}, f32[4,16,640]{2,1,0:T(8,128)S(1)}) custom-call(s32[1]{0:T(128)} %bitcast.1.place_ref, bf16[4,128,128]{2,1,0:T(8,128)(2,1)S(1)} %sum_all.2.proj_i.proj, f32[4,128,640]{2,1,0:T(8,128)S(1)} %get-tuple-element.107.step_i, ...), custom_call_target="tpu_custom_call" | custom-call | flops 14300000256 | bytes 45500000 | tf_op jit(solution)/shard_map/scan_output/pallas_call | solution.py:1634
  117.1 1.3 copy-done.43
  118.4 82.8 %middle.1 = (bf16[3072,2304]{1,0:T(8,128)(2,1)}, f32[128,1152]{1,0:T(8,128)S(1)}, f32[128,1152]{1,0:T(8,128)S(1)}, bf16[128,1152]{1,0:T(8,128)(2,1)S(1)}, f32[12...) custom-call(bf16[4,128,1152]{2,1,0:T(8,128)(2,1)S(1)} %copy-done.43, ...), custom_call_target="tpu_custom_call" | custom-call | flops 93499998208 | bytes 297500000 | tf_op jit(solution)/shard_map/middle/pallas_call | solution.py:1302
  205.1 28.9 %gather_7.1.d_mix = bf16[4,128,1152]{2,1,0:T(8,128)(2,1)S(1)} custom-call(bf16[128,1152]{1,0:T(8,128)(2,1)S(1)} %copy-done.61), custom_call_target="tpu_custom_call" | custom-call | flops 30799998976 | bytes 98000000 | tf_op jit(solution)/shard_map/gather_7/pallas_call | solution.py:159
  234.1 10.8 %gate_back.1 = (f32[4,128,640]{2,1,0:T(8,128)S(1)}, bf16[4,144,640]{2,1,0:T(8,128)(2,1)S(1)}, f32[1,640]{1,0:T(1,128)S(1)}, f32[4,16,8,640]{3,2,1,0:T(8,128)S(1)...) custom-call(bf16[4,128,1152]{2,1,0:T(8,128)(2,1)S(1)} %gather_7.1.d_mix, bf16[640,1152]{1,0:T(8,128)(2,1)S(1)} %copy-done.13, ...), custom_call_target="tpu_custom_call" | custom-call | flops 12099999744 | bytes 38500000 | tf_op jit(solution)/shard_map/gate_back/pallas_call | solution.py:1634
  244.8 2.4 pack_zo.1.refs_1_.g_ref
  247.4 13.4 %carry_8.1 = (bf16[8,4,16,640]{3,2,1,0:T(8,128)(2,1)S(1)}, bf16[4,144,1280]{2,1,0:T(8,128)(2,1)S(1)}) custom-call(bf16[4,16,640]{2,1,0:T(8,128)(2,1)S(1)} %get-tuple-element.125.refs_0_, bf16[4,2,144,1280]{3,2,1,0:T(8,128)(2,1)S(1)} %pack_zo.1.refs_1_.g_ref), custom_call_target="tpu_custom_call" | custom-call | flops 11000000512 | bytes 35000000 | tf_op jit(solution)/shard_map/carry_8/pallas_call | solution.py:259
  260.9 42.3 %scan_back.1 = (bf16[4,128,128]{2,1,0:T(8,128)(2,1)S(1)}, f32[4,128,640]{2,1,0:T(8,128)S(1)}, f32[128,640]{1,0:T(8,128)S(1)}, f32[1,640]{1,0:T(1,128)S(1)}, f32[...) custom-call(bf16[4,128,128]{2,1,0:T(8,128)(2,1)S(1)} %copy-done.51, f32[4,128,640]{2,1,0:T(8,128)S(1)} %copy-done.31, ...), custom_call_target="tpu_custom_call" | custom-call | flops 37399998464 | bytes 119000000 | tf_op jit(solution)/shard_map/scan_back/pallas_call | solution.py:1634
  303.3 9.4 %sum_all.3.proj_i = bf16[4,128,128]{2,1,0:T(8,128)(2,1)S(1)} custom-call(bf16[4,128,128]{2,1,0:T(8,128)(2,1)S(1)} %get-tuple-element.130.x_ref), custom_call_target="tpu_custom_call" | custom-call | flops 12099999744 | bytes 38500000 | tf_op jit(solution)/shard_map/sum_all/pallas_call | solution.py:143
  312.8 7.3 %conv_back.1 = (bf16[4,144,640]{2,1,0:T(8,128)(2,1)S(1)}, bf16[4,144,1152]{2,1,0:T(8,128)(2,1)S(1)}, f32[8,640]{1,0:T(8,128)S(1)}, f32[128,640]{1,0:T(8,128)S(1)}, f32[1,1152]{1,0:T(1,128)S(1)}) custom-call(s32[1]{0:T(128)} %bitcast.1.place_ref, s32[4,8,128]{2,1,0:T(8,128)S(1)} %copy-done.59, bf16[4,128,128]{2,1,0:T(8,128)(2,1)S(1)} %sum_all.3.proj_i, ...), custom_call_target="tpu_custom_call" | custom-call | flops 11000000512 | bytes 35000000 | tf_op jit(solution)/shard_map/conv_back/pallas_call | solution.py:1634
  320.1 1.6 pack_rest.1.g_ref
  321.8 63.0 %finish.1 = (bf16[8,480,640]{2,1,0:T(8,128)(2,1)S(1)}, bf16[4,144,1152]{2,1,0:T(8,128)(2,1)S(1)}, bf16[4,16,1152]{2,1,0:T(8,128)(2,1)S(1)}) custom-call(bf16[4,2,192,640]{3,2,1,0:T(8,128)(2,1)S(1)} %pack_rest.1.g_ref, bf16[144,1280]{1,0:T(8,128)(2,1)S(1)} %get-tuple-element.147.zf_ref, bf16[4,144,1152]{2,1,0:T(8,128)(2,1)S(1)} %get-tuple-element.148.d_ref), custom_call_target="tpu_custom_call" | custom-call | flops 65999998976 | bytes 210000000 | tf_op jit(solution)/shard_map/finish/pallas_call | solution.py:459
  384.8 2.2 copy-done.14
  387.1 1.5 copy-done
  388.6 2.4 copy-done.15
  391.0 9.1 %unpack.1 = (f32[1152,1152]{1,0:T(8,128)}, f32[576,1152]{1,0:T(8,128)}, f32[1152,384]{1,0:T(8,128)}, f32[384,1152]{1,0:T(8,128)}, f32[4,576]{1,0:T(4,128)}, /*in...) custom-call(s32[1]{0:T(128)} %bitcast.mine_ref, ...), custom_call_target="tpu_custom_call" | custom-call | flops 9900000256 | bytes 31500000 | tf_op jit(solution)/shard_map/unpack/pallas_call | solution.py:1634
  (153 shorter events, 10.8 us)
Async XLA Ops:
  7.2 109.9 %all-gather.2.cloned.1.call-start = ((), (), s32[]{:S(2)}) async-start(), calls=%async_computation.1 | async-start | bytes 15925248 | tf_op jit(solution)/shard_map/all_gather | solution.py:1688
  10.6 376.5 %reduce-scatter.2.cloned.1.call-start = ((), (), s32[]{:S(2)}) async-start(), calls=%async_computation.2 | async-start | bytes 15925248 | tf_op jit(solution)/shard_map/reduce_scatter | solution.py:1754
  12.8 46.6 %copy-start.1 = (bf16[576,1152]{1,0:T(8,128)(2,1)S(1)}, bf16[576,1152]{1,0:T(8,128)(2,1)}, u32[]{:S(2)}) copy-start(bf16[576,1152]{1,0:T(8,128)(2,1)} %wout.1) | copy-start | bytes 3981316
  12.8 46.6 %copy-start.4 = (bf16[576,104]{0,1:T(8,128)(2,1)S(1)}, bf16[576,104]{0,1:T(8,128)(2,1)}, u32[]{:S(2)}) copy-start(bf16[576,104]{0,1:T(8,128)(2,1)} %param.28) | copy-start | bytes 359428
  12.8 46.5 %copy-start.5 = (bf16[72,576]{1,0:T(8,128)(2,1)S(1)}, bf16[72,576]{1,0:T(8,128)(2,1)}, u32[]{:S(2)}) copy-start(bf16[72,576]{1,0:T(8,128)(2,1)} %wdt.1) | copy-start | bytes 248836
  12.8 46.5 %copy-start.6 = (bf16[16,576]{1,0:T(8,128)(2,1)S(1)}, bf16[16,576]{1,0:T(8,128)(2,1)}, u32[]{:S(2)}) copy-start(bf16[16,576]{1,0:T(8,128)(2,1)} %a_log.1) | copy-start | bytes 55300
  12.8 46.5 %copy-start.7 = (bf16[4,576]{1,0:T(4,128)(2,1)S(1)}, bf16[4,576]{1,0:T(4,128)(2,1)}, u32[]{:S(2)}) copy-start(bf16[4,576]{1,0:T(4,128)(2,1)} %conv_w.1) | copy-start | bytes 13828
  59.6 19.5 %copy-start.24 = (bf16[128,640]{1,0:T(8,128)(2,1)}, bf16[128,640]{1,0:T(8,128)(2,1)S(1)}, u32[]{:S(2)}) copy-start(bf16[128,640]{1,0:T(8,128)(2,1)S(1)} %get-tuple-element.102.wdt) | copy-start | bytes 491524
  59.6 42.5 %copy-start.12 = (bf16[640,1152]{1,0:T(8,128)(2,1)}, bf16[640,1152]{1,0:T(8,128)(2,1)S(1)}, u32[]{:S(2)}) copy-start(bf16[640,1152]{1,0:T(8,128)(2,1)S(1)} %get-tuple-element.116.wout) | copy-start | bytes 4423684
  59.6 42.5 %copy-start.48 = (f32[8,640]{1,0:T(8,128)}, f32[8,640]{1,0:T(8,128)S(1)}, u32[]{:S(2)}) copy-start(f32[8,640]{1,0:T(8,128)S(1)} %get-tuple-element.103.bias.skip) | copy-start | bytes 61444
  68.2 33.9 %copy-start.20 = (f32[4,128,640]{2,1,0:T(8,128)}, f32[4,128,640]{2,1,0:T(8,128)S(1)}, u32[]{:S(2)}) copy-start(f32[4,128,640]{2,1,0:T(8,128)S(1)} %get-tuple-element.104.uf) | copy-start | bytes 3932164
  68.2 33.9 %copy-start.28 = (bf16[4,128,640]{2,1,0:T(8,128)(2,1)}, bf16[4,128,640]{2,1,0:T(8,128)(2,1)S(1)}, u32[]{:S(2)}) copy-start(bf16[4,128,640]{2,1,0:T(8,128)(2,1)S(1)} %get-tuple-element.115.z) | copy-start | bytes 1966084
  68.2 33.9 %copy-start.44 = (f32[4,128,128]{2,1,0:T(8,128)}, f32[4,128,128]{2,1,0:T(8,128)S(1)}, u32[]{:S(2)}) copy-start(f32[4,128,128]{2,1,0:T(8,128)S(1)} %get-tuple-element.105.cut) | copy-start | bytes 786436
  79.0 23.1 %copy-start.50 = (bf16[4,128,128]{2,1,0:T(8,128)(2,1)}, bf16[4,128,128]{2,1,0:T(8,128)(2,1)S(1)}, u32[]{:S(2)}) copy-start(bf16[4,128,128]{2,1,0:T(8,128)(2,1)S(1)} %sum_all.2.proj_i.proj) | copy-start | bytes 393220
  87.2 15.0 %copy-start.30 = (f32[4,128,640]{2,1,0:T(8,128)}, f32[4,128,640]{2,1,0:T(8,128)S(1)}, u32[]{:S(2)}) copy-start(f32[4,128,640]{2,1,0:T(8,128)S(1)} %get-tuple-element.107.step_i) | copy-start | bytes 3932164
  205.0 29.0 %copy-start.13 = (bf16[640,1152]{1,0:T(8,128)(2,1)S(1)}, bf16[640,1152]{1,0:T(8,128)(2,1)}, u32[]{:S(2)}) copy-start(bf16[640,1152]{1,0:T(8,128)(2,1)} %copy-done.12) | copy-start | bytes 4423684
  205.0 29.0 %copy-start.21 = (f32[4,128,640]{2,1,0:T(8,128)S(1)}, f32[4,128,640]{2,1,0:T(8,128)}, u32[]{:S(2)}) copy-start(f32[4,128,640]{2,1,0:T(8,128)} %copy-done.20) | copy-start | bytes 3932164
  205.0 29.0 %copy-start.29 = (bf16[4,128,640]{2,1,0:T(8,128)(2,1)S(1)}, bf16[4,128,640]{2,1,0:T(8,128)(2,1)}, u32[]{:S(2)}) copy-start(bf16[4,128,640]{2,1,0:T(8,128)(2,1)} %copy-done.28) | copy-start | bytes 1966084
  205.1 29.0 %copy-start.31 = (f32[4,128,640]{2,1,0:T(8,128)S(1)}, f32[4,128,640]{2,1,0:T(8,128)}, u32[]{:S(2)}) copy-start(f32[4,128,640]{2,1,0:T(8,128)} %copy-done.30) | copy-start | bytes 3932164
  205.1 29.0 %copy-start.33 = (f32[4,128,640]{2,1,0:T(8,128)S(1)}, f32[4,128,640]{2,1,0:T(8,128)}, u32[]{:S(2)}) copy-start(f32[4,128,640]{2,1,0:T(8,128)} %copy-done.32) | copy-start | bytes 3932164
  205.1 29.0 %copy-start.45 = (f32[4,128,128]{2,1,0:T(8,128)S(1)}, f32[4,128,128]{2,1,0:T(8,128)}, u32[]{:S(2)}) copy-start(f32[4,128,128]{2,1,0:T(8,128)} %copy-done.44) | copy-start | bytes 786436
  205.1 29.0 %copy-start.51 = (bf16[4,128,128]{2,1,0:T(8,128)(2,1)S(1)}, bf16[4,128,128]{2,1,0:T(8,128)(2,1)}, u32[]{:S(2)}) copy-start(bf16[4,128,128]{2,1,0:T(8,128)(2,1)} %copy-done.50) | copy-start | bytes 393220
  321.8 65.3 %copy-start.39 = (f32[128,1152]{1,0:T(8,128)S(1)}, f32[128,1152]{1,0:T(8,128)}, u32[]{:S(2)}) copy-start(f32[128,1152]{1,0:T(8,128)} %copy-done.38) | copy-start | bytes 1769476
  321.8 65.3 %copy-start.41 = (f32[128,1152]{1,0:T(8,128)S(1)}, f32[128,1152]{1,0:T(8,128)}, u32[]{:S(2)}) copy-start(f32[128,1152]{1,0:T(8,128)} %copy-done.40) | copy-start | bytes 1769476
  (49 other events, 333.0 us)
Sparse Core Ops, SparseCore 0:
  10.8 100.0 all-gather.1
  204.2 121.5 reduce-scatter.1

commit v6 on v5

--- a/solution.py
+++ b/solution.py
@@ -306,8 +306,11 @@
 
     to_pair = remote(g_ref.at[:, 1 - lane], from_pair, pair_s, pair_r, {"ctx": pair})
     to_pair.start()
-    ready = 2 * in_rows + small_rows + 16
-    parts = [pl.ds(ready, in_rows), pl.ds(0, ready)]
+    small_at = 2 * in_rows + 16
+    parts = [
+        pl.ds(small_at + small_rows, in_rows), pl.ds(small_at, small_rows),
+        pl.ds(0, in_rows), pl.ds(in_rows, in_rows + 16),
+    ]
     fin[parts[0]] = zf_ref[:, lanes:]
     stored = []
 
@@ -395,22 +398,30 @@
         copy = remote(own.at[tile], tiles.at[k], tile_s.at[k], tile_r.at[k], {"wa": who})
         copy.start()
         spread_tiles.append(copy)
+    fin[parts[1]] = own[pl.ds(in_rows, small_rows)]
+    middle_rows = to_all(1)
     forward(0, early)
-    fin[pl.ds(2 * in_rows, small_rows)] = own[pl.ds(in_rows, small_rows)]
+
+    def landed(slot):
+        pltpu.make_async_copy(zin.at[slot], zin.at[slot], z_r.at[slot]).wait()
+        fin[pl.ds(slot * in_rows, in_rows)] = zin[slot]
+
+    landed(0)
+    late = [to_all(2)]
+    forward(1, middle_rows)
     for copy in spread_tiles:
         copy.wait_recv()
     add_rows(
-        fin.at[pl.ds(2 * in_rows + small_rows, 16)],
+        fin.at[pl.ds(2 * in_rows, 16)],
         [own.at[tile]] + [tiles.at[k] for k in range(group - 1)],
         16,
     )
-    for s in range(2):
-        pltpu.make_async_copy(zin.at[s], zin.at[s], z_r.at[s]).wait()
-        fin[pl.ds(s * in_rows, in_rows)] = zin[s]
-    late = to_all(1)
+    landed(1)
+    late.append(to_all(3))
     trade_rows(1)
     kept.wait()
-    forward(1, late)
+    forward(2, late[0])
+    forward(3, late[1])
 
     for copy in trades:
         copy.wait_recv()
@@ -421,14 +432,14 @@
     def _():
         to_last.start()
 
-    for copies in (early, late):
+    for copies in [early, middle_rows] + late:
         for copy in copies[half - 1 :]:
             copy.wait_recv()
 
     for copy in stored:
         copy.wait()
     to_pair.wait_send()
-    for copy in scattered + spread_tiles + early + late + trades:
+    for copy in scattered + spread_tiles + early + middle_rows + late[0] + late[1] + trades:
         copy.wait_send()
 
     @pl.when(x_to != mine)
@@ -473,13 +484,13 @@
             pltpu.VMEM((2, in_rows, lanes), BF16),
             pltpu.VMEM((group - 1, 16, lanes), BF16),
             pltpu.VMEM((out_rows, lanes), BF16),
-            dma((2,)), dma, dma,
+            dma((4,)), dma, dma,
             dma((half - 1,)), dma((half - 1,)),
             dma((2,)), dma((2,)),
             dma((group - 1,)), dma((group - 1,)),
             dma((2, group - 1)), dma((2, group - 1)), dma,
-            dma((2, half - 1)), dma((2, half - 1)),
-            dma((2, half)), dma((2, half)),
+            dma((4, half - 1)), dma((4, half - 1)),
+            dma((4, half)), dma((4, half)),
             dma, dma,
         ],
         compiler_params=pltpu.CompilerParams(
@@ -1121,14 +1132,14 @@
     def _():
         rows = done[0, :base, :].astype(F32)
         in_o[...] = jnp.concatenate([rows[:in_rows, :local], rows[in_rows:, :local]], axis=1)
-        low = base + small_rows + 16
+        low = base + 16 + small_rows
         rows = done[0, low : low + in_rows, :].astype(F32)
         half = in_rows // 2
         out_o[...] = jnp.concatenate([rows[:half, :local], rows[half:, :local]], axis=1)
 
-    small = done[0, base : base + small_rows, :].astype(F32)
+    small = done[0, base + 16 : base + 16 + small_rows, :].astype(F32)
     small_s[pl.ds(pl.multiple_of(c * small_each, SEG), small_each), :] = small[:small_each]
-    tile = done[0, base + small_rows : base + small_rows + 16, :].astype(F32)
+    tile = done[0, base : base + 16, :].astype(F32)
     row = lax.broadcasted_iota(jnp.int32, tile.shape, 0)
     own = jnp.sum(jnp.where(row == mine_ref[0], tile, 0.0), axis=0, keepdims=True)
     spot = lax.broadcasted_iota(jnp.int32, full_s.shape, 0)
@@ -1160,6 +1171,7 @@
     experts, group, chunks,
     mix_ref, tok, gain, router, route, keep, grad, w_ref,
     g_ref, layer_o, dh_o, dmix_o, router_o, gain_o, sums_o, mix_o,
+    layer_s, dh_s, dmix_s, leave_sem,
     mix_s, h1_s, n2_s, up_s, cols_s, match_s, x_ref, r_ref,
     got, w_s, g_s, act_s, slope_s, pre_s, acc, out_s,
     w_sem, g_sem, s0, r0, own0, s1, r1, own1, s2, r2, own2,
@@ -1279,8 +1291,16 @@
         copy.wait()
     combine_kernel(
         experts, r_ref, match_s, h1_s, n2_s, up_s, cols_s, gain, router,
-        layer_o, dh_o, dmix_o, router_o, gain_o, sums_o,
-    )
+        layer_s, dh_s, dmix_s, router_o, gain_o, sums_o,
+    )
+    leaving = [
+        pltpu.make_async_copy(src, dst, leave_sem.at[i])
+        for i, (src, dst) in enumerate(((dmix_s, dmix_o), (dh_s, dh_o), (layer_s, layer_o)))
+    ]
+    for copy in leaving:
+        copy.start()
+    for copy in leaving:
+        copy.wait()
 
 
 def middle(experts, mix_part, tok, gains, router, route, keep, grad, w, chunks, cid, us):
@@ -1292,6 +1312,7 @@
     dma = pltpu.SemaphoreType.DMA
     hbm = pl.BlockSpec(memory_space=pltpu.HBM)
     vmem = pl.BlockSpec(memory_space=pltpu.VMEM)
+    anywhere = pl.BlockSpec(memory_space=pl.ANY)
     two = dma((2, group - 1))
     one = dma((group - 1,))
     rows = pltpu.VMEM((2, group, slots // group, width), BF16)
@@ -1302,9 +1323,11 @@
     return pl.pallas_call(
         functools.partial(middle_kernel, experts, group, chunks),
         out_shape=[jax.ShapeDtypeStruct(shape, dtype) for shape, dtype in shapes],
-        in_specs=[vmem] * 7 + [hbm],
-        out_specs=[hbm] + [vmem] * 7,
+        in_specs=[anywhere] + [vmem] * 6 + [hbm],
+        out_specs=[hbm] + [anywhere] * 3 + [vmem] * 4,
         scratch_shapes=[
+            pltpu.VMEM((length, width), F32), pltpu.VMEM((length, width), F32),
+            pltpu.VMEM((length, width), BF16), dma((3,)),
             pltpu.VMEM(mix_part.shape, BF16),
             pltpu.VMEM((length, width), F32),
             pltpu.VMEM((length, width), BF16),

time: 409 us -> 400 us (0.978)
  Pallas kernels: 373 us -> 364 us
    pallas_call x1, Pallas kernels: 63 us -> 53.1 us  [finish(): pl.pallas_call(functools.partial(finish_kernel, ring, group, in_rows, sma...]
  transfers between devices with their start and end apart: 2 -> 2, of which waited for: 0 -> 0; matrix products, arithmetic and copies ran while one was open for 0% -> 0% of each run, Pallas kernels for 68% -> 67%
where the time goes in v6:
time: 400 us; the launch traced here: 399 us
  Pallas kernels  364 us (91%)
  local copies, waits for them, and re-layouts  20.2 us (5%)
  between operations  15 us (4%)
    pallas_call x11, Pallas kernels, call(): pl.pallas_call(kernel, grid=(grid,), out_shape=[jax.ShapeDtypeStruct(shap...  104 us
    pallas_call x1, Pallas kernels, middle(): pl.pallas_call(functools.partial(middle_kernel, experts, group, chunks),...  83.1 us
    pallas_call x1, Pallas kernels, finish(): pl.pallas_call(functools.partial(finish_kernel, ring, group, in_rows, sma...  53.1 us
    pallas_call x1, Pallas kernels, start(): pl.pallas_call(functools.partial(start_kernel, ring, group), out_shape=[j...  46.5 us
    pallas_call x1, Pallas kernels, gather_all(): pl.pallas_call(functools.partial(gather_kernel, axis, count, arrays), out...  28.9 us
    pallas_call x2, Pallas kernels, carry(): pl.pallas_call(functools.partial(carry_kernel, ring, arrays, len(xs) - ar...  28.3 us
    pallas_call x2, Pallas kernels, sum_all(): pl.pallas_call(functools.partial(sum_all_kernel, group), out_shape=jax.Sh...  20.2 us
    unnamed x142, local copies, waits for them, and re-layouts  17 us
  transfers between devices with their start and end apart: 2, of which 0 were waited for; matrix products, arithmetic and copies ran while one was open for 0% of the time, Pallas kernels for 67%

profile of v6, /device:TPU:11, one launch (start us, length us, event | category | flops | bytes accessed | tf_op | source)
XLA Modules:
  0.0 399.2 jit_solution(2881399486483903403)
XLA Ops:
  7.2 3.3 pack.1
  11.5 1.2 dynamic-slice_bitcast_fusion.1
  12.8 46.5 %start.1 = (bf16[4,128,1152]{2,1,0:T(8,128)(2,1)S(1)}, bf16[4,16,1152]{2,1,0:T(8,128)(2,1)S(1)}, bf16[4,16,384]{2,1,0:T(8,128)(2,1)S(1)}, s32[4,8,128]{2,1,0:T(8,128)S(1)}, bf16[2,8,144,640]{3,2,1,0:T(8,128)(2,1)S(1)}) custom-call(bf16[128,1152]{1,0:T(8,128)(2,1)S(1)} %bitcast.29, bf16[16,384]{1,0:T(8,128)(2,1)S(1)} %pad.17.par.own, s32[8,128]{1,0:T(8,128)S(1)} %pad.18.doc, ...), custom_call_target="tpu_custom_call" | custom-call | flops 38499999744 | bytes 122500000 | tf_op jit(solution)/shard_map/start/pallas_call | solution.py:633
  59.6 1.3 copy-done.10
  60.9 6.4 %enter.1 = (bf16[4,144,1152]{2,1,0:T(8,128)(2,1)S(1)}, f32[4,152,640]{2,1,0:T(8,128)S(1)}, f32[4,128,640]{2,1,0:T(8,128)S(1)}, f32[4,128,640]{2,1,0:T(8,128)S(1)...) custom-call(s32[1]{0:T(128)} %bitcast.1.place_ref, ...), custom_call_target="tpu_custom_call" | custom-call | flops 8800000000 | bytes 28000000 | tf_op jit(solution)/shard_map/enter/pallas_call | solution.py:1657
  68.2 10.8 %sum_all.2.proj_i.proj = bf16[4,128,128]{2,1,0:T(8,128)(2,1)S(1)} custom-call(bf16[4,128,128]{2,1,0:T(8,128)(2,1)S(1)} %get-tuple-element.101.x_ref), custom_call_target="tpu_custom_call" | custom-call | flops 12099999744 | bytes 38500000 | tf_op jit(solution)/shard_map/sum_all/pallas_call | solution.py:143
  79.1 8.1 %scan_summary.1 = (f32[4,128,640]{2,1,0:T(8,128)S(1)}, f32[4,128,640]{2,1,0:T(8,128)S(1)}, f32[4,16,8,640]{3,2,1,0:T(8,128)S(1)}, f32[4,8,640]{2,1,0:T(8,128)S(1...) custom-call(bf16[4,128,128]{2,1,0:T(8,128)(2,1)S(1)} %sum_all.2.proj_i.proj, ...), custom_call_target="tpu_custom_call" | custom-call | flops 11000000512 | bytes 35000000 | tf_op jit(solution)/shard_map/scan_summary/pallas_call | solution.py:1657
  87.2 14.9 %carry_3.1 = (bf16[8,4,16,640]{3,2,1,0:T(8,128)(2,1)S(1)}, f32[8,4,1,640]{3,2,1,0:T(1,128)S(1)}) custom-call(bf16[4,16,640]{2,1,0:T(8,128)(2,1)S(1)} %get-tuple-element.111.refs_0_, f32[4,1,640]{2,1,0:T(1,128)S(1)} %get-tuple-element.112.refs_1_), custom_call_target="tpu_custom_call" | custom-call | flops 11000000512 | bytes 35000000 | tf_op jit(solution)/shard_map/carry_3/pallas_call | solution.py:259
  102.2 12.1 %scan_output.1 = (f32[4,128,640]{2,1,0:T(8,128)S(1)}, bf16[4,128,640]{2,1,0:T(8,128)(2,1)S(1)}, bf16[4,128,1152]{2,1,0:T(8,128)(2,1)S(1)}, f32[4,16,640]{2,1,0:T(8,128)S(1)}) custom-call(s32[1]{0:T(128)} %bitcast.1.place_ref, bf16[4,128,128]{2,1,0:T(8,128)(2,1)S(1)} %sum_all.2.proj_i.proj, f32[4,128,640]{2,1,0:T(8,128)S(1)} %get-tuple-element.107.step_i, ...), custom_call_target="tpu_custom_call" | custom-call | flops 14300000256 | bytes 45500000 | tf_op jit(solution)/shard_map/scan_output/pallas_call | solution.py:1657
  117.1 1.3 copy-done.43
  118.4 83.1 %middle.1 = (bf16[3072,2304]{1,0:T(8,128)(2,1)}, f32[128,1152]{1,0:T(8,128)S(1)}, f32[128,1152]{1,0:T(8,128)S(1)}, bf16[128,1152]{1,0:T(8,128)(2,1)S(1)}, f32[12...) custom-call(bf16[4,128,1152]{2,1,0:T(8,128)(2,1)S(1)} %copy-done.43, ...), custom_call_target="tpu_custom_call" | custom-call | flops 93499998208 | bytes 297500000 | tf_op jit(solution)/shard_map/middle/pallas_call | solution.py:1323
  205.4 28.9 %gather_7.1.d_mix = bf16[4,128,1152]{2,1,0:T(8,128)(2,1)S(1)} custom-call(bf16[128,1152]{1,0:T(8,128)(2,1)S(1)} %copy-done.61), custom_call_target="tpu_custom_call" | custom-call | flops 30799998976 | bytes 98000000 | tf_op jit(solution)/shard_map/gather_7/pallas_call | solution.py:159
  234.4 10.8 %gate_back.1 = (f32[4,128,640]{2,1,0:T(8,128)S(1)}, bf16[4,144,640]{2,1,0:T(8,128)(2,1)S(1)}, f32[1,640]{1,0:T(1,128)S(1)}, f32[4,16,8,640]{3,2,1,0:T(8,128)S(1)...) custom-call(bf16[4,128,1152]{2,1,0:T(8,128)(2,1)S(1)} %gather_7.1.d_mix, bf16[640,1152]{1,0:T(8,128)(2,1)S(1)} %copy-done.13, ...), custom_call_target="tpu_custom_call" | custom-call | flops 12099999744 | bytes 38500000 | tf_op jit(solution)/shard_map/gate_back/pallas_call | solution.py:1657
  245.2 2.4 pack_zo.1.refs_1_.g_ref
  247.7 13.5 %carry_8.1 = (bf16[8,4,16,640]{3,2,1,0:T(8,128)(2,1)S(1)}, bf16[4,144,1280]{2,1,0:T(8,128)(2,1)S(1)}) custom-call(bf16[4,16,640]{2,1,0:T(8,128)(2,1)S(1)} %get-tuple-element.125.refs_0_, bf16[4,2,144,1280]{3,2,1,0:T(8,128)(2,1)S(1)} %pack_zo.1.refs_1_.g_ref), custom_call_target="tpu_custom_call" | custom-call | flops 11000000512 | bytes 35000000 | tf_op jit(solution)/shard_map/carry_8/pallas_call | solution.py:259
  261.3 42.3 %scan_back.1 = (bf16[4,128,128]{2,1,0:T(8,128)(2,1)S(1)}, f32[4,128,640]{2,1,0:T(8,128)S(1)}, f32[128,640]{1,0:T(8,128)S(1)}, f32[1,640]{1,0:T(1,128)S(1)}, f32[...) custom-call(bf16[4,128,128]{2,1,0:T(8,128)(2,1)S(1)} %copy-done.51, f32[4,128,640]{2,1,0:T(8,128)S(1)} %copy-done.31, ...), custom_call_target="tpu_custom_call" | custom-call | flops 37399998464 | bytes 119000000 | tf_op jit(solution)/shard_map/scan_back/pallas_call | solution.py:1657
  303.7 9.4 %sum_all.3.proj_i = bf16[4,128,128]{2,1,0:T(8,128)(2,1)S(1)} custom-call(bf16[4,128,128]{2,1,0:T(8,128)(2,1)S(1)} %get-tuple-element.130.x_ref), custom_call_target="tpu_custom_call" | custom-call | flops 12099999744 | bytes 38500000 | tf_op jit(solution)/shard_map/sum_all/pallas_call | solution.py:143
  313.1 7.3 %conv_back.1 = (bf16[4,144,640]{2,1,0:T(8,128)(2,1)S(1)}, bf16[4,144,1152]{2,1,0:T(8,128)(2,1)S(1)}, f32[8,640]{1,0:T(8,128)S(1)}, f32[128,640]{1,0:T(8,128)S(1)}, f32[1,1152]{1,0:T(1,128)S(1)}) custom-call(s32[1]{0:T(128)} %bitcast.1.place_ref, s32[4,8,128]{2,1,0:T(8,128)S(1)} %copy-done.59, bf16[4,128,128]{2,1,0:T(8,128)(2,1)S(1)} %sum_all.3.proj_i, ...), custom_call_target="tpu_custom_call" | custom-call | flops 11000000512 | bytes 35000000 | tf_op jit(solution)/shard_map/conv_back/pallas_call | solution.py:1657
  320.5 1.6 pack_rest.1.g_ref
  322.1 53.1 %finish.1 = (bf16[8,480,640]{2,1,0:T(8,128)(2,1)S(1)}, bf16[4,144,1152]{2,1,0:T(8,128)(2,1)S(1)}, bf16[4,16,1152]{2,1,0:T(8,128)(2,1)S(1)}) custom-call(bf16[4,2,192,640]{3,2,1,0:T(8,128)(2,1)S(1)} %pack_rest.1.g_ref, bf16[144,1280]{1,0:T(8,128)(2,1)S(1)} %get-tuple-element.147.zf_ref, bf16[4,144,1152]{2,1,0:T(8,128)(2,1)S(1)} %get-tuple-element.148.d_ref), custom_call_target="tpu_custom_call" | custom-call | flops 65999998976 | bytes 210000000 | tf_op jit(solution)/shard_map/finish/pallas_call | solution.py:470
  375.2 2.2 copy-done.14
  377.5 1.5 copy-done
  379.0 2.4 copy-done.15
  381.4 9.1 %unpack.1 = (f32[1152,1152]{1,0:T(8,128)}, f32[576,1152]{1,0:T(8,128)}, f32[1152,384]{1,0:T(8,128)}, f32[384,1152]{1,0:T(8,128)}, f32[4,576]{1,0:T(4,128)}, /*in...) custom-call(s32[1]{0:T(128)} %bitcast.mine_ref, ...), custom_call_target="tpu_custom_call" | custom-call | flops 9900000256 | bytes 31500000 | tf_op jit(solution)/shard_map/unpack/pallas_call | solution.py:1657
  (153 shorter events, 10.8 us)
Async XLA Ops:
  7.2 109.9 %all-gather.2.cloned.1.call-start = ((), (), s32[]{:S(2)}) async-start(), calls=%async_computation.1 | async-start | bytes 15925248 | tf_op jit(solution)/shard_map/all_gather | solution.py:1711
  10.6 366.9 %reduce-scatter.2.cloned.1.call-start = ((), (), s32[]{:S(2)}) async-start(), calls=%async_computation.2 | async-start | bytes 15925248 | tf_op jit(solution)/shard_map/reduce_scatter | solution.py:1777
  12.8 46.6 %copy-start.1 = (bf16[576,1152]{1,0:T(8,128)(2,1)S(1)}, bf16[576,1152]{1,0:T(8,128)(2,1)}, u32[]{:S(2)}) copy-start(bf16[576,1152]{1,0:T(8,128)(2,1)} %wout.1) | copy-start | bytes 3981316
  12.8 46.6 %copy-start.4 = (bf16[576,104]{0,1:T(8,128)(2,1)S(1)}, bf16[576,104]{0,1:T(8,128)(2,1)}, u32[]{:S(2)}) copy-start(bf16[576,104]{0,1:T(8,128)(2,1)} %param.28) | copy-start | bytes 359428
  12.8 46.5 %copy-start.5 = (bf16[72,576]{1,0:T(8,128)(2,1)S(1)}, bf16[72,576]{1,0:T(8,128)(2,1)}, u32[]{:S(2)}) copy-start(bf16[72,576]{1,0:T(8,128)(2,1)} %wdt.1) | copy-start | bytes 248836
  12.8 46.5 %copy-start.6 = (bf16[16,576]{1,0:T(8,128)(2,1)S(1)}, bf16[16,576]{1,0:T(8,128)(2,1)}, u32[]{:S(2)}) copy-start(bf16[16,576]{1,0:T(8,128)(2,1)} %a_log.1) | copy-start | bytes 55300
  12.8 46.5 %copy-start.7 = (bf16[4,576]{1,0:T(4,128)(2,1)S(1)}, bf16[4,576]{1,0:T(4,128)(2,1)}, u32[]{:S(2)}) copy-start(bf16[4,576]{1,0:T(4,128)(2,1)} %conv_w.1) | copy-start | bytes 13828
  59.6 19.5 %copy-start.24 = (bf16[128,640]{1,0:T(8,128)(2,1)}, bf16[128,640]{1,0:T(8,128)(2,1)S(1)}, u32[]{:S(2)}) copy-start(bf16[128,640]{1,0:T(8,128)(2,1)S(1)} %get-tuple-element.102.wdt) | copy-start | bytes 491524
  59.6 42.5 %copy-start.12 = (bf16[640,1152]{1,0:T(8,128)(2,1)}, bf16[640,1152]{1,0:T(8,128)(2,1)S(1)}, u32[]{:S(2)}) copy-start(bf16[640,1152]{1,0:T(8,128)(2,1)S(1)} %get-tuple-element.116.wout) | copy-start | bytes 4423684
  59.6 42.5 %copy-start.48 = (f32[8,640]{1,0:T(8,128)}, f32[8,640]{1,0:T(8,128)S(1)}, u32[]{:S(2)}) copy-start(f32[8,640]{1,0:T(8,128)S(1)} %get-tuple-element.103.bias.skip) | copy-start | bytes 61444
  68.2 33.9 %copy-start.20 = (f32[4,128,640]{2,1,0:T(8,128)}, f32[4,128,640]{2,1,0:T(8,128)S(1)}, u32[]{:S(2)}) copy-start(f32[4,128,640]{2,1,0:T(8,128)S(1)} %get-tuple-element.104.uf) | copy-start | bytes 3932164
  68.2 33.9 %copy-start.28 = (bf16[4,128,640]{2,1,0:T(8,128)(2,1)}, bf16[4,128,640]{2,1,0:T(8,128)(2,1)S(1)}, u32[]{:S(2)}) copy-start(bf16[4,128,640]{2,1,0:T(8,128)(2,1)S(1)} %get-tuple-element.115.z) | copy-start | bytes 1966084
  68.2 33.9 %copy-start.44 = (f32[4,128,128]{2,1,0:T(8,128)}, f32[4,128,128]{2,1,0:T(8,128)S(1)}, u32[]{:S(2)}) copy-start(f32[4,128,128]{2,1,0:T(8,128)S(1)} %get-tuple-element.105.cut) | copy-start | bytes 786436
  79.0 23.1 %copy-start.50 = (bf16[4,128,128]{2,1,0:T(8,128)(2,1)}, bf16[4,128,128]{2,1,0:T(8,128)(2,1)S(1)}, u32[]{:S(2)}) copy-start(bf16[4,128,128]{2,1,0:T(8,128)(2,1)S(1)} %sum_all.2.proj_i.proj) | copy-start | bytes 393220
  87.2 15.0 %copy-start.30 = (f32[4,128,640]{2,1,0:T(8,128)}, f32[4,128,640]{2,1,0:T(8,128)S(1)}, u32[]{:S(2)}) copy-start(f32[4,128,640]{2,1,0:T(8,128)S(1)} %get-tuple-element.107.step_i) | copy-start | bytes 3932164
  205.4 29.0 %copy-start.13 = (bf16[640,1152]{1,0:T(8,128)(2,1)S(1)}, bf16[640,1152]{1,0:T(8,128)(2,1)}, u32[]{:S(2)}) copy-start(bf16[640,1152]{1,0:T(8,128)(2,1)} %copy-done.12) | copy-start | bytes 4423684
  205.4 29.0 %copy-start.21 = (f32[4,128,640]{2,1,0:T(8,128)S(1)}, f32[4,128,640]{2,1,0:T(8,128)}, u32[]{:S(2)}) copy-start(f32[4,128,640]{2,1,0:T(8,128)} %copy-done.20) | copy-start | bytes 3932164
  205.4 29.0 %copy-start.29 = (bf16[4,128,640]{2,1,0:T(8,128)(2,1)S(1)}, bf16[4,128,640]{2,1,0:T(8,128)(2,1)}, u32[]{:S(2)}) copy-start(bf16[4,128,640]{2,1,0:T(8,128)(2,1)} %copy-done.28) | copy-start | bytes 1966084
  205.4 29.0 %copy-start.31 = (f32[4,128,640]{2,1,0:T(8,128)S(1)}, f32[4,128,640]{2,1,0:T(8,128)}, u32[]{:S(2)}) copy-start(f32[4,128,640]{2,1,0:T(8,128)} %copy-done.30) | copy-start | bytes 3932164
  205.4 29.0 %copy-start.33 = (f32[4,128,640]{2,1,0:T(8,128)S(1)}, f32[4,128,640]{2,1,0:T(8,128)}, u32[]{:S(2)}) copy-start(f32[4,128,640]{2,1,0:T(8,128)} %copy-done.32) | copy-start | bytes 3932164
  205.4 29.0 %copy-start.45 = (f32[4,128,128]{2,1,0:T(8,128)S(1)}, f32[4,128,128]{2,1,0:T(8,128)}, u32[]{:S(2)}) copy-start(f32[4,128,128]{2,1,0:T(8,128)} %copy-done.44) | copy-start | bytes 786436
  205.4 29.0 %copy-start.51 = (bf16[4,128,128]{2,1,0:T(8,128)(2,1)S(1)}, bf16[4,128,128]{2,1,0:T(8,128)(2,1)}, u32[]{:S(2)}) copy-start(bf16[4,128,128]{2,1,0:T(8,128)(2,1)} %copy-done.50) | copy-start | bytes 393220
  322.1 55.4 %copy-start.39 = (f32[128,1152]{1,0:T(8,128)S(1)}, f32[128,1152]{1,0:T(8,128)}, u32[]{:S(2)}) copy-start(f32[128,1152]{1,0:T(8,128)} %copy-done.38) | copy-start | bytes 1769476
  322.1 55.4 %copy-start.41 = (f32[128,1152]{1,0:T(8,128)S(1)}, f32[128,1152]{1,0:T(8,128)}, u32[]{:S(2)}) copy-start(f32[128,1152]{1,0:T(8,128)} %copy-done.40) | copy-start | bytes 1769476
  (49 other events, 333.1 us)
Sparse Core Ops, SparseCore 0:
  10.8 100.0 all-gather.1
  204.6 121.5 reduce-scatter.1

commit v7 on v6

--- a/solution.py
+++ b/solution.py
@@ -862,21 +862,35 @@
 
 
 def output_kernel(
-    states, b_at, place_ref, proj, step_i, uf, cut, a_ref, hx_ref, sx_ref, finals, sums, z, skip, wout,
-    y_o, gated_o, mix_o, e_o, bb, cb, st_s, dr_s,
+    group, states, b_at, proj, step_i, uf, cut, a_ref, hx_ref, sx_ref, finals, sums, z, skip, wout,
+    y_o, gated_o, terms_o, e_o, bb, cb, st_s, dr_s, mix_s, send, recv, own_s,
 ):
+    at = pl.program_id(0)
+    mine = lax.axis_index("wa")
+    barrier = pltpu.get_barrier_semaphore()
+    goals = [lax.rem(mine + 1 + i, group) for i in range(group - 1)]
+    sends = [
+        remote(mix_s.at[i], terms_o.at[mine], send.at[i], recv.at[i], {"wa": who})
+        for i, who in enumerate(goals)
+    ]
+
+    @pl.when(at == 0)
+    def _():
+        for who in goals:
+            hello(barrier, "wa", who)
+
     length, width = step_i.shape[1:]
     groups, steps = width // LANE, length // SEG
     bb[...] = spread(proj[0], states, b_at)
     cb[...] = spread(proj[0], states, b_at + states)
     e_ref = e_o.at[0]
-    entering(e_ref, finals, sums, a_ref, place_ref[0], True)
+    entering(e_ref, finals, sums, a_ref, lax.axis_index("ctx"), True)
     dr_s[...] = step_i[0] * uf[0]
     for g in range(groups):
         cols = slice(g * LANE, (g + 1) * LANE)
         st_s[:, cols] = step_i[0, :, cols] + cut[0]
 
-    def group(g, _):
+    def lane_group(g, _):
         lanes = lanes_of(g)
         a = [wide(a_ref, n, lanes) for n in range(states)]
         sx = sx_ref[0, :, lanes]
@@ -902,11 +916,25 @@
         lax.fori_loop(0, steps, step, first, unroll=8)
         return 0
 
-    lax.fori_loop(0, groups, group, 0)
+    lax.fori_loop(0, groups, lane_group, 0)
     zf = z[0].astype(F32)
     gated = (y_o[0] * (zf * jax.nn.sigmoid(zf))).astype(BF16)
     gated_o[0] = gated
-    mix_o[0] = dot_nn(gated, wout[...]).astype(BF16)
+    mix_s[at] = dot_nn(gated, wout[...]).astype(BF16)
+    for i, copy in enumerate(sends):
+
+        @pl.when(at == i)
+        def _():
+            if i == 0:
+                pl.semaphore_wait(barrier, group - 1)
+            copy.start()
+
+    @pl.when(at == group - 1)
+    def _():
+        kept = pltpu.make_async_copy(mix_s.at[group - 1], terms_o.at[mine], own_s)
+        kept.start()
+        for copy in sends + [kept]:
+            copy.wait()
 
 
 def route_kernel(
@@ -1172,9 +1200,9 @@
     mix_ref, tok, gain, router, route, keep, grad, w_ref,
     g_ref, layer_o, dh_o, dmix_o, router_o, gain_o, sums_o, mix_o,
     layer_s, dh_s, dmix_s, leave_sem,
-    mix_s, h1_s, n2_s, up_s, cols_s, match_s, x_ref, r_ref,
+    h1_s, n2_s, up_s, cols_s, match_s, x_ref, r_ref,
     got, w_s, g_s, act_s, slope_s, pre_s, acc, out_s,
-    w_sem, g_sem, s0, r0, own0, s1, r1, own1, s2, r2, own2,
+    w_sem, g_sem, s1, r1, own1, s2, r2, own2,
 ):
     mine, mates = mates_of(group)
     count, width = x_ref.shape[2:]
@@ -1188,17 +1216,8 @@
 
     load(0).start()
     greet("wa", group)
-    terms = []
-    for k, who in enumerate(mates):
-        copy = remote(mix_ref.at[who], mix_s.at[mine], s0.at[k], r0.at[k], {"wa": who})
-        copy.start()
-        terms.append(copy)
-    kept = pltpu.make_async_copy(mix_ref.at[mine], mix_s.at[mine], own0)
-    kept.start()
-    for copy in terms + [kept]:
-        copy.wait()
     route_kernel(
-        experts, mix_s, tok, gain, router, route, keep, grad,
+        experts, mix_ref, tok, gain, router, route, keep, grad,
         h1_s, n2_s, up_s, cols_s, match_s, x_ref, mix_o,
     )
     sent = []
@@ -1303,7 +1322,7 @@
         copy.wait()
 
 
-def middle(experts, mix_part, tok, gains, router, route, keep, grad, w, chunks, cid, us):
+def middle(experts, terms, tok, gains, router, route, keep, grad, w, chunks, cid, us):
     group = lax.axis_size("wa")
     units = w.shape[0]
     length, width = tok.shape
@@ -1314,7 +1333,6 @@
     vmem = pl.BlockSpec(memory_space=pltpu.VMEM)
     anywhere = pl.BlockSpec(memory_space=pl.ANY)
     two = dma((2, group - 1))
-    one = dma((group - 1,))
     rows = pltpu.VMEM((2, group, slots // group, width), BF16)
     shapes = [
         (w.shape, BF16), ((length, width), F32), ((length, width), F32), ((length, width), BF16),
@@ -1323,12 +1341,11 @@
     return pl.pallas_call(
         functools.partial(middle_kernel, experts, group, chunks),
         out_shape=[jax.ShapeDtypeStruct(shape, dtype) for shape, dtype in shapes],
-        in_specs=[anywhere] + [vmem] * 6 + [hbm],
+        in_specs=[vmem] * 7 + [hbm],
         out_specs=[hbm] + [anywhere] * 3 + [vmem] * 4,
         scratch_shapes=[
             pltpu.VMEM((length, width), F32), pltpu.VMEM((length, width), F32),
             pltpu.VMEM((length, width), BF16), dma((3,)),
-            pltpu.VMEM(mix_part.shape, BF16),
             pltpu.VMEM((length, width), F32),
             pltpu.VMEM((length, width), BF16),
             pltpu.VMEM((length, width), F32),
@@ -1343,14 +1360,14 @@
             pltpu.VMEM((slots, width), F32),
             rows,
             dma((2,)), dma((2,)),
-            one, one, dma, two, two, dma((2,)), two, two, dma((2,)),
+            two, two, dma((2,)), two, two, dma((2,)),
         ],
         compiler_params=pltpu.CompilerParams(
             collective_id=cid, has_side_effects=True, vmem_limit_bytes=VMEM_LIMIT + 20 * 2**20
         ),
         cost_estimate=lasting(us),
         name="middle",
-    )(mix_part, tok, gains, router, route, keep, grad, w)
+    )(terms, tok, gains, router, route, keep, grad, w)
 
 
 def combine_kernel(
@@ -1622,12 +1639,12 @@
 ANY = "any"
 
 
-def by_stream(shape, at=0):
+def by_stream(shape, at, order):
     block = tuple(1 if i == at else n for i, n in enumerate(shape))
     rank = len(shape)
 
     def index(s):
-        return tuple(s if i == at else 0 for i in range(rank))
+        return tuple(order(s) if i == at else 0 for i in range(rank))
 
     return pl.BlockSpec(block, index)
 
@@ -1636,7 +1653,7 @@
     return pl.BlockSpec(shape, lambda s: (0,) * len(shape))
 
 
-def call(kernel, name, grid, args, outs, scratch, us, cid=None, limit=VMEM_LIMIT):
+def call(kernel, name, grid, args, outs, scratch, us, cid=None, limit=VMEM_LIMIT, order=lambda s: s):
     arrays, specs = [], []
     for array, at in args:
         arrays.append(array)
@@ -1647,13 +1664,15 @@
         elif callable(at):
             specs.append(at(array.shape))
         else:
-            specs.append(whole(array.shape) if at is None else by_stream(array.shape, at))
+            specs.append(whole(array.shape) if at is None else by_stream(array.shape, at, order))
     out_specs = []
     for shape, _, at in outs:
         if callable(at):
             out_specs.append(at(shape))
+        elif at == ANY:
+            out_specs.append(pl.BlockSpec(memory_space=pl.ANY))
         else:
-            out_specs.append(whole(shape) if at is None else by_stream(shape, at))
+            out_specs.append(whole(shape) if at is None else by_stream(shape, at, order))
     return pl.pallas_call(
         kernel,
         grid=(grid,),
@@ -1762,17 +1781,20 @@
         [spread_vmem, lane_vmem, lane_vmem, state_vmem], 10,
     )
     all_h, all_s = carry([h_dev, s_dev], 3, 10)
-    y_full, gated, mix_part, e_in = call(
-        functools.partial(output_kernel, states, ranked), "scan_output", group,
-        [(place_s, SMEM), (projected, 0), (step_size, 0), (u_f, 0), (cut, 0), (a_mat, None), (h_in, 0),
+    dma = pltpu.SemaphoreType.DMA
+    y_full, gated, mix_terms, e_in = call(
+        functools.partial(output_kernel, group, states, ranked), "scan_output", group,
+        [(projected, 0), (step_size, 0), (u_f, 0), (cut, 0), (a_mat, None), (h_in, 0),
          (s_in, 0), (all_h, 1), (all_s, 1), (z, 0), (vectors, None), (wout, None)],
-        [(vec, F32, 0), (vec, BF16, 0), ((group, length, width), BF16, 0), (dev_states, F32, 0)],
-        [spread_vmem, spread_vmem, lane_vmem, lane_vmem], 13,
+        [(vec, F32, 0), (vec, BF16, 0), ((group, length, width), BF16, ANY), (dev_states, F32, 0)],
+        [spread_vmem, spread_vmem, lane_vmem, lane_vmem, pltpu.VMEM((group, length, width), BF16),
+         dma((group - 1,)), dma((group - 1,)), dma], 27, 4, VMEM_LIMIT,
+        lambda s: lax.rem(lax.axis_index("wa") + 1 + s, group),
     )
 
     row_f = (length, width)
     grad_experts, result, d_h1, d_mix_own, grad_router, grad_gain_moe, out_sums, mix_sum = middle(
-        experts, mix_part, tokens[0], gains, router, routes[0].T, keep_mask, out_grad[0], expert_w, 8, 5, 85
+        experts, mix_terms, tokens[0], gains, router, routes[0].T, keep_mask, out_grad[0], expert_w, 8, 5, 85
     )
     share_experts = lax.psum_scatter(grad_experts, "ctx", scatter_dimension=0, tiled=True)
     (d_mix,) = gather_all([d_mix_own], "wa", 7, 28)

time: 400 us -> 393 us (0.983)
  Pallas kernels: 364 us -> 357 us
    pallas_call x1, Pallas kernels: 83.1 us -> 57.2 us  [middle(): pl.pallas_call(functools.partial(middle_kernel, experts, group, chunks),...]
    pallas_call x11, Pallas kernels: 104 us -> 123 us  [call(): pl.pallas_call(kernel, grid=(grid,), out_shape=[jax.ShapeDtypeStruct(shap...]
  transfers between devices with their start and end apart: 2 -> 2, of which waited for: 0 -> 0; matrix products, arithmetic and copies ran while one was open for 0% -> 0% of each run, Pallas kernels for 67% -> 73%
where the time goes in v7:
time: 393 us
  Pallas kernels  357 us (91%)
  local copies, waits for them, and re-layouts  20.8 us (5%)
  between operations  15 us (4%)
    pallas_call x11, Pallas kernels, call(): pl.pallas_call(kernel, grid=(grid,), out_shape=[jax.ShapeDtypeStruct(shap...  123 us
    pallas_call x1, Pallas kernels, middle(): pl.pallas_call(functools.partial(middle_kernel, experts, group, chunks),...  57.2 us
    pallas_call x1, Pallas kernels, finish(): pl.pallas_call(functools.partial(finish_kernel, ring, group, in_rows, sma...  53.8 us
    pallas_call x1, Pallas kernels, start(): pl.pallas_call(functools.partial(start_kernel, ring, group), out_shape=[j...  46.5 us
    pallas_call x1, Pallas kernels, gather_all(): pl.pallas_call(functools.partial(gather_kernel, axis, count, arrays), out...  28.2 us
    pallas_call x2, Pallas kernels, carry(): pl.pallas_call(functools.partial(carry_kernel, ring, arrays, len(xs) - ar...  27.7 us
    pallas_call x2, Pallas kernels, sum_all(): pl.pallas_call(functools.partial(sum_all_kernel, group), out_shape=jax.Sh...  20 us
    unnamed x142, local copies, waits for them, and re-layouts  17.6 us
  transfers between devices with their start and end apart: 2, of which 0 were waited for; matrix products, arithmetic and copies ran while one was open for 0% of the time, Pallas kernels for 73%

profile of v7, /device:TPU:11, one launch (start us, length us, event | category | flops | bytes accessed | tf_op | source)
XLA Modules:
  0.0 392.7 jit_solution(1752345217163194929)
XLA Ops:
  7.2 3.3 pack.1
  11.5 1.2 dynamic-slice_bitcast_fusion.1
  12.8 46.5 %start.1 = (bf16[4,128,1152]{2,1,0:T(8,128)(2,1)S(1)}, bf16[4,16,1152]{2,1,0:T(8,128)(2,1)S(1)}, bf16[4,16,384]{2,1,0:T(8,128)(2,1)S(1)}, s32[4,8,128]{2,1,0:T(8,128)S(1)}, bf16[2,8,144,640]{3,2,1,0:T(8,128)(2,1)S(1)}) custom-call(bf16[128,1152]{1,0:T(8,128)(2,1)S(1)} %bitcast.29, bf16[16,384]{1,0:T(8,128)(2,1)S(1)} %pad.17.par.own, s32[8,128]{1,0:T(8,128)S(1)} %pad.18.doc, ...), custom_call_target="tpu_custom_call" | custom-call | flops 38499999744 | bytes 122500000 | tf_op jit(solution)/shard_map/start/pallas_call | solution.py:633
  59.6 1.3 copy-done.10
  60.9 6.4 %enter.1 = (bf16[4,144,1152]{2,1,0:T(8,128)(2,1)S(1)}, f32[4,152,640]{2,1,0:T(8,128)S(1)}, f32[4,128,640]{2,1,0:T(8,128)S(1)}, f32[4,128,640]{2,1,0:T(8,128)S(1)...) custom-call(s32[1]{0:T(128)} %bitcast.1.place_ref, ...), custom_call_target="tpu_custom_call" | custom-call | flops 8800000000 | bytes 28000000 | tf_op jit(solution)/shard_map/enter/pallas_call | solution.py:1676
  68.2 10.8 %sum_all.2.proj_i.proj = bf16[4,128,128]{2,1,0:T(8,128)(2,1)S(1)} custom-call(bf16[4,128,128]{2,1,0:T(8,128)(2,1)S(1)} %get-tuple-element.101.x_ref), custom_call_target="tpu_custom_call" | custom-call | flops 12099999744 | bytes 38500000 | tf_op jit(solution)/shard_map/sum_all/pallas_call | solution.py:143
  79.0 8.1 %scan_summary.1 = (f32[4,128,640]{2,1,0:T(8,128)S(1)}, f32[4,128,640]{2,1,0:T(8,128)S(1)}, f32[4,16,8,640]{3,2,1,0:T(8,128)S(1)}, f32[4,8,640]{2,1,0:T(8,128)S(1...) custom-call(bf16[4,128,128]{2,1,0:T(8,128)(2,1)S(1)} %sum_all.2.proj_i.proj, ...), custom_call_target="tpu_custom_call" | custom-call | flops 11000000512 | bytes 35000000 | tf_op jit(solution)/shard_map/scan_summary/pallas_call | solution.py:1676
  87.2 14.8 %carry_3.1 = (bf16[8,4,16,640]{3,2,1,0:T(8,128)(2,1)S(1)}, f32[8,4,1,640]{3,2,1,0:T(1,128)S(1)}) custom-call(bf16[4,16,640]{2,1,0:T(8,128)(2,1)S(1)} %get-tuple-element.111.refs_0_, f32[4,1,640]{2,1,0:T(1,128)S(1)} %get-tuple-element.112.refs_1_), custom_call_target="tpu_custom_call" | custom-call | flops 11000000512 | bytes 35000000 | tf_op jit(solution)/shard_map/carry_3/pallas_call | solution.py:259
  102.2 31.2 %scan_output.1 = (f32[4,128,640]{2,1,0:T(8,128)S(1)}, bf16[4,128,640]{2,1,0:T(8,128)(2,1)S(1)}, bf16[4,128,1152]{2,1,0:T(8,128)(2,1)S(1)}, f32[4,16,640]{2,1,0:T(8,128)S(1)}) custom-call(bf16[4,128,128]{2,1,0:T(8,128)(2,1)S(1)} %sum_all.2.proj_i.proj, f32[4,128,640]{2,1,0:T(8,128)S(1)} %get-tuple-element.107.step_i, ...), custom_call_target="tpu_custom_call" | custom-call | flops 29699999744 | bytes 94500000 | tf_op jit(solution)/shard_map/scan_output/pallas_call | solution.py:1676
  136.9 1.3 copy-done.49
  138.1 57.2 %middle.1 = (bf16[3072,2304]{1,0:T(8,128)(2,1)}, f32[128,1152]{1,0:T(8,128)S(1)}, f32[128,1152]{1,0:T(8,128)S(1)}, bf16[128,1152]{1,0:T(8,128)(2,1)S(1)}, f32[12...) custom-call(bf16[4,128,1152]{2,1,0:T(8,128)(2,1)S(1)} %copy-done.49, ...), custom_call_target="tpu_custom_call" | custom-call | flops 93499998208 | bytes 297500000 | tf_op jit(solution)/shard_map/middle/pallas_call | solution.py:1341
  199.3 28.2 %gather_7.1.d_mix = bf16[4,128,1152]{2,1,0:T(8,128)(2,1)S(1)} custom-call(bf16[128,1152]{1,0:T(8,128)(2,1)S(1)} %copy-done.59), custom_call_target="tpu_custom_call" | custom-call | flops 30799998976 | bytes 98000000 | tf_op jit(solution)/shard_map/gather_7/pallas_call | solution.py:159
  227.5 10.8 %gate_back.1 = (f32[4,128,640]{2,1,0:T(8,128)S(1)}, bf16[4,144,640]{2,1,0:T(8,128)(2,1)S(1)}, f32[1,640]{1,0:T(1,128)S(1)}, f32[4,16,8,640]{3,2,1,0:T(8,128)S(1)...) custom-call(bf16[4,128,1152]{2,1,0:T(8,128)(2,1)S(1)} %gather_7.1.d_mix, bf16[640,1152]{1,0:T(8,128)(2,1)S(1)} %copy-done.13, ...), custom_call_target="tpu_custom_call" | custom-call | flops 12099999744 | bytes 38500000 | tf_op jit(solution)/shard_map/gate_back/pallas_call | solution.py:1676
  238.3 2.4 pack_zo.1.refs_1_.g_ref
  240.8 12.9 %carry_8.1 = (bf16[8,4,16,640]{3,2,1,0:T(8,128)(2,1)S(1)}, bf16[4,144,1280]{2,1,0:T(8,128)(2,1)S(1)}) custom-call(bf16[4,16,640]{2,1,0:T(8,128)(2,1)S(1)} %get-tuple-element.125.refs_0_, bf16[4,2,144,1280]{3,2,1,0:T(8,128)(2,1)S(1)} %pack_zo.1.refs_1_.g_ref), custom_call_target="tpu_custom_call" | custom-call | flops 11000000512 | bytes 35000000 | tf_op jit(solution)/shard_map/carry_8/pallas_call | solution.py:259
  253.8 42.8 %scan_back.1 = (bf16[4,128,128]{2,1,0:T(8,128)(2,1)S(1)}, f32[4,128,640]{2,1,0:T(8,128)S(1)}, f32[128,640]{1,0:T(8,128)S(1)}, f32[1,640]{1,0:T(1,128)S(1)}, f32[...) custom-call(bf16[4,128,128]{2,1,0:T(8,128)(2,1)S(1)} %copy-done.51, f32[4,128,640]{2,1,0:T(8,128)S(1)} %copy-done.31, ...), custom_call_target="tpu_custom_call" | custom-call | flops 37399998464 | bytes 119000000 | tf_op jit(solution)/shard_map/scan_back/pallas_call | solution.py:1676
  296.7 9.2 %sum_all.3.proj_i = bf16[4,128,128]{2,1,0:T(8,128)(2,1)S(1)} custom-call(bf16[4,128,128]{2,1,0:T(8,128)(2,1)S(1)} %get-tuple-element.130.x_ref), custom_call_target="tpu_custom_call" | custom-call | flops 12099999744 | bytes 38500000 | tf_op jit(solution)/shard_map/sum_all/pallas_call | solution.py:143
  306.0 7.3 %conv_back.1 = (bf16[4,144,640]{2,1,0:T(8,128)(2,1)S(1)}, bf16[4,144,1152]{2,1,0:T(8,128)(2,1)S(1)}, f32[8,640]{1,0:T(8,128)S(1)}, f32[128,640]{1,0:T(8,128)S(1)}, f32[1,1152]{1,0:T(1,128)S(1)}) custom-call(s32[1]{0:T(128)} %bitcast.1.place_ref, s32[4,8,128]{2,1,0:T(8,128)S(1)} %copy-done.57, bf16[4,128,128]{2,1,0:T(8,128)(2,1)S(1)} %sum_all.3.proj_i, ...), custom_call_target="tpu_custom_call" | custom-call | flops 11000000512 | bytes 35000000 | tf_op jit(solution)/shard_map/conv_back/pallas_call | solution.py:1676
  313.4 1.6 pack_rest.1.g_ref
  315.0 53.8 %finish.1 = (bf16[8,480,640]{2,1,0:T(8,128)(2,1)S(1)}, bf16[4,144,1152]{2,1,0:T(8,128)(2,1)S(1)}, bf16[4,16,1152]{2,1,0:T(8,128)(2,1)S(1)}) custom-call(bf16[4,2,192,640]{3,2,1,0:T(8,128)(2,1)S(1)} %pack_rest.1.g_ref, bf16[144,1280]{1,0:T(8,128)(2,1)S(1)} %get-tuple-element.147.zf_ref, bf16[4,144,1152]{2,1,0:T(8,128)(2,1)S(1)} %get-tuple-element.148.d_ref), custom_call_target="tpu_custom_call" | custom-call | flops 65999998976 | bytes 210000000 | tf_op jit(solution)/shard_map/finish/pallas_call | solution.py:470
  368.8 2.2 copy-done.14
  371.0 1.5 copy-done
  372.5 2.4 copy-done.15
  374.9 9.1 %unpack.1 = (f32[1152,1152]{1,0:T(8,128)}, f32[576,1152]{1,0:T(8,128)}, f32[1152,384]{1,0:T(8,128)}, f32[384,1152]{1,0:T(8,128)}, f32[4,576]{1,0:T(4,128)}, /*in...) custom-call(s32[1]{0:T(128)} %bitcast.mine_ref, ...), custom_call_target="tpu_custom_call" | custom-call | flops 9900000256 | bytes 31500000 | tf_op jit(solution)/shard_map/unpack/pallas_call | solution.py:1676
  (153 shorter events, 11.4 us)
Async XLA Ops:
  7.2 129.7 %all-gather.2.cloned.1.call-start = ((), (), s32[]{:S(2)}) async-start(), calls=%async_computation.1 | async-start | bytes 15925248 | tf_op jit(solution)/shard_map/all_gather | solution.py:1730
  10.6 360.4 %reduce-scatter.2.cloned.1.call-start = ((), (), s32[]{:S(2)}) async-start(), calls=%async_computation.2 | async-start | bytes 15925248 | tf_op jit(solution)/shard_map/reduce_scatter | solution.py:1799
  12.8 46.6 %copy-start.1 = (bf16[576,1152]{1,0:T(8,128)(2,1)S(1)}, bf16[576,1152]{1,0:T(8,128)(2,1)}, u32[]{:S(2)}) copy-start(bf16[576,1152]{1,0:T(8,128)(2,1)} %wout.1) | copy-start | bytes 3981316
  12.8 46.6 %copy-start.4 = (bf16[576,104]{0,1:T(8,128)(2,1)S(1)}, bf16[576,104]{0,1:T(8,128)(2,1)}, u32[]{:S(2)}) copy-start(bf16[576,104]{0,1:T(8,128)(2,1)} %param.28) | copy-start | bytes 359428
  12.8 46.5 %copy-start.5 = (bf16[72,576]{1,0:T(8,128)(2,1)S(1)}, bf16[72,576]{1,0:T(8,128)(2,1)}, u32[]{:S(2)}) copy-start(bf16[72,576]{1,0:T(8,128)(2,1)} %wdt.1) | copy-start | bytes 248836
  12.8 46.5 %copy-start.6 = (bf16[16,576]{1,0:T(8,128)(2,1)S(1)}, bf16[16,576]{1,0:T(8,128)(2,1)}, u32[]{:S(2)}) copy-start(bf16[16,576]{1,0:T(8,128)(2,1)} %a_log.1) | copy-start | bytes 55300
  12.8 46.5 %copy-start.7 = (bf16[4,576]{1,0:T(4,128)(2,1)S(1)}, bf16[4,576]{1,0:T(4,128)(2,1)}, u32[]{:S(2)}) copy-start(bf16[4,576]{1,0:T(4,128)(2,1)} %conv_w.1) | copy-start | bytes 13828
  59.6 42.4 %copy-start.12 = (bf16[640,1152]{1,0:T(8,128)(2,1)}, bf16[640,1152]{1,0:T(8,128)(2,1)S(1)}, u32[]{:S(2)}) copy-start(bf16[640,1152]{1,0:T(8,128)(2,1)S(1)} %get-tuple-element.116.wout) | copy-start | bytes 4423684
  59.6 42.4 %copy-start.46 = (f32[8,640]{1,0:T(8,128)}, f32[8,640]{1,0:T(8,128)S(1)}, u32[]{:S(2)}) copy-start(f32[8,640]{1,0:T(8,128)S(1)} %get-tuple-element.103.bias.skip) | copy-start | bytes 61444
  68.2 33.9 %copy-start.20 = (f32[4,128,640]{2,1,0:T(8,128)}, f32[4,128,640]{2,1,0:T(8,128)S(1)}, u32[]{:S(2)}) copy-start(f32[4,128,640]{2,1,0:T(8,128)S(1)} %get-tuple-element.104.uf) | copy-start | bytes 3932164
  68.2 33.9 %copy-start.28 = (bf16[4,128,640]{2,1,0:T(8,128)(2,1)}, bf16[4,128,640]{2,1,0:T(8,128)(2,1)S(1)}, u32[]{:S(2)}) copy-start(bf16[4,128,640]{2,1,0:T(8,128)(2,1)S(1)} %get-tuple-element.115.z) | copy-start | bytes 1966084
  68.2 33.9 %copy-start.42 = (f32[4,128,128]{2,1,0:T(8,128)}, f32[4,128,128]{2,1,0:T(8,128)S(1)}, u32[]{:S(2)}) copy-start(f32[4,128,128]{2,1,0:T(8,128)S(1)} %get-tuple-element.105.cut) | copy-start | bytes 786436
  102.1 34.7 %copy-start.2 = (bf16[1,128,1152]{2,1,0:T(8,128)(2,1)S(1)}, bf16[1,128,1152]{2,1,0:T(8,128)(2,1)}, u32[]{:S(2)}) copy-start(bf16[1,128,1152]{2,1,0:T(8,128)(2,1)} %param.20) | copy-start | bytes 884740
  102.1 34.7 %copy-start.8 = (s32[1,128,1]{1,2,0:T(1,128)S(1)}, s32[1,128,1]{1,2,0:T(1,128)}, u32[]{:S(2)}) copy-start(s32[1,128,1]{1,2,0:T(1,128)} %param.22) | copy-start | bytes 1540
  102.2 34.7 %copy-start.9 = (s32[1,128]{1,0:T(1,128)S(1)}, s32[1,128]{1,0:T(1,128)}, u32[]{:S(2)}) copy-start(s32[1,128]{1,0:T(1,128)} %keep.1) | copy-start | bytes 1540
  199.3 28.2 %copy-start.13 = (bf16[640,1152]{1,0:T(8,128)(2,1)S(1)}, bf16[640,1152]{1,0:T(8,128)(2,1)}, u32[]{:S(2)}) copy-start(bf16[640,1152]{1,0:T(8,128)(2,1)} %copy-done.12) | copy-start | bytes 4423684
  199.3 28.2 %copy-start.21 = (f32[4,128,640]{2,1,0:T(8,128)S(1)}, f32[4,128,640]{2,1,0:T(8,128)}, u32[]{:S(2)}) copy-start(f32[4,128,640]{2,1,0:T(8,128)} %copy-done.20) | copy-start | bytes 3932164
  199.3 28.2 %copy-start.29 = (bf16[4,128,640]{2,1,0:T(8,128)(2,1)S(1)}, bf16[4,128,640]{2,1,0:T(8,128)(2,1)}, u32[]{:S(2)}) copy-start(bf16[4,128,640]{2,1,0:T(8,128)(2,1)} %copy-done.28) | copy-start | bytes 1966084
  199.3 28.2 %copy-start.31 = (f32[4,128,640]{2,1,0:T(8,128)S(1)}, f32[4,128,640]{2,1,0:T(8,128)}, u32[]{:S(2)}) copy-start(f32[4,128,640]{2,1,0:T(8,128)} %copy-done.30) | copy-start | bytes 3932164
  199.3 28.2 %copy-start.33 = (f32[4,128,640]{2,1,0:T(8,128)S(1)}, f32[4,128,640]{2,1,0:T(8,128)}, u32[]{:S(2)}) copy-start(f32[4,128,640]{2,1,0:T(8,128)} %copy-done.32) | copy-start | bytes 3932164
  199.3 28.2 %copy-start.43 = (f32[4,128,128]{2,1,0:T(8,128)S(1)}, f32[4,128,128]{2,1,0:T(8,128)}, u32[]{:S(2)}) copy-start(f32[4,128,128]{2,1,0:T(8,128)} %copy-done.42) | copy-start | bytes 786436
  199.3 28.2 %copy-start.51 = (bf16[4,128,128]{2,1,0:T(8,128)(2,1)S(1)}, bf16[4,128,128]{2,1,0:T(8,128)(2,1)}, u32[]{:S(2)}) copy-start(bf16[4,128,128]{2,1,0:T(8,128)(2,1)} %copy-done.50) | copy-start | bytes 393220
  315.0 56.1 %copy-start.39 = (f32[128,1152]{1,0:T(8,128)S(1)}, f32[128,1152]{1,0:T(8,128)}, u32[]{:S(2)}) copy-start(f32[128,1152]{1,0:T(8,128)} %copy-done.38) | copy-start | bytes 1769476
  315.0 56.0 %copy-start.41 = (f32[128,1152]{1,0:T(8,128)S(1)}, f32[128,1152]{1,0:T(8,128)}, u32[]{:S(2)}) copy-start(f32[128,1152]{1,0:T(8,128)} %copy-done.40) | copy-start | bytes 1769476
  (49 other events, 329.0 us)
Sparse Core Ops, SparseCore 0:
  10.8 100.0 all-gather.1
  198.4 121.0 reduce-scatter.1

commit v8 on v7

--- a/solution.py
+++ b/solution.py
@@ -1403,12 +1403,36 @@
 
 
 def gate_back_kernel(
-    states, c_at, d_mix, wout, y, z, uf, proj, step_i, cut, a_ref,
-    dy_o, dz_o, skip_o, fx_ref, tx_ref, fd_o, cb, st_s, fd_s,
+    count, states, c_at, own, wout, y, z, uf, proj, step_i, cut, a_ref,
+    dy_o, dz_o, skip_o, fx_ref, tx_ref, fd_o, mix_o, cb, st_s, fd_s, got, send, recv, own_s,
 ):
     length, width = step_i.shape[1:]
     groups, steps = width // LANE, length // SEG
-    d_gated = dot_nt(d_mix[0], wout[...])
+    at = pl.program_id(0)
+    mine = lax.axis_index("wa")
+    goals = [lax.rem(mine + k, count) for k in range(1, count)]
+    sends = [
+        remote(own, got.at[mine], send.at[k], recv.at[k], {"wa": who}) for k, who in enumerate(goals)
+    ]
+    kept = pltpu.make_async_copy(own, got.at[mine], own_s)
+
+    @pl.when(at == 0)
+    def _():
+        kept.start()
+        greet("wa", count)
+        for copy in sends:
+            copy.start()
+        kept.wait()
+
+    for k, copy in enumerate(sends):
+
+        @pl.when(at == k + 1)
+        def _():
+            copy.wait_recv()
+
+    d_mix = got[lax.rem(mine + count - at, count)]
+    mix_o[0] = d_mix
+    d_gated = dot_nt(d_mix, wout[...])
     zf = z[0].astype(F32)
     dy = d_gated * (zf * jax.nn.sigmoid(zf))
     dy_o[0] = dy
@@ -1456,6 +1480,11 @@
 
     lax.fori_loop(0, groups, group, 0)
     fd_o[0] = fd_s[...].astype(BF16)
+
+    @pl.when(at == count - 1)
+    def _():
+        for copy in sends:
+            copy.wait_send()
 
 
 def scan_back_kernel(
@@ -1797,15 +1826,16 @@
         experts, mix_terms, tokens[0], gains, router, routes[0].T, keep_mask, out_grad[0], expert_w, 8, 5, 85
     )
     share_experts = lax.psum_scatter(grad_experts, "ctx", scatter_dimension=0, tiled=True)
-    (d_mix,) = gather_all([d_mix_own], "wa", 7, 28)
-
-    d_y, d_z, grad_skip, f_in, t_in, f_dev = call(
-        functools.partial(gate_back_kernel, states, ranked + states), "gate_back", group,
-        [(d_mix, 0), (wout, None), (y_full, 0), (z, 0), (u_f, 0), (projected, 0), (step_size, 0),
+
+    d_y, d_z, grad_skip, f_in, t_in, f_dev, d_mix = call(
+        functools.partial(gate_back_kernel, group, states, ranked + states), "gate_back", group,
+        [(d_mix_own, ANY), (wout, None), (y_full, 0), (z, 0), (u_f, 0), (projected, 0), (step_size, 0),
          (cut, 0), (a_mat, None)],
         [(vec, F32, 0), ((group, rows, padded), BF16, 0), ((1, padded), F32, None),
-         (seg_states, F32, 0), (seg_sums, F32, 0), (dev_states, BF16, 0)],
-        [spread_vmem, lane_vmem, state_vmem], 11,
+         (seg_states, F32, 0), (seg_sums, F32, 0), (dev_states, BF16, 0), ((group, length, width), BF16, 0)],
+        [spread_vmem, lane_vmem, state_vmem, pltpu.VMEM((group, length, width), BF16),
+         dma((group - 1,)), dma((group - 1,)), dma], 28, 7, VMEM_LIMIT,
+        lambda s: lax.rem(lax.axis_index("wa") + group - s, group),
     )
     flat_n1 = n1.reshape(group * rows, width)
     zo_shape = (ring // 2, 2, in_rows, 2 * padded)

time: 393 us -> 393 us (level)
  Pallas kernels: 357 us -> 349 us
  local copies, waits for them, and re-layouts: 20.8 us -> 27.6 us
    pallas_call x1 -> x0, Pallas kernels: 28.2 us -> none  [gather_all(): pl.pallas_call(functools.partial(gather_kernel, axis, count, arrays), out...]
    pallas_call x11, Pallas kernels: 123 us -> 144 us  [call(): pl.pallas_call(kernel, grid=(grid,), out_shape=[jax.ShapeDtypeStruct(shap...]
    unnamed x142 -> x146, local copies, waits for them, and re-layouts: 17.6 us -> 24.5 us
  transfers between devices with their start and end apart: 2 -> 2, of which waited for: 0 -> 0; matrix products, arithmetic and copies ran while one was open for 0% -> 0% of each run, Pallas kernels for 73% -> 71%
where the time goes in v8:
time: 393 us; the launch traced here: 392 us
  Pallas kernels  349 us (89%)
  local copies, waits for them, and re-layouts  27.6 us (7%)
  between operations  15 us (4%)
    pallas_call x11, Pallas kernels, call(): pl.pallas_call(kernel, grid=(grid,), out_shape=[jax.ShapeDtypeStruct(shap...  144 us
    pallas_call x1, Pallas kernels, middle(): pl.pallas_call(functools.partial(middle_kernel, experts, group, chunks),...  57.2 us
    pallas_call x1, Pallas kernels, finish(): pl.pallas_call(functools.partial(finish_kernel, ring, group, in_rows, sma...  53.4 us
    pallas_call x1, Pallas kernels, start(): pl.pallas_call(functools.partial(start_kernel, ring, group), out_shape=[j...  46.5 us
    pallas_call x2, Pallas kernels, carry(): pl.pallas_call(functools.partial(carry_kernel, ring, arrays, len(xs) - ar...  27.7 us
    unnamed x146, local copies, waits for them, and re-layouts  24.5 us
    pallas_call x2, Pallas kernels, sum_all(): pl.pallas_call(functools.partial(sum_all_kernel, group), out_shape=jax.Sh...  20.6 us
  transfers between devices with their start and end apart: 2, of which 0 were waited for; matrix products, arithmetic and copies ran while one was open for 0% of the time, Pallas kernels for 71%

profile of v8, /device:TPU:11, one launch (start us, length us, event | category | flops | bytes accessed | tf_op | source)
XLA Modules:
  0.0 391.9 jit_solution(6387059264249706544)
XLA Ops:
  7.2 3.3 pack.1
  12.8 46.5 %start.1 = (bf16[4,128,1152]{2,1,0:T(8,128)(2,1)S(1)}, bf16[4,16,1152]{2,1,0:T(8,128)(2,1)S(1)}, bf16[4,16,384]{2,1,0:T(8,128)(2,1)S(1)}, s32[4,8,128]{2,1,0:T(8,128)S(1)}, bf16[2,8,144,640]{3,2,1,0:T(8,128)(2,1)S(1)}) custom-call(bf16[128,1152]{1,0:T(8,128)(2,1)S(1)} %bitcast.29, bf16[16,384]{1,0:T(8,128)(2,1)S(1)} %pad.17.par.own, s32[8,128]{1,0:T(8,128)S(1)} %pad.18.doc, ...), custom_call_target="tpu_custom_call" | custom-call | flops 38499999744 | bytes 122500000 | tf_op jit(solution)/shard_map/start/pallas_call | solution.py:633
  60.9 6.4 %enter.1 = (bf16[4,144,1152]{2,1,0:T(8,128)(2,1)S(1)}, f32[4,152,640]{2,1,0:T(8,128)S(1)}, f32[4,128,640]{2,1,0:T(8,128)S(1)}, f32[4,128,640]{2,1,0:T(8,128)S(1)...) custom-call(s32[1]{0:T(128)} %bitcast.1.place_ref, ...), custom_call_target="tpu_custom_call" | custom-call | flops 8800000000 | bytes 28000000 | tf_op jit(solution)/shard_map/enter/pallas_call | solution.py:1705
  68.2 10.8 %sum_all.2.proj_i.proj = bf16[4,128,128]{2,1,0:T(8,128)(2,1)S(1)} custom-call(bf16[4,128,128]{2,1,0:T(8,128)(2,1)S(1)} %get-tuple-element.102.x_ref), custom_call_target="tpu_custom_call" | custom-call | flops 12099999744 | bytes 38500000 | tf_op jit(solution)/shard_map/sum_all/pallas_call | solution.py:143
  79.0 8.1 %scan_summary.1 = (f32[4,128,640]{2,1,0:T(8,128)S(1)}, f32[4,128,640]{2,1,0:T(8,128)S(1)}, f32[4,16,8,640]{3,2,1,0:T(8,128)S(1)}, f32[4,8,640]{2,1,0:T(8,128)S(1...) custom-call(bf16[4,128,128]{2,1,0:T(8,128)(2,1)S(1)} %sum_all.2.proj_i.proj, ...), custom_call_target="tpu_custom_call" | custom-call | flops 11000000512 | bytes 35000000 | tf_op jit(solution)/shard_map/scan_summary/pallas_call | solution.py:1705
  87.2 14.8 %carry_3.1 = (bf16[8,4,16,640]{3,2,1,0:T(8,128)(2,1)S(1)}, f32[8,4,1,640]{3,2,1,0:T(1,128)S(1)}) custom-call(bf16[4,16,640]{2,1,0:T(8,128)(2,1)S(1)} %get-tuple-element.112.refs_0_, f32[4,1,640]{2,1,0:T(1,128)S(1)} %get-tuple-element.113.refs_1_), custom_call_target="tpu_custom_call" | custom-call | flops 11000000512 | bytes 35000000 | tf_op jit(solution)/shard_map/carry_3/pallas_call | solution.py:259
  102.2 31.2 %scan_output.1 = (f32[4,128,640]{2,1,0:T(8,128)S(1)}, bf16[4,128,640]{2,1,0:T(8,128)(2,1)S(1)}, bf16[4,128,1152]{2,1,0:T(8,128)(2,1)S(1)}, f32[4,16,640]{2,1,0:T(8,128)S(1)}) custom-call(bf16[4,128,128]{2,1,0:T(8,128)(2,1)S(1)} %sum_all.2.proj_i.proj, f32[4,128,640]{2,1,0:T(8,128)S(1)} %get-tuple-element.108.step_i, ...), custom_call_target="tpu_custom_call" | custom-call | flops 29699999744 | bytes 94500000 | tf_op jit(solution)/shard_map/scan_output/pallas_call | solution.py:1705
  137.5 57.2 %middle.1 = (bf16[3072,2304]{1,0:T(8,128)(2,1)}, f32[128,1152]{1,0:T(8,128)S(1)}, f32[128,1152]{1,0:T(8,128)S(1)}, bf16[128,1152]{1,0:T(8,128)(2,1)S(1)}, f32[12...) custom-call(bf16[4,128,1152]{2,1,0:T(8,128)(2,1)S(1)} %copy-done.51, ...), custom_call_target="tpu_custom_call" | custom-call | flops 93499998208 | bytes 297500000 | tf_op jit(solution)/shard_map/middle/pallas_call | solution.py:1341
  198.6 1.4 copy-done.13
  200.0 1.3 copy-done.21
  202.4 1.3 copy-done.32
  203.7 1.4 copy-done.49
  206.1 31.0 %gate_back.1 = (f32[4,128,640]{2,1,0:T(8,128)S(1)}, bf16[4,144,640]{2,1,0:T(8,128)(2,1)S(1)}, f32[1,640]{1,0:T(1,128)S(1)}, f32[4,16,8,640]{3,2,1,0:T(8,128)S(1)...) custom-call(bf16[128,1152]{1,0:T(8,128)(2,1)S(1)} %copy-done.61, ...), custom_call_target="tpu_custom_call" | custom-call | flops 30799998976 | bytes 98000000 | tf_op jit(solution)/shard_map/gate_back/pallas_call | solution.py:1705
  237.2 2.4 pack_zo.1.refs_1_.g_ref
  239.7 12.9 %carry_8.1 = (bf16[8,4,16,640]{3,2,1,0:T(8,128)(2,1)S(1)}, bf16[4,144,1280]{2,1,0:T(8,128)(2,1)S(1)}) custom-call(bf16[4,16,640]{2,1,0:T(8,128)(2,1)S(1)} %get-tuple-element.126.refs_0_, bf16[4,2,144,1280]{3,2,1,0:T(8,128)(2,1)S(1)} %pack_zo.1.refs_1_.g_ref), custom_call_target="tpu_custom_call" | custom-call | flops 11000000512 | bytes 35000000 | tf_op jit(solution)/shard_map/carry_8/pallas_call | solution.py:259
  252.7 43.0 %scan_back.1 = (bf16[4,128,128]{2,1,0:T(8,128)(2,1)S(1)}, f32[4,128,640]{2,1,0:T(8,128)S(1)}, f32[128,640]{1,0:T(8,128)S(1)}, f32[1,640]{1,0:T(1,128)S(1)}, f32[...) custom-call(bf16[4,128,128]{2,1,0:T(8,128)(2,1)S(1)} %copy-done.53, f32[4,128,640]{2,1,0:T(8,128)S(1)} %copy-done.33, ...), custom_call_target="tpu_custom_call" | custom-call | flops 37399998464 | bytes 119000000 | tf_op jit(solution)/shard_map/scan_back/pallas_call | solution.py:1705
  295.7 9.8 %sum_all.3.proj_i = bf16[4,128,128]{2,1,0:T(8,128)(2,1)S(1)} custom-call(bf16[4,128,128]{2,1,0:T(8,128)(2,1)S(1)} %get-tuple-element.132.x_ref), custom_call_target="tpu_custom_call" | custom-call | flops 12099999744 | bytes 38500000 | tf_op jit(solution)/shard_map/sum_all/pallas_call | solution.py:143
  305.6 7.3 %conv_back.1 = (bf16[4,144,640]{2,1,0:T(8,128)(2,1)S(1)}, bf16[4,144,1152]{2,1,0:T(8,128)(2,1)S(1)}, f32[8,640]{1,0:T(8,128)S(1)}, f32[128,640]{1,0:T(8,128)S(1)}, f32[1,1152]{1,0:T(1,128)S(1)}) custom-call(s32[1]{0:T(128)} %bitcast.1.place_ref, s32[4,8,128]{2,1,0:T(8,128)S(1)} %copy-done.59, bf16[4,128,128]{2,1,0:T(8,128)(2,1)S(1)} %sum_all.3.proj_i, ...), custom_call_target="tpu_custom_call" | custom-call | flops 11000000512 | bytes 35000000 | tf_op jit(solution)/shard_map/conv_back/pallas_call | solution.py:1705
  313.0 1.6 pack_rest.1.g_ref
  314.6 53.4 %finish.1 = (bf16[8,480,640]{2,1,0:T(8,128)(2,1)S(1)}, bf16[4,144,1152]{2,1,0:T(8,128)(2,1)S(1)}, bf16[4,16,1152]{2,1,0:T(8,128)(2,1)S(1)}) custom-call(bf16[4,2,192,640]{3,2,1,0:T(8,128)(2,1)S(1)} %pack_rest.1.g_ref, bf16[144,1280]{1,0:T(8,128)(2,1)S(1)} %get-tuple-element.149.zf_ref, bf16[4,144,1152]{2,1,0:T(8,128)(2,1)S(1)} %get-tuple-element.150.d_ref), custom_call_target="tpu_custom_call" | custom-call | flops 65999998976 | bytes 210000000 | tf_op jit(solution)/shard_map/finish/pallas_call | solution.py:470
  368.0 2.2 copy-done.14
  370.3 1.5 copy-done
  371.7 2.4 copy-done.15
  374.1 9.1 %unpack.1 = (f32[1152,1152]{1,0:T(8,128)}, f32[576,1152]{1,0:T(8,128)}, f32[1152,384]{1,0:T(8,128)}, f32[384,1152]{1,0:T(8,128)}, f32[4,576]{1,0:T(4,128)}, /*in...) custom-call(s32[1]{0:T(128)} %bitcast.mine_ref, ...), custom_call_target="tpu_custom_call" | custom-call | flops 9900000256 | bytes 31500000 | tf_op jit(solution)/shard_map/unpack/pallas_call | solution.py:1705
  (156 shorter events, 16.6 us)
Async XLA Ops:
  7.2 129.0 %all-gather.2.cloned.1.call-start = ((), (), s32[]{:S(2)}) async-start(), calls=%async_computation.1 | async-start | bytes 15925248 | tf_op jit(solution)/shard_map/all_gather | solution.py:1759
  10.6 359.6 %reduce-scatter.2.cloned.1.call-start = ((), (), s32[]{:S(2)}) async-start(), calls=%async_computation.2 | async-start | bytes 15925248 | tf_op jit(solution)/shard_map/reduce_scatter | solution.py:1828
  12.8 46.6 %copy-start.1 = (bf16[576,1152]{1,0:T(8,128)(2,1)S(1)}, bf16[576,1152]{1,0:T(8,128)(2,1)}, u32[]{:S(2)}) copy-start(bf16[576,1152]{1,0:T(8,128)(2,1)} %wout.1) | copy-start | bytes 3981316
  12.8 46.6 %copy-start.4 = (bf16[576,104]{0,1:T(8,128)(2,1)S(1)}, bf16[576,104]{0,1:T(8,128)(2,1)}, u32[]{:S(2)}) copy-start(bf16[576,104]{0,1:T(8,128)(2,1)} %param.28) | copy-start | bytes 359428
  12.8 46.5 %copy-start.5 = (bf16[72,576]{1,0:T(8,128)(2,1)S(1)}, bf16[72,576]{1,0:T(8,128)(2,1)}, u32[]{:S(2)}) copy-start(bf16[72,576]{1,0:T(8,128)(2,1)} %wdt.1) | copy-start | bytes 248836
  12.8 46.5 %copy-start.6 = (bf16[16,576]{1,0:T(8,128)(2,1)S(1)}, bf16[16,576]{1,0:T(8,128)(2,1)}, u32[]{:S(2)}) copy-start(bf16[16,576]{1,0:T(8,128)(2,1)} %a_log.1) | copy-start | bytes 55300
  12.8 46.5 %copy-start.7 = (bf16[4,576]{1,0:T(4,128)(2,1)S(1)}, bf16[4,576]{1,0:T(4,128)(2,1)}, u32[]{:S(2)}) copy-start(bf16[4,576]{1,0:T(4,128)(2,1)} %conv_w.1) | copy-start | bytes 13828
  59.6 19.4 %copy-start.25 = (bf16[128,640]{1,0:T(8,128)(2,1)}, bf16[128,640]{1,0:T(8,128)(2,1)S(1)}, u32[]{:S(2)}) copy-start(bf16[128,640]{1,0:T(8,128)(2,1)S(1)} %get-tuple-element.103.wdt) | copy-start | bytes 491524
  59.6 42.4 %copy-start.12 = (bf16[640,1152]{1,0:T(8,128)(2,1)}, bf16[640,1152]{1,0:T(8,128)(2,1)S(1)}, u32[]{:S(2)}) copy-start(bf16[640,1152]{1,0:T(8,128)(2,1)S(1)} %get-tuple-element.117.wout) | copy-start | bytes 4423684
  59.6 42.4 %copy-start.46 = (f32[8,640]{1,0:T(8,128)}, f32[8,640]{1,0:T(8,128)S(1)}, u32[]{:S(2)}) copy-start(f32[8,640]{1,0:T(8,128)S(1)} %get-tuple-element.104.bias.skip) | copy-start | bytes 61444
  68.2 33.9 %copy-start.20 = (f32[4,128,640]{2,1,0:T(8,128)}, f32[4,128,640]{2,1,0:T(8,128)S(1)}, u32[]{:S(2)}) copy-start(f32[4,128,640]{2,1,0:T(8,128)S(1)} %get-tuple-element.105.uf) | copy-start | bytes 3932164
  68.2 33.9 %copy-start.29 = (bf16[4,128,640]{2,1,0:T(8,128)(2,1)}, bf16[4,128,640]{2,1,0:T(8,128)(2,1)S(1)}, u32[]{:S(2)}) copy-start(bf16[4,128,640]{2,1,0:T(8,128)(2,1)S(1)} %get-tuple-element.116.z) | copy-start | bytes 1966084
  68.2 33.9 %copy-start.42 = (f32[4,128,128]{2,1,0:T(8,128)}, f32[4,128,128]{2,1,0:T(8,128)S(1)}, u32[]{:S(2)}) copy-start(f32[4,128,128]{2,1,0:T(8,128)S(1)} %get-tuple-element.106.cut) | copy-start | bytes 786436
  79.0 23.1 %copy-start.52 = (bf16[4,128,128]{2,1,0:T(8,128)(2,1)}, bf16[4,128,128]{2,1,0:T(8,128)(2,1)S(1)}, u32[]{:S(2)}) copy-start(bf16[4,128,128]{2,1,0:T(8,128)(2,1)S(1)} %sum_all.2.proj_i.proj) | copy-start | bytes 393220
  87.1 14.9 %copy-start.34 = (f32[4,128,640]{2,1,0:T(8,128)}, f32[4,128,640]{2,1,0:T(8,128)S(1)}, u32[]{:S(2)}) copy-start(f32[4,128,640]{2,1,0:T(8,128)S(1)} %get-tuple-element.109.sig) | copy-start | bytes 3932164
  87.2 14.9 %copy-start.31 = (f32[4,128,640]{2,1,0:T(8,128)}, f32[4,128,640]{2,1,0:T(8,128)S(1)}, u32[]{:S(2)}) copy-start(f32[4,128,640]{2,1,0:T(8,128)S(1)} %get-tuple-element.108.step_i) | copy-start | bytes 3932164
  87.2 14.9 %copy-start.36 = (f32[4,16,8,640]{3,2,1,0:T(8,128)}, f32[4,16,8,640]{3,2,1,0:T(8,128)S(1)}, u32[]{:S(2)}) copy-start(f32[4,16,8,640]{3,2,1,0:T(8,128)S(1)} %get-tuple-element.110.hx_ref) | copy-start | bytes 3932164
  87.2 14.9 %copy-start.54 = (f32[4,8,640]{2,1,0:T(8,128)}, f32[4,8,640]{2,1,0:T(8,128)S(1)}, u32[]{:S(2)}) copy-start(f32[4,8,640]{2,1,0:T(8,128)S(1)} %get-tuple-element.111.sx_ref) | copy-start | bytes 245764
  102.0 31.4 %copy-start.56 = (f32[8,4,1,640]{3,2,1,0:T(1,128)}, f32[8,4,1,640]{3,2,1,0:T(1,128)S(1)}, u32[]{:S(2)}) copy-start(f32[8,4,1,640]{3,2,1,0:T(1,128)S(1)} %get-tuple-element.115.sums) | copy-start | bytes 245764
  102.1 34.1 %copy-start.2 = (bf16[1,128,1152]{2,1,0:T(8,128)(2,1)S(1)}, bf16[1,128,1152]{2,1,0:T(8,128)(2,1)}, u32[]{:S(2)}) copy-start(bf16[1,128,1152]{2,1,0:T(8,128)(2,1)} %param.20) | copy-start | bytes 884740
  102.1 34.1 %copy-start.8 = (s32[1,128,1]{1,2,0:T(1,128)S(1)}, s32[1,128,1]{1,2,0:T(1,128)}, u32[]{:S(2)}) copy-start(s32[1,128,1]{1,2,0:T(1,128)} %param.22) | copy-start | bytes 1540
  102.2 34.0 %copy-start.9 = (s32[1,128]{1,0:T(1,128)S(1)}, s32[1,128]{1,0:T(1,128)}, u32[]{:S(2)}) copy-start(s32[1,128]{1,0:T(1,128)} %keep.1) | copy-start | bytes 1540
  314.6 55.7 %copy-start.39 = (f32[128,1152]{1,0:T(8,128)S(1)}, f32[128,1152]{1,0:T(8,128)}, u32[]{:S(2)}) copy-start(f32[128,1152]{1,0:T(8,128)} %copy-done.38) | copy-start | bytes 1769476
  314.6 55.7 %copy-start.41 = (f32[128,1152]{1,0:T(8,128)S(1)}, f32[128,1152]{1,0:T(8,128)}, u32[]{:S(2)}) copy-start(f32[128,1152]{1,0:T(8,128)} %copy-done.40) | copy-start | bytes 1769476
  (51 other events, 264.6 us)
Sparse Core Ops, SparseCore 0:
  10.8 100.0 all-gather.1
  197.8 120.0 reduce-scatter.1

commit v9 on v8

--- a/solution.py
+++ b/solution.py
@@ -13,6 +13,7 @@
 SEG = 8
 LANE = 128
 EDGE = 16
+LOG2E = 1.4426950408889634
 CUT = 1e30
 MESH = pl.DeviceIdType.MESH
 VMEM_LIMIT = 24 * 2**20
@@ -815,6 +816,7 @@
     def group(g, _):
         lanes = lanes_of(g)
         a = [wide(a_ref, n, lanes) for n in range(states)]
+        a_two = [LOG2E * value for value in a]
 
         def step(j, carry):
             rows = rows_of(j)
@@ -822,7 +824,7 @@
             dr = dr_s[rows, lanes]
             new = [carry[0] + st]
             for n in range(states):
-                new.append(jnp.exp(st * a[n]) * carry[n + 1] + bb[rows, state_cols(n)] * dr)
+                new.append(jnp.exp2(st * a_two[n]) * carry[n + 1] + bb[rows, state_cols(n)] * dr)
             return tuple(new)
 
         out = lax.fori_loop(0, steps, step, (zero,) * (states + 1), unroll=8)
@@ -893,6 +895,7 @@
     def lane_group(g, _):
         lanes = lanes_of(g)
         a = [wide(a_ref, n, lanes) for n in range(states)]
+        a_two = [LOG2E * value for value in a]
         sx = sx_ref[0, :, lanes]
         first = tuple(
             jnp.exp(sx * a[n]) * wide(e_ref, n, lanes) + hx_ref[0, n, :, lanes]
@@ -907,7 +910,7 @@
             new = []
             y = gain * uf[0, rows, lanes]
             for n in range(states):
-                state = jnp.exp(st * a[n]) * h[n] + bb[rows, state_cols(n)] * dr
+                state = jnp.exp2(st * a_two[n]) * h[n] + bb[rows, state_cols(n)] * dr
                 new.append(state)
                 y = y + cb[rows, state_cols(n)] * state
             y_o[0, rows, lanes] = y
@@ -1454,6 +1457,7 @@
     def group(g, _):
         lanes = lanes_of(g)
         a = [wide(a_ref, n, lanes) for n in range(states)]
+        a_two = [LOG2E * value for value in a]
 
         def step(lap, carry):
             rows = rows_of(steps - 1 - lap)
@@ -1461,7 +1465,7 @@
             d = dy_o[0, rows, lanes]
             new = [carry[0] + st]
             for n in range(states):
-                new.append(jnp.exp(st * a[n]) * (carry[n + 1] + cb[rows, state_cols(n)] * d))
+                new.append(jnp.exp2(st * a_two[n]) * (carry[n + 1] + cb[rows, state_cols(n)] * d))
             return tuple(new)
 
         out = lax.fori_loop(0, steps, step, (zero,) * (states + 1), unroll=8)
@@ -1549,6 +1553,7 @@
     def group(g, _):
         lanes = lanes_of(g)
         a = [wide(a_ref, n, lanes) for n in range(states)]
+        a_two = [LOG2E * value for value in a]
         sx = sx_ref[0, :, lanes]
         first = tuple(
             jnp.exp(sx * a[n]) * wide(e_ref, n, lanes) + hx_ref[0, n, :, lanes]
@@ -1561,7 +1566,7 @@
             dr = dr_s[rows, lanes]
             new = []
             for n in range(states):
-                decay = jnp.exp(st * a[n])
+                decay = jnp.exp2(st * a_two[n])
                 dec[rows, state_cols(n)] = decay
                 pri[rows, state_cols(n)] = h[n]
                 new.append(decay * h[n] + bb[rows, state_cols(n)] * dr)

time: 393 us -> 392 us (level)
  no operation moved by 1% of the time
where the time goes in v9:
time: 392 us
  Pallas kernels  349 us (89%)
  local copies, waits for them, and re-layouts  27.6 us (7%)
  between operations  15 us (4%)
    pallas_call x11, Pallas kernels, call(): pl.pallas_call(kernel, grid=(grid,), out_shape=[jax.ShapeDtypeStruct(shap...  144 us
    pallas_call x1, Pallas kernels, middle(): pl.pallas_call(functools.partial(middle_kernel, experts, group, chunks),...  57.2 us
    pallas_call x1, Pallas kernels, finish(): pl.pallas_call(functools.partial(finish_kernel, ring, group, in_rows, sma...  53.2 us
    pallas_call x1, Pallas kernels, start(): pl.pallas_call(functools.partial(start_kernel, ring, group), out_shape=[j...  46.5 us
    pallas_call x2, Pallas kernels, carry(): pl.pallas_call(functools.partial(carry_kernel, ring, arrays, len(xs) - ar...  27.7 us
    unnamed x146, local copies, waits for them, and re-layouts  24.5 us
    pallas_call x2, Pallas kernels, sum_all(): pl.pallas_call(functools.partial(sum_all_kernel, group), out_shape=jax.Sh...  20.7 us
  transfers between devices with their start and end apart: 2, of which 0 were waited for; matrix products, arithmetic and copies ran while one was open for 0% of the time, Pallas kernels for 71%

profile of v9, /device:TPU:11, one launch (start us, length us, event | category | flops | bytes accessed | tf_op | source)
XLA Modules:
  0.0 391.6 jit_solution(5919250473837164361)
XLA Ops:
  7.2 3.3 pack.1
  12.8 46.5 %start.1 = (bf16[4,128,1152]{2,1,0:T(8,128)(2,1)S(1)}, bf16[4,16,1152]{2,1,0:T(8,128)(2,1)S(1)}, bf16[4,16,384]{2,1,0:T(8,128)(2,1)S(1)}, s32[4,8,128]{2,1,0:T(8,128)S(1)}, bf16[2,8,144,640]{3,2,1,0:T(8,128)(2,1)S(1)}) custom-call(bf16[128,1152]{1,0:T(8,128)(2,1)S(1)} %bitcast.29, bf16[16,384]{1,0:T(8,128)(2,1)S(1)} %pad.17.par.own, s32[8,128]{1,0:T(8,128)S(1)} %pad.18.doc, ...), custom_call_target="tpu_custom_call" | custom-call | flops 38499999744 | bytes 122500000 | tf_op jit(solution)/shard_map/start/pallas_call | solution.py:634
  60.9 6.4 %enter.1 = (bf16[4,144,1152]{2,1,0:T(8,128)(2,1)S(1)}, f32[4,152,640]{2,1,0:T(8,128)S(1)}, f32[4,128,640]{2,1,0:T(8,128)S(1)}, f32[4,128,640]{2,1,0:T(8,128)S(1)...) custom-call(s32[1]{0:T(128)} %bitcast.1.place_ref, ...), custom_call_target="tpu_custom_call" | custom-call | flops 8800000000 | bytes 28000000 | tf_op jit(solution)/shard_map/enter/pallas_call | solution.py:1710
  68.2 10.8 %sum_all.2.proj_i.proj = bf16[4,128,128]{2,1,0:T(8,128)(2,1)S(1)} custom-call(bf16[4,128,128]{2,1,0:T(8,128)(2,1)S(1)} %get-tuple-element.102.x_ref), custom_call_target="tpu_custom_call" | custom-call | flops 12099999744 | bytes 38500000 | tf_op jit(solution)/shard_map/sum_all/pallas_call | solution.py:144
  79.0 8.0 %scan_summary.1 = (f32[4,128,640]{2,1,0:T(8,128)S(1)}, f32[4,128,640]{2,1,0:T(8,128)S(1)}, f32[4,16,8,640]{3,2,1,0:T(8,128)S(1)}, f32[4,8,640]{2,1,0:T(8,128)S(1...) custom-call(bf16[4,128,128]{2,1,0:T(8,128)(2,1)S(1)} %sum_all.2.proj_i.proj, ...), custom_call_target="tpu_custom_call" | custom-call | flops 11000000512 | bytes 35000000 | tf_op jit(solution)/shard_map/scan_summary/pallas_call | solution.py:1710
  87.1 14.8 %carry_3.1 = (bf16[8,4,16,640]{3,2,1,0:T(8,128)(2,1)S(1)}, f32[8,4,1,640]{3,2,1,0:T(1,128)S(1)}) custom-call(bf16[4,16,640]{2,1,0:T(8,128)(2,1)S(1)} %get-tuple-element.112.refs_0_, f32[4,1,640]{2,1,0:T(1,128)S(1)} %get-tuple-element.113.refs_1_), custom_call_target="tpu_custom_call" | custom-call | flops 11000000512 | bytes 35000000 | tf_op jit(solution)/shard_map/carry_3/pallas_call | solution.py:260
  102.1 31.2 %scan_output.1 = (f32[4,128,640]{2,1,0:T(8,128)S(1)}, bf16[4,128,640]{2,1,0:T(8,128)(2,1)S(1)}, bf16[4,128,1152]{2,1,0:T(8,128)(2,1)S(1)}, f32[4,16,640]{2,1,0:T(8,128)S(1)}) custom-call(bf16[4,128,128]{2,1,0:T(8,128)(2,1)S(1)} %sum_all.2.proj_i.proj, f32[4,128,640]{2,1,0:T(8,128)S(1)} %get-tuple-element.108.step_i, ...), custom_call_target="tpu_custom_call" | custom-call | flops 29699999744 | bytes 94500000 | tf_op jit(solution)/shard_map/scan_output/pallas_call | solution.py:1710
  137.4 57.2 %middle.1 = (bf16[3072,2304]{1,0:T(8,128)(2,1)}, f32[128,1152]{1,0:T(8,128)S(1)}, f32[128,1152]{1,0:T(8,128)S(1)}, bf16[128,1152]{1,0:T(8,128)(2,1)S(1)}, f32[12...) custom-call(bf16[4,128,1152]{2,1,0:T(8,128)(2,1)S(1)} %copy-done.51, ...), custom_call_target="tpu_custom_call" | custom-call | flops 93499998208 | bytes 297500000 | tf_op jit(solution)/shard_map/middle/pallas_call | solution.py:1344
  198.6 1.4 copy-done.13
  200.0 1.3 copy-done.21
  202.4 1.3 copy-done.32
  203.7 1.4 copy-done.49
  206.1 31.0 %gate_back.1 = (f32[4,128,640]{2,1,0:T(8,128)S(1)}, bf16[4,144,640]{2,1,0:T(8,128)(2,1)S(1)}, f32[1,640]{1,0:T(1,128)S(1)}, f32[4,16,8,640]{3,2,1,0:T(8,128)S(1)...) custom-call(bf16[128,1152]{1,0:T(8,128)(2,1)S(1)} %copy-done.61, ...), custom_call_target="tpu_custom_call" | custom-call | flops 30799998976 | bytes 98000000 | tf_op jit(solution)/shard_map/gate_back/pallas_call | solution.py:1710
  237.1 2.4 pack_zo.1.refs_1_.g_ref
  239.6 12.9 %carry_8.1 = (bf16[8,4,16,640]{3,2,1,0:T(8,128)(2,1)S(1)}, bf16[4,144,1280]{2,1,0:T(8,128)(2,1)S(1)}) custom-call(bf16[4,16,640]{2,1,0:T(8,128)(2,1)S(1)} %get-tuple-element.126.refs_0_, bf16[4,2,144,1280]{3,2,1,0:T(8,128)(2,1)S(1)} %pack_zo.1.refs_1_.g_ref), custom_call_target="tpu_custom_call" | custom-call | flops 11000000512 | bytes 35000000 | tf_op jit(solution)/shard_map/carry_8/pallas_call | solution.py:260
  252.6 42.9 %scan_back.1 = (bf16[4,128,128]{2,1,0:T(8,128)(2,1)S(1)}, f32[4,128,640]{2,1,0:T(8,128)S(1)}, f32[128,640]{1,0:T(8,128)S(1)}, f32[1,640]{1,0:T(1,128)S(1)}, f32[...) custom-call(bf16[4,128,128]{2,1,0:T(8,128)(2,1)S(1)} %copy-done.53, f32[4,128,640]{2,1,0:T(8,128)S(1)} %copy-done.33, ...), custom_call_target="tpu_custom_call" | custom-call | flops 37399998464 | bytes 119000000 | tf_op jit(solution)/shard_map/scan_back/pallas_call | solution.py:1710
  295.6 9.9 %sum_all.3.proj_i = bf16[4,128,128]{2,1,0:T(8,128)(2,1)S(1)} custom-call(bf16[4,128,128]{2,1,0:T(8,128)(2,1)S(1)} %get-tuple-element.132.x_ref), custom_call_target="tpu_custom_call" | custom-call | flops 12099999744 | bytes 38500000 | tf_op jit(solution)/shard_map/sum_all/pallas_call | solution.py:144
  305.6 7.3 %conv_back.1 = (bf16[4,144,640]{2,1,0:T(8,128)(2,1)S(1)}, bf16[4,144,1152]{2,1,0:T(8,128)(2,1)S(1)}, f32[8,640]{1,0:T(8,128)S(1)}, f32[128,640]{1,0:T(8,128)S(1)}, f32[1,1152]{1,0:T(1,128)S(1)}) custom-call(s32[1]{0:T(128)} %bitcast.1.place_ref, s32[4,8,128]{2,1,0:T(8,128)S(1)} %copy-done.59, bf16[4,128,128]{2,1,0:T(8,128)(2,1)S(1)} %sum_all.3.proj_i, ...), custom_call_target="tpu_custom_call" | custom-call | flops 11000000512 | bytes 35000000 | tf_op jit(solution)/shard_map/conv_back/pallas_call | solution.py:1710
  312.9 1.6 pack_rest.1.g_ref
  314.5 53.2 %finish.1 = (bf16[8,480,640]{2,1,0:T(8,128)(2,1)S(1)}, bf16[4,144,1152]{2,1,0:T(8,128)(2,1)S(1)}, bf16[4,16,1152]{2,1,0:T(8,128)(2,1)S(1)}) custom-call(bf16[4,2,192,640]{3,2,1,0:T(8,128)(2,1)S(1)} %pack_rest.1.g_ref, bf16[144,1280]{1,0:T(8,128)(2,1)S(1)} %get-tuple-element.149.zf_ref, bf16[4,144,1152]{2,1,0:T(8,128)(2,1)S(1)} %get-tuple-element.150.d_ref), custom_call_target="tpu_custom_call" | custom-call | flops 65999998976 | bytes 210000000 | tf_op jit(solution)/shard_map/finish/pallas_call | solution.py:471
  367.7 2.2 copy-done.14
  370.0 1.5 copy-done
  371.4 2.4 copy-done.15
  373.8 9.1 %unpack.1 = (f32[1152,1152]{1,0:T(8,128)}, f32[576,1152]{1,0:T(8,128)}, f32[1152,384]{1,0:T(8,128)}, f32[384,1152]{1,0:T(8,128)}, f32[4,576]{1,0:T(4,128)}, /*in...) custom-call(s32[1]{0:T(128)} %bitcast.mine_ref, ...), custom_call_target="tpu_custom_call" | custom-call | flops 9900000256 | bytes 31500000 | tf_op jit(solution)/shard_map/unpack/pallas_call | solution.py:1710
  (156 shorter events, 16.6 us)
Async XLA Ops:
  7.2 129.0 %all-gather.2.cloned.1.call-start = ((), (), s32[]{:S(2)}) async-start(), calls=%async_computation.1 | async-start | bytes 15925248 | tf_op jit(solution)/shard_map/all_gather | solution.py:1764
  10.6 359.3 %reduce-scatter.2.cloned.1.call-start = ((), (), s32[]{:S(2)}) async-start(), calls=%async_computation.2 | async-start | bytes 15925248 | tf_op jit(solution)/shard_map/reduce_scatter | solution.py:1833
  12.8 46.6 %copy-start.1 = (bf16[576,1152]{1,0:T(8,128)(2,1)S(1)}, bf16[576,1152]{1,0:T(8,128)(2,1)}, u32[]{:S(2)}) copy-start(bf16[576,1152]{1,0:T(8,128)(2,1)} %wout.1) | copy-start | bytes 3981316
  12.8 46.6 %copy-start.4 = (bf16[576,104]{0,1:T(8,128)(2,1)S(1)}, bf16[576,104]{0,1:T(8,128)(2,1)}, u32[]{:S(2)}) copy-start(bf16[576,104]{0,1:T(8,128)(2,1)} %param.28) | copy-start | bytes 359428
  12.8 46.5 %copy-start.5 = (bf16[72,576]{1,0:T(8,128)(2,1)S(1)}, bf16[72,576]{1,0:T(8,128)(2,1)}, u32[]{:S(2)}) copy-start(bf16[72,576]{1,0:T(8,128)(2,1)} %wdt.1) | copy-start | bytes 248836
  12.8 46.5 %copy-start.6 = (bf16[16,576]{1,0:T(8,128)(2,1)S(1)}, bf16[16,576]{1,0:T(8,128)(2,1)}, u32[]{:S(2)}) copy-start(bf16[16,576]{1,0:T(8,128)(2,1)} %a_log.1) | copy-start | bytes 55300
  12.8 46.5 %copy-start.7 = (bf16[4,576]{1,0:T(4,128)(2,1)S(1)}, bf16[4,576]{1,0:T(4,128)(2,1)}, u32[]{:S(2)}) copy-start(bf16[4,576]{1,0:T(4,128)(2,1)} %conv_w.1) | copy-start | bytes 13828
  59.6 19.4 %copy-start.25 = (bf16[128,640]{1,0:T(8,128)(2,1)}, bf16[128,640]{1,0:T(8,128)(2,1)S(1)}, u32[]{:S(2)}) copy-start(bf16[128,640]{1,0:T(8,128)(2,1)S(1)} %get-tuple-element.103.wdt) | copy-start | bytes 491524
  59.6 42.4 %copy-start.12 = (bf16[640,1152]{1,0:T(8,128)(2,1)}, bf16[640,1152]{1,0:T(8,128)(2,1)S(1)}, u32[]{:S(2)}) copy-start(bf16[640,1152]{1,0:T(8,128)(2,1)S(1)} %get-tuple-element.117.wout) | copy-start | bytes 4423684
  59.6 42.4 %copy-start.46 = (f32[8,640]{1,0:T(8,128)}, f32[8,640]{1,0:T(8,128)S(1)}, u32[]{:S(2)}) copy-start(f32[8,640]{1,0:T(8,128)S(1)} %get-tuple-element.104.bias.skip) | copy-start | bytes 61444
  68.2 33.8 %copy-start.20 = (f32[4,128,640]{2,1,0:T(8,128)}, f32[4,128,640]{2,1,0:T(8,128)S(1)}, u32[]{:S(2)}) copy-start(f32[4,128,640]{2,1,0:T(8,128)S(1)} %get-tuple-element.105.uf) | copy-start | bytes 3932164
  68.2 33.8 %copy-start.29 = (bf16[4,128,640]{2,1,0:T(8,128)(2,1)}, bf16[4,128,640]{2,1,0:T(8,128)(2,1)S(1)}, u32[]{:S(2)}) copy-start(bf16[4,128,640]{2,1,0:T(8,128)(2,1)S(1)} %get-tuple-element.116.z) | copy-start | bytes 1966084
  68.2 33.8 %copy-start.42 = (f32[4,128,128]{2,1,0:T(8,128)}, f32[4,128,128]{2,1,0:T(8,128)S(1)}, u32[]{:S(2)}) copy-start(f32[4,128,128]{2,1,0:T(8,128)S(1)} %get-tuple-element.106.cut) | copy-start | bytes 786436
  79.0 23.0 %copy-start.52 = (bf16[4,128,128]{2,1,0:T(8,128)(2,1)}, bf16[4,128,128]{2,1,0:T(8,128)(2,1)S(1)}, u32[]{:S(2)}) copy-start(bf16[4,128,128]{2,1,0:T(8,128)(2,1)S(1)} %sum_all.2.proj_i.proj) | copy-start | bytes 393220
  87.1 14.9 %copy-start.34 = (f32[4,128,640]{2,1,0:T(8,128)}, f32[4,128,640]{2,1,0:T(8,128)S(1)}, u32[]{:S(2)}) copy-start(f32[4,128,640]{2,1,0:T(8,128)S(1)} %get-tuple-element.109.sig) | copy-start | bytes 3932164
  87.1 14.9 %copy-start.31 = (f32[4,128,640]{2,1,0:T(8,128)}, f32[4,128,640]{2,1,0:T(8,128)S(1)}, u32[]{:S(2)}) copy-start(f32[4,128,640]{2,1,0:T(8,128)S(1)} %get-tuple-element.108.step_i) | copy-start | bytes 3932164
  87.1 14.9 %copy-start.36 = (f32[4,16,8,640]{3,2,1,0:T(8,128)}, f32[4,16,8,640]{3,2,1,0:T(8,128)S(1)}, u32[]{:S(2)}) copy-start(f32[4,16,8,640]{3,2,1,0:T(8,128)S(1)} %get-tuple-element.110.hx_ref) | copy-start | bytes 3932164
  87.1 14.9 %copy-start.54 = (f32[4,8,640]{2,1,0:T(8,128)}, f32[4,8,640]{2,1,0:T(8,128)S(1)}, u32[]{:S(2)}) copy-start(f32[4,8,640]{2,1,0:T(8,128)S(1)} %get-tuple-element.111.sx_ref) | copy-start | bytes 245764
  102.0 31.4 %copy-start.56 = (f32[8,4,1,640]{3,2,1,0:T(1,128)}, f32[8,4,1,640]{3,2,1,0:T(1,128)S(1)}, u32[]{:S(2)}) copy-start(f32[8,4,1,640]{3,2,1,0:T(1,128)S(1)} %get-tuple-element.115.sums) | copy-start | bytes 245764
  102.1 34.1 %copy-start.2 = (bf16[1,128,1152]{2,1,0:T(8,128)(2,1)S(1)}, bf16[1,128,1152]{2,1,0:T(8,128)(2,1)}, u32[]{:S(2)}) copy-start(bf16[1,128,1152]{2,1,0:T(8,128)(2,1)} %param.20) | copy-start | bytes 884740
  102.1 34.1 %copy-start.8 = (s32[1,128,1]{1,2,0:T(1,128)S(1)}, s32[1,128,1]{1,2,0:T(1,128)}, u32[]{:S(2)}) copy-start(s32[1,128,1]{1,2,0:T(1,128)} %param.22) | copy-start | bytes 1540
  102.1 34.1 %copy-start.9 = (s32[1,128]{1,0:T(1,128)S(1)}, s32[1,128]{1,0:T(1,128)}, u32[]{:S(2)}) copy-start(s32[1,128]{1,0:T(1,128)} %keep.1) | copy-start | bytes 1540
  314.5 55.4 %copy-start.39 = (f32[128,1152]{1,0:T(8,128)S(1)}, f32[128,1152]{1,0:T(8,128)}, u32[]{:S(2)}) copy-start(f32[128,1152]{1,0:T(8,128)} %copy-done.38) | copy-start | bytes 1769476
  314.5 55.4 %copy-start.41 = (f32[128,1152]{1,0:T(8,128)S(1)}, f32[128,1152]{1,0:T(8,128)}, u32[]{:S(2)}) copy-start(f32[128,1152]{1,0:T(8,128)} %copy-done.40) | copy-start | bytes 1769476
  (51 other events, 265.0 us)
Sparse Core Ops, SparseCore 0:
  10.8 100.0 all-gather.1
  197.8 120.0 reduce-scatter.1
